TPU v7x, 32 devices: a whole 2x2x4 slice. The times are simulated.
32 devices in a mesh: node: 8 (over z, core), local: 4 (over y, x).
Axes of the slice: x: 2, y: 2, z: 4, core: 2. Of those that a mesh axis runs over, the one named last changes fastest.
Arguments:
- tokens: bfloat16 [512, 4096], P('local', 'node'), may hold values from -6 to 6
- gate_up_codes: bfloat16 [2, 4096, 14336], P(None, 'local', 'node'), may hold values from -127 to 127
- gate_up_scales: bfloat16 [2, 32, 14336], P(None, 'local', 'node'), may hold values from 2.9921532e-05 to 0.00029945374
- d_hidden: bfloat16 [512, 14336], P('local', 'node'), may hold values from -6 to 6
Outputs:
- hidden: bfloat16 [512, 14336], P('local', 'node')
- d_tokens: bfloat16 [512, 4096], P('local', 'node')
- grad_gate_up: float32 [2, 4096, 14336], P(None, 'local', 'node')
All inputs are finite; a program needn't handle non-finite values.
Results may differ from a plain program's by a relative error of at most 0.023.
Values may be sent and summed in bfloat16 or wider, within the bound.
No kernel may reach another device: no remote copies, remote signals or barrier semaphores. Data moves between devices by JAX's collectives and lax.ppermute only.
A program may use at most 128 MiB of HBM per device.

v0:
```python
import math

import jax
import jax.numpy as jnp
from jax import lax
from jax.sharding import PartitionSpec as P

BLOCK = 128


def dequant(codes, scales):
    shape = codes.shape
    blocked = codes.astype(jnp.float32).reshape(shape[:-2] + (shape[-2] // BLOCK, BLOCK, shape[-1]))
    weight = blocked * scales.astype(jnp.float32)[..., :, None, :]
    return weight.reshape(shape).astype(jnp.bfloat16)


def body(tokens, gate_up_codes, gate_up_scales, d_hidden):
    rows = tokens.shape[0]
    local_count = lax.axis_size("local")
    features = lax.all_gather(tokens, "node", axis=1, tiled=True)
    width = features.shape[1]
    all_codes, all_scales = (
        lax.all_gather(gate_up_codes, "local", axis=1, tiled=True),
        lax.all_gather(gate_up_scales, "local", axis=1, tiled=True),
    )
    w_gu = dequant(all_codes, all_scales)
    group = w_gu.shape[2]
    gate = jnp.dot(features, w_gu[0], preferred_element_type=jnp.float32)
    up = jnp.dot(features, w_gu[1], preferred_element_type=jnp.float32)
    sigmoid_gate = jax.nn.sigmoid(gate)
    active = gate * sigmoid_gate
    hidden = (active * up).astype(jnp.bfloat16)
    grad_in = d_hidden.astype(jnp.float32)
    d_gate = (grad_in * up * sigmoid_gate * (1.0 + gate * (1.0 - sigmoid_gate))).astype(
        jnp.bfloat16
    )
    d_up = (grad_in * active).astype(jnp.bfloat16)
    term = lax.dot_general(
        d_gate, w_gu[0], (((1,), (1,)), ((), ())), preferred_element_type=jnp.float32
    )
    term = term + lax.dot_general(
        d_up, w_gu[1], (((1,), (1,)), ((), ())), preferred_element_type=jnp.float32
    )
    rounded = lax.optimization_barrier(term.astype(jnp.bfloat16)).astype(jnp.float32)
    d_tokens = lax.psum_scatter(
        rounded.astype(jnp.bfloat16), "node", scatter_dimension=1, tiled=True
    )
    factor = 1.0 / math.sqrt(rows * local_count)
    owned = width // local_count
    columns = lax.all_to_all(features, "local", split_axis=1, concat_axis=0, tiled=True)
    gate_all, up_all = (
        lax.all_gather(d_gate, "local", axis=0, tiled=True),
        lax.all_gather(d_up, "local", axis=0, tiled=True),
    )
    both_all = jnp.concatenate(
        [gate_all.reshape(local_count, rows, group), up_all.reshape(local_count, rows, group)],
        axis=2,
    )
    blocks = columns.reshape(local_count, rows, owned)
    numbers = (((1,), (1,)), ((0,), (0,)))
    partial_value = lax.dot_general(
        blocks, both_all, numbers, preferred_element_type=jnp.float32
    ).astype(jnp.bfloat16)
    summed = jnp.sum(partial_value.astype(jnp.float32), axis=0) * factor
    grads = summed.reshape(owned, 2, group).transpose(1, 0, 2)
    return (hidden, d_tokens, grads)


def solution(mesh):
    placed = (
        P("local", "node"),
        P(None, "local", "node"),
        P(None, "local", "node"),
        P("local", "node"),
    )
    return jax.shard_map(
        body,
        mesh=mesh,
        in_specs=placed,
        out_specs=(P("local", "node"), P("local", "node"), P(None, "local", "node")),
        check_vma=False,
    )
```

profile of v0, /device:TPU:0, one launch (start us, length us, event | category | flops | bytes accessed | tf_op | source)
XLA Modules:
  0.0 449.2 jit_solution(18105298593148176720)
XLA Ops:
  7.2 0.0 all-gather.5.cloned.1.call-start
  7.2 0.7 all-gather.5.cloned.1.call-update
  7.9 0.0 all-gather.7.cloned.1.call-start
  7.9 1.7 copy.11
  9.6 0.0 all-gather.7.cloned.1.call-update
  9.6 0.0 all-gather.11.cloned.1.call-start
  9.7 10.7 %all_gather.16 = bf16[2,32,1792]{2,1,0:T(8,128)(2,1)S(1)} all-gather(bf16[2,8,1792]{2,1,0:T(8,128)(2,1)} %param.6), channel_id=1, replica_groups=mesh['node'=8,'local'=4] {'local'}, dimensions={1}, use_global_device_ids=true | all-gather | bytes 286720 | tf_op jit(solution)/shard_map/all_gather | solution.py:25
  20.4 1.4 copy.12
  21.9 253.0 %all-gather.5.cloned.1.call-done = bf16[2,4096,1792]{2,1,0:T(8,128)(2,1)} async-done(((bf16[2,1024,1792]{2,1,0:T(8,128)(2,1)}), bf16[2,4096,1792]{2,1,0:T(8,128)(2,1)}) %all-gather.5.cloned.1.call-update) | async-done | bytes 29360144 | tf_op jit(solution)/shard_map/all_gather | solution.py:24
  274.9 20.7 %fusion = bf16[2,4096,1792]{2,1,0:T(8,128)(2,1)} fusion(bf16[2,4096,1792]{2,1,0:T(8,128)(2,1)} %all-gather.5.cloned.1.call-done, f32[2,32,1792]{2,1,0:T(8,128)S(1)} %convert_element_type.35), kind=kLoop, calls=%fused_computation.1 | loop fusion | flops 44040192 | bytes 59179008 | tf_op jit(solution)/shard_map/convert_element_type | solution.py:15
  295.6 3.6 all-gather.7.cloned.1.call-done
  299.2 9.5 %fusion.11 = f32[128,1792]{0,1:T(8,128)S(1)} fusion(bf16[128,4096]{0,1:T(8,128)(2,1)} %all-gather.7.cloned.1.call-done, bf16[2,4096,1792]{2,1,0:T(8,128)(2,1)} %fusion), kind=kOutput, calls=%fused_computation.16 | convolution fusion | flops 1879048192 | bytes 16646144 | tf_op jit(solution)/shard_map/dot_general | solution.py:29
  308.7 0.0 copy-done
  308.7 10.4 %fusion.15 = (bf16[128,1792]{0,1:T(8,128)(2,1)}, bf16[128,1792]{0,1:T(8,128)(2,1)S(1)}, bf16[128,1792]{0,1:T(8,128)(2,1)}) fusion(bf16[128,1792]{0,1:T(8,128)(2,1)S(1)} %copy.12, f32[128,1792]{0,1:T(8,128)S(1)} %fusion.11, bf16[128,4096]{0,1:T(8,128)(2,1)S(1)} %copy-done, bf16[2,4096,1792]{2,1,0:T(8,128)(2,1)} %fusion), kind=kOutput, calls=%fused_computation.24 | convolution fusion | flops 1882718208 | bytes 18481152 | tf_op jit(solution)/shard_map/dot_general | solution.py:30
  319.1 0.0 all-gather.11.cloned.1.call-update
  319.1 0.0 all-gather.9.cloned.1.call-start
  319.2 0.5 all-gather.9.cloned.1.call-update
  319.7 1.3 copy.15
  321.0 3.6 all-to-all-start
  324.7 0.1 reduce-scatter.2.cloned.1.call-start
  324.8 8.5 %fusion.1 = f32[128,4096]{1,0:T(8,128)S(1)} fusion(bf16[128,1792]{0,1:T(8,128)(2,1)} %get-tuple-element.9, bf16[2,4096,1792]{2,1,0:T(8,128)(2,1)} %fusion), kind=kOutput, calls=%fused_computation.5 | convolution fusion | flops 1879048192 | bytes 17235968 | tf_op jit(solution)/shard_map/dot_general | solution.py:39
  333.3 11.1 %fusion.6 = bf16[128,4096]{1,0:T(8,128)(2,1)} fusion(f32[128,4096]{1,0:T(8,128)S(1)} %fusion.1, bf16[128,1792]{0,1:T(8,128)(2,1)S(1)} %copy-done.1, bf16[2,4096,1792]{2,1,0:T(8,128)(2,1)} %fusion), kind=kOutput, calls=%fused_computation.11 | convolution fusion | flops 1880096768 | bytes 18284544 | tf_op jit(solution)/shard_map/dot_general | solution.py:42
  344.5 1.0 copy.16
  345.4 0.0 reduce-scatter.2.cloned.1.call-update
  345.5 14.6 %all-gather.11.cloned.1.call-done = bf16[512,1792]{0,1:T(8,128)(2,1)} async-done(((bf16[128,1792]{0,1:T(8,128)(2,1)}), bf16[512,1792]{0,1:T(8,128)(2,1)}) %all-gather.11.cloned.1.call-update) | async-done | bytes 1835024 | tf_op jit(solution)/shard_map/all_gather | solution.py:54
  360.1 1.8 copy_bitcast_fusion
  361.9 32.9 %all-gather.9.cloned.1.call-done = bf16[512,1792]{0,1:T(8,128)(2,1)} async-done(((bf16[128,1792]{0,1:T(8,128)(2,1)}), bf16[512,1792]{0,1:T(8,128)(2,1)}) %all-gather.9.cloned.1.call-update) | async-done | bytes 1835024 | tf_op jit(solution)/shard_map/all_gather | solution.py:53
  394.8 3.1 copy_bitcast_fusion.1
  397.9 0.0 all-to-all-done
  397.9 16.5 %convert_reduce_fusion = f32[3584,1024]{1,0:T(8,128)} fusion(bf16[4,128,1792]{1,2,0:T(8,128)(2,1)S(1)} %copy_bitcast_fusion, bf16[4,128,1792]{1,2,0:T(8,128)(2,1)} %copy_bitcast_fusion.1, bf16[128,4,1024]{2,0,1:T(8,128)(2,1)S(1)} %all-to-all-done), kind=kOutput, calls=%fused_computation.2 | convolution fusion | flops 3805806592 | bytes 19398656 | tf_op jit(solution)/shard_map/dot_general | solution.py:62
  414.3 14.1 %broadcast_multiply_fusion = f32[3584,1024]{1,0:T(8,128)} fusion(f32[3584,1024]{1,0:T(8,128)} %convert_reduce_fusion), kind=kLoop, calls=%fused_computation.9 | loop fusion | flops 3670016 | bytes 29360128 | tf_op jit(solution)/shard_map/mul | solution.py:65
  428.4 14.3 %copy.17 = f32[2,1024,1792]{2,1,0:T(8,128)} copy(f32[2,1024,1792]{1,2,0:T(8,128)} %bitcast.49) | data formatting | bytes 29360128
  (5 shorter events, 0.0 us)
Async XLA Ops:
  7.2 267.7 %all-gather.5.cloned.1.call-start = ((), (), s32[]{:S(2)}) async-start(), calls=%async_computation.2 | async-start | bytes 36700160 | tf_op jit(solution)/shard_map/all_gather | solution.py:24
  7.9 291.3 %all-gather.7.cloned.1.call-start = ((), (), s32[]{:S(2)}) async-start(), calls=%async_computation.3 | async-start | bytes 1179648 | tf_op jit(solution)/shard_map/all_gather | solution.py:21
  9.6 350.4 %all-gather.11.cloned.1.call-start = ((), (), s32[]{:S(2)}) async-start(), calls=%async_computation.6 | async-start | bytes 2293760 | tf_op jit(solution)/shard_map/all_gather | solution.py:54
  299.2 9.5 %copy-start = (bf16[128,4096]{0,1:T(8,128)(2,1)S(1)}, bf16[128,4096]{0,1:T(8,128)(2,1)}, u32[]{:S(2)}) copy-start(bf16[128,4096]{0,1:T(8,128)(2,1)} %all-gather.7.cloned.1.call-done) | copy-start | bytes 3145732
  319.1 14.2 %copy-start.1 = (bf16[128,1792]{0,1:T(8,128)(2,1)S(1)}, bf16[128,1792]{0,1:T(8,128)(2,1)}, u32[]{:S(2)}) copy-start(bf16[128,1792]{0,1:T(8,128)(2,1)} %get-tuple-element.11) | copy-start | bytes 1376260
  319.1 75.6 %all-gather.9.cloned.1.call-start = ((), (), s32[]{:S(2)}) async-start(), calls=%async_computation.5 | async-start | bytes 2293760 | tf_op jit(solution)/shard_map/all_gather | solution.py:53
  321.0 76.8 %all-to-all-start = ((bf16[128,4,1024]{2,0,1:T(8,128)(2,1)}), bf16[128,4,1024]{2,0,1:T(8,128)(2,1)S(1)}, u32[]{:S(2)}, u32[]{:S(2)}) async-start(bf16[128,4,1024]{2,0,1:T(8,128)(2,1)} %copy.15), calls=%async_computation.1 | async-start | bytes 2097152 | tf_op jit(solution)/shard_map/all_to_all | solution.py:51
  324.7 118.1 %reduce-scatter.2.cloned.1.call-start = ((), (), s32[]{:S(2)}) async-start(), calls=%async_computation.4 | async-start | bytes 1179648 | tf_op jit(solution)/shard_map/reduce_scatter | solution.py:46
Sparse Core Ops, SparseCore 0:
  9.8 264.9 all-gather.4
  277.0 22.0 all-gather.6
  319.2 40.7 all-gather.10
  361.7 32.9 all-gather.8
  397.5 32.4 reduce-scatter.1
where the time goes:
time: 450 us; the launch traced here: 449 us
  waiting for transfers between devices  305 us (68%)
  matrix products  56 us (12%)
  other arithmetic  34.9 us (8%)
  local copies, waits for them, and re-layouts  24.6 us (5%)
  between operations  13.8 us (3%)
  blocking collectives  10.7 us (2%)
    all_gather x1, waiting for transfers between devices, body(): lax.all_gather(gate_up_codes, 'local', axis=1, tiled=True)  253 us
    all_gather x1, waiting for transfers between devices, body(): lax.all_gather(d_gate, 'local', axis=0, tiled=True)  32.9 us
    convert_element_type x1, other arithmetic, dequant(): return weight.reshape(shape).astype(jnp.bfloat16)  20.7 us
    unnamed x8, local copies, waits for them, and re-layouts  18.4 us
    dot_general x1, matrix products, body(): lax.dot_general(blocks, both_all, numbers, preferred_element_type=jnp.flo...  16.5 us
    all_gather x1, waiting for transfers between devices, body(): lax.all_gather(d_up, 'local', axis=0, tiled=True)  14.6 us
    mul x1, other arithmetic, body(): summed = jnp.sum(partial_value.astype(jnp.float32), axis=0) * factor  14.1 us
    dot_general x1, matrix products, body(): lax.dot_general(d_up, w_gu[1], (((1,), (1,)), ((), ())), preferred_elemen...  11.1 us
  transfers between devices with their start and end apart: 6, of which 4 were waited for; matrix products, arithmetic and copies ran while one was open for 21% of the time, Pallas kernels for 0%

commit v1 on v0

v1 whole, which is shorter than its diff:
```python
import math

import jax
import jax.numpy as jnp
from jax import lax
from jax.sharding import PartitionSpec as P

BLOCK = 128


def dequant(codes, scales):
    shape = codes.shape
    blocked = codes.astype(jnp.float32).reshape(shape[:-2] + (shape[-2] // BLOCK, BLOCK, shape[-1]))
    weight = blocked * scales.astype(jnp.float32)[..., :, None, :]
    return weight.reshape(shape).astype(jnp.bfloat16)


def swap(nodes, locals_):
    ratio = nodes // locals_
    pairs = []
    for a in range(locals_):
        for h in range(ratio):
            for b in range(locals_):
                pairs.append(((ratio * a + h) * locals_ + b, (ratio * b + h) * locals_ + a))
    return pairs


def body(tokens, gate_up_codes, gate_up_scales, d_hidden):
    rows, feats = tokens.shape
    nodes, locals_ = lax.axis_size("node"), lax.axis_size("local")
    ratio = nodes // locals_
    _, owned, group = gate_up_codes.shape
    pairs = swap(nodes, locals_)
    total = rows * locals_

    mine = lax.ppermute(tokens, ("node", "local"), pairs)
    pieces = lax.all_gather(mine, "node", axis=0)
    features = pieces.reshape(locals_, ratio, rows, feats).transpose(0, 2, 1, 3).reshape(total, owned)

    w_gu = dequant(gate_up_codes, gate_up_scales)
    partial = lax.dot_general(
        features, w_gu, (((1,), (1,)), ((), ())), preferred_element_type=jnp.float32
    ).astype(jnp.bfloat16)
    both = lax.psum_scatter(partial, "local", scatter_dimension=0, tiled=True).astype(jnp.float32)
    gate, up = both[:, 0], both[:, 1]
    sigmoid_gate = jax.nn.sigmoid(gate)
    active = gate * sigmoid_gate
    hidden = (active * up).astype(jnp.bfloat16)
    grad_in = d_hidden.astype(jnp.float32)
    d_gate = (grad_in * up * sigmoid_gate * (1.0 + gate * (1.0 - sigmoid_gate))).astype(jnp.bfloat16)
    d_up = (grad_in * active).astype(jnp.bfloat16)
    d_both = lax.all_gather(jnp.stack([d_gate, d_up], axis=1), "local", axis=0, tiled=True)

    term = lax.dot_general(
        d_both, w_gu, (((1, 2), (0, 2)), ((), ())), preferred_element_type=jnp.float32
    ).astype(jnp.bfloat16)
    term = term.reshape(locals_, rows, ratio, feats).transpose(0, 2, 1, 3).reshape(nodes * rows, feats)
    summed = lax.psum_scatter(term, "node", scatter_dimension=0, tiled=True)
    d_tokens = lax.ppermute(summed, ("node", "local"), pairs)

    grads = lax.dot_general(
        features, d_both, (((0,), (0,)), ((), ())), preferred_element_type=jnp.float32
    ) * (1.0 / math.sqrt(total))
    return (hidden, d_tokens, grads.transpose(1, 0, 2))


def solution(mesh):
    placed = (
        P("local", "node"),
        P(None, "local", "node"),
        P(None, "local", "node"),
        P("local", "node"),
    )
    return jax.shard_map(
        body,
        mesh=mesh,
        in_specs=placed,
        out_specs=(P("local", "node"), P("local", "node"), P(None, "local", "node")),
        check_vma=False,
    )
```

time: 450 us -> 244 us (0.54)
  waiting for transfers between devices: 305 us -> 157 us
  matrix products: 56 us -> 27.1 us
  other arithmetic: 34.9 us -> 10.8 us
  blocking collectives: 10.7 us -> 0 us
  local copies, waits for them, and re-layouts: 24.6 us -> 29.7 us
    all_gather x4 -> x2, waiting for transfers between devices: 304 us -> 76.3 us  [the longest x1 48.4 us: body(): lax.all_gather(jnp.stack([d_gate, d_up], axis=1), 'local', axis=0, tiled=...]
    unnamed x5, waiting for transfers between devices: 1.25 us -> 48.1 us
    reduce_scatter x1, waiting for transfers between devices: 0.01 us -> 32.6 us  [body(): summed = lax.psum_scatter(term, 'node', scatter_dimension=0, tiled=True)]
    dot_general x5 -> x3, matrix products: 56 us -> 27.1 us  [the longest x1 9.32 us: body(): lax.dot_general(features, d_both, (((0,), (0,)), ((), ())), preferred_ele...]
    mul x1 -> x0, other arithmetic: 14.1 us -> none  [body(): summed = jnp.sum(partial_value.astype(jnp.float32), axis=0) * factor]
    convert_element_type x1, other arithmetic: 20.7 us -> 7.55 us  [dequant(): return weight.reshape(shape).astype(jnp.bfloat16)]
    all_gather x1 -> x0, blocking collectives: 10.7 us -> none  [body(): lax.all_gather(gate_up_scales, 'local', axis=1, tiled=True)]
    unnamed x8, local copies, waits for them, and re-layouts: 18.4 us -> 23.2 us
  transfers between devices with their start and end apart: 6 -> 6, of which waited for: 4 -> 4; matrix products, arithmetic and copies ran while one was open for 21% -> 13% of each run, Pallas kernels for 0% -> 0%
where the time goes in v1:
time: 244 us; the launch traced here: 242 us
  waiting for transfers between devices  157 us (64%)
  local copies, waits for them, and re-layouts  29.7 us (12%)
  matrix products  27.1 us (11%)
  between operations  13.8 us (6%)
  other arithmetic  10.8 us (4%)
  starting transfers between devices  3.28 us (1%)
    all_gather x1, waiting for transfers between devices, body(): lax.all_gather(jnp.stack([d_gate, d_up], axis=1), 'local', axis=0, tiled=...  48.4 us
    unnamed x5, waiting for transfers between devices  48.1 us
    reduce_scatter x1, waiting for transfers between devices, body(): summed = lax.psum_scatter(term, 'node', scatter_dimension=0, tiled=True)  32.6 us
    all_gather x1, waiting for transfers between devices, body(): pieces = lax.all_gather(mine, 'node', axis=0)  27.9 us
    unnamed x8, local copies, waits for them, and re-layouts  23.2 us
    dot_general x1, matrix products, body(): lax.dot_general(features, d_both, (((0,), (0,)), ((), ())), preferred_ele...  9.32 us
    dot_general x1, matrix products, body(): lax.dot_general(d_both, w_gu, (((1, 2), (0, 2)), ((), ())), preferred_ele...  9.15 us
    dot_general x1, matrix products, body(): lax.dot_general(features, w_gu, (((1,), (1,)), ((), ())), preferred_eleme...  8.6 us
  transfers between devices with their start and end apart: 6, of which 4 were waited for; matrix products, arithmetic and copies ran while one was open for 13% of the time, Pallas kernels for 0%

profile of v1, /device:TPU:0, one launch (start us, length us, event | category | flops | bytes accessed | tf_op | source)
XLA Modules:
  0.0 241.8 jit_solution(3938702117258548818)
XLA Ops:
  7.2 0.0 all-gather.6.cloned.1.call-start
  7.2 1.6 collective-permute-start
  8.8 0.7 copy-done.1
  9.4 0.0 all-gather.6.cloned.1.call-update
  9.5 0.0 reduce-scatter.7.cloned.1.call-start
  9.5 0.8 convert_element_type.34
  10.3 7.5 %fusion = bf16[2,1024,1792]{2,1,0:T(8,128)(2,1)} fusion(bf16[2,1024,1792]{2,1,0:T(8,128)(2,1)} %param.5, f32[2,8,1792]{2,1,0:T(8,128)S(1)} %convert_element_type.34), kind=kLoop, calls=%fused_computation.1 | loop fusion | flops 11010048 | bytes 14794752 | tf_op jit(solution)/shard_map/convert_element_type | solution.py:15
  17.9 27.9 %all-gather.6.cloned.1.call-done = bf16[1024,512]{1,0:T(8,128)(2,1)} async-done(((bf16[128,512]{1,0:T(8,128)(2,1)}), bf16[1024,512]{1,0:T(8,128)(2,1)}) %all-gather.6.cloned.1.call-update) | async-done | bytes 1048592 | tf_op jit(solution)/shard_map/all_gather | solution.py:37
  45.8 2.3 copy.27
  48.1 0.8 reshape.28
  48.9 8.6 %convolution_convert_fusion = bf16[2,1792,512]{2,1,0:T(8,128)(2,1)} fusion(bf16[2,1024,1792]{2,1,0:T(8,128)(2,1)} %fusion, bf16[512,1024,1]{1,0,2:T(8,128)(2,1)S(1)} %reshape.28), kind=kOutput, calls=%fused_computation.3 | convolution fusion | flops 3759931392 | bytes 12058624 | tf_op jit(solution)/shard_map/dot_general | solution.py:41
  57.5 6.0 %copy.24 = bf16[512,3584]{1,0:T(8,128)(2,1)} copy(bf16[512,3584]{0,1:T(8,128)(2,1)} %bitcast.52) | data formatting | bytes 7340032
  63.5 0.0 reduce-scatter.7.cloned.1.call-update
  63.5 0.0 all-gather.4.cloned.1.call-start
  63.6 48.0 %reduce-scatter.7.cloned.1.call-done = bf16[128,3584]{1,0:T(8,128)(2,1)} async-done(((bf16[512,3584]{1,0:T(8,128)(2,1)}), bf16[128,3584]{1,0:T(8,128)(2,1)}) %reduce-scatter.7.cloned.1.call-update) | async-done | bytes 917520
  111.6 1.5 copy.25
  113.2 0.5 copy.16
  113.7 0.1 convert_element_type.38
  113.9 1.3 fusion.7
  115.2 1.0 pad_maximum_fusion
  116.2 0.0 all-gather.4.cloned.1.call-update
  116.2 0.0 reduce-scatter.5.cloned.1.call-start
  116.2 48.4 %all-gather.4.cloned.1.call-done = bf16[512,2,1792]{2,0,1:T(8,128)(2,1)} async-done(((bf16[128,2,1792]{2,0,1:T(8,128)(2,1)}), bf16[512,2,1792]{2,0,1:T(8,128)(2,1)}) %all-gather.4.cloned.1.call-update) | async-done | bytes 3670032 | tf_op jit(solution)/shard_map/all_gather | solution.py:52
  164.7 9.1 %bitcast_convert_fusion = bf16[512,1024]{1,0:T(8,128)(2,1)} fusion(bf16[512,2,1792]{2,0,1:T(8,128)(2,1)} %all-gather.4.cloned.1.call-done, bf16[2,1024,1792]{2,1,0:T(8,128)(2,1)} %fusion), kind=kOutput, calls=%fused_computation.4 | convolution fusion | flops 3758620672 | bytes 12058624 | tf_op jit(solution)/shard_map/dot_general | solution.py:54
  173.8 1.8 reshape.24
  175.7 1.2 copy.17
  176.8 0.0 reduce-scatter.5.cloned.1.call-update
  176.8 32.6 %reduce-scatter.5.cloned.1.call-done = bf16[128,512]{1,0:T(8,128)(2,1)} async-done(((bf16[1024,512]{1,0:T(8,128)(2,1)}), bf16[128,512]{1,0:T(8,128)(2,1)}) %reduce-scatter.5.cloned.1.call-update) | async-done | bytes 131088 | tf_op jit(solution)/shard_map/reduce_scatter | solution.py:58
  209.5 1.6 collective-permute-start.1
  211.0 9.3 %multiply_bitcast_fusion = f32[2,1024,1792]{1,2,0:T(8,128)} fusion(bf16[512,2,1792]{2,0,1:T(8,128)(2,1)} %all-gather.4.cloned.1.call-done, bf16[512,1024,1]{1,0,2:T(8,128)(2,1)S(1)} %reshape.28), kind=kOutput, calls=%fused_computation.2 | convolution fusion | flops 3761766400 | bytes 19398656 | tf_op jit(solution)/shard_map/dot_general | solution.py:61
  220.3 14.3 %copy.19 = f32[2,1024,1792]{2,1,0:T(8,128)} copy(f32[2,1024,1792]{1,2,0:T(8,128)} %multiply_bitcast_fusion) | data formatting | bytes 29360128
  234.6 0.7 copy.29
  (5 shorter events, 0.0 us)
Async XLA Ops:
  7.2 38.6 %all-gather.6.cloned.1.call-start = ((), (), s32[]{:S(2)}) async-start(), calls=%async_computation.4 | async-start | bytes 1179648 | tf_op jit(solution)/shard_map/all_gather | solution.py:37
  7.2 1.6 collective-permute-start
  8.8 0.7 copy-start.1
  9.5 102.2 %reduce-scatter.7.cloned.1.call-start = ((), (), s32[]{:S(2)}) async-start(), calls=%async_computation.5 | async-start | bytes 4587520
  57.5 56.4 %copy-start = (bf16[128,1792]{1,0:T(8,128)(2,1)S(1)}, bf16[128,1792]{1,0:T(8,128)(2,1)}, u32[]{:S(2)}) copy-start(bf16[128,1792]{1,0:T(8,128)(2,1)} %param.7) | copy-start | bytes 1376260
  63.5 101.2 %all-gather.4.cloned.1.call-start = ((), (), s32[]{:S(2)}) async-start(), calls=%async_computation.2 | async-start | bytes 4587520 | tf_op jit(solution)/shard_map/all_gather | solution.py:52
  116.2 93.3 %reduce-scatter.5.cloned.1.call-start = ((), (), s32[]{:S(2)}) async-start(), calls=%async_computation.3 | async-start | bytes 1179648 | tf_op jit(solution)/shard_map/reduce_scatter | solution.py:58
  209.5 25.1 %collective-permute-start.1 = (bf16[128,512]{1,0:T(8,128)(2,1)}, bf16[128,512]{1,0:T(8,128)(2,1)S(1)}, u32[]{:S(2)}, u32[]{:S(2)}) collective-permute-start(bf16[128,512]{1,0:T(8,128)(2,1)} %reduce-scatter.5.cloned.1.call-done), channel_id=1, source_target_pairs={{0,0},{1,8},{2,16},{3,24},{4,4},{5,12},{6,20},{7,28},{8,1},{9,9},{... | collective-permute-start | bytes 393224 | tf_op jit(solution)/shard_map/ppermute | solution.py:59
Sparse Core Ops, SparseCore 0:
  10.2 35.5 all-gather.5
  63.6 47.9 reduce-scatter.6
  116.3 48.3 all-gather.3
  177.0 32.4 reduce-scatter.4

commit v2 on v1

v2 whole, which is shorter than its diff:
```python
import functools
import math

import jax
import jax.numpy as jnp
from jax import lax
from jax.experimental import pallas as pl
from jax.experimental.pallas import tpu as pltpu
from jax.sharding import PartitionSpec as P

BLOCK = 128
CHUNKS = 2
AXES = ("node", "local")


def dequant(codes, scales):
    shape = codes.shape
    blocked = codes.astype(jnp.float32).reshape(shape[:-2] + (shape[-2] // BLOCK, BLOCK, shape[-1]))
    weight = blocked * scales.astype(jnp.float32)[..., :, None, :]
    return weight.reshape(shape).astype(jnp.bfloat16)


def pairs(move, places, ratio):
    out = []
    for plane in range(places):
        for half in range(ratio):
            for place in range(places):
                p, h, q = move(plane, half, place)
                out.append(
                    ((plane * ratio + half) * places + place, (p * ratio + h) * places + q)
                )
    return out


def reorder(x, mask, axis=0):
    size = x.shape[axis]
    return jnp.concatenate(
        [lax.dynamic_slice_in_dim(x, i ^ mask, 1, axis) for i in range(size)], axis=axis
    )


def weight_grad_kernel(scale, features_ref, d_ref, out_ref):
    out_ref[0] = scale * lax.dot_general(
        features_ref[...], d_ref[0], (((0,), (0,)), ((), ())), preferred_element_type=jnp.float32
    )


def weight_grad(features, d_both, scale):
    total, owned = features.shape
    group = d_both.shape[2]
    step = min(owned, 256)
    return pl.pallas_call(
        functools.partial(weight_grad_kernel, scale),
        grid=(2, owned // step),
        in_specs=[
            pl.BlockSpec((total, step), lambda g, i: (0, i)),
            pl.BlockSpec((1, total, group), lambda g, i: (g, 0, 0)),
        ],
        out_specs=pl.BlockSpec((1, step, group), lambda g, i: (g, i, 0)),
        out_shape=jax.ShapeDtypeStruct((2, owned, group), jnp.float32),
        compiler_params=pltpu.CompilerParams(vmem_limit_bytes=40 * 1024 * 1024),
    )(features, d_both)


def body(tokens, gate_up_codes, gate_up_scales, d_hidden):
    rows, feats = tokens.shape
    nodes, places = lax.axis_size("node"), lax.axis_size("local")
    ratio = nodes // places
    _, owned, group = gate_up_codes.shape
    bits = [1 << b for b in range(places.bit_length() - 1)]
    node, place = lax.axis_index("node"), lax.axis_index("local")
    plane, half = node // ratio, node % ratio
    mask = plane ^ place
    chunk = rows // CHUNKS
    part = chunk // 2

    def permute(x, move):
        return lax.ppermute(x, AXES, pairs(move, places, ratio))

    def features_of(x):
        got = jnp.stack(
            [permute(x, lambda p, h, q, j=j: (q ^ j, h, p)) for j in range(places)]
        )
        halves = jnp.stack(
            [got] + [permute(got, lambda p, h, q, e=e: (p, h ^ e, q)) for e in range(1, ratio)]
        )
        halves = reorder(reorder(halves, half, 0), mask, 1)
        return halves.transpose(1, 2, 0, 3).reshape(places, x.shape[0], owned)

    def reduce_local(x, order):
        ks = list(range(places))
        x = x.astype(jnp.float32)
        for bit in order:
            away = [i for i, k in enumerate(ks) if k & bit]
            stay = [i for i, k in enumerate(ks) if not k & bit]
            sent = jnp.stack([x[:, i] for i in away], axis=1).astype(jnp.bfloat16)
            got = permute(sent, lambda p, h, q: (p, h, q ^ bit))
            x = jnp.stack([x[:, i] for i in stay], axis=1) + got.astype(jnp.float32)
            ks = [ks[i] for i in stay]
        return x[:, 0]

    def gather_local(x, order):
        x, ks = x[:, None], [0]
        for bit in order:
            got = permute(x, lambda p, h, q: (p, h, q ^ bit))
            x = jnp.concatenate([x, got], axis=1)
            ks = ks + [k ^ bit for k in ks]
        return x, ks

    w_gu = dequant(gate_up_codes, gate_up_scales)
    hidden, all_features, all_d, d_tokens = [], [], [], []
    for c in range(CHUNKS):
        features = features_of(tokens[c * chunk : (c + 1) * chunk])
        flat = features.reshape(places * chunk, owned)
        partial = [
            jnp.dot(flat, w_gu[g], preferred_element_type=jnp.float32)
            .astype(jnp.bfloat16)
            .reshape(places, chunk, group)
            for g in range(2)
        ]
        gathered = []
        for s in range(2):
            order = bits if s == 0 else bits[::-1]
            at = slice(s * part, (s + 1) * part)
            both = reduce_local(jnp.stack([p[:, at] for p in partial]), order)
            gate, up = both[0], both[1]
            sigmoid_gate = jax.nn.sigmoid(gate)
            active = gate * sigmoid_gate
            hidden.append((active * up).astype(jnp.bfloat16))
            first = c * chunk + s * part
            grad_in = d_hidden[first : first + part].astype(jnp.float32)
            d_gate = grad_in * up * sigmoid_gate * (1.0 + gate * (1.0 - sigmoid_gate))
            d_up = grad_in * active
            d_both, ks = gather_local(jnp.stack([d_gate, d_up]).astype(jnp.bfloat16), order)
            gathered.append((d_both, ks))
            all_d.append(d_both.reshape(2, places * part, group))
            all_features += [features[k, at] for k in ks]
        d_chunk = jnp.concatenate([d.reshape(2, places * part, group) for d, _ in gathered], axis=1)
        term = lax.dot_general(
            d_chunk[0], w_gu[0], (((1,), (1,)), ((), ())), preferred_element_type=jnp.float32
        ) + lax.dot_general(
            d_chunk[1], w_gu[1], (((1,), (1,)), ((), ())), preferred_element_type=jnp.float32
        )
        streams = []
        for s, (_, ks) in enumerate(gathered):
            piece = term[s * places * part : (s + 1) * places * part].reshape(places, part, ratio, feats)
            back = [ks.index(k) for k in range(places)]
            streams.append(jnp.stack([piece[i] for i in back]))
        term = jnp.concatenate(streams, axis=1)
        term = reorder(term, half, 2)
        summed = term[:, :, 0]
        for e in range(1, ratio):
            got = permute(term[:, :, e].astype(jnp.bfloat16), lambda p, h, q: (p, h ^ e, q))
            summed = summed + got.astype(jnp.float32)
        summed = summed.astype(jnp.bfloat16)
        arrived = jnp.stack(
            [summed[0]]
            + [permute(summed[k], lambda p, h, q: (p, h, q ^ k)) for k in range(1, places)]
        )
        arrived = reorder(arrived, mask, 0)
        result = arrived[0].astype(jnp.float32)
        for j in range(1, places):
            got = permute(arrived[j], lambda p, h, q: (p ^ j, h, q))
            result = result + got.astype(jnp.float32)
        d_tokens.append(result.astype(jnp.bfloat16))

    grads = weight_grad(
        jnp.concatenate(all_features), jnp.concatenate(all_d, axis=1), 1.0 / math.sqrt(rows * places)
    )
    return jnp.concatenate(hidden), jnp.concatenate(d_tokens), grads


def solution(mesh):
    placed = (
        P("local", "node"),
        P(None, "local", "node"),
        P(None, "local", "node"),
        P("local", "node"),
    )
    return jax.shard_map(
        body,
        mesh=mesh,
        in_specs=placed,
        out_specs=(P("local", "node"), P("local", "node"), P(None, "local", "node")),
        check_vma=False,
    )
```

time: 244 us -> 202 us (0.83)
  waiting for transfers between devices: 157 us -> 50.5 us
  starting transfers between devices: 3.28 us -> 58.9 us
  local copies, waits for them, and re-layouts: 29.7 us -> 48.3 us
  matrix products: 27.1 us -> 11.7 us
  between operations: 13.8 us -> 1.62 us
  other arithmetic: 10.8 us -> 21.6 us
  Pallas kernels: 0 us -> 8.56 us
    all_gather x2 -> x0, waiting for transfers between devices: 76.3 us -> none  [the longest x1 48.4 us: body(): lax.all_gather(jnp.stack([d_gate, d_up], axis=1), 'local', axis=0, tiled=...]
    ppermute x2 -> x40, starting transfers between devices: 3.11 us -> 58.9 us  [permute(): return lax.ppermute(x, AXES, pairs(move, places, ratio))]
    ppermute x2 -> x40, waiting for transfers between devices: 0.01 us -> 50.5 us  [permute(): return lax.ppermute(x, AXES, pairs(move, places, ratio))]
    unnamed x5 -> x0, waiting for transfers between devices: 48.1 us -> none
    slice x0 -> x43, local copies, waits for them, and re-layouts: none -> 45.4 us  [the longest x34 44.2 us: body(): streams.append(jnp.stack([piece[i] for i in back]))]
    reduce_scatter x1 -> x0, waiting for transfers between devices: 32.6 us -> none  [body(): summed = lax.psum_scatter(term, 'node', scatter_dimension=0, tiled=True)]
    unnamed x8 -> x39, local copies, waits for them, and re-layouts: 23.2 us -> 0.62 us
    dot_general x3 -> x8, matrix products: 27.1 us -> 11.7 us  [the longest x2 4.87 us: body(): lax.dot_general(d_chunk[0], w_gu[0], (((1,), (1,)), ((), ())), preferred_...]
  transfers between devices with their start and end apart: 6 -> 40, of which waited for: 4 -> 14; matrix products, arithmetic and copies ran while one was open for 13% -> 36% of each run, Pallas kernels for 0% -> 4%
where the time goes in v2:
time: 202 us; the launch traced here: 201 us
  starting transfers between devices  58.9 us (29%)
  waiting for transfers between devices  50.5 us (25%)
  local copies, waits for them, and re-layouts  48.3 us (24%)
  other arithmetic  21.6 us (11%)
  matrix products  11.7 us (6%)
  Pallas kernels  8.56 us (4%)
    ppermute x40, starting transfers between devices, permute(): return lax.ppermute(x, AXES, pairs(move, places, ratio))  58.9 us
    ppermute x40, waiting for transfers between devices, permute(): return lax.ppermute(x, AXES, pairs(move, places, ratio))  50.5 us
    slice x34, local copies, waits for them, and re-layouts, body(): streams.append(jnp.stack([piece[i] for i in back]))  44.2 us
    pallas_call x1, Pallas kernels, weight_grad(): pl.pallas_call(functools.partial(weight_grad_kernel, scale), grid=(2, own...  8.56 us
    concatenate x8, other arithmetic, gather_local(): x = jnp.concatenate([x, got], axis=1)  5.31 us
    dot_general x2, matrix products, body(): lax.dot_general(d_chunk[0], w_gu[0], (((1,), (1,)), ((), ())), preferred_...  4.87 us
    dot_general x4, matrix products, body(): jnp.dot(flat, w_gu[g], preferred_element_type=jnp.float32)  4.53 us
    convert_element_type x1, other arithmetic, dequant(): return weight.reshape(shape).astype(jnp.bfloat16)  4.48 us
  transfers between devices with their start and end apart: 40, of which 14 were waited for; matrix products, arithmetic and copies ran while one was open for 36% of the time, Pallas kernels for 4%

profile of v2, /device:TPU:0, one launch (start us, length us, event | category | flops | bytes accessed | tf_op | source)
XLA Modules:
  0.0 201.2 jit_solution(7420346319623073145)
XLA Ops:
  1.5 5.1 %collective-permute-start.3 = (bf16[64,512]{1,0:T(8,128)(2,1)S(1)}, bf16[64,512]{1,0:T(8,128)(2,1)S(1)}, u32[]{:S(2)}, u32[]{:S(2)}) collective-permute-start(bf16[64,512]{1,0:T(8,128)(2,1)S(1)} %get-tuple-element.84), channel_id=1, source_target_pairs={{0,24},{1,16},{2,8},{3,0},{4,28},{5,20},{6,12},{7,4},{8,25},{9,17}... | collective-permute-start | bytes 196616 | tf_op jit(solution)/shard_map/ppermute | solution.py:78
  9.2 6.5 %collective-permute-start.12 = (bf16[64,512]{1,0:T(8,128)(2,1)S(1)}, bf16[64,512]{1,0:T(8,128)(2,1)S(1)}, u32[]{:S(2)}, u32[]{:S(2)}) collective-permute-start(bf16[64,512]{1,0:T(8,128)(2,1)S(1)} %get-tuple-element.85), channel_id=1, source_target_pairs={{0,24},{1,16},{2,8},{3,0},{4,28},{5,20},{6,12},{7,4},{8,25},{9,17}... | collective-permute-start | bytes 196616 | tf_op jit(solution)/shard_map/ppermute | solution.py:78
  18.3 1.7 collective-permute-done.11
  21.1 4.5 %fusion = bf16[2,1024,1792]{2,1,0:T(8,128)(2,1)S(1)} fusion(bf16[2,1024,1792]{2,1,0:T(8,128)(2,1)} %param.5, f32[2,8,1792]{2,1,0:T(8,128)S(1)} %convert_element_type.178), kind=kLoop, calls=%fused_computation.1 | loop fusion | flops 11010048 | bytes 14794752 | tf_op jit(solution)/shard_map/convert_element_type | solution.py:20
  33.2 6.3 %collective-permute-start.14 = (bf16[2,2,32,1792]{3,2,1,0:T(8,128)(2,1)S(1)}, bf16[2,2,32,1792]{3,2,1,0:T(8,128)(2,1)S(1)}, u32[]{:S(2)}, u32[]{:S(2)}) collective-permute-start(bf16[2,2,32,1792]{3,2,1,0:T(8,128)(2,1)S(1)} %pad_maximum_fusion.14), channel_id=1, source_target_pairs={{0,1},{1,0},{2,3},{3,2},{4,5},{5,4},{6,7},{7,6},{8,9},{9,8},{10,11... | collective-permute-start | bytes 1376264 | tf_op jit(solution)/shard_map/ppermute | solution.py:78
  39.5 3.9 %collective-permute-start.16 = (bf16[2,2,32,1792]{3,2,1,0:T(8,128)(2,1)S(1)}, bf16[2,2,32,1792]{3,2,1,0:T(8,128)(2,1)S(1)}, u32[]{:S(2)}, u32[]{:S(2)}) collective-permute-start(bf16[2,2,32,1792]{3,2,1,0:T(8,128)(2,1)S(1)} %pad_maximum_fusion.11), channel_id=1, source_target_pairs={{0,2},{1,3},{2,0},{3,1},{4,6},{5,7},{6,4},{7,5},{8,10},{9,11},{10,... | collective-permute-start | bytes 1376264 | tf_op jit(solution)/shard_map/ppermute | solution.py:78
  44.9 9.9 %collective-permute-done.16 = bf16[2,2,32,1792]{3,2,1,0:T(8,128)(2,1)S(1)} collective-permute-done((bf16[2,2,32,1792]{3,2,1,0:T(8,128)(2,1)S(1)}, bf16[2,2,32,1792]{3,2,1,0:T(8,128)(2,1)S(1)}, u32[]{:S(2)}, u32[]{:S(2)}) %collective-permute-start.16) | collective-permute-done | bytes 458784 | tf_op jit(solution)/shard_map/ppermute | solution.py:78
  56.2 2.1 %collective-permute-start.15 = (bf16[2,1,32,1792]{3,2,1,0:T(8,128)(2,1)S(1)}, bf16[2,1,32,1792]{3,2,1,0:T(8,128)(2,1)S(1)}, u32[]{:S(2)}, u32[]{:S(2)}) collective-permute-start(bf16[2,1,32,1792]{3,2,1,0:T(8,128)(2,1)S(1)} %slice.749), channel_id=1, source_target_pairs={{0,2},{1,3},{2,0},{3,1},{4,6},{5,7},{6,4},{7,5},{8,10},{9,11},{10,... | collective-permute-start | bytes 688136 | tf_op jit(solution)/shard_map/ppermute | solution.py:78
  58.3 6.3 %collective-permute-done.7 = bf16[2,2,32,1792]{3,2,1,0:T(8,128)(2,1)S(1)} collective-permute-done((bf16[2,2,32,1792]{3,2,1,0:T(8,128)(2,1)S(1)}, bf16[2,2,32,1792]{3,2,1,0:T(8,128)(2,1)S(1)}, u32[]{:S(2)}, u32[]{:S(2)}) %collective-permute-start.7) | collective-permute-done | bytes 458784 | tf_op jit(solution)/shard_map/ppermute | solution.py:78
  66.0 2.1 %collective-permute-start.6 = (bf16[2,1,32,1792]{3,2,1,0:T(8,128)(2,1)S(1)}, bf16[2,1,32,1792]{3,2,1,0:T(8,128)(2,1)S(1)}, u32[]{:S(2)}, u32[]{:S(2)}) collective-permute-start(bf16[2,1,32,1792]{3,2,1,0:T(8,128)(2,1)S(1)} %slice.751), channel_id=1, source_target_pairs={{0,2},{1,3},{2,0},{3,1},{4,6},{5,7},{6,4},{7,5},{8,10},{9,11},{10,... | collective-permute-start | bytes 688136 | tf_op jit(solution)/shard_map/ppermute | solution.py:78
  71.6 2.3 %collective-permute-done.6 = bf16[2,1,32,1792]{3,2,1,0:T(8,128)(2,1)S(1)} collective-permute-done((bf16[2,1,32,1792]{3,2,1,0:T(8,128)(2,1)S(1)}, bf16[2,1,32,1792]{3,2,1,0:T(8,128)(2,1)S(1)}, u32[]{:S(2)}, u32[]{:S(2)}) %collective-permute-start.6) | collective-permute-done | bytes 229408 | tf_op jit(solution)/shard_map/ppermute | solution.py:78
  74.5 1.8 collective-permute-start.31
  79.5 1.8 collective-permute-start.30
  82.9 2.0 collective-permute-start.19
  84.9 3.2 %collective-permute-done.20 = bf16[2,1,32,1792]{3,2,1,0:T(8,128)(2,1)S(1)} collective-permute-done((bf16[2,1,32,1792]{3,2,1,0:T(8,128)(2,1)S(1)}, bf16[2,1,32,1792]{3,2,1,0:T(8,128)(2,1)S(1)}, u32[]{:S(2)}, u32[]{:S(2)}) %collective-permute-start.20) | collective-permute-done | bytes 229408 | tf_op jit(solution)/shard_map/ppermute | solution.py:78
  91.1 15.1 %collective-permute-done.19 = bf16[2,2,32,1792]{3,2,1,0:T(8,128)(2,1)S(1)} collective-permute-done((bf16[2,2,32,1792]{3,2,1,0:T(8,128)(2,1)S(1)}, bf16[2,2,32,1792]{3,2,1,0:T(8,128)(2,1)S(1)}, u32[]{:S(2)}, u32[]{:S(2)}) %collective-permute-start.19) | collective-permute-done | bytes 458784 | tf_op jit(solution)/shard_map/ppermute | solution.py:78
  109.8 1.7 slice.399
  113.0 1.7 slice.413
  116.3 1.7 slice.411
  119.5 1.7 slice.409
  122.8 1.7 slice.407
  126.0 1.7 slice.405
  129.3 1.7 slice.403
  136.7 1.8 pad_maximum_fusion.7
  140.0 3.5 %fusion.1 = f32[256,1024]{1,0:T(8,128)S(1)} fusion(bf16[2,1024,1792]{2,1,0:T(8,128)(2,1)} %copy-done, bf16[2,128,1792]{2,1,0:T(8,128)(2,1)S(1)} %bitcast.306, bf16[2,128,1792]{2,1,0:T(8,128)(2,1)S(1)} %bitcast.309), kind=kOutput, calls=%fused_computation.9 | convolution fusion | flops 941359104 | bytes 6553600 | tf_op jit(solution)/shard_map/dot_general | solution.py:139
  164.9 3.2 %pad_maximum_fusion.d_ref = bf16[2,512,1792]{2,1,0:T(8,128)(2,1)S(1)} fusion(bf16[2,128,1792]{2,1,0:T(8,128)(2,1)} %bitcast.311, bf16[2,128,1792]{2,1,0:T(8,128)(2,1)} %bitcast.308, bf16[2,128,1792]{2,1,0:T(8,128)(2,1)S(1)} %bitcast.305, bf16[2,128,1792]{2,1,0:T(8,128)(2,1)S(1)} %bitcast.302), kind=kLoop, calls=%fused_computation.4 | loop fusion | flops 14680064 | bytes 7340032 | tf_op jit(solution)/shard_map/concatenate | solution.py:168
  168.2 8.6 %shard_map.67 = f32[2,1024,1792]{2,1,0:T(8,128)} custom-call(bf16[512,1024]{1,0:T(8,128)(2,1)S(1)} %fusion.81.features_ref, bf16[2,512,1792]{2,1,0:T(8,128)(2,1)S(1)} %pad_maximum_fusion.d_ref), custom_call_target="tpu_custom_call" | custom-call | tf_op jit(solution)/shard_map/pallas_call | solution.py:52
  177.8 2.1 %collective-permute-start.25 = (bf16[64,512]{1,0:T(8,128)(2,1)S(1)}, bf16[64,512]{1,0:T(8,128)(2,1)S(1)}, u32[]{:S(2)}, u32[]{:S(2)}) collective-permute-start(bf16[64,512]{1,0:T(8,128)(2,1)S(1)} %get-tuple-element.70), channel_id=1, source_target_pairs={{0,3},{1,2},{2,1},{3,0},{4,7},{5,6},{6,5},{7,4},{8,11},{9,10},{10,... | collective-permute-start | bytes 196616 | tf_op jit(solution)/shard_map/ppermute | solution.py:78
  181.4 2.1 %collective-permute-start.36 = (bf16[64,512]{1,0:T(8,128)(2,1)S(1)}, bf16[64,512]{1,0:T(8,128)(2,1)S(1)}, u32[]{:S(2)}, u32[]{:S(2)}) collective-permute-start(bf16[64,512]{1,0:T(8,128)(2,1)S(1)} %get-tuple-element.77), channel_id=1, source_target_pairs={{0,3},{1,2},{2,1},{3,0},{4,7},{5,6},{6,5},{7,4},{8,11},{9,10},{10,... | collective-permute-start | bytes 196616 | tf_op jit(solution)/shard_map/ppermute | solution.py:78
  188.7 2.5 %collective-permute-start.37 = (bf16[64,512]{1,0:T(8,128)(2,1)S(1)}, bf16[64,512]{1,0:T(8,128)(2,1)S(1)}, u32[]{:S(2)}, u32[]{:S(2)}) collective-permute-start(bf16[64,512]{1,0:T(8,128)(2,1)S(1)} %get-tuple-element.73), channel_id=1, source_target_pairs={{0,8},{1,9},{2,10},{3,11},{4,12},{5,13},{6,14},{7,15},{8,0},{9,1},... | collective-permute-start | bytes 196616 | tf_op jit(solution)/shard_map/ppermute | solution.py:78
  193.4 5.2 %collective-permute-done.27 = bf16[64,512]{1,0:T(8,128)(2,1)S(1)} collective-permute-done((bf16[64,512]{1,0:T(8,128)(2,1)S(1)}, bf16[64,512]{1,0:T(8,128)(2,1)S(1)}, u32[]{:S(2)}, u32[]{:S(2)}) %collective-permute-start.27) | collective-permute-done | bytes 65568 | tf_op jit(solution)/shard_map/ppermute | solution.py:78
  198.7 1.9 collective-permute-done.38
  (204 shorter events, 82.5 us)
Async XLA Ops:
  1.5 14.2 %collective-permute-start.3 = (bf16[64,512]{1,0:T(8,128)(2,1)S(1)}, bf16[64,512]{1,0:T(8,128)(2,1)S(1)}, u32[]{:S(2)}, u32[]{:S(2)}) collective-permute-start(bf16[64,512]{1,0:T(8,128)(2,1)S(1)} %get-tuple-element.84), channel_id=1, source_target_pairs={{0,24},{1,16},{2,8},{3,0},{4,28},{5,20},{6,12},{7,4},{8,25},{9,17}... | collective-permute-start | bytes 196616 | tf_op jit(solution)/shard_map/ppermute | solution.py:78
  6.6 9.1 %collective-permute-start.2 = (bf16[64,512]{1,0:T(8,128)(2,1)S(1)}, bf16[64,512]{1,0:T(8,128)(2,1)S(1)}, u32[]{:S(2)}, u32[]{:S(2)}) collective-permute-start(bf16[64,512]{1,0:T(8,128)(2,1)S(1)} %get-tuple-element.84), channel_id=1, source_target_pairs={{0,16},{1,24},{2,0},{3,8},{4,20},{5,28},{6,4},{7,12},{8,17},{9,25}... | collective-permute-start | bytes 196616 | tf_op jit(solution)/shard_map/ppermute | solution.py:78
  8.1 8.6 %collective-permute-start.1 = (bf16[64,512]{1,0:T(8,128)(2,1)S(1)}, bf16[64,512]{1,0:T(8,128)(2,1)S(1)}, u32[]{:S(2)}, u32[]{:S(2)}) collective-permute-start(bf16[64,512]{1,0:T(8,128)(2,1)S(1)} %get-tuple-element.84), channel_id=1, source_target_pairs={{0,8},{1,0},{2,24},{3,16},{4,12},{5,4},{6,28},{7,20},{8,9},{9,1},{... | collective-permute-start | bytes 196616 | tf_op jit(solution)/shard_map/ppermute | solution.py:78
  8.6 8.8 %collective-permute-start = (bf16[64,512]{1,0:T(8,128)(2,1)S(1)}, bf16[64,512]{1,0:T(8,128)(2,1)S(1)}, u32[]{:S(2)}, u32[]{:S(2)}) collective-permute-start(bf16[64,512]{1,0:T(8,128)(2,1)S(1)} %get-tuple-element.84), channel_id=1, source_target_pairs={{0,0},{1,8},{2,16},{3,24},{4,4},{5,12},{6,20},{7,28},{8,1},{9,9},{... | collective-permute-start | bytes 196616 | tf_op jit(solution)/shard_map/ppermute | solution.py:78
  9.2 9.0 %collective-permute-start.12 = (bf16[64,512]{1,0:T(8,128)(2,1)S(1)}, bf16[64,512]{1,0:T(8,128)(2,1)S(1)}, u32[]{:S(2)}, u32[]{:S(2)}) collective-permute-start(bf16[64,512]{1,0:T(8,128)(2,1)S(1)} %get-tuple-element.85), channel_id=1, source_target_pairs={{0,24},{1,16},{2,8},{3,0},{4,28},{5,20},{6,12},{7,4},{8,25},{9,17}... | collective-permute-start | bytes 196616 | tf_op jit(solution)/shard_map/ppermute | solution.py:78
  17.4 8.2 %collective-permute-start.4 = (bf16[4,64,512]{2,1,0:T(8,128)(2,1)S(1)}, bf16[4,64,512]{2,1,0:T(8,128)(2,1)S(1)}, u32[]{:S(2)}, u32[]{:S(2)}) collective-permute-start(bf16[4,64,512]{2,1,0:T(8,128)(2,1)S(1)} %get-tuple-element.80), channel_id=1, source_target_pairs={{0,4},{1,5},{2,6},{3,7},{4,0},{5,1},{6,2},{7,3},{8,12},{9,13},{10,... | collective-permute-start | bytes 786440 | tf_op jit(solution)/shard_map/ppermute | solution.py:78
  33.2 22.8 %collective-permute-start.14 = (bf16[2,2,32,1792]{3,2,1,0:T(8,128)(2,1)S(1)}, bf16[2,2,32,1792]{3,2,1,0:T(8,128)(2,1)S(1)}, u32[]{:S(2)}, u32[]{:S(2)}) collective-permute-start(bf16[2,2,32,1792]{3,2,1,0:T(8,128)(2,1)S(1)} %pad_maximum_fusion.14), channel_id=1, source_target_pairs={{0,1},{1,0},{2,3},{3,2},{4,5},{5,4},{6,7},{7,6},{8,9},{9,8},{10,11... | collective-permute-start | bytes 1376264 | tf_op jit(solution)/shard_map/ppermute | solution.py:78
  39.5 15.2 %collective-permute-start.16 = (bf16[2,2,32,1792]{3,2,1,0:T(8,128)(2,1)S(1)}, bf16[2,2,32,1792]{3,2,1,0:T(8,128)(2,1)S(1)}, u32[]{:S(2)}, u32[]{:S(2)}) collective-permute-start(bf16[2,2,32,1792]{3,2,1,0:T(8,128)(2,1)S(1)} %pad_maximum_fusion.11), channel_id=1, source_target_pairs={{0,2},{1,3},{2,0},{3,1},{4,6},{5,7},{6,4},{7,5},{8,10},{9,11},{10,... | collective-permute-start | bytes 1376264 | tf_op jit(solution)/shard_map/ppermute | solution.py:78
  43.6 22.3 %collective-permute-start.5 = (bf16[2,2,32,1792]{3,2,1,0:T(8,128)(2,1)S(1)}, bf16[2,2,32,1792]{3,2,1,0:T(8,128)(2,1)S(1)}, u32[]{:S(2)}, u32[]{:S(2)}) collective-permute-start(bf16[2,2,32,1792]{3,2,1,0:T(8,128)(2,1)S(1)} %pad_maximum_fusion.13), channel_id=1, source_target_pairs={{0,1},{1,0},{2,3},{3,2},{4,5},{5,4},{6,7},{7,6},{8,9},{9,8},{10,11... | collective-permute-start | bytes 1376264 | tf_op jit(solution)/shard_map/ppermute | solution.py:78
  44.7 19.8 %collective-permute-start.7 = (bf16[2,2,32,1792]{3,2,1,0:T(8,128)(2,1)S(1)}, bf16[2,2,32,1792]{3,2,1,0:T(8,128)(2,1)S(1)}, u32[]{:S(2)}, u32[]{:S(2)}) collective-permute-start(bf16[2,2,32,1792]{3,2,1,0:T(8,128)(2,1)S(1)} %pad_maximum_fusion.12), channel_id=1, source_target_pairs={{0,2},{1,3},{2,0},{3,1},{4,6},{5,7},{6,4},{7,5},{8,10},{9,11},{10,... | collective-permute-start | bytes 1376264 | tf_op jit(solution)/shard_map/ppermute | solution.py:78
  54.9 16.0 %collective-permute-start.17 = (bf16[2,1,32,1792]{3,2,1,0:T(8,128)(2,1)S(1)}, bf16[2,1,32,1792]{3,2,1,0:T(8,128)(2,1)S(1)}, u32[]{:S(2)}, u32[]{:S(2)}) collective-permute-start(bf16[2,1,32,1792]{3,2,1,0:T(8,128)(2,1)S(1)} %slice.748), channel_id=1, source_target_pairs={{0,1},{1,0},{2,3},{3,2},{4,5},{5,4},{6,7},{7,6},{8,9},{9,8},{10,11... | collective-permute-start | bytes 688136 | tf_op jit(solution)/shard_map/ppermute | solution.py:78
  56.2 13.3 %collective-permute-start.15 = (bf16[2,1,32,1792]{3,2,1,0:T(8,128)(2,1)S(1)}, bf16[2,1,32,1792]{3,2,1,0:T(8,128)(2,1)S(1)}, u32[]{:S(2)}, u32[]{:S(2)}) collective-permute-start(bf16[2,1,32,1792]{3,2,1,0:T(8,128)(2,1)S(1)} %slice.749), channel_id=1, source_target_pairs={{0,2},{1,3},{2,0},{3,1},{4,6},{5,7},{6,4},{7,5},{8,10},{9,11},{10,... | collective-permute-start | bytes 688136 | tf_op jit(solution)/shard_map/ppermute | solution.py:78
  64.7 6.8 %collective-permute-start.8 = (bf16[2,1,32,1792]{3,2,1,0:T(8,128)(2,1)S(1)}, bf16[2,1,32,1792]{3,2,1,0:T(8,128)(2,1)S(1)}, u32[]{:S(2)}, u32[]{:S(2)}) collective-permute-start(bf16[2,1,32,1792]{3,2,1,0:T(8,128)(2,1)S(1)} %slice.750), channel_id=1, source_target_pairs={{0,1},{1,0},{2,3},{3,2},{4,5},{5,4},{6,7},{7,6},{8,9},{9,8},{10,11... | collective-permute-start | bytes 688136 | tf_op jit(solution)/shard_map/ppermute | solution.py:78
  66.0 8.0 %collective-permute-start.6 = (bf16[2,1,32,1792]{3,2,1,0:T(8,128)(2,1)S(1)}, bf16[2,1,32,1792]{3,2,1,0:T(8,128)(2,1)S(1)}, u32[]{:S(2)}, u32[]{:S(2)}) collective-permute-start(bf16[2,1,32,1792]{3,2,1,0:T(8,128)(2,1)S(1)} %slice.751), channel_id=1, source_target_pairs={{0,2},{1,3},{2,0},{3,1},{4,6},{5,7},{6,4},{7,5},{8,10},{9,11},{10,... | collective-permute-start | bytes 688136 | tf_op jit(solution)/shard_map/ppermute | solution.py:78
  69.7 8.9 %collective-permute-start.29 = (bf16[2,1,32,1792]{3,2,1,0:T(8,128)(2,1)S(1)}, bf16[2,1,32,1792]{3,2,1,0:T(8,128)(2,1)S(1)}, u32[]{:S(2)}, u32[]{:S(2)}) collective-permute-start(bf16[2,1,32,1792]{3,2,1,0:T(8,128)(2,1)S(1)} %pad_maximum_fusion.26), channel_id=1, source_target_pairs={{0,1},{1,0},{2,3},{3,2},{4,5},{5,4},{6,7},{7,6},{8,9},{9,8},{10,11... | collective-permute-start | bytes 688136 | tf_op jit(solution)/shard_map/ppermute | solution.py:78
  74.5 14.7 %collective-permute-start.31 = (bf16[2,1,32,1792]{3,2,1,0:T(8,128)(2,1)S(1)}, bf16[2,1,32,1792]{3,2,1,0:T(8,128)(2,1)S(1)}, u32[]{:S(2)}, u32[]{:S(2)}) collective-permute-start(bf16[2,1,32,1792]{3,2,1,0:T(8,128)(2,1)S(1)} %pad_maximum_fusion.27), channel_id=1, source_target_pairs={{0,2},{1,3},{2,0},{3,1},{4,6},{5,7},{6,4},{7,5},{8,10},{9,11},{10,... | collective-permute-start | bytes 688136 | tf_op jit(solution)/shard_map/ppermute | solution.py:78
  76.3 6.5 %collective-permute-start.18 = (bf16[2,1,32,1792]{3,2,1,0:T(8,128)(2,1)S(1)}, bf16[2,1,32,1792]{3,2,1,0:T(8,128)(2,1)S(1)}, u32[]{:S(2)}, u32[]{:S(2)}) collective-permute-start(bf16[2,1,32,1792]{3,2,1,0:T(8,128)(2,1)S(1)} %pad_maximum_fusion.24), channel_id=1, source_target_pairs={{0,1},{1,0},{2,3},{3,2},{4,5},{5,4},{6,7},{7,6},{8,9},{9,8},{10,11... | collective-permute-start | bytes 688136 | tf_op jit(solution)/shard_map/ppermute | solution.py:78
  77.5 10.5 %collective-permute-start.20 = (bf16[2,1,32,1792]{3,2,1,0:T(8,128)(2,1)S(1)}, bf16[2,1,32,1792]{3,2,1,0:T(8,128)(2,1)S(1)}, u32[]{:S(2)}, u32[]{:S(2)}) collective-permute-start(bf16[2,1,32,1792]{3,2,1,0:T(8,128)(2,1)S(1)} %pad_maximum_fusion.25), channel_id=1, source_target_pairs={{0,2},{1,3},{2,0},{3,1},{4,6},{5,7},{6,4},{7,5},{8,10},{9,11},{10,... | collective-permute-start | bytes 688136 | tf_op jit(solution)/shard_map/ppermute | solution.py:78
  79.5 57.2 %collective-permute-start.30 = (bf16[2,2,32,1792]{3,2,1,0:T(8,128)(2,1)}, bf16[2,2,32,1792]{3,2,1,0:T(8,128)(2,1)}, u32[]{:S(2)}, u32[]{:S(2)}) collective-permute-start(bf16[2,2,32,1792]{3,2,1,0:T(8,128)(2,1)} %pad_maximum_fusion.18), channel_id=1, source_target_pairs={{0,2},{1,3},{2,0},{3,1},{4,6},{5,7},{6,4},{7,5},{8,10},{9,11},{10,... | collective-permute-start | bytes 1376264 | tf_op jit(solution)/shard_map/ppermute | solution.py:78
  82.9 23.3 %collective-permute-start.19 = (bf16[2,2,32,1792]{3,2,1,0:T(8,128)(2,1)S(1)}, bf16[2,2,32,1792]{3,2,1,0:T(8,128)(2,1)S(1)}, u32[]{:S(2)}, u32[]{:S(2)}) collective-permute-start(bf16[2,2,32,1792]{3,2,1,0:T(8,128)(2,1)S(1)} %pad_maximum_fusion.16), channel_id=1, source_target_pairs={{0,2},{1,3},{2,0},{3,1},{4,6},{5,7},{6,4},{7,5},{8,10},{9,11},{10,... | collective-permute-start | bytes 1376264 | tf_op jit(solution)/shard_map/ppermute | solution.py:78
  88.1 18.2 %collective-permute-start.21 = (bf16[2,2,32,1792]{3,2,1,0:T(8,128)(2,1)S(1)}, bf16[2,2,32,1792]{3,2,1,0:T(8,128)(2,1)S(1)}, u32[]{:S(2)}, u32[]{:S(2)}) collective-permute-start(bf16[2,2,32,1792]{3,2,1,0:T(8,128)(2,1)S(1)} %pad_maximum_fusion.17), channel_id=1, source_target_pairs={{0,1},{1,0},{2,3},{3,2},{4,5},{5,4},{6,7},{7,6},{8,9},{9,8},{10,11... | collective-permute-start | bytes 1376264 | tf_op jit(solution)/shard_map/ppermute | solution.py:78
  90.1 48.5 %collective-permute-start.32 = (bf16[2,2,32,1792]{3,2,1,0:T(8,128)(2,1)}, bf16[2,2,32,1792]{3,2,1,0:T(8,128)(2,1)}, u32[]{:S(2)}, u32[]{:S(2)}) collective-permute-start(bf16[2,2,32,1792]{3,2,1,0:T(8,128)(2,1)} %pad_maximum_fusion.19), channel_id=1, source_target_pairs={{0,1},{1,0},{2,3},{3,2},{4,5},{5,4},{6,7},{7,6},{8,9},{9,8},{10,11... | collective-permute-start | bytes 1376264 | tf_op jit(solution)/shard_map/ppermute | solution.py:78
  136.4 40.3 %collective-permute-start.22 = (bf16[4,64,512]{2,1,0:T(8,128)(2,1)}, bf16[4,64,512]{2,1,0:T(8,128)(2,1)}, u32[]{:S(2)}, u32[]{:S(2)}) collective-permute-start(bf16[4,64,512]{2,1,0:T(8,128)(2,1)} %fusion.25), channel_id=1, source_target_pairs={{0,4},{1,5},{2,6},{3,7},{4,0},{5,1},{6,2},{7,3},{8,12},{9,13},{10,... | collective-permute-start | bytes 786440 | tf_op jit(solution)/shard_map/ppermute | solution.py:78
  164.8 16.5 %collective-permute-start.33 = (bf16[4,64,512]{2,1,0:T(8,128)(2,1)S(1)}, bf16[4,64,512]{2,1,0:T(8,128)(2,1)S(1)}, u32[]{:S(2)}, u32[]{:S(2)}) collective-permute-start(bf16[4,64,512]{2,1,0:T(8,128)(2,1)S(1)} %fusion.26), channel_id=1, source_target_pairs={{0,4},{1,5},{2,6},{3,7},{4,0},{5,1},{6,2},{7,3},{8,12},{9,13},{10,... | collective-permute-start | bytes 786440 | tf_op jit(solution)/shard_map/ppermute | solution.py:78
  177.8 6.3 %collective-permute-start.25 = (bf16[64,512]{1,0:T(8,128)(2,1)S(1)}, bf16[64,512]{1,0:T(8,128)(2,1)S(1)}, u32[]{:S(2)}, u32[]{:S(2)}) collective-permute-start(bf16[64,512]{1,0:T(8,128)(2,1)S(1)} %get-tuple-element.70), channel_id=1, source_target_pairs={{0,3},{1,2},{2,1},{3,0},{4,7},{5,6},{6,5},{7,4},{8,11},{9,10},{10,... | collective-permute-start | bytes 196616 | tf_op jit(solution)/shard_map/ppermute | solution.py:78
  181.4 6.9 %collective-permute-start.36 = (bf16[64,512]{1,0:T(8,128)(2,1)S(1)}, bf16[64,512]{1,0:T(8,128)(2,1)S(1)}, u32[]{:S(2)}, u32[]{:S(2)}) collective-permute-start(bf16[64,512]{1,0:T(8,128)(2,1)S(1)} %get-tuple-element.77), channel_id=1, source_target_pairs={{0,3},{1,2},{2,1},{3,0},{4,7},{5,6},{6,5},{7,4},{8,11},{9,10},{10,... | collective-permute-start | bytes 196616 | tf_op jit(solution)/shard_map/ppermute | solution.py:78
  185.1 7.8 %collective-permute-start.26 = (bf16[64,512]{1,0:T(8,128)(2,1)S(1)}, bf16[64,512]{1,0:T(8,128)(2,1)S(1)}, u32[]{:S(2)}, u32[]{:S(2)}) collective-permute-start(bf16[64,512]{1,0:T(8,128)(2,1)S(1)} %get-tuple-element.66), channel_id=1, source_target_pairs={{0,8},{1,9},{2,10},{3,11},{4,12},{5,13},{6,14},{7,15},{8,0},{9,1},... | collective-permute-start | bytes 196616 | tf_op jit(solution)/shard_map/ppermute | solution.py:78
  186.7 6.7 %collective-permute-start.28 = (bf16[64,512]{1,0:T(8,128)(2,1)S(1)}, bf16[64,512]{1,0:T(8,128)(2,1)S(1)}, u32[]{:S(2)}, u32[]{:S(2)}) collective-permute-start(bf16[64,512]{1,0:T(8,128)(2,1)S(1)} %get-tuple-element.67), channel_id=1, source_target_pairs={{0,24},{1,25},{2,26},{3,27},{4,28},{5,29},{6,30},{7,31},{8,16},{9,... | collective-permute-start | bytes 196616 | tf_op jit(solution)/shard_map/ppermute | solution.py:78
  188.3 10.3 %collective-permute-start.27 = (bf16[64,512]{1,0:T(8,128)(2,1)S(1)}, bf16[64,512]{1,0:T(8,128)(2,1)S(1)}, u32[]{:S(2)}, u32[]{:S(2)}) collective-permute-start(bf16[64,512]{1,0:T(8,128)(2,1)S(1)} %get-tuple-element.68), channel_id=1, source_target_pairs={{0,16},{1,17},{2,18},{3,19},{4,20},{5,21},{6,22},{7,23},{8,24},{9,... | collective-permute-start | bytes 196616 | tf_op jit(solution)/shard_map/ppermute | solution.py:78
  188.7 9.9 %collective-permute-start.37 = (bf16[64,512]{1,0:T(8,128)(2,1)S(1)}, bf16[64,512]{1,0:T(8,128)(2,1)S(1)}, u32[]{:S(2)}, u32[]{:S(2)}) collective-permute-start(bf16[64,512]{1,0:T(8,128)(2,1)S(1)} %get-tuple-element.73), channel_id=1, source_target_pairs={{0,8},{1,9},{2,10},{3,11},{4,12},{5,13},{6,14},{7,15},{8,0},{9,1},... | collective-permute-start | bytes 196616 | tf_op jit(solution)/shard_map/ppermute | solution.py:78
  191.3 7.4 %collective-permute-start.39 = (bf16[64,512]{1,0:T(8,128)(2,1)S(1)}, bf16[64,512]{1,0:T(8,128)(2,1)S(1)}, u32[]{:S(2)}, u32[]{:S(2)}) collective-permute-start(bf16[64,512]{1,0:T(8,128)(2,1)S(1)} %get-tuple-element.74), channel_id=1, source_target_pairs={{0,24},{1,25},{2,26},{3,27},{4,28},{5,29},{6,30},{7,31},{8,16},{9,... | collective-permute-start | bytes 196616 | tf_op jit(solution)/shard_map/ppermute | solution.py:78
  192.8 7.7 %collective-permute-start.38 = (bf16[64,512]{1,0:T(8,128)(2,1)S(1)}, bf16[64,512]{1,0:T(8,128)(2,1)S(1)}, u32[]{:S(2)}, u32[]{:S(2)}) collective-permute-start(bf16[64,512]{1,0:T(8,128)(2,1)S(1)} %get-tuple-element.75), channel_id=1, source_target_pairs={{0,16},{1,17},{2,18},{3,19},{4,20},{5,21},{6,22},{7,23},{8,24},{9,... | collective-permute-start | bytes 196616 | tf_op jit(solution)/shard_map/ppermute | solution.py:78
  (19 other events, 213.6 us)

commit v3 on v2

v3 whole, which is shorter than its diff:
```python
import functools
import math

import jax
import jax.numpy as jnp
from jax import lax
from jax.experimental import pallas as pl
from jax.experimental.pallas import tpu as pltpu
from jax.sharding import PartitionSpec as P

BLOCK = 128
CHUNKS = 2
AXES = ("node", "local")


def dequant(codes, scales):
    shape = codes.shape
    blocked = codes.astype(jnp.float32).reshape(shape[:-2] + (shape[-2] // BLOCK, BLOCK, shape[-1]))
    weight = blocked * scales.astype(jnp.float32)[..., :, None, :]
    return weight.reshape(shape).astype(jnp.bfloat16)


def pairs(move, places, ratio):
    out = []
    for plane in range(places):
        for half in range(ratio):
            for place in range(places):
                p, h, q = move(plane, half, place)
                out.append(
                    ((plane * ratio + half) * places + place, (p * ratio + h) * places + q)
                )
    return out


def pick(choices, index):
    out = choices[0]
    for i in range(1, len(choices)):
        out = jnp.where(index == i, choices[i], out)
    return out


def after(x, earlier):
    return lax.optimization_barrier((x, earlier))[0]


def input_grad_kernel(spots, place_ref, *refs):
    pieces, (w_ref, d_ref, term_ref) = refs[: len(spots)], refs[len(spots) :]

    @pl.when((pl.program_id(0) == 0) & (pl.program_id(1) == 0))
    def _():
        for piece, first in zip(pieces, spots):
            streams, _, part, _ = piece.shape
            for s in range(streams):
                d_ref[:, pl.ds(first + s * part, part), :] = piece[s]

    numbers = (((1,), (1,)), ((), ()))
    term = lax.dot_general(d_ref[0], w_ref[0], numbers, preferred_element_type=jnp.float32)
    term += lax.dot_general(d_ref[1], w_ref[1], numbers, preferred_element_type=jnp.float32)
    term_ref[0] = term.astype(jnp.bfloat16)


def input_grad(pieces, spots, w_gu, half, ratio, total):
    _, owned, group = w_gu.shape
    feats = owned // ratio
    step = min(feats, 256)
    blocks = feats // step
    whole = lambda x: pl.BlockSpec(x.shape, lambda e, i, place: (0,) * x.ndim)
    return pl.pallas_call(
        functools.partial(input_grad_kernel, spots),
        grid_spec=pltpu.PrefetchScalarGridSpec(
            num_scalar_prefetch=1,
            grid=(ratio, blocks),
            in_specs=[whole(x) for x in pieces]
            + [pl.BlockSpec((2, step, group), lambda e, i, place: (0, (place[0] ^ e) * blocks + i, 0))],
            out_specs=[
                pl.BlockSpec((2, total, group), lambda e, i, place: (0, 0, 0)),
                pl.BlockSpec((1, total, step), lambda e, i, place: (e, 0, i)),
            ],
        ),
        out_shape=[
            jax.ShapeDtypeStruct((2, total, group), jnp.bfloat16),
            jax.ShapeDtypeStruct((ratio, total, feats), jnp.bfloat16),
        ],
        compiler_params=pltpu.CompilerParams(vmem_limit_bytes=40 * 1024 * 1024),
    )(half[None], *pieces, w_gu)


def weight_grad_kernel(scale, *refs):
    count = (len(refs) - 1) // 2
    total = 0.0
    for features_ref, d_ref in zip(refs[:count], refs[count:-1]):
        total += lax.dot_general(
            features_ref[...], d_ref[0], (((0,), (0,)), ((), ())), preferred_element_type=jnp.float32
        )
    refs[-1][0] = scale * total


def weight_grad(features, d_both, scale):
    owned, group = features[0].shape[1], d_both[0].shape[2]
    step = min(owned, 256)
    return pl.pallas_call(
        functools.partial(weight_grad_kernel, scale),
        grid=(2, owned // step),
        in_specs=[pl.BlockSpec((f.shape[0], step), lambda g, i: (0, i)) for f in features]
        + [pl.BlockSpec((1, d.shape[1], group), lambda g, i: (g, 0, 0)) for d in d_both],
        out_specs=pl.BlockSpec((1, step, group), lambda g, i: (g, i, 0)),
        out_shape=jax.ShapeDtypeStruct((2, owned, group), jnp.float32),
        compiler_params=pltpu.CompilerParams(vmem_limit_bytes=40 * 1024 * 1024),
    )(*features, *d_both)


def body(tokens, gate_up_codes, gate_up_scales, d_hidden):
    rows, feats = tokens.shape
    nodes, places = lax.axis_size("node"), lax.axis_size("local")
    ratio = nodes // places
    _, owned, group = gate_up_codes.shape
    bits = [1 << b for b in range(places.bit_length() - 1)]
    node, place = lax.axis_index("node"), lax.axis_index("local")
    plane, half = node // ratio, node % ratio
    mask = plane ^ place
    chunk = rows // CHUNKS
    part = chunk // 2
    orders = (bits, bits[::-1])

    def permute(x, move):
        return lax.ppermute(x, AXES, pairs(move, places, ratio))

    def features_of(x):
        got = [permute(x, lambda p, h, q, j=j: (q ^ j, h, p)) for j in range(places)]
        got = jnp.stack([pick(got, k ^ mask) for k in range(places)])
        halves = [got] + [permute(got, lambda p, h, q, e=e: (p, h ^ e, q)) for e in range(1, ratio)]
        return jnp.concatenate([pick(halves, half ^ e) for e in range(ratio)], axis=2)

    def reduce_local(x, order):
        ks = list(range(places))
        x = x.astype(jnp.float32)
        for bit in order:
            away = [i for i, k in enumerate(ks) if k & bit]
            stay = [i for i, k in enumerate(ks) if not k & bit]
            sent = jnp.stack([x[:, i] for i in away], axis=1).astype(jnp.bfloat16)
            got = permute(sent, lambda p, h, q: (p, h, q ^ bit))
            x = jnp.stack([x[:, i] for i in stay], axis=1) + got.astype(jnp.float32)
            ks = [ks[i] for i in stay]
        return x[:, 0]

    def gather_local(x):
        direct = {bit: permute(x, lambda p, h, q: (p, h, q ^ bit)) for bit in bits}
        pieces, spots = [x] + [direct[bit] for bit in bits], [0] + [bit * chunk for bit in bits]
        for s, order in enumerate(orders):
            held = {0: None}
            for bit in order:
                for k in list(held):
                    if k == 0:
                        held[bit] = direct[bit][s : s + 1]
                    else:
                        held[k ^ bit] = permute(held[k], lambda p, h, q: (p, h, q ^ bit))
                        pieces.append(held[k ^ bit])
                        spots.append((k ^ bit) * chunk + s * part)
        return pieces, spots

    w_gu = dequant(gate_up_codes, gate_up_scales)
    hidden, all_features, all_d, d_tokens = [], [], [], []
    for c in range(CHUNKS):
        features = features_of(tokens[c * chunk : (c + 1) * chunk])
        flat = features.reshape(places * chunk, owned)
        all_features.append(flat)
        partial = [
            jnp.dot(flat, w_gu[g], preferred_element_type=jnp.float32)
            .astype(jnp.bfloat16)
            .reshape(places, chunk, group)
            for g in range(2)
        ]
        streams = []
        for s in range(2):
            at = slice(s * part, (s + 1) * part)
            both = reduce_local(jnp.stack([p[:, at] for p in partial]), orders[s])
            gate, up = both[0], both[1]
            sigmoid_gate = jax.nn.sigmoid(gate)
            active = gate * sigmoid_gate
            hidden.append((active * up).astype(jnp.bfloat16))
            first = c * chunk + s * part
            grad_in = d_hidden[first : first + part].astype(jnp.float32)
            d_gate = grad_in * up * sigmoid_gate * (1.0 + gate * (1.0 - sigmoid_gate))
            d_up = grad_in * active
            streams.append(jnp.stack([d_gate, d_up]).astype(jnp.bfloat16))
        pieces, spots = gather_local(jnp.stack(streams))
        d_all, term = input_grad(pieces, spots, w_gu, half, ratio, places * chunk)
        all_d.append(d_all)
        summed = term[0].astype(jnp.float32)
        for e in range(1, ratio):
            got = permute(term[e], lambda p, h, q: (p, h ^ e, q))
            summed = summed + got.astype(jnp.float32)
        summed = summed.astype(jnp.bfloat16).reshape(places, chunk, feats)
        arrived = [summed[0]] + [
            permute(summed[k], lambda p, h, q: (p, h, q ^ k)) for k in range(1, places)
        ]
        arrived = [pick(arrived, j ^ mask) for j in range(places)]
        result = arrived[0].astype(jnp.float32)
        for j in range(1, places):
            got = permute(arrived[j], lambda p, h, q: (p ^ j, h, q))
            result = result + got.astype(jnp.float32)
        d_tokens.append(result.astype(jnp.bfloat16))

    grads = weight_grad(all_features, all_d, 1.0 / math.sqrt(rows * places))
    return jnp.concatenate(hidden), jnp.concatenate(d_tokens), grads


def solution(mesh):
    placed = (
        P("local", "node"),
        P(None, "local", "node"),
        P(None, "local", "node"),
        P("local", "node"),
    )
    return jax.shard_map(
        body,
        mesh=mesh,
        in_specs=placed,
        out_specs=(P("local", "node"), P("local", "node"), P(None, "local", "node")),
        check_vma=False,
    )
```

time: 202 us -> 141 us (0.70)
  local copies, waits for them, and re-layouts: 48.3 us -> 1.5 us
  other arithmetic: 21.6 us -> 9.32 us
  matrix products: 11.7 us -> 4.62 us
  Pallas kernels: 8.56 us -> 15.4 us
  starting transfers between devices: 58.9 us -> 56.7 us
    slice x36 -> x6, local copies, waits for them, and re-layouts: 44.3 us -> 0.09 us  [the longest x4 0.06 us: gather_local(): held[bit] = direct[bit][s:s + 1]]
    concatenate x13 -> x2, other arithmetic: 11.1 us -> 0.11 us  [features_of(): jnp.concatenate([pick(halves, half ^ e) for e in range(ratio)], axis=2)]
    dot_general x4 -> x0, matrix products: 7.17 us -> none  [the longest x2 4.87 us: body(): lax.dot_general(d_chunk[0], w_gu[0], (((1,), (1,)), ((), ())), preferred_...]
    pallas_call x0 -> x2, Pallas kernels: none -> 6.9 us  [input_grad(): pl.pallas_call(functools.partial(input_grad_kernel, spots), grid_spec=plt...]
    ppermute x40, starting transfers between devices: 58.9 us -> 56.7 us  [permute(): return lax.ppermute(x, AXES, pairs(move, places, ratio))]
  transfers between devices with their start and end apart: 40 -> 40, of which waited for: 14 -> 13; matrix products, arithmetic and copies ran while one was open for 36% -> 7% of each run, Pallas kernels for 4% -> 11%
where the time goes in v3:
time: 141 us
  starting transfers between devices  56.7 us (40%)
  waiting for transfers between devices  52.3 us (37%)
  Pallas kernels  15.4 us (11%)
  other arithmetic  9.32 us (7%)
  matrix products  4.62 us (3%)
  local copies, waits for them, and re-layouts  1.5 us (1%)
    ppermute x40, starting transfers between devices, permute(): return lax.ppermute(x, AXES, pairs(move, places, ratio))  56.7 us
    ppermute x40, waiting for transfers between devices, permute(): return lax.ppermute(x, AXES, pairs(move, places, ratio))  52.3 us
    pallas_call x1, Pallas kernels, weight_grad(): pl.pallas_call(functools.partial(weight_grad_kernel, scale), grid=(2, own...  8.49 us
    pallas_call x2, Pallas kernels, input_grad(): pl.pallas_call(functools.partial(input_grad_kernel, spots), grid_spec=plt...  6.9 us
    dot_general x4, matrix products, body(): jnp.dot(flat, w_gu[g], preferred_element_type=jnp.float32)  4.62 us
    convert_element_type x1, other arithmetic, dequant(): return weight.reshape(shape).astype(jnp.bfloat16)  4.5 us
  transfers between devices with their start and end apart: 40, of which 13 were waited for; matrix products, arithmetic and copies ran while one was open for 7% of the time, Pallas kernels for 11%

profile of v3, /device:TPU:0, one launch (start us, length us, event | category | flops | bytes accessed | tf_op | source)
XLA Modules:
  0.0 141.0 jit_solution(6203996539623452265)
XLA Ops:
  2.2 5.7 %collective-permute-start.11 = (bf16[64,512]{1,0:T(8,128)(2,1)S(1)}, bf16[64,512]{1,0:T(8,128)(2,1)S(1)}, u32[]{:S(2)}, u32[]{:S(2)}) collective-permute-start(bf16[64,512]{1,0:T(8,128)(2,1)S(1)} %get-tuple-element.67), channel_id=1, source_target_pairs={{0,8},{1,0},{2,24},{3,16},{4,12},{5,4},{6,28},{7,20},{8,9},{9,1},{... | collective-permute-start | bytes 196616 | tf_op jit(solution)/shard_map/ppermute | solution.py:126
  7.9 3.5 %collective-permute-start.10 = (bf16[64,512]{1,0:T(8,128)(2,1)S(1)}, bf16[64,512]{1,0:T(8,128)(2,1)S(1)}, u32[]{:S(2)}, u32[]{:S(2)}) collective-permute-start(bf16[64,512]{1,0:T(8,128)(2,1)S(1)} %get-tuple-element.67), channel_id=1, source_target_pairs={{0,16},{1,24},{2,0},{3,8},{4,20},{5,28},{6,4},{7,12},{8,17},{9,25}... | collective-permute-start | bytes 196616 | tf_op jit(solution)/shard_map/ppermute | solution.py:126
  11.4 1.9 %collective-permute-start.9 = (bf16[64,512]{1,0:T(8,128)(2,1)S(1)}, bf16[64,512]{1,0:T(8,128)(2,1)S(1)}, u32[]{:S(2)}, u32[]{:S(2)}) collective-permute-start(bf16[64,512]{1,0:T(8,128)(2,1)S(1)} %get-tuple-element.67), channel_id=1, source_target_pairs={{0,24},{1,16},{2,8},{3,0},{4,28},{5,20},{6,12},{7,4},{8,25},{9,17}... | collective-permute-start | bytes 196616 | tf_op jit(solution)/shard_map/ppermute | solution.py:126
  14.8 4.5 %fusion.refs_5_ = bf16[2,1024,1792]{2,1,0:T(8,128)(2,1)S(1)} fusion(bf16[2,1024,1792]{2,1,0:T(8,128)(2,1)} %param.5, f32[2,8,1792]{2,1,0:T(8,128)S(1)} %convert_element_type.172), kind=kLoop, calls=%fused_computation.1 | loop fusion | flops 11010048 | bytes 14794752 | tf_op jit(solution)/shard_map/convert_element_type | solution.py:20
  19.4 4.2 %collective-permute-start.2 = (bf16[64,512]{1,0:T(8,128)(2,1)S(1)}, bf16[64,512]{1,0:T(8,128)(2,1)S(1)}, u32[]{:S(2)}, u32[]{:S(2)}) collective-permute-start(bf16[64,512]{1,0:T(8,128)(2,1)S(1)} %get-tuple-element.66), channel_id=1, source_target_pairs={{0,8},{1,0},{2,24},{3,16},{4,12},{5,4},{6,28},{7,20},{8,9},{9,1},{... | collective-permute-start | bytes 196616 | tf_op jit(solution)/shard_map/ppermute | solution.py:126
  23.6 2.6 %collective-permute-start.1 = (bf16[64,512]{1,0:T(8,128)(2,1)S(1)}, bf16[64,512]{1,0:T(8,128)(2,1)S(1)}, u32[]{:S(2)}, u32[]{:S(2)}) collective-permute-start(bf16[64,512]{1,0:T(8,128)(2,1)S(1)} %get-tuple-element.66), channel_id=1, source_target_pairs={{0,16},{1,24},{2,0},{3,8},{4,20},{5,28},{6,4},{7,12},{8,17},{9,25}... | collective-permute-start | bytes 196616 | tf_op jit(solution)/shard_map/ppermute | solution.py:126
  29.0 3.0 %collective-permute-done = bf16[64,512]{1,0:T(8,128)(2,1)S(1)} collective-permute-done((bf16[64,512]{1,0:T(8,128)(2,1)S(1)}, bf16[64,512]{1,0:T(8,128)(2,1)S(1)}, u32[]{:S(2)}, u32[]{:S(2)}) %collective-permute-start) | collective-permute-done | bytes 65568 | tf_op jit(solution)/shard_map/ppermute | solution.py:126
  37.7 2.1 %collective-permute-start.14 = (bf16[2,2,32,1792]{3,2,1,0:T(8,128)(2,1)S(1)}, bf16[2,2,32,1792]{3,2,1,0:T(8,128)(2,1)S(1)}, u32[]{:S(2)}, u32[]{:S(2)}) collective-permute-start(bf16[2,2,32,1792]{3,2,1,0:T(8,128)(2,1)S(1)} %pad_maximum_fusion.7), channel_id=1, source_target_pairs={{0,1},{1,0},{2,3},{3,2},{4,5},{5,4},{6,7},{7,6},{8,9},{9,8},{10,11... | collective-permute-start | bytes 1376264 | tf_op jit(solution)/shard_map/ppermute | solution.py:126
  40.8 2.1 %collective-permute-start.5 = (bf16[2,2,32,1792]{3,2,1,0:T(8,128)(2,1)S(1)}, bf16[2,2,32,1792]{3,2,1,0:T(8,128)(2,1)S(1)}, u32[]{:S(2)}, u32[]{:S(2)}) collective-permute-start(bf16[2,2,32,1792]{3,2,1,0:T(8,128)(2,1)S(1)} %pad_maximum_fusion.6), channel_id=1, source_target_pairs={{0,1},{1,0},{2,3},{3,2},{4,5},{5,4},{6,7},{7,6},{8,9},{9,8},{10,11... | collective-permute-start | bytes 1376264 | tf_op jit(solution)/shard_map/ppermute | solution.py:126
  43.0 10.3 %collective-permute-done.16 = bf16[2,2,32,1792]{3,2,1,0:T(8,128)(2,1)S(1)} collective-permute-done((bf16[2,2,32,1792]{3,2,1,0:T(8,128)(2,1)S(1)}, bf16[2,2,32,1792]{3,2,1,0:T(8,128)(2,1)S(1)}, u32[]{:S(2)}, u32[]{:S(2)}) %collective-permute-start.16) | collective-permute-done | bytes 458784 | tf_op jit(solution)/shard_map/ppermute | solution.py:126
  54.3 2.1 %collective-permute-start.15 = (bf16[2,1,32,1792]{3,2,1,0:T(8,128)(2,1)S(1)}, bf16[2,1,32,1792]{3,2,1,0:T(8,128)(2,1)S(1)}, u32[]{:S(2)}, u32[]{:S(2)}) collective-permute-start(bf16[2,1,32,1792]{3,2,1,0:T(8,128)(2,1)S(1)} %slice.463), channel_id=1, source_target_pairs={{0,2},{1,3},{2,0},{3,1},{4,6},{5,7},{6,4},{7,5},{8,10},{9,11},{10,... | collective-permute-start | bytes 688136 | tf_op jit(solution)/shard_map/ppermute | solution.py:126
  56.4 6.7 %collective-permute-done.7 = bf16[2,2,32,1792]{3,2,1,0:T(8,128)(2,1)S(1)} collective-permute-done((bf16[2,2,32,1792]{3,2,1,0:T(8,128)(2,1)S(1)}, bf16[2,2,32,1792]{3,2,1,0:T(8,128)(2,1)S(1)}, u32[]{:S(2)}, u32[]{:S(2)}) %collective-permute-start.7) | collective-permute-done | bytes 458784 | tf_op jit(solution)/shard_map/ppermute | solution.py:126
  64.1 2.1 %collective-permute-start.6 = (bf16[2,1,32,1792]{3,2,1,0:T(8,128)(2,1)S(1)}, bf16[2,1,32,1792]{3,2,1,0:T(8,128)(2,1)S(1)}, u32[]{:S(2)}, u32[]{:S(2)}) collective-permute-start(bf16[2,1,32,1792]{3,2,1,0:T(8,128)(2,1)S(1)} %slice.465), channel_id=1, source_target_pairs={{0,2},{1,3},{2,0},{3,1},{4,6},{5,7},{6,4},{7,5},{8,10},{9,11},{10,... | collective-permute-start | bytes 688136 | tf_op jit(solution)/shard_map/ppermute | solution.py:126
  66.3 1.7 %collective-permute-done.15 = bf16[2,1,32,1792]{3,2,1,0:T(8,128)(2,1)S(1)} collective-permute-done((bf16[2,1,32,1792]{3,2,1,0:T(8,128)(2,1)S(1)}, bf16[2,1,32,1792]{3,2,1,0:T(8,128)(2,1)S(1)}, u32[]{:S(2)}, u32[]{:S(2)}) %collective-permute-start.15) | collective-permute-done | bytes 229408 | tf_op jit(solution)/shard_map/ppermute | solution.py:126
  68.1 2.6 %collective-permute-done.8 = bf16[2,1,32,1792]{3,2,1,0:T(8,128)(2,1)S(1)} collective-permute-done((bf16[2,1,32,1792]{3,2,1,0:T(8,128)(2,1)S(1)}, bf16[2,1,32,1792]{3,2,1,0:T(8,128)(2,1)S(1)}, u32[]{:S(2)}, u32[]{:S(2)}) %collective-permute-start.8) | collective-permute-done | bytes 229408 | tf_op jit(solution)/shard_map/ppermute | solution.py:126
  73.9 1.6 %collective-permute-start.29 = (bf16[2,2,32,1792]{3,2,1,0:T(8,128)(2,1)S(1)}, bf16[2,2,32,1792]{3,2,1,0:T(8,128)(2,1)S(1)}, u32[]{:S(2)}, u32[]{:S(2)}) collective-permute-start(bf16[2,2,32,1792]{3,2,1,0:T(8,128)(2,1)S(1)} %maximum_maximum_fusion.1.refs_0_), channel_id=1, source_target_pairs={{0,1},{1,0},{2,3},{3,2},{4,5},{5,4},{6,7},{7,6},{8,9},{9,8},{10,11... | collective-permute-start | bytes 1376264 | tf_op jit(solution)/shard_map/ppermute | solution.py:126
  77.0 9.3 %collective-permute-done.30.refs_2_ = bf16[2,2,32,1792]{3,2,1,0:T(8,128)(2,1)S(1)} collective-permute-done((bf16[2,2,32,1792]{3,2,1,0:T(8,128)(2,1)S(1)}, bf16[2,2,32,1792]{3,2,1,0:T(8,128)(2,1)S(1)}, u32[]{:S(2)}, u32[]{:S(2)}) %collective-permute-start.30) | collective-permute-done | bytes 458784 | tf_op jit(solution)/shard_map/ppermute | solution.py:126
  87.4 1.8 %collective-permute-start.31 = (bf16[1,2,32,1792]{3,2,1,0:T(8,128)(2,1)S(1)}, bf16[1,2,32,1792]{3,2,1,0:T(8,128)(2,1)S(1)}, u32[]{:S(2)}, u32[]{:S(2)}) collective-permute-start(bf16[1,2,32,1792]{3,2,1,0:T(8,128)(2,1)S(1)} %slice.310), channel_id=1, source_target_pairs={{0,2},{1,3},{2,0},{3,1},{4,6},{5,7},{6,4},{7,5},{8,10},{9,11},{10,... | collective-permute-start | bytes 688136 | tf_op jit(solution)/shard_map/ppermute | solution.py:126
  89.3 6.9 %collective-permute-done.19.refs_2_ = bf16[2,2,32,1792]{3,2,1,0:T(8,128)(2,1)S(1)} collective-permute-done((bf16[2,2,32,1792]{3,2,1,0:T(8,128)(2,1)S(1)}, bf16[2,2,32,1792]{3,2,1,0:T(8,128)(2,1)S(1)}, u32[]{:S(2)}, u32[]{:S(2)}) %collective-permute-start.19) | collective-permute-done | bytes 458784 | tf_op jit(solution)/shard_map/ppermute | solution.py:126
  97.2 1.8 %collective-permute-start.20 = (bf16[1,2,32,1792]{3,2,1,0:T(8,128)(2,1)S(1)}, bf16[1,2,32,1792]{3,2,1,0:T(8,128)(2,1)S(1)}, u32[]{:S(2)}, u32[]{:S(2)}) collective-permute-start(bf16[1,2,32,1792]{3,2,1,0:T(8,128)(2,1)S(1)} %slice.304), channel_id=1, source_target_pairs={{0,2},{1,3},{2,0},{3,1},{4,6},{5,7},{6,4},{7,5},{8,10},{9,11},{10,... | collective-permute-start | bytes 688136 | tf_op jit(solution)/shard_map/ppermute | solution.py:126
  99.0 3.1 %collective-permute-done.32.refs_4_ = bf16[1,2,32,1792]{3,2,1,0:T(8,128)(2,1)S(1)} collective-permute-done((bf16[1,2,32,1792]{3,2,1,0:T(8,128)(2,1)S(1)}, bf16[1,2,32,1792]{3,2,1,0:T(8,128)(2,1)S(1)}, u32[]{:S(2)}, u32[]{:S(2)}) %collective-permute-start.32) | collective-permute-done | bytes 229408 | tf_op jit(solution)/shard_map/ppermute | solution.py:126
  102.1 3.4 %shard_map.68 = (bf16[2,256,1792]{2,1,0:T(8,128)(2,1)S(1)}, bf16[2,256,512]{2,1,0:T(8,128)(2,1)S(1)}) custom-call(s32[1]{0:T(128)} %bitcast.33.place_ref, bf16[2,2,32,1792]{3,2,1,0:T(8,128)(2,1)S(1)} %maximum_maximum_fusion.1.refs_0_, bf16[2,2,32,1792]{3,2,1,0:T(8,128)(2,1)S(1)} %collective-permute-done.29.refs_1_, ...), custom_call_target="tpu_custom_call" | custom-call | tf_op jit(solution)/shard_map/pallas_call | solution.py:68
  106.5 3.5 %shard_map.67 = (bf16[2,256,1792]{2,1,0:T(8,128)(2,1)S(1)}, bf16[2,256,512]{2,1,0:T(8,128)(2,1)S(1)}) custom-call(s32[1]{0:T(128)} %bitcast.33.place_ref, bf16[2,2,32,1792]{3,2,1,0:T(8,128)(2,1)S(1)} %maximum_maximum_fusion.refs_0_, bf16[2,2,32,1792]{3,2,1,0:T(8,128)(2,1)S(1)} %collective-permute-done.18.refs_1_, ...), custom_call_target="tpu_custom_call" | custom-call | tf_op jit(solution)/shard_map/pallas_call | solution.py:68
  110.6 8.5 %shard_map.69 = f32[2,1024,1792]{2,1,0:T(8,128)} custom-call(bf16[256,1024]{1,0:T(8,128)(2,1)S(1)} %bitcast.174, bf16[256,1024]{1,0:T(8,128)(2,1)S(1)} %bitcast.171, bf16[2,256,1792]{2,1,0:T(8,128)(2,1)S(1)} %get-tuple-element.9.refs_2_, bf16[2,256,1792]{2,1,0:T(8,128)(2,1)S(1)} %get-tuple-element.10.refs_3_), custom_call_target="tpu_custom_call" | custom-call | tf_op jit(solution)/shard_map/pallas_call | solution.py:101
  119.1 1.7 %collective-permute-start.36 = (bf16[64,512]{1,0:T(8,128)(2,1)S(1)}, bf16[64,512]{1,0:T(8,128)(2,1)S(1)}, u32[]{:S(2)}, u32[]{:S(2)}) collective-permute-start(bf16[64,512]{1,0:T(8,128)(2,1)S(1)} %get-tuple-element.55), channel_id=1, source_target_pairs={{0,1},{1,0},{2,3},{3,2},{4,5},{5,4},{6,7},{7,6},{8,9},{9,8},{10,11... | collective-permute-start | bytes 196616 | tf_op jit(solution)/shard_map/ppermute | solution.py:126
  121.1 1.6 %collective-permute-start.34 = (bf16[64,512]{1,0:T(8,128)(2,1)S(1)}, bf16[64,512]{1,0:T(8,128)(2,1)S(1)}, u32[]{:S(2)}, u32[]{:S(2)}) collective-permute-start(bf16[64,512]{1,0:T(8,128)(2,1)S(1)} %get-tuple-element.57), channel_id=1, source_target_pairs={{0,3},{1,2},{2,1},{3,0},{4,7},{5,6},{6,5},{7,4},{8,11},{9,10},{10,... | collective-permute-start | bytes 196616 | tf_op jit(solution)/shard_map/ppermute | solution.py:126
  122.8 1.7 %collective-permute-start.25 = (bf16[64,512]{1,0:T(8,128)(2,1)S(1)}, bf16[64,512]{1,0:T(8,128)(2,1)S(1)}, u32[]{:S(2)}, u32[]{:S(2)}) collective-permute-start(bf16[64,512]{1,0:T(8,128)(2,1)S(1)} %get-tuple-element.52), channel_id=1, source_target_pairs={{0,1},{1,0},{2,3},{3,2},{4,5},{5,4},{6,7},{7,6},{8,9},{9,8},{10,11... | collective-permute-start | bytes 196616 | tf_op jit(solution)/shard_map/ppermute | solution.py:126
  124.8 1.6 %collective-permute-start.23 = (bf16[64,512]{1,0:T(8,128)(2,1)S(1)}, bf16[64,512]{1,0:T(8,128)(2,1)S(1)}, u32[]{:S(2)}, u32[]{:S(2)}) collective-permute-start(bf16[64,512]{1,0:T(8,128)(2,1)S(1)} %get-tuple-element.54), channel_id=1, source_target_pairs={{0,3},{1,2},{2,1},{3,0},{4,7},{5,6},{6,5},{7,4},{8,11},{9,10},{10,... | collective-permute-start | bytes 196616 | tf_op jit(solution)/shard_map/ppermute | solution.py:126
  126.7 3.1 %collective-permute-start.39 = (bf16[64,512]{1,0:T(8,128)(2,1)S(1)}, bf16[64,512]{1,0:T(8,128)(2,1)S(1)}, u32[]{:S(2)}, u32[]{:S(2)}) collective-permute-start(bf16[64,512]{1,0:T(8,128)(2,1)S(1)} %get-tuple-element.49), channel_id=1, source_target_pairs={{0,24},{1,25},{2,26},{3,27},{4,28},{5,29},{6,30},{7,31},{8,16},{9,... | collective-permute-start | bytes 196616 | tf_op jit(solution)/shard_map/ppermute | solution.py:126
  131.2 3.1 %collective-permute-start.28 = (bf16[64,512]{1,0:T(8,128)(2,1)S(1)}, bf16[64,512]{1,0:T(8,128)(2,1)S(1)}, u32[]{:S(2)}, u32[]{:S(2)}) collective-permute-start(bf16[64,512]{1,0:T(8,128)(2,1)S(1)} %get-tuple-element.40), channel_id=1, source_target_pairs={{0,24},{1,25},{2,26},{3,27},{4,28},{5,29},{6,30},{7,31},{8,16},{9,... | collective-permute-start | bytes 196616 | tf_op jit(solution)/shard_map/ppermute | solution.py:126
  134.3 4.2 %collective-permute-done.38 = bf16[64,512]{1,0:T(8,128)(2,1)S(1)} collective-permute-done((bf16[64,512]{1,0:T(8,128)(2,1)S(1)}, bf16[64,512]{1,0:T(8,128)(2,1)S(1)}, u32[]{:S(2)}, u32[]{:S(2)}) %collective-permute-start.38) | collective-permute-done | bytes 65568 | tf_op jit(solution)/shard_map/ppermute | solution.py:126
  138.6 1.6 %collective-permute-done.27 = bf16[64,512]{1,0:T(8,128)(2,1)S(1)} collective-permute-done((bf16[64,512]{1,0:T(8,128)(2,1)S(1)}, bf16[64,512]{1,0:T(8,128)(2,1)S(1)}, u32[]{:S(2)}, u32[]{:S(2)}) %collective-permute-start.27) | collective-permute-done | bytes 65568 | tf_op jit(solution)/shard_map/ppermute | solution.py:126
  (113 shorter events, 26.2 us)
Async XLA Ops:
  1.5 17.8 %collective-permute-start.12 = (bf16[64,512]{1,0:T(8,128)(2,1)S(1)}, bf16[64,512]{1,0:T(8,128)(2,1)S(1)}, u32[]{:S(2)}, u32[]{:S(2)}) collective-permute-start(bf16[64,512]{1,0:T(8,128)(2,1)S(1)} %get-tuple-element.67), channel_id=1, source_target_pairs={{0,0},{1,8},{2,16},{3,24},{4,4},{5,12},{6,20},{7,28},{8,1},{9,9},{... | collective-permute-start | bytes 196616 | tf_op jit(solution)/shard_map/ppermute | solution.py:126
  2.2 21.4 %collective-permute-start.11 = (bf16[64,512]{1,0:T(8,128)(2,1)S(1)}, bf16[64,512]{1,0:T(8,128)(2,1)S(1)}, u32[]{:S(2)}, u32[]{:S(2)}) collective-permute-start(bf16[64,512]{1,0:T(8,128)(2,1)S(1)} %get-tuple-element.67), channel_id=1, source_target_pairs={{0,8},{1,0},{2,24},{3,16},{4,12},{5,4},{6,28},{7,20},{8,9},{9,1},{... | collective-permute-start | bytes 196616 | tf_op jit(solution)/shard_map/ppermute | solution.py:126
  7.9 18.3 %collective-permute-start.10 = (bf16[64,512]{1,0:T(8,128)(2,1)S(1)}, bf16[64,512]{1,0:T(8,128)(2,1)S(1)}, u32[]{:S(2)}, u32[]{:S(2)}) collective-permute-start(bf16[64,512]{1,0:T(8,128)(2,1)S(1)} %get-tuple-element.67), channel_id=1, source_target_pairs={{0,16},{1,24},{2,0},{3,8},{4,20},{5,28},{6,4},{7,12},{8,17},{9,25}... | collective-permute-start | bytes 196616 | tf_op jit(solution)/shard_map/ppermute | solution.py:126
  11.4 16.1 %collective-permute-start.9 = (bf16[64,512]{1,0:T(8,128)(2,1)S(1)}, bf16[64,512]{1,0:T(8,128)(2,1)S(1)}, u32[]{:S(2)}, u32[]{:S(2)}) collective-permute-start(bf16[64,512]{1,0:T(8,128)(2,1)S(1)} %get-tuple-element.67), channel_id=1, source_target_pairs={{0,24},{1,16},{2,8},{3,0},{4,28},{5,20},{6,12},{7,4},{8,25},{9,17}... | collective-permute-start | bytes 196616 | tf_op jit(solution)/shard_map/ppermute | solution.py:126
  13.3 14.4 %collective-permute-start.3 = (bf16[64,512]{1,0:T(8,128)(2,1)S(1)}, bf16[64,512]{1,0:T(8,128)(2,1)S(1)}, u32[]{:S(2)}, u32[]{:S(2)}) collective-permute-start(bf16[64,512]{1,0:T(8,128)(2,1)S(1)} %get-tuple-element.66), channel_id=1, source_target_pairs={{0,0},{1,8},{2,16},{3,24},{4,4},{5,12},{6,20},{7,28},{8,1},{9,9},{... | collective-permute-start | bytes 196616 | tf_op jit(solution)/shard_map/ppermute | solution.py:126
  19.4 8.3 %collective-permute-start.2 = (bf16[64,512]{1,0:T(8,128)(2,1)S(1)}, bf16[64,512]{1,0:T(8,128)(2,1)S(1)}, u32[]{:S(2)}, u32[]{:S(2)}) collective-permute-start(bf16[64,512]{1,0:T(8,128)(2,1)S(1)} %get-tuple-element.66), channel_id=1, source_target_pairs={{0,8},{1,0},{2,24},{3,16},{4,12},{5,4},{6,28},{7,20},{8,9},{9,1},{... | collective-permute-start | bytes 196616 | tf_op jit(solution)/shard_map/ppermute | solution.py:126
  26.2 5.8 %collective-permute-start = (bf16[64,512]{1,0:T(8,128)(2,1)S(1)}, bf16[64,512]{1,0:T(8,128)(2,1)S(1)}, u32[]{:S(2)}, u32[]{:S(2)}) collective-permute-start(bf16[64,512]{1,0:T(8,128)(2,1)S(1)} %get-tuple-element.66), channel_id=1, source_target_pairs={{0,24},{1,16},{2,8},{3,0},{4,28},{5,20},{6,12},{7,4},{8,25},{9,17}... | collective-permute-start | bytes 196616 | tf_op jit(solution)/shard_map/ppermute | solution.py:126
  37.7 16.4 %collective-permute-start.14 = (bf16[2,2,32,1792]{3,2,1,0:T(8,128)(2,1)S(1)}, bf16[2,2,32,1792]{3,2,1,0:T(8,128)(2,1)S(1)}, u32[]{:S(2)}, u32[]{:S(2)}) collective-permute-start(bf16[2,2,32,1792]{3,2,1,0:T(8,128)(2,1)S(1)} %pad_maximum_fusion.7), channel_id=1, source_target_pairs={{0,1},{1,0},{2,3},{3,2},{4,5},{5,4},{6,7},{7,6},{8,9},{9,8},{10,11... | collective-permute-start | bytes 1376264 | tf_op jit(solution)/shard_map/ppermute | solution.py:126
  39.9 13.4 %collective-permute-start.16 = (bf16[2,2,32,1792]{3,2,1,0:T(8,128)(2,1)S(1)}, bf16[2,2,32,1792]{3,2,1,0:T(8,128)(2,1)S(1)}, u32[]{:S(2)}, u32[]{:S(2)}) collective-permute-start(bf16[2,2,32,1792]{3,2,1,0:T(8,128)(2,1)S(1)} %pad_maximum_fusion.4), channel_id=1, source_target_pairs={{0,2},{1,3},{2,0},{3,1},{4,6},{5,7},{6,4},{7,5},{8,10},{9,11},{10,... | collective-permute-start | bytes 1376264 | tf_op jit(solution)/shard_map/ppermute | solution.py:126
  40.8 23.2 %collective-permute-start.5 = (bf16[2,2,32,1792]{3,2,1,0:T(8,128)(2,1)S(1)}, bf16[2,2,32,1792]{3,2,1,0:T(8,128)(2,1)S(1)}, u32[]{:S(2)}, u32[]{:S(2)}) collective-permute-start(bf16[2,2,32,1792]{3,2,1,0:T(8,128)(2,1)S(1)} %pad_maximum_fusion.6), channel_id=1, source_target_pairs={{0,1},{1,0},{2,3},{3,2},{4,5},{5,4},{6,7},{7,6},{8,9},{9,8},{10,11... | collective-permute-start | bytes 1376264 | tf_op jit(solution)/shard_map/ppermute | solution.py:126
  42.9 20.2 %collective-permute-start.7 = (bf16[2,2,32,1792]{3,2,1,0:T(8,128)(2,1)S(1)}, bf16[2,2,32,1792]{3,2,1,0:T(8,128)(2,1)S(1)}, u32[]{:S(2)}, u32[]{:S(2)}) collective-permute-start(bf16[2,2,32,1792]{3,2,1,0:T(8,128)(2,1)S(1)} %pad_maximum_fusion.5), channel_id=1, source_target_pairs={{0,2},{1,3},{2,0},{3,1},{4,6},{5,7},{6,4},{7,5},{8,10},{9,11},{10,... | collective-permute-start | bytes 1376264 | tf_op jit(solution)/shard_map/ppermute | solution.py:126
  53.4 12.8 %collective-permute-start.17 = (bf16[2,1,32,1792]{3,2,1,0:T(8,128)(2,1)S(1)}, bf16[2,1,32,1792]{3,2,1,0:T(8,128)(2,1)S(1)}, u32[]{:S(2)}, u32[]{:S(2)}) collective-permute-start(bf16[2,1,32,1792]{3,2,1,0:T(8,128)(2,1)S(1)} %slice.462), channel_id=1, source_target_pairs={{0,1},{1,0},{2,3},{3,2},{4,5},{5,4},{6,7},{7,6},{8,9},{9,8},{10,11... | collective-permute-start | bytes 688136 | tf_op jit(solution)/shard_map/ppermute | solution.py:126
  54.3 13.8 %collective-permute-start.15 = (bf16[2,1,32,1792]{3,2,1,0:T(8,128)(2,1)S(1)}, bf16[2,1,32,1792]{3,2,1,0:T(8,128)(2,1)S(1)}, u32[]{:S(2)}, u32[]{:S(2)}) collective-permute-start(bf16[2,1,32,1792]{3,2,1,0:T(8,128)(2,1)S(1)} %slice.463), channel_id=1, source_target_pairs={{0,2},{1,3},{2,0},{3,1},{4,6},{5,7},{6,4},{7,5},{8,10},{9,11},{10,... | collective-permute-start | bytes 688136 | tf_op jit(solution)/shard_map/ppermute | solution.py:126
  63.3 7.4 %collective-permute-start.8 = (bf16[2,1,32,1792]{3,2,1,0:T(8,128)(2,1)S(1)}, bf16[2,1,32,1792]{3,2,1,0:T(8,128)(2,1)S(1)}, u32[]{:S(2)}, u32[]{:S(2)}) collective-permute-start(bf16[2,1,32,1792]{3,2,1,0:T(8,128)(2,1)S(1)} %slice.464), channel_id=1, source_target_pairs={{0,1},{1,0},{2,3},{3,2},{4,5},{5,4},{6,7},{7,6},{8,9},{9,8},{10,11... | collective-permute-start | bytes 688136 | tf_op jit(solution)/shard_map/ppermute | solution.py:126
  64.1 8.1 %collective-permute-start.6 = (bf16[2,1,32,1792]{3,2,1,0:T(8,128)(2,1)S(1)}, bf16[2,1,32,1792]{3,2,1,0:T(8,128)(2,1)S(1)}, u32[]{:S(2)}, u32[]{:S(2)}) collective-permute-start(bf16[2,1,32,1792]{3,2,1,0:T(8,128)(2,1)S(1)} %slice.465), channel_id=1, source_target_pairs={{0,2},{1,3},{2,0},{3,1},{4,6},{5,7},{6,4},{7,5},{8,10},{9,11},{10,... | collective-permute-start | bytes 688136 | tf_op jit(solution)/shard_map/ppermute | solution.py:126
  72.8 13.5 %collective-permute-start.30 = (bf16[2,2,32,1792]{3,2,1,0:T(8,128)(2,1)S(1)}, bf16[2,2,32,1792]{3,2,1,0:T(8,128)(2,1)S(1)}, u32[]{:S(2)}, u32[]{:S(2)}) collective-permute-start(bf16[2,2,32,1792]{3,2,1,0:T(8,128)(2,1)S(1)} %maximum_maximum_fusion.1.refs_0_), channel_id=1, source_target_pairs={{0,2},{1,3},{2,0},{3,1},{4,6},{5,7},{6,4},{7,5},{8,10},{9,11},{10,... | collective-permute-start | bytes 1376264 | tf_op jit(solution)/shard_map/ppermute | solution.py:126
  73.9 13.5 %collective-permute-start.29 = (bf16[2,2,32,1792]{3,2,1,0:T(8,128)(2,1)S(1)}, bf16[2,2,32,1792]{3,2,1,0:T(8,128)(2,1)S(1)}, u32[]{:S(2)}, u32[]{:S(2)}) collective-permute-start(bf16[2,2,32,1792]{3,2,1,0:T(8,128)(2,1)S(1)} %maximum_maximum_fusion.1.refs_0_), channel_id=1, source_target_pairs={{0,1},{1,0},{2,3},{3,2},{4,5},{5,4},{6,7},{7,6},{8,9},{9,8},{10,11... | collective-permute-start | bytes 1376264 | tf_op jit(solution)/shard_map/ppermute | solution.py:126
  75.6 20.5 %collective-permute-start.19 = (bf16[2,2,32,1792]{3,2,1,0:T(8,128)(2,1)S(1)}, bf16[2,2,32,1792]{3,2,1,0:T(8,128)(2,1)S(1)}, u32[]{:S(2)}, u32[]{:S(2)}) collective-permute-start(bf16[2,2,32,1792]{3,2,1,0:T(8,128)(2,1)S(1)} %maximum_maximum_fusion.refs_0_), channel_id=1, source_target_pairs={{0,2},{1,3},{2,0},{3,1},{4,6},{5,7},{6,4},{7,5},{8,10},{9,11},{10,... | collective-permute-start | bytes 1376264 | tf_op jit(solution)/shard_map/ppermute | solution.py:126
  76.0 21.3 %collective-permute-start.18 = (bf16[2,2,32,1792]{3,2,1,0:T(8,128)(2,1)S(1)}, bf16[2,2,32,1792]{3,2,1,0:T(8,128)(2,1)S(1)}, u32[]{:S(2)}, u32[]{:S(2)}) collective-permute-start(bf16[2,2,32,1792]{3,2,1,0:T(8,128)(2,1)S(1)} %maximum_maximum_fusion.refs_0_), channel_id=1, source_target_pairs={{0,1},{1,0},{2,3},{3,2},{4,5},{5,4},{6,7},{7,6},{8,9},{9,8},{10,11... | collective-permute-start | bytes 1376264 | tf_op jit(solution)/shard_map/ppermute | solution.py:126
  86.3 15.8 %collective-permute-start.32 = (bf16[1,2,32,1792]{3,2,1,0:T(8,128)(2,1)S(1)}, bf16[1,2,32,1792]{3,2,1,0:T(8,128)(2,1)S(1)}, u32[]{:S(2)}, u32[]{:S(2)}) collective-permute-start(bf16[1,2,32,1792]{3,2,1,0:T(8,128)(2,1)S(1)} %slice.311), channel_id=1, source_target_pairs={{0,1},{1,0},{2,3},{3,2},{4,5},{5,4},{6,7},{7,6},{8,9},{9,8},{10,11... | collective-permute-start | bytes 688136 | tf_op jit(solution)/shard_map/ppermute | solution.py:126
  87.4 14.7 %collective-permute-start.31 = (bf16[1,2,32,1792]{3,2,1,0:T(8,128)(2,1)S(1)}, bf16[1,2,32,1792]{3,2,1,0:T(8,128)(2,1)S(1)}, u32[]{:S(2)}, u32[]{:S(2)}) collective-permute-start(bf16[1,2,32,1792]{3,2,1,0:T(8,128)(2,1)S(1)} %slice.310), channel_id=1, source_target_pairs={{0,2},{1,3},{2,0},{3,1},{4,6},{5,7},{6,4},{7,5},{8,10},{9,11},{10,... | collective-permute-start | bytes 688136 | tf_op jit(solution)/shard_map/ppermute | solution.py:126
  96.2 10.3 %collective-permute-start.21 = (bf16[1,2,32,1792]{3,2,1,0:T(8,128)(2,1)S(1)}, bf16[1,2,32,1792]{3,2,1,0:T(8,128)(2,1)S(1)}, u32[]{:S(2)}, u32[]{:S(2)}) collective-permute-start(bf16[1,2,32,1792]{3,2,1,0:T(8,128)(2,1)S(1)} %slice.305), channel_id=1, source_target_pairs={{0,1},{1,0},{2,3},{3,2},{4,5},{5,4},{6,7},{7,6},{8,9},{9,8},{10,11... | collective-permute-start | bytes 688136 | tf_op jit(solution)/shard_map/ppermute | solution.py:126
  97.2 9.3 %collective-permute-start.20 = (bf16[1,2,32,1792]{3,2,1,0:T(8,128)(2,1)S(1)}, bf16[1,2,32,1792]{3,2,1,0:T(8,128)(2,1)S(1)}, u32[]{:S(2)}, u32[]{:S(2)}) collective-permute-start(bf16[1,2,32,1792]{3,2,1,0:T(8,128)(2,1)S(1)} %slice.304), channel_id=1, source_target_pairs={{0,2},{1,3},{2,0},{3,1},{4,6},{5,7},{6,4},{7,5},{8,10},{9,11},{10,... | collective-permute-start | bytes 688136 | tf_op jit(solution)/shard_map/ppermute | solution.py:126
  105.6 13.4 %collective-permute-start.33 = (bf16[256,512]{1,0:T(8,128)(2,1)S(1)}, bf16[256,512]{1,0:T(8,128)(2,1)S(1)}, u32[]{:S(2)}, u32[]{:S(2)}) collective-permute-start(bf16[256,512]{1,0:T(8,128)(2,1)S(1)} %slice_bitcast_fusion.22), channel_id=1, source_target_pairs={{0,4},{1,5},{2,6},{3,7},{4,0},{5,1},{6,2},{7,3},{8,12},{9,13},{10,... | collective-permute-start | bytes 786440 | tf_op jit(solution)/shard_map/ppermute | solution.py:126
  110.0 12.7 %collective-permute-start.22 = (bf16[256,512]{1,0:T(8,128)(2,1)S(1)}, bf16[256,512]{1,0:T(8,128)(2,1)S(1)}, u32[]{:S(2)}, u32[]{:S(2)}) collective-permute-start(bf16[256,512]{1,0:T(8,128)(2,1)S(1)} %slice_bitcast_fusion.23), channel_id=1, source_target_pairs={{0,4},{1,5},{2,6},{3,7},{4,0},{5,1},{6,2},{7,3},{8,12},{9,13},{10,... | collective-permute-start | bytes 786440 | tf_op jit(solution)/shard_map/ppermute | solution.py:126
  122.8 7.0 %collective-permute-start.25 = (bf16[64,512]{1,0:T(8,128)(2,1)S(1)}, bf16[64,512]{1,0:T(8,128)(2,1)S(1)}, u32[]{:S(2)}, u32[]{:S(2)}) collective-permute-start(bf16[64,512]{1,0:T(8,128)(2,1)S(1)} %get-tuple-element.52), channel_id=1, source_target_pairs={{0,1},{1,0},{2,3},{3,2},{4,5},{5,4},{6,7},{7,6},{8,9},{9,8},{10,11... | collective-permute-start | bytes 196616 | tf_op jit(solution)/shard_map/ppermute | solution.py:126
  126.5 7.8 %collective-permute-start.37 = (bf16[64,512]{1,0:T(8,128)(2,1)S(1)}, bf16[64,512]{1,0:T(8,128)(2,1)S(1)}, u32[]{:S(2)}, u32[]{:S(2)}) collective-permute-start(bf16[64,512]{1,0:T(8,128)(2,1)S(1)} %get-tuple-element.48), channel_id=1, source_target_pairs={{0,8},{1,9},{2,10},{3,11},{4,12},{5,13},{6,14},{7,15},{8,0},{9,1},... | collective-permute-start | bytes 196616 | tf_op jit(solution)/shard_map/ppermute | solution.py:126
  126.7 7.6 %collective-permute-start.39 = (bf16[64,512]{1,0:T(8,128)(2,1)S(1)}, bf16[64,512]{1,0:T(8,128)(2,1)S(1)}, u32[]{:S(2)}, u32[]{:S(2)}) collective-permute-start(bf16[64,512]{1,0:T(8,128)(2,1)S(1)} %get-tuple-element.49), channel_id=1, source_target_pairs={{0,24},{1,25},{2,26},{3,27},{4,28},{5,29},{6,30},{7,31},{8,16},{9,... | collective-permute-start | bytes 196616 | tf_op jit(solution)/shard_map/ppermute | solution.py:126
  129.8 8.7 %collective-permute-start.38 = (bf16[64,512]{1,0:T(8,128)(2,1)S(1)}, bf16[64,512]{1,0:T(8,128)(2,1)S(1)}, u32[]{:S(2)}, u32[]{:S(2)}) collective-permute-start(bf16[64,512]{1,0:T(8,128)(2,1)S(1)} %get-tuple-element.50), channel_id=1, source_target_pairs={{0,16},{1,17},{2,18},{3,19},{4,20},{5,21},{6,22},{7,23},{8,24},{9,... | collective-permute-start | bytes 196616 | tf_op jit(solution)/shard_map/ppermute | solution.py:126
  130.1 8.5 %collective-permute-start.26 = (bf16[64,512]{1,0:T(8,128)(2,1)S(1)}, bf16[64,512]{1,0:T(8,128)(2,1)S(1)}, u32[]{:S(2)}, u32[]{:S(2)}) collective-permute-start(bf16[64,512]{1,0:T(8,128)(2,1)S(1)} %get-tuple-element.39), channel_id=1, source_target_pairs={{0,8},{1,9},{2,10},{3,11},{4,12},{5,13},{6,14},{7,15},{8,0},{9,1},... | collective-permute-start | bytes 196616 | tf_op jit(solution)/shard_map/ppermute | solution.py:126
  131.2 7.5 %collective-permute-start.28 = (bf16[64,512]{1,0:T(8,128)(2,1)S(1)}, bf16[64,512]{1,0:T(8,128)(2,1)S(1)}, u32[]{:S(2)}, u32[]{:S(2)}) collective-permute-start(bf16[64,512]{1,0:T(8,128)(2,1)S(1)} %get-tuple-element.40), channel_id=1, source_target_pairs={{0,24},{1,25},{2,26},{3,27},{4,28},{5,29},{6,30},{7,31},{8,16},{9,... | collective-permute-start | bytes 196616 | tf_op jit(solution)/shard_map/ppermute | solution.py:126
  134.3 5.9 %collective-permute-start.27 = (bf16[64,512]{1,0:T(8,128)(2,1)S(1)}, bf16[64,512]{1,0:T(8,128)(2,1)S(1)}, u32[]{:S(2)}, u32[]{:S(2)}) collective-permute-start(bf16[64,512]{1,0:T(8,128)(2,1)S(1)} %get-tuple-element.41), channel_id=1, source_target_pairs={{0,16},{1,17},{2,18},{3,19},{4,20},{5,21},{6,22},{7,23},{8,24},{9,... | collective-permute-start | bytes 196616 | tf_op jit(solution)/shard_map/ppermute | solution.py:126
  (9 other events, 47.7 us)

commit v4 on v3

v4 whole, which is shorter than its diff:
```python
import functools
import math

import jax
import jax.numpy as jnp
from jax import lax
from jax.experimental import pallas as pl
from jax.experimental.pallas import tpu as pltpu
from jax.sharding import PartitionSpec as P

BLOCK = 128
CHUNKS = 2
AXES = ("node", "local")


def in_vmem(x):
    return pltpu.with_memory_space_constraint(x, pltpu.VMEM)


def dequant_kernel(codes_ref, scales_ref, w_ref, done_ref):
    done_ref[0] = 0
    row = pl.ds(pl.program_id(0), 1)
    for g in range(2):
        w_ref[g] = (codes_ref[g].astype(jnp.float32) * scales_ref[g, row, :]).astype(jnp.bfloat16)


def dequant(codes, scales):
    _, owned, group = codes.shape
    blocks = owned // BLOCK
    return pl.pallas_call(
        dequant_kernel,
        grid=(blocks,),
        in_specs=[
            pl.BlockSpec((2, BLOCK, group), lambda i: (0, i, 0)),
            pl.BlockSpec((2, blocks, group), lambda i: (0, 0, 0)),
        ],
        out_specs=[
            pl.BlockSpec((2, BLOCK, group), lambda i: (0, i, 0)),
            pl.BlockSpec(memory_space=pltpu.SMEM),
        ],
        out_shape=[
            pltpu.VMEM(codes.shape, jnp.bfloat16),
            jax.ShapeDtypeStruct((1,), jnp.int32),
        ],
        compiler_params=pltpu.CompilerParams(vmem_limit_bytes=16 * 1024 * 1024),
    )(pltpu.with_memory_space_constraint(codes, pltpu.HBM), scales.astype(jnp.float32))


def pairs(move, places, ratio):
    out = []
    for plane in range(places):
        for half in range(ratio):
            for place in range(places):
                p, h, q = move(plane, half, place)
                out.append(
                    ((plane * ratio + half) * places + place, (p * ratio + h) * places + q)
                )
    return out


def after(x, earlier):
    return lax.optimization_barrier((x, earlier))[0]


def shuffle_kernel(count, write, index_ref, *refs):
    choices, outs = refs[:count], refs[-1:] if write else refs[-count:]
    for i in range(count):
        for j in range(count):

            @pl.when(index_ref[0] == i ^ j)
            def _():
                if write:
                    write(outs[0], i, choices[j][...])
                else:
                    outs[i][...] = choices[j][...]


def shuffle(choices, index, earlier=(), shape=None, write=None):
    one = choices[0]
    shapes = [shape] if write else [one.shape] * len(choices)
    out = pl.pallas_call(
        functools.partial(shuffle_kernel, len(choices), write),
        in_specs=[pl.BlockSpec(memory_space=pltpu.SMEM)]
        + [pl.BlockSpec(memory_space=pltpu.VMEM)] * len(choices)
        + [pl.BlockSpec(memory_space=pl.ANY)] * len(earlier),
        out_specs=[pl.BlockSpec(memory_space=pltpu.VMEM)] * len(shapes),
        out_shape=[pltpu.VMEM(s, one.dtype) for s in shapes],
        compiler_params=pltpu.CompilerParams(vmem_limit_bytes=16 * 1024 * 1024),
    )(index, *[in_vmem(x) for x in choices], *earlier)
    return out[0] if write else list(out)


def input_grad_kernel(spots, half_ref, *refs):
    pieces, w_ref, d_ref = refs[: len(spots)], refs[len(spots)], refs[len(spots) + 1]
    term_refs = refs[len(spots) + 2 :]
    for piece, first in zip(pieces, spots):
        streams, _, part, _ = piece.shape
        for s in range(streams):
            d_ref[:, pl.ds(first + s * part, part), :] = piece[s]
    numbers = (((1,), (1,)), ((), ()))
    for e, term_ref in enumerate(term_refs):
        feats = term_ref.shape[1]
        rows = pl.ds(pl.multiple_of((half_ref[0] ^ e) * feats, feats), feats)
        term = lax.dot_general(d_ref[0], w_ref[0, rows, :], numbers, preferred_element_type=jnp.float32)
        term += lax.dot_general(d_ref[1], w_ref[1, rows, :], numbers, preferred_element_type=jnp.float32)
        term_ref[...] = term.astype(jnp.bfloat16)


def input_grad(pieces, spots, w_gu, half, ratio, total):
    _, owned, group = w_gu.shape
    feats = owned // ratio
    return pl.pallas_call(
        functools.partial(input_grad_kernel, spots),
        in_specs=[pl.BlockSpec(memory_space=pltpu.SMEM)]
        + [pl.BlockSpec(memory_space=pltpu.VMEM)] * (len(pieces) + 1),
        out_specs=[pl.BlockSpec(memory_space=pltpu.VMEM)] * (ratio + 1),
        out_shape=[pltpu.VMEM((2, total, group), jnp.bfloat16)]
        + [pltpu.VMEM((total, feats), jnp.bfloat16)] * ratio,
        compiler_params=pltpu.CompilerParams(vmem_limit_bytes=24 * 1024 * 1024),
    )(half, *[in_vmem(x) for x in pieces], in_vmem(w_gu))


def weight_grad_kernel(scale, features_ref, d_ref, *refs):
    out_ref, done_ref = refs[-2:]
    done_ref[0] = 0
    out_ref[0] = scale * jnp.dot(features_ref[...], d_ref[0], preferred_element_type=jnp.float32)


def weight_grad(which, features, d_both, scale, earlier, grads=None):
    owned, total = features.shape
    group = d_both.shape[2]
    step = min(owned, 256)
    operands = [features, in_vmem(d_both), earlier] + ([] if grads is None else [grads])
    return pl.pallas_call(
        functools.partial(weight_grad_kernel, scale),
        grid=(owned // step,),
        in_specs=[
            pl.BlockSpec((step, total), lambda i: (i, 0)),
            pl.BlockSpec((1, total, group), lambda i: (which, 0, 0)),
        ]
        + [pl.BlockSpec(memory_space=pl.ANY)] * (len(operands) - 2),
        out_specs=[
            pl.BlockSpec((1, step, group), lambda i: (which, i, 0)),
            pl.BlockSpec(memory_space=pltpu.SMEM),
        ],
        out_shape=[
            jax.ShapeDtypeStruct((2, owned, group), jnp.float32),
            jax.ShapeDtypeStruct((1,), jnp.int32),
        ],
        input_output_aliases={} if grads is None else {3: 0},
        compiler_params=pltpu.CompilerParams(vmem_limit_bytes=16 * 1024 * 1024),
    )(*operands)


def body(tokens, gate_up_codes, gate_up_scales, d_hidden):
    rows, feats = tokens.shape
    nodes, places = lax.axis_size("node"), lax.axis_size("local")
    ratio = nodes // places
    _, owned, group = gate_up_codes.shape
    bits = [1 << b for b in range(places.bit_length() - 1)]
    node, place = lax.axis_index("node"), lax.axis_index("local")
    tokens, half, mask = lax.optimization_barrier(
        (tokens, (node & (ratio - 1))[None], ((node >> (ratio.bit_length() - 1)) ^ place)[None])
    )
    chunk = rows // CHUNKS
    part = chunk // 2
    orders = (bits, bits[::-1])

    def permute(x, move):
        return lax.ppermute(x, AXES, pairs(move, places, ratio))

    def features_of(x, earlier):
        got = [permute(x, lambda p, h, q, j=j: (q ^ j, h, p)) for j in range(places)]

        def by_place(out_ref, i, value):
            out_ref[i] = value

        def by_half(out_ref, i, value):
            out_ref[:, :, i * feats : (i + 1) * feats] = value

        got = shuffle(got, mask, earlier, (places, rows, feats), by_place)
        halves = [got] + [permute(got, lambda p, h, q, e=e: (p, h ^ e, q)) for e in range(1, ratio)]
        return shuffle(halves, half, (), (places, rows, owned), by_half)

    def reduce_local(x, order):
        ks = list(range(places))
        x = x.astype(jnp.float32)
        for bit in order:
            away = [i for i, k in enumerate(ks) if k & bit]
            stay = [i for i, k in enumerate(ks) if not k & bit]
            sent = jnp.stack([x[:, i] for i in away], axis=1).astype(jnp.bfloat16)
            got = permute(sent, lambda p, h, q: (p, h, q ^ bit))
            x = jnp.stack([x[:, i] for i in stay], axis=1) + got.astype(jnp.float32)
            ks = [ks[i] for i in stay]
        return x[:, 0]

    def gather_local(x):
        direct = {bit: permute(x, lambda p, h, q: (p, h, q ^ bit)) for bit in bits}
        pieces, spots = [x] + [direct[bit] for bit in bits], [(0, 0)] + [(bit, 0) for bit in bits]
        for s, order in enumerate(orders):
            held = {0: None}
            for bit in order:
                for k in list(held):
                    if k == 0:
                        held[bit] = direct[bit][s : s + 1]
                    else:
                        held[k ^ bit] = permute(held[k], lambda p, h, q: (p, h, q ^ bit))
                        pieces.append(held[k ^ bit])
                        spots.append((k ^ bit, s * part))
        return pieces, spots

    w_gu, done = dequant(gate_up_codes, gate_up_scales)
    features = features_of(tokens, [done])
    hidden, pieces, spots = [], [], []
    for c in range(CHUNKS):
        flat = features[:, c * chunk : (c + 1) * chunk].reshape(places * chunk, owned)
        partial = [
            jnp.dot(flat, w_gu[g], preferred_element_type=jnp.float32)
            .astype(jnp.bfloat16)
            .reshape(places, chunk, group)
            for g in range(2)
        ]
        streams = []
        for s in range(2):
            at = slice(s * part, (s + 1) * part)
            both = reduce_local(jnp.stack([p[:, at] for p in partial]), orders[s])
            gate, up = both[0], both[1]
            sigmoid_gate = jax.nn.sigmoid(gate)
            active = gate * sigmoid_gate
            hidden.append((active * up).astype(jnp.bfloat16))
            first = c * chunk + s * part
            grad_in = d_hidden[first : first + part].astype(jnp.float32)
            d_gate = grad_in * up * sigmoid_gate * (1.0 + gate * (1.0 - sigmoid_gate))
            d_up = grad_in * active
            streams.append(jnp.stack([d_gate, d_up]).astype(jnp.bfloat16))
        blocks, places_of = gather_local(jnp.stack(streams))
        pieces += blocks
        spots += [k * rows + c * chunk + first for k, first in places_of]
    d_all, *term = input_grad(pieces, spots, w_gu, half, ratio, places * rows)
    summed = term[0].astype(jnp.float32)
    for e in range(1, ratio):
        got = permute(term[e], lambda p, h, q: (p, h ^ e, q))
        summed = summed + got.astype(jnp.float32)
    summed = summed.astype(jnp.bfloat16).reshape(places, rows, feats)
    arrived = [summed[0]] + [
        permute(summed[k], lambda p, h, q: (p, h, q ^ k)) for k in range(1, places)
    ]
    arrived = shuffle(arrived, mask)
    summands = [arrived[0]] + [
        permute(arrived[j], lambda p, h, q: (p ^ j, h, q)) for j in range(1, places)
    ]
    scale = 1.0 / math.sqrt(rows * places)
    turned = features.reshape(places * rows, owned).T
    grads, _ = weight_grad(0, turned, d_all, scale, summed[0, :16])
    grads, done = weight_grad(1, turned, d_all, scale, arrived[0][:16], grads)
    summands[0] = after(summands[0], done)
    d_tokens = sum(x.astype(jnp.float32) for x in summands).astype(jnp.bfloat16)
    return jnp.concatenate(hidden), d_tokens, grads


def solution(mesh):
    placed = (
        P("local", "node"),
        P(None, "local", "node"),
        P(None, "local", "node"),
        P("local", "node"),
    )
    return jax.shard_map(
        body,
        mesh=mesh,
        in_specs=placed,
        out_specs=(P("local", "node"), P("local", "node"), P(None, "local", "node")),
        check_vma=False,
    )
```

time: 141 us -> 129 us (0.915)
  starting transfers between devices: 56.7 us -> 39.4 us
  Pallas kernels: 15.4 us -> 20.5 us
  other arithmetic: 9.32 us -> 6.57 us
  waiting for transfers between devices: 52.3 us -> 54.1 us
  local copies, waits for them, and re-layouts: 1.5 us -> 3.04 us
    ppermute x40 -> x28, starting transfers between devices: 56.7 us -> 39.4 us  [permute(): return lax.ppermute(x, AXES, pairs(move, places, ratio))]
    pallas_call x3 -> x7, Pallas kernels: 15.4 us -> 20.5 us  [the longest x2 8.83 us: weight_grad(): pl.pallas_call(functools.partial(weight_grad_kernel, scale), grid=(owned...]
    convert_element_type x6 -> x3, other arithmetic: 5.59 us -> 2.73 us  [the longest x1 1.17 us: body(): summed = summed.astype(jnp.bfloat16).reshape(places, rows, feats)]
    unnamed x2 -> x8, local copies, waits for them, and re-layouts: 0.01 us -> 1.85 us
    ppermute x40 -> x28, waiting for transfers between devices: 52.3 us -> 54.1 us  [permute(): return lax.ppermute(x, AXES, pairs(move, places, ratio))]
  transfers between devices with their start and end apart: 40 -> 28, of which waited for: 13 -> 14; matrix products, arithmetic and copies ran while one was open for 7% -> 4% of each run, Pallas kernels for 11% -> 12%
where the time goes in v4:
time: 129 us
  waiting for transfers between devices  54.1 us (42%)
  starting transfers between devices  39.4 us (31%)
  Pallas kernels  20.5 us (16%)
  other arithmetic  6.57 us (5%)
  matrix products  4.56 us (4%)
  local copies, waits for them, and re-layouts  3.04 us (2%)
    ppermute x28, waiting for transfers between devices, permute(): return lax.ppermute(x, AXES, pairs(move, places, ratio))  54.1 us
    ppermute x28, starting transfers between devices, permute(): return lax.ppermute(x, AXES, pairs(move, places, ratio))  39.4 us
    pallas_call x2, Pallas kernels, weight_grad(): pl.pallas_call(functools.partial(weight_grad_kernel, scale), grid=(owned...  8.83 us
    pallas_call x1, Pallas kernels, dequant(): pl.pallas_call(dequant_kernel, grid=(blocks,), in_specs=[pl.BlockSpec((2,...  6.67 us
    dot_general x4, matrix products, body(): jnp.dot(flat, w_gu[g], preferred_element_type=jnp.float32)  4.56 us
    pallas_call x1, Pallas kernels, input_grad(): pl.pallas_call(functools.partial(input_grad_kernel, spots), in_specs=[pl....  3.98 us
  transfers between devices with their start and end apart: 28, of which 14 were waited for; matrix products, arithmetic and copies ran while one was open for 4% of the time, Pallas kernels for 12%

profile of v4, /device:TPU:0, one launch (start us, length us, event | category | flops | bytes accessed | tf_op | source)
XLA Modules:
  0.0 129.2 jit_solution(4107023655215334540)
XLA Ops:
  0.6 5.1 %collective-permute-start.3 = (bf16[128,512]{1,0:T(8,128)(2,1)}, bf16[128,512]{1,0:T(8,128)(2,1)S(1)}, u32[]{:S(2)}, u32[]{:S(2)}) collective-permute-start(bf16[128,512]{1,0:T(8,128)(2,1)} %param.4), channel_id=1, source_target_pairs={{0,24},{1,16},{2,8},{3,0},{4,28},{5,20},{6,12},{7,4},{8,25},{9,17}... | collective-permute-start | bytes 393224 | tf_op jit(solution)/shard_map/ppermute | solution.py:170
  5.7 1.5 %collective-permute-start.2 = (bf16[128,512]{1,0:T(8,128)(2,1)}, bf16[128,512]{1,0:T(8,128)(2,1)S(1)}, u32[]{:S(2)}, u32[]{:S(2)}) collective-permute-start(bf16[128,512]{1,0:T(8,128)(2,1)} %param.4), channel_id=1, source_target_pairs={{0,16},{1,24},{2,0},{3,8},{4,20},{5,28},{6,4},{7,12},{8,17},{9,25}... | collective-permute-start | bytes 393224 | tf_op jit(solution)/shard_map/ppermute | solution.py:170
  7.7 1.6 %collective-permute-start = (bf16[128,512]{1,0:T(8,128)(2,1)}, bf16[128,512]{1,0:T(8,128)(2,1)S(1)}, u32[]{:S(2)}, u32[]{:S(2)}) collective-permute-start(bf16[128,512]{1,0:T(8,128)(2,1)} %param.4), channel_id=1, source_target_pairs={{0,0},{1,8},{2,16},{3,24},{4,4},{5,12},{6,20},{7,28},{8,1},{9,9},{... | collective-permute-start | bytes 393224 | tf_op jit(solution)/shard_map/ppermute | solution.py:170
  10.1 6.7 %shard_map.67 = (bf16[2,1024,1792]{2,1,0:T(8,128)(2,1)S(1)}, s32[1]{0:T(128)}) custom-call(bf16[2,1024,1792]{2,1,0:T(8,128)(2,1)} %codes_ref.1, f32[2,8,1792]{2,1,0:T(8,128)S(1)} %convert_element_type.135.scales_ref), custom_call_target="tpu_custom_call" | custom-call | tf_op jit(solution)/shard_map/pallas_call | solution.py:30
  17.7 1.9 %collective-permute-done.4.refs_1_ = bf16[4,128,512]{2,1,0:T(8,128)(2,1)S(1)} collective-permute-done((bf16[4,128,512]{2,1,0:T(8,128)(2,1)S(1)}, bf16[4,128,512]{2,1,0:T(8,128)(2,1)S(1)}, u32[]{:S(2)}, u32[]{:S(2)}) %collective-permute-start.4) | collective-permute-done | bytes 524320 | tf_op jit(solution)/shard_map/ppermute | solution.py:170
  25.0 6.5 %collective-permute-start.9 = (bf16[2,2,32,1792]{3,2,1,0:T(8,128)(2,1)S(1)}, bf16[2,2,32,1792]{3,2,1,0:T(8,128)(2,1)S(1)}, u32[]{:S(2)}, u32[]{:S(2)}) collective-permute-start(bf16[2,2,32,1792]{3,2,1,0:T(8,128)(2,1)S(1)} %pad_maximum_fusion.5), channel_id=1, source_target_pairs={{0,1},{1,0},{2,3},{3,2},{4,5},{5,4},{6,7},{7,6},{8,9},{9,8},{10,11... | collective-permute-start | bytes 1376264 | tf_op jit(solution)/shard_map/ppermute | solution.py:170
  32.0 2.1 %collective-permute-start.5 = (bf16[2,2,32,1792]{3,2,1,0:T(8,128)(2,1)S(1)}, bf16[2,2,32,1792]{3,2,1,0:T(8,128)(2,1)S(1)}, u32[]{:S(2)}, u32[]{:S(2)}) collective-permute-start(bf16[2,2,32,1792]{3,2,1,0:T(8,128)(2,1)S(1)} %pad_maximum_fusion.4), channel_id=1, source_target_pairs={{0,1},{1,0},{2,3},{3,2},{4,5},{5,4},{6,7},{7,6},{8,9},{9,8},{10,11... | collective-permute-start | bytes 1376264 | tf_op jit(solution)/shard_map/ppermute | solution.py:170
  34.3 10.8 %collective-permute-done.11 = bf16[2,2,32,1792]{3,2,1,0:T(8,128)(2,1)S(1)} collective-permute-done((bf16[2,2,32,1792]{3,2,1,0:T(8,128)(2,1)S(1)}, bf16[2,2,32,1792]{3,2,1,0:T(8,128)(2,1)S(1)}, u32[]{:S(2)}, u32[]{:S(2)}) %collective-permute-start.11) | collective-permute-done | bytes 458784 | tf_op jit(solution)/shard_map/ppermute | solution.py:170
  45.6 2.1 %collective-permute-start.10 = (bf16[2,1,32,1792]{3,2,1,0:T(8,128)(2,1)S(1)}, bf16[2,1,32,1792]{3,2,1,0:T(8,128)(2,1)S(1)}, u32[]{:S(2)}, u32[]{:S(2)}) collective-permute-start(bf16[2,1,32,1792]{3,2,1,0:T(8,128)(2,1)S(1)} %slice.431), channel_id=1, source_target_pairs={{0,2},{1,3},{2,0},{3,1},{4,6},{5,7},{6,4},{7,5},{8,10},{9,11},{10,... | collective-permute-start | bytes 688136 | tf_op jit(solution)/shard_map/ppermute | solution.py:170
  47.7 7.2 %collective-permute-done.7 = bf16[2,2,32,1792]{3,2,1,0:T(8,128)(2,1)S(1)} collective-permute-done((bf16[2,2,32,1792]{3,2,1,0:T(8,128)(2,1)S(1)}, bf16[2,2,32,1792]{3,2,1,0:T(8,128)(2,1)S(1)}, u32[]{:S(2)}, u32[]{:S(2)}) %collective-permute-start.7) | collective-permute-done | bytes 458784 | tf_op jit(solution)/shard_map/ppermute | solution.py:170
  55.5 2.1 %collective-permute-start.6 = (bf16[2,1,32,1792]{3,2,1,0:T(8,128)(2,1)S(1)}, bf16[2,1,32,1792]{3,2,1,0:T(8,128)(2,1)S(1)}, u32[]{:S(2)}, u32[]{:S(2)}) collective-permute-start(bf16[2,1,32,1792]{3,2,1,0:T(8,128)(2,1)S(1)} %slice.433), channel_id=1, source_target_pairs={{0,2},{1,3},{2,0},{3,1},{4,6},{5,7},{6,4},{7,5},{8,10},{9,11},{10,... | collective-permute-start | bytes 688136 | tf_op jit(solution)/shard_map/ppermute | solution.py:170
  57.6 2.3 %collective-permute-done.10 = bf16[2,1,32,1792]{3,2,1,0:T(8,128)(2,1)S(1)} collective-permute-done((bf16[2,1,32,1792]{3,2,1,0:T(8,128)(2,1)S(1)}, bf16[2,1,32,1792]{3,2,1,0:T(8,128)(2,1)S(1)}, u32[]{:S(2)}, u32[]{:S(2)}) %collective-permute-start.10) | collective-permute-done | bytes 229408 | tf_op jit(solution)/shard_map/ppermute | solution.py:170
  59.9 2.1 %collective-permute-done.8 = bf16[2,1,32,1792]{3,2,1,0:T(8,128)(2,1)S(1)} collective-permute-done((bf16[2,1,32,1792]{3,2,1,0:T(8,128)(2,1)S(1)}, bf16[2,1,32,1792]{3,2,1,0:T(8,128)(2,1)S(1)}, u32[]{:S(2)}, u32[]{:S(2)}) %collective-permute-start.8) | collective-permute-done | bytes 229408 | tf_op jit(solution)/shard_map/ppermute | solution.py:170
  62.1 1.5 %collective-permute-done.6 = bf16[2,1,32,1792]{3,2,1,0:T(8,128)(2,1)S(1)} collective-permute-done((bf16[2,1,32,1792]{3,2,1,0:T(8,128)(2,1)S(1)}, bf16[2,1,32,1792]{3,2,1,0:T(8,128)(2,1)S(1)}, u32[]{:S(2)}, u32[]{:S(2)}) %collective-permute-start.6) | collective-permute-done | bytes 229408 | tf_op jit(solution)/shard_map/ppermute | solution.py:170
  64.8 1.7 %collective-permute-start.13 = (bf16[2,2,32,1792]{3,2,1,0:T(8,128)(2,1)S(1)}, bf16[2,2,32,1792]{3,2,1,0:T(8,128)(2,1)S(1)}, u32[]{:S(2)}, u32[]{:S(2)}) collective-permute-start(bf16[2,2,32,1792]{3,2,1,0:T(8,128)(2,1)S(1)} %maximum_maximum_fusion.refs_0_), channel_id=1, source_target_pairs={{0,1},{1,0},{2,3},{3,2},{4,5},{5,4},{6,7},{7,6},{8,9},{9,8},{10,11... | collective-permute-start | bytes 1376264 | tf_op jit(solution)/shard_map/ppermute | solution.py:170
  67.1 1.5 %collective-permute-start.17 = (bf16[2,2,32,1792]{3,2,1,0:T(8,128)(2,1)S(1)}, bf16[2,2,32,1792]{3,2,1,0:T(8,128)(2,1)S(1)}, u32[]{:S(2)}, u32[]{:S(2)}) collective-permute-start(bf16[2,2,32,1792]{3,2,1,0:T(8,128)(2,1)S(1)} %maximum_maximum_fusion.1.refs_5_), channel_id=1, source_target_pairs={{0,1},{1,0},{2,3},{3,2},{4,5},{5,4},{6,7},{7,6},{8,9},{9,8},{10,11... | collective-permute-start | bytes 1376264 | tf_op jit(solution)/shard_map/ppermute | solution.py:170
  68.7 9.1 %collective-permute-done.14.refs_2_ = bf16[2,2,32,1792]{3,2,1,0:T(8,128)(2,1)S(1)} collective-permute-done((bf16[2,2,32,1792]{3,2,1,0:T(8,128)(2,1)S(1)}, bf16[2,2,32,1792]{3,2,1,0:T(8,128)(2,1)S(1)}, u32[]{:S(2)}, u32[]{:S(2)}) %collective-permute-start.14) | collective-permute-done | bytes 458784 | tf_op jit(solution)/shard_map/ppermute | solution.py:170
  78.3 1.8 %collective-permute-start.15 = (bf16[1,2,32,1792]{3,2,1,0:T(8,128)(2,1)S(1)}, bf16[1,2,32,1792]{3,2,1,0:T(8,128)(2,1)S(1)}, u32[]{:S(2)}, u32[]{:S(2)}) collective-permute-start(bf16[1,2,32,1792]{3,2,1,0:T(8,128)(2,1)S(1)} %slice.276), channel_id=1, source_target_pairs={{0,2},{1,3},{2,0},{3,1},{4,6},{5,7},{6,4},{7,5},{8,10},{9,11},{10,... | collective-permute-start | bytes 688136 | tf_op jit(solution)/shard_map/ppermute | solution.py:170
  80.1 7.4 %collective-permute-done.18.refs_7_ = bf16[2,2,32,1792]{3,2,1,0:T(8,128)(2,1)S(1)} collective-permute-done((bf16[2,2,32,1792]{3,2,1,0:T(8,128)(2,1)S(1)}, bf16[2,2,32,1792]{3,2,1,0:T(8,128)(2,1)S(1)}, u32[]{:S(2)}, u32[]{:S(2)}) %collective-permute-start.18) | collective-permute-done | bytes 458784 | tf_op jit(solution)/shard_map/ppermute | solution.py:170
  88.2 1.8 %collective-permute-start.19 = (bf16[1,2,32,1792]{3,2,1,0:T(8,128)(2,1)S(1)}, bf16[1,2,32,1792]{3,2,1,0:T(8,128)(2,1)S(1)}, u32[]{:S(2)}, u32[]{:S(2)}) collective-permute-start(bf16[1,2,32,1792]{3,2,1,0:T(8,128)(2,1)S(1)} %slice.278), channel_id=1, source_target_pairs={{0,2},{1,3},{2,0},{3,1},{4,6},{5,7},{6,4},{7,5},{8,10},{9,11},{10,... | collective-permute-start | bytes 688136 | tf_op jit(solution)/shard_map/ppermute | solution.py:170
  90.0 3.0 %collective-permute-done.16.refs_4_ = bf16[1,2,32,1792]{3,2,1,0:T(8,128)(2,1)S(1)} collective-permute-done((bf16[1,2,32,1792]{3,2,1,0:T(8,128)(2,1)S(1)}, bf16[1,2,32,1792]{3,2,1,0:T(8,128)(2,1)S(1)}, u32[]{:S(2)}, u32[]{:S(2)}) %collective-permute-start.16) | collective-permute-done | bytes 229408 | tf_op jit(solution)/shard_map/ppermute | solution.py:170
  93.0 2.8 %collective-permute-done.20.refs_9_ = bf16[1,2,32,1792]{3,2,1,0:T(8,128)(2,1)S(1)} collective-permute-done((bf16[1,2,32,1792]{3,2,1,0:T(8,128)(2,1)S(1)}, bf16[1,2,32,1792]{3,2,1,0:T(8,128)(2,1)S(1)}, u32[]{:S(2)}, u32[]{:S(2)}) %collective-permute-start.20) | collective-permute-done | bytes 229408 | tf_op jit(solution)/shard_map/ppermute | solution.py:170
  95.8 4.0 %shard_map.70 = (bf16[2,512,1792]{2,1,0:T(8,128)(2,1)S(1)}, bf16[512,512]{1,0:T(8,128)(2,1)S(1)}, bf16[512,512]{1,0:T(8,128)(2,1)S(1)}) custom-call(s32[1]{0:T(128)} %bitcast.index_ref.half_ref, bf16[2,2,32,1792]{3,2,1,0:T(8,128)(2,1)S(1)} %maximum_maximum_fusion.refs_0_, bf16[2,2,32,1792]{3,2,1,0:T(8,128)(2,1)S(1)} %collective-permute-done.13.refs_1_, ...), custom_call_target="tpu_custom_call" | custom-call | tf_op jit(solution)/shard_map/pallas_call | solution.py:112
  99.8 1.8 %copy-done = bf16[2,512,1792]{2,1,0:T(8,128)(2,1)} copy-done((bf16[2,512,1792]{2,1,0:T(8,128)(2,1)}, bf16[2,512,1792]{2,1,0:T(8,128)(2,1)S(1)}, u32[]{:S(2)}) %copy-start) | copy-done | bytes 3670040
  104.9 1.3 %collective-permute-start.24 = (bf16[128,512]{1,0:T(8,128)(2,1)S(1)}, bf16[128,512]{1,0:T(8,128)(2,1)S(1)}, u32[]{:S(2)}, u32[]{:S(2)}) collective-permute-start(bf16[128,512]{1,0:T(8,128)(2,1)S(1)} %get-tuple-element.57), channel_id=1, source_target_pairs={{0,3},{1,2},{2,1},{3,0},{4,7},{5,6},{6,5},{7,4},{8,11},{9,10},{10,... | collective-permute-start | bytes 393224 | tf_op jit(solution)/shard_map/ppermute | solution.py:170
  106.2 1.7 %collective-permute-start.23 = (bf16[128,512]{1,0:T(8,128)(2,1)S(1)}, bf16[128,512]{1,0:T(8,128)(2,1)S(1)}, u32[]{:S(2)}, u32[]{:S(2)}) collective-permute-start(bf16[128,512]{1,0:T(8,128)(2,1)S(1)} %get-tuple-element.58), channel_id=1, source_target_pairs={{0,2},{1,3},{2,0},{3,1},{4,6},{5,7},{6,4},{7,5},{8,10},{9,11},{10,... | collective-permute-start | bytes 393224 | tf_op jit(solution)/shard_map/ppermute | solution.py:170
  109.3 3.0 %collective-permute-done.24.refs_3_ = bf16[128,512]{1,0:T(8,128)(2,1)S(1)} collective-permute-done((bf16[128,512]{1,0:T(8,128)(2,1)S(1)}, bf16[128,512]{1,0:T(8,128)(2,1)S(1)}, u32[]{:S(2)}, u32[]{:S(2)}) %collective-permute-start.24) | collective-permute-done | bytes 131104 | tf_op jit(solution)/shard_map/ppermute | solution.py:170
  112.2 2.2 %collective-permute-done.23.refs_2_ = bf16[128,512]{1,0:T(8,128)(2,1)S(1)} collective-permute-done((bf16[128,512]{1,0:T(8,128)(2,1)S(1)}, bf16[128,512]{1,0:T(8,128)(2,1)S(1)}, u32[]{:S(2)}, u32[]{:S(2)}) %collective-permute-start.23) | collective-permute-done | bytes 131104 | tf_op jit(solution)/shard_map/ppermute | solution.py:170
  115.8 1.6 %collective-permute-start.26 = (bf16[128,512]{1,0:T(8,128)(2,1)S(1)}, bf16[128,512]{1,0:T(8,128)(2,1)S(1)}, u32[]{:S(2)}, u32[]{:S(2)}) collective-permute-start(bf16[128,512]{1,0:T(8,128)(2,1)S(1)} %get-tuple-element.26), channel_id=1, source_target_pairs={{0,16},{1,17},{2,18},{3,19},{4,20},{5,21},{6,22},{7,23},{8,24},{9,... | collective-permute-start | bytes 393224 | tf_op jit(solution)/shard_map/ppermute | solution.py:170
  117.3 1.7 %collective-permute-start.27 = (bf16[128,512]{1,0:T(8,128)(2,1)S(1)}, bf16[128,512]{1,0:T(8,128)(2,1)S(1)}, u32[]{:S(2)}, u32[]{:S(2)}) collective-permute-start(bf16[128,512]{1,0:T(8,128)(2,1)S(1)} %get-tuple-element.27), channel_id=1, source_target_pairs={{0,24},{1,25},{2,26},{3,27},{4,28},{5,29},{6,30},{7,31},{8,16},{9,... | collective-permute-start | bytes 393224 | tf_op jit(solution)/shard_map/ppermute | solution.py:170
  119.0 4.4 %shard_map.72 = (f32[2,1024,1792]{2,1,0:T(8,128)}, s32[1]{0:T(128)}) custom-call(bf16[1024,512]{1,0:T(8,128)(2,1)S(1)} %bitcast.148, bf16[2,512,1792]{2,1,0:T(8,128)(2,1)S(1)} %copy-done.1, bf16[16,512]{1,0:T(8,128)(2,1)S(1)} %slice_bitcast_fusion.16.refs_0_), custom_call_target="tpu_custom_call" | custom-call | tf_op jit(solution)/shard_map/pallas_call | solution.py:134
  123.5 4.4 %shard_map.73 = (f32[2,1024,1792]{2,1,0:T(8,128)}, s32[1]{0:T(128)}) custom-call(bf16[1024,512]{1,0:T(8,128)(2,1)S(1)} %bitcast.149, bf16[2,512,1792]{2,1,0:T(8,128)(2,1)S(1)} %copy-done.1, bf16[16,512]{1,0:T(8,128)(2,1)S(1)} %slice.236.refs_0_, f32[2,1024,1792]{2,1,0:T(8,128)} %get-tuple-element.29.refs_1_), custom_call_target="tpu_custom_call", output_to_operand_aliasing={{0}: (3, {})} | custom-call | tf_op jit(solution)/shard_map/pallas_call | solution.py:134
  (85 shorter events, 19.3 us)
Async XLA Ops:
  0.6 16.1 %collective-permute-start.3 = (bf16[128,512]{1,0:T(8,128)(2,1)}, bf16[128,512]{1,0:T(8,128)(2,1)S(1)}, u32[]{:S(2)}, u32[]{:S(2)}) collective-permute-start(bf16[128,512]{1,0:T(8,128)(2,1)} %param.4), channel_id=1, source_target_pairs={{0,24},{1,16},{2,8},{3,0},{4,28},{5,20},{6,12},{7,4},{8,25},{9,17}... | collective-permute-start | bytes 393224 | tf_op jit(solution)/shard_map/ppermute | solution.py:170
  5.7 11.0 %collective-permute-start.2 = (bf16[128,512]{1,0:T(8,128)(2,1)}, bf16[128,512]{1,0:T(8,128)(2,1)S(1)}, u32[]{:S(2)}, u32[]{:S(2)}) collective-permute-start(bf16[128,512]{1,0:T(8,128)(2,1)} %param.4), channel_id=1, source_target_pairs={{0,16},{1,24},{2,0},{3,8},{4,20},{5,28},{6,4},{7,12},{8,17},{9,25}... | collective-permute-start | bytes 393224 | tf_op jit(solution)/shard_map/ppermute | solution.py:170
  7.3 9.5 %collective-permute-start.1 = (bf16[128,512]{1,0:T(8,128)(2,1)}, bf16[128,512]{1,0:T(8,128)(2,1)S(1)}, u32[]{:S(2)}, u32[]{:S(2)}) collective-permute-start(bf16[128,512]{1,0:T(8,128)(2,1)} %param.4), channel_id=1, source_target_pairs={{0,8},{1,0},{2,24},{3,16},{4,12},{5,4},{6,28},{7,20},{8,9},{9,1},{... | collective-permute-start | bytes 393224 | tf_op jit(solution)/shard_map/ppermute | solution.py:170
  7.7 9.1 %collective-permute-start = (bf16[128,512]{1,0:T(8,128)(2,1)}, bf16[128,512]{1,0:T(8,128)(2,1)S(1)}, u32[]{:S(2)}, u32[]{:S(2)}) collective-permute-start(bf16[128,512]{1,0:T(8,128)(2,1)} %param.4), channel_id=1, source_target_pairs={{0,0},{1,8},{2,16},{3,24},{4,4},{5,12},{6,20},{7,28},{8,1},{9,9},{... | collective-permute-start | bytes 393224 | tf_op jit(solution)/shard_map/ppermute | solution.py:170
  17.6 2.0 %collective-permute-start.4 = (bf16[4,128,512]{2,1,0:T(8,128)(2,1)S(1)}, bf16[4,128,512]{2,1,0:T(8,128)(2,1)S(1)}, u32[]{:S(2)}, u32[]{:S(2)}) collective-permute-start(bf16[4,128,512]{2,1,0:T(8,128)(2,1)S(1)} %shard_map.68.refs_0_), channel_id=1, source_target_pairs={{0,4},{1,5},{2,6},{3,7},{4,0},{5,1},{6,2},{7,3},{8,12},{9,13},{10,... | collective-permute-start | bytes 1572872 | tf_op jit(solution)/shard_map/ppermute | solution.py:170
  25.0 20.4 %collective-permute-start.9 = (bf16[2,2,32,1792]{3,2,1,0:T(8,128)(2,1)S(1)}, bf16[2,2,32,1792]{3,2,1,0:T(8,128)(2,1)S(1)}, u32[]{:S(2)}, u32[]{:S(2)}) collective-permute-start(bf16[2,2,32,1792]{3,2,1,0:T(8,128)(2,1)S(1)} %pad_maximum_fusion.5), channel_id=1, source_target_pairs={{0,1},{1,0},{2,3},{3,2},{4,5},{5,4},{6,7},{7,6},{8,9},{9,8},{10,11... | collective-permute-start | bytes 1376264 | tf_op jit(solution)/shard_map/ppermute | solution.py:170
  31.6 13.5 %collective-permute-start.11 = (bf16[2,2,32,1792]{3,2,1,0:T(8,128)(2,1)S(1)}, bf16[2,2,32,1792]{3,2,1,0:T(8,128)(2,1)S(1)}, u32[]{:S(2)}, u32[]{:S(2)}) collective-permute-start(bf16[2,2,32,1792]{3,2,1,0:T(8,128)(2,1)S(1)} %pad_maximum_fusion.2), channel_id=1, source_target_pairs={{0,2},{1,3},{2,0},{3,1},{4,6},{5,7},{6,4},{7,5},{8,10},{9,11},{10,... | collective-permute-start | bytes 1376264 | tf_op jit(solution)/shard_map/ppermute | solution.py:170
  32.0 23.3 %collective-permute-start.5 = (bf16[2,2,32,1792]{3,2,1,0:T(8,128)(2,1)S(1)}, bf16[2,2,32,1792]{3,2,1,0:T(8,128)(2,1)S(1)}, u32[]{:S(2)}, u32[]{:S(2)}) collective-permute-start(bf16[2,2,32,1792]{3,2,1,0:T(8,128)(2,1)S(1)} %pad_maximum_fusion.4), channel_id=1, source_target_pairs={{0,1},{1,0},{2,3},{3,2},{4,5},{5,4},{6,7},{7,6},{8,9},{9,8},{10,11... | collective-permute-start | bytes 1376264 | tf_op jit(solution)/shard_map/ppermute | solution.py:170
  34.2 20.8 %collective-permute-start.7 = (bf16[2,2,32,1792]{3,2,1,0:T(8,128)(2,1)S(1)}, bf16[2,2,32,1792]{3,2,1,0:T(8,128)(2,1)S(1)}, u32[]{:S(2)}, u32[]{:S(2)}) collective-permute-start(bf16[2,2,32,1792]{3,2,1,0:T(8,128)(2,1)S(1)} %pad_maximum_fusion.3), channel_id=1, source_target_pairs={{0,2},{1,3},{2,0},{3,1},{4,6},{5,7},{6,4},{7,5},{8,10},{9,11},{10,... | collective-permute-start | bytes 1376264 | tf_op jit(solution)/shard_map/ppermute | solution.py:170
  45.2 21.3 %collective-permute-start.12 = (bf16[2,1,32,1792]{3,2,1,0:T(8,128)(2,1)S(1)}, bf16[2,1,32,1792]{3,2,1,0:T(8,128)(2,1)S(1)}, u32[]{:S(2)}, u32[]{:S(2)}) collective-permute-start(bf16[2,1,32,1792]{3,2,1,0:T(8,128)(2,1)S(1)} %slice.430), channel_id=1, source_target_pairs={{0,1},{1,0},{2,3},{3,2},{4,5},{5,4},{6,7},{7,6},{8,9},{9,8},{10,11... | collective-permute-start | bytes 688136 | tf_op jit(solution)/shard_map/ppermute | solution.py:170
  45.6 14.2 %collective-permute-start.10 = (bf16[2,1,32,1792]{3,2,1,0:T(8,128)(2,1)S(1)}, bf16[2,1,32,1792]{3,2,1,0:T(8,128)(2,1)S(1)}, u32[]{:S(2)}, u32[]{:S(2)}) collective-permute-start(bf16[2,1,32,1792]{3,2,1,0:T(8,128)(2,1)S(1)} %slice.431), channel_id=1, source_target_pairs={{0,2},{1,3},{2,0},{3,1},{4,6},{5,7},{6,4},{7,5},{8,10},{9,11},{10,... | collective-permute-start | bytes 688136 | tf_op jit(solution)/shard_map/ppermute | solution.py:170
  55.0 8.7 %copy-start.3 = (bf16[128,1792]{1,0:T(8,128)(2,1)S(1)}, bf16[128,1792]{1,0:T(8,128)(2,1)}, u32[]{:S(2)}) copy-start(bf16[128,1792]{1,0:T(8,128)(2,1)} %param.7) | copy-start | bytes 1376260
  55.1 7.0 %collective-permute-start.8 = (bf16[2,1,32,1792]{3,2,1,0:T(8,128)(2,1)S(1)}, bf16[2,1,32,1792]{3,2,1,0:T(8,128)(2,1)S(1)}, u32[]{:S(2)}, u32[]{:S(2)}) collective-permute-start(bf16[2,1,32,1792]{3,2,1,0:T(8,128)(2,1)S(1)} %slice.432), channel_id=1, source_target_pairs={{0,1},{1,0},{2,3},{3,2},{4,5},{5,4},{6,7},{7,6},{8,9},{9,8},{10,11... | collective-permute-start | bytes 688136 | tf_op jit(solution)/shard_map/ppermute | solution.py:170
  55.5 8.2 %collective-permute-start.6 = (bf16[2,1,32,1792]{3,2,1,0:T(8,128)(2,1)S(1)}, bf16[2,1,32,1792]{3,2,1,0:T(8,128)(2,1)S(1)}, u32[]{:S(2)}, u32[]{:S(2)}) collective-permute-start(bf16[2,1,32,1792]{3,2,1,0:T(8,128)(2,1)S(1)} %slice.433), channel_id=1, source_target_pairs={{0,2},{1,3},{2,0},{3,1},{4,6},{5,7},{6,4},{7,5},{8,10},{9,11},{10,... | collective-permute-start | bytes 688136 | tf_op jit(solution)/shard_map/ppermute | solution.py:170
  59.9 6.8 %copy-start.2 = (f32[2,1,32,1792]{3,2,1,0:T(8,128)}, f32[2,1,32,1792]{3,2,1,0:T(8,128)S(1)}, u32[]{:S(2)}) copy-start(f32[2,1,32,1792]{3,2,1,0:T(8,128)S(1)} %slice_add_fusion.1) | copy-start | bytes 1376260
  64.2 13.5 %collective-permute-start.14 = (bf16[2,2,32,1792]{3,2,1,0:T(8,128)(2,1)S(1)}, bf16[2,2,32,1792]{3,2,1,0:T(8,128)(2,1)S(1)}, u32[]{:S(2)}, u32[]{:S(2)}) collective-permute-start(bf16[2,2,32,1792]{3,2,1,0:T(8,128)(2,1)S(1)} %maximum_maximum_fusion.refs_0_), channel_id=1, source_target_pairs={{0,2},{1,3},{2,0},{3,1},{4,6},{5,7},{6,4},{7,5},{8,10},{9,11},{10,... | collective-permute-start | bytes 1376264 | tf_op jit(solution)/shard_map/ppermute | solution.py:170
  64.8 13.5 %collective-permute-start.13 = (bf16[2,2,32,1792]{3,2,1,0:T(8,128)(2,1)S(1)}, bf16[2,2,32,1792]{3,2,1,0:T(8,128)(2,1)S(1)}, u32[]{:S(2)}, u32[]{:S(2)}) collective-permute-start(bf16[2,2,32,1792]{3,2,1,0:T(8,128)(2,1)S(1)} %maximum_maximum_fusion.refs_0_), channel_id=1, source_target_pairs={{0,1},{1,0},{2,3},{3,2},{4,5},{5,4},{6,7},{7,6},{8,9},{9,8},{10,11... | collective-permute-start | bytes 1376264 | tf_op jit(solution)/shard_map/ppermute | solution.py:170
  66.8 20.8 %collective-permute-start.18 = (bf16[2,2,32,1792]{3,2,1,0:T(8,128)(2,1)S(1)}, bf16[2,2,32,1792]{3,2,1,0:T(8,128)(2,1)S(1)}, u32[]{:S(2)}, u32[]{:S(2)}) collective-permute-start(bf16[2,2,32,1792]{3,2,1,0:T(8,128)(2,1)S(1)} %maximum_maximum_fusion.1.refs_5_), channel_id=1, source_target_pairs={{0,2},{1,3},{2,0},{3,1},{4,6},{5,7},{6,4},{7,5},{8,10},{9,11},{10,... | collective-permute-start | bytes 1376264 | tf_op jit(solution)/shard_map/ppermute | solution.py:170
  67.1 21.0 %collective-permute-start.17 = (bf16[2,2,32,1792]{3,2,1,0:T(8,128)(2,1)S(1)}, bf16[2,2,32,1792]{3,2,1,0:T(8,128)(2,1)S(1)}, u32[]{:S(2)}, u32[]{:S(2)}) collective-permute-start(bf16[2,2,32,1792]{3,2,1,0:T(8,128)(2,1)S(1)} %maximum_maximum_fusion.1.refs_5_), channel_id=1, source_target_pairs={{0,1},{1,0},{2,3},{3,2},{4,5},{5,4},{6,7},{7,6},{8,9},{9,8},{10,11... | collective-permute-start | bytes 1376264 | tf_op jit(solution)/shard_map/ppermute | solution.py:170
  77.7 15.2 %collective-permute-start.16 = (bf16[1,2,32,1792]{3,2,1,0:T(8,128)(2,1)S(1)}, bf16[1,2,32,1792]{3,2,1,0:T(8,128)(2,1)S(1)}, u32[]{:S(2)}, u32[]{:S(2)}) collective-permute-start(bf16[1,2,32,1792]{3,2,1,0:T(8,128)(2,1)S(1)} %slice.277), channel_id=1, source_target_pairs={{0,1},{1,0},{2,3},{3,2},{4,5},{5,4},{6,7},{7,6},{8,9},{9,8},{10,11... | collective-permute-start | bytes 688136 | tf_op jit(solution)/shard_map/ppermute | solution.py:170
  78.3 14.7 %collective-permute-start.15 = (bf16[1,2,32,1792]{3,2,1,0:T(8,128)(2,1)S(1)}, bf16[1,2,32,1792]{3,2,1,0:T(8,128)(2,1)S(1)}, u32[]{:S(2)}, u32[]{:S(2)}) collective-permute-start(bf16[1,2,32,1792]{3,2,1,0:T(8,128)(2,1)S(1)} %slice.276), channel_id=1, source_target_pairs={{0,2},{1,3},{2,0},{3,1},{4,6},{5,7},{6,4},{7,5},{8,10},{9,11},{10,... | collective-permute-start | bytes 688136 | tf_op jit(solution)/shard_map/ppermute | solution.py:170
  87.6 8.2 %collective-permute-start.20 = (bf16[1,2,32,1792]{3,2,1,0:T(8,128)(2,1)S(1)}, bf16[1,2,32,1792]{3,2,1,0:T(8,128)(2,1)S(1)}, u32[]{:S(2)}, u32[]{:S(2)}) collective-permute-start(bf16[1,2,32,1792]{3,2,1,0:T(8,128)(2,1)S(1)} %slice.279), channel_id=1, source_target_pairs={{0,1},{1,0},{2,3},{3,2},{4,5},{5,4},{6,7},{7,6},{8,9},{9,8},{10,11... | collective-permute-start | bytes 688136 | tf_op jit(solution)/shard_map/ppermute | solution.py:170
  88.2 7.7 %collective-permute-start.19 = (bf16[1,2,32,1792]{3,2,1,0:T(8,128)(2,1)S(1)}, bf16[1,2,32,1792]{3,2,1,0:T(8,128)(2,1)S(1)}, u32[]{:S(2)}, u32[]{:S(2)}) collective-permute-start(bf16[1,2,32,1792]{3,2,1,0:T(8,128)(2,1)S(1)} %slice.278), channel_id=1, source_target_pairs={{0,2},{1,3},{2,0},{3,1},{4,6},{5,7},{6,4},{7,5},{8,10},{9,11},{10,... | collective-permute-start | bytes 688136 | tf_op jit(solution)/shard_map/ppermute | solution.py:170
  99.8 1.8 %copy-start = (bf16[2,512,1792]{2,1,0:T(8,128)(2,1)}, bf16[2,512,1792]{2,1,0:T(8,128)(2,1)S(1)}, u32[]{:S(2)}) copy-start(bf16[2,512,1792]{2,1,0:T(8,128)(2,1)S(1)} %get-tuple-element.28.d_ref) | copy-start | bytes 11010052
  101.7 2.0 %collective-permute-start.21 = (bf16[512,512]{1,0:T(8,128)(2,1)S(1)}, bf16[512,512]{1,0:T(8,128)(2,1)}, u32[]{:S(2)}, u32[]{:S(2)}) collective-permute-start(bf16[512,512]{1,0:T(8,128)(2,1)S(1)} %get-tuple-element.23), channel_id=1, source_target_pairs={{0,4},{1,5},{2,6},{3,7},{4,0},{5,1},{6,2},{7,3},{8,12},{9,13},{10,... | collective-permute-start | bytes 1572872 | tf_op jit(solution)/shard_map/ppermute | solution.py:170
  102.2 16.8 %copy-start.1 = (bf16[2,512,1792]{2,1,0:T(8,128)(2,1)S(1)}, bf16[2,512,1792]{2,1,0:T(8,128)(2,1)}, u32[]{:S(2)}) copy-start(bf16[2,512,1792]{2,1,0:T(8,128)(2,1)} %copy-done) | copy-start | bytes 11010052
  104.9 7.3 %collective-permute-start.24 = (bf16[128,512]{1,0:T(8,128)(2,1)S(1)}, bf16[128,512]{1,0:T(8,128)(2,1)S(1)}, u32[]{:S(2)}, u32[]{:S(2)}) collective-permute-start(bf16[128,512]{1,0:T(8,128)(2,1)S(1)} %get-tuple-element.57), channel_id=1, source_target_pairs={{0,3},{1,2},{2,1},{3,0},{4,7},{5,6},{6,5},{7,4},{8,11},{9,10},{10,... | collective-permute-start | bytes 393224 | tf_op jit(solution)/shard_map/ppermute | solution.py:170
  106.2 8.2 %collective-permute-start.23 = (bf16[128,512]{1,0:T(8,128)(2,1)S(1)}, bf16[128,512]{1,0:T(8,128)(2,1)S(1)}, u32[]{:S(2)}, u32[]{:S(2)}) collective-permute-start(bf16[128,512]{1,0:T(8,128)(2,1)S(1)} %get-tuple-element.58), channel_id=1, source_target_pairs={{0,2},{1,3},{2,0},{3,1},{4,6},{5,7},{6,4},{7,5},{8,10},{9,11},{10,... | collective-permute-start | bytes 393224 | tf_op jit(solution)/shard_map/ppermute | solution.py:170
  107.9 6.5 %collective-permute-start.22 = (bf16[128,512]{1,0:T(8,128)(2,1)S(1)}, bf16[128,512]{1,0:T(8,128)(2,1)S(1)}, u32[]{:S(2)}, u32[]{:S(2)}) collective-permute-start(bf16[128,512]{1,0:T(8,128)(2,1)S(1)} %get-tuple-element.59), channel_id=1, source_target_pairs={{0,1},{1,0},{2,3},{3,2},{4,5},{5,4},{6,7},{7,6},{8,9},{9,8},{10,11... | collective-permute-start | bytes 393224 | tf_op jit(solution)/shard_map/ppermute | solution.py:170
  114.6 13.3 %collective-permute-start.25 = (bf16[128,512]{1,0:T(8,128)(2,1)S(1)}, bf16[128,512]{1,0:T(8,128)(2,1)S(1)}, u32[]{:S(2)}, u32[]{:S(2)}) collective-permute-start(bf16[128,512]{1,0:T(8,128)(2,1)S(1)} %get-tuple-element.25), channel_id=1, source_target_pairs={{0,8},{1,9},{2,10},{3,11},{4,12},{5,13},{6,14},{7,15},{8,0},{9,1},... | collective-permute-start | bytes 393224 | tf_op jit(solution)/shard_map/ppermute | solution.py:170
  115.8 12.7 %collective-permute-start.26 = (bf16[128,512]{1,0:T(8,128)(2,1)S(1)}, bf16[128,512]{1,0:T(8,128)(2,1)S(1)}, u32[]{:S(2)}, u32[]{:S(2)}) collective-permute-start(bf16[128,512]{1,0:T(8,128)(2,1)S(1)} %get-tuple-element.26), channel_id=1, source_target_pairs={{0,16},{1,17},{2,18},{3,19},{4,20},{5,21},{6,22},{7,23},{8,24},{9,... | collective-permute-start | bytes 393224 | tf_op jit(solution)/shard_map/ppermute | solution.py:170
  117.3 11.1 %collective-permute-start.27 = (bf16[128,512]{1,0:T(8,128)(2,1)S(1)}, bf16[128,512]{1,0:T(8,128)(2,1)S(1)}, u32[]{:S(2)}, u32[]{:S(2)}) collective-permute-start(bf16[128,512]{1,0:T(8,128)(2,1)S(1)} %get-tuple-element.27), channel_id=1, source_target_pairs={{0,24},{1,25},{2,26},{3,27},{4,28},{5,29},{6,30},{7,31},{8,16},{9,... | collective-permute-start | bytes 393224 | tf_op jit(solution)/shard_map/ppermute | solution.py:170

commit v5 on v4

--- a/solution.py
+++ b/solution.py
@@ -90,44 +90,56 @@
     return out[0] if write else list(out)
 
 
-def input_grad_kernel(spots, half_ref, *refs):
-    pieces, w_ref, d_ref = refs[: len(spots)], refs[len(spots)], refs[len(spots) + 1]
-    term_refs = refs[len(spots) + 2 :]
-    for piece, first in zip(pieces, spots):
+def input_grad_kernel(spots, outs, first, rows, chunk, half_ref, *refs):
+    pieces, w_ref = refs[: len(spots)], refs[len(spots)]
+    d_ref, *term_refs = refs[len(refs) - outs - 1 : -1]
+    mine_ref = refs[-1]
+    for piece, (k, row) in zip(pieces, spots):
         streams, _, part, _ = piece.shape
         for s in range(streams):
-            d_ref[:, pl.ds(first + s * part, part), :] = piece[s]
+            d_ref[:, pl.ds(k * rows + first + row + s * part, part), :] = piece[s]
+            mine_ref[:, pl.ds(k * chunk + row + s * part, part), :] = piece[s]
     numbers = (((1,), (1,)), ((), ()))
     for e, term_ref in enumerate(term_refs):
         feats = term_ref.shape[1]
-        rows = pl.ds(pl.multiple_of((half_ref[0] ^ e) * feats, feats), feats)
-        term = lax.dot_general(d_ref[0], w_ref[0, rows, :], numbers, preferred_element_type=jnp.float32)
-        term += lax.dot_general(d_ref[1], w_ref[1, rows, :], numbers, preferred_element_type=jnp.float32)
-        term_ref[...] = term.astype(jnp.bfloat16)
-
-
-def input_grad(pieces, spots, w_gu, half, ratio, total):
+        at = pl.ds(pl.multiple_of((half_ref[0] ^ e) * feats, feats), feats)
+        term = lax.dot_general(mine_ref[0], w_ref[0, at, :], numbers, preferred_element_type=jnp.float32)
+        term += lax.dot_general(mine_ref[1], w_ref[1, at, :], numbers, preferred_element_type=jnp.float32)
+        term = term.astype(jnp.bfloat16)
+        for k in range(mine_ref.shape[1] // chunk):
+            term_ref[pl.ds(k * rows + first, chunk), :] = term[k * chunk : (k + 1) * chunk]
+
+
+def input_grad(pieces, spots, w_gu, half, ratio, first, rows, chunk, earlier, filled=()):
     _, owned, group = w_gu.shape
     feats = owned // ratio
+    places = 1 + max(k for k, _ in spots)
+    operands = [half, *[in_vmem(x) for x in pieces], in_vmem(w_gu), *earlier, *[in_vmem(x) for x in filled]]
     return pl.pallas_call(
-        functools.partial(input_grad_kernel, spots),
+        functools.partial(input_grad_kernel, spots, ratio + 1, first, rows, chunk),
         in_specs=[pl.BlockSpec(memory_space=pltpu.SMEM)]
-        + [pl.BlockSpec(memory_space=pltpu.VMEM)] * (len(pieces) + 1),
+        + [pl.BlockSpec(memory_space=pltpu.VMEM)] * (len(pieces) + 1)
+        + [pl.BlockSpec(memory_space=pl.ANY)] * len(earlier)
+        + [pl.BlockSpec(memory_space=pltpu.VMEM)] * len(filled),
         out_specs=[pl.BlockSpec(memory_space=pltpu.VMEM)] * (ratio + 1),
-        out_shape=[pltpu.VMEM((2, total, group), jnp.bfloat16)]
-        + [pltpu.VMEM((total, feats), jnp.bfloat16)] * ratio,
-        compiler_params=pltpu.CompilerParams(vmem_limit_bytes=24 * 1024 * 1024),
-    )(half, *[in_vmem(x) for x in pieces], in_vmem(w_gu))
+        out_shape=[pltpu.VMEM((2, places * rows, group), jnp.bfloat16)]
+        + [pltpu.VMEM((places * rows, feats), jnp.bfloat16)] * ratio,
+        scratch_shapes=[pltpu.VMEM((2, places * chunk, group), jnp.bfloat16)],
+        input_output_aliases={len(operands) - len(filled) + i: i for i in range(len(filled))},
+        compiler_params=pltpu.CompilerParams(vmem_limit_bytes=16 * 1024 * 1024),
+    )(*operands)
 
 
 def weight_grad_kernel(scale, features_ref, d_ref, *refs):
     out_ref, done_ref = refs[-2:]
     done_ref[0] = 0
-    out_ref[0] = scale * jnp.dot(features_ref[...], d_ref[0], preferred_element_type=jnp.float32)
+    out_ref[0] = scale * lax.dot_general(
+        features_ref[...], d_ref[0], (((0,), (0,)), ((), ())), preferred_element_type=jnp.float32
+    )
 
 
 def weight_grad(which, features, d_both, scale, earlier, grads=None):
-    owned, total = features.shape
+    total, owned = features.shape
     group = d_both.shape[2]
     step = min(owned, 256)
     operands = [features, in_vmem(d_both), earlier] + ([] if grads is None else [grads])
@@ -135,7 +147,7 @@
         functools.partial(weight_grad_kernel, scale),
         grid=(owned // step,),
         in_specs=[
-            pl.BlockSpec((step, total), lambda i: (i, 0)),
+            pl.BlockSpec((total, step), lambda i: (0, i)),
             pl.BlockSpec((1, total, group), lambda i: (which, 0, 0)),
         ]
         + [pl.BlockSpec(memory_space=pl.ANY)] * (len(operands) - 2),
@@ -163,7 +175,6 @@
         (tokens, (node & (ratio - 1))[None], ((node >> (ratio.bit_length() - 1)) ^ place)[None])
     )
     chunk = rows // CHUNKS
-    part = chunk // 2
     orders = (bits, bits[::-1])
 
     def permute(x, move):
@@ -182,20 +193,50 @@
         halves = [got] + [permute(got, lambda p, h, q, e=e: (p, h ^ e, q)) for e in range(1, ratio)]
         return shuffle(halves, half, (), (places, rows, owned), by_half)
 
-    def reduce_local(x, order):
-        ks = list(range(places))
-        x = x.astype(jnp.float32)
-        for bit in order:
-            away = [i for i, k in enumerate(ks) if k & bit]
-            stay = [i for i, k in enumerate(ks) if not k & bit]
-            sent = jnp.stack([x[:, i] for i in away], axis=1).astype(jnp.bfloat16)
-            got = permute(sent, lambda p, h, q: (p, h, q ^ bit))
-            x = jnp.stack([x[:, i] for i in stay], axis=1) + got.astype(jnp.float32)
-            ks = [ks[i] for i in stay]
-        return x[:, 0]
-
-    def gather_local(x):
-        direct = {bit: permute(x, lambda p, h, q: (p, h, q ^ bit)) for bit in bits}
+    def sent(x, order, step):
+        ks = [k for k in range(places) if not any(k & bit for bit in order[:step])]
+        bit = order[step]
+        away = [i for i, k in enumerate(ks) if k & bit]
+        stay = [i for i, k in enumerate(ks) if not k & bit]
+        out = jnp.stack([x[:, i] for i in away], axis=1).astype(jnp.bfloat16)
+        keep = jnp.stack([x[:, i] for i in stay], axis=1).astype(jnp.float32)
+        return keep, permute(out, lambda p, h, q: (p, h, q ^ bit))
+
+    def start_forward(c):
+        part = chunk // 2
+        flat = features[:, c * chunk : (c + 1) * chunk].reshape(places * chunk, owned)
+        partial = [
+            jnp.dot(flat, w_gu[g], preferred_element_type=jnp.float32)
+            .astype(jnp.bfloat16)
+            .reshape(places, chunk, group)
+            for g in range(2)
+        ]
+        halves = [jnp.stack([p[:, s * part : (s + 1) * part] for p in partial]) for s in range(2)]
+        return list(zip(*[sent(x, orders[s], 0) for s, x in enumerate(halves)]))
+
+    def next_sums(keep, got, step):
+        summed = [k + g.astype(jnp.float32) for k, g in zip(keep, got)]
+        return list(zip(*[sent(x, orders[s], step) for s, x in enumerate(summed)]))
+
+    def gradients(keep, got, first):
+        hidden, streams = [], []
+        for k, g in zip(keep, got):
+            gate, up = (k + g.astype(jnp.float32))[:, 0]
+            sigmoid_gate = jax.nn.sigmoid(gate)
+            active = gate * sigmoid_gate
+            hidden.append((active * up).astype(jnp.bfloat16))
+            grad_in = d_hidden[first : first + gate.shape[0]].astype(jnp.float32)
+            first += gate.shape[0]
+            d_gate = grad_in * up * sigmoid_gate * (1.0 + gate * (1.0 - sigmoid_gate))
+            d_up = grad_in * active
+            streams.append(jnp.stack([d_gate, d_up]).astype(jnp.bfloat16))
+        return hidden, jnp.stack(streams)
+
+    def send_direct(x):
+        return {bit: permute(x, lambda p, h, q: (p, h, q ^ bit)) for bit in bits}
+
+    def forward_rest(x, direct):
+        part = x.shape[2]
         pieces, spots = [x] + [direct[bit] for bit in bits], [(0, 0)] + [(bit, 0) for bit in bits]
         for s, order in enumerate(orders):
             held = {0: None}
@@ -211,32 +252,18 @@
 
     w_gu, done = dequant(gate_up_codes, gate_up_scales)
     features = features_of(tokens, [done])
-    hidden, pieces, spots = [], [], []
-    for c in range(CHUNKS):
-        flat = features[:, c * chunk : (c + 1) * chunk].reshape(places * chunk, owned)
-        partial = [
-            jnp.dot(flat, w_gu[g], preferred_element_type=jnp.float32)
-            .astype(jnp.bfloat16)
-            .reshape(places, chunk, group)
-            for g in range(2)
-        ]
-        streams = []
-        for s in range(2):
-            at = slice(s * part, (s + 1) * part)
-            both = reduce_local(jnp.stack([p[:, at] for p in partial]), orders[s])
-            gate, up = both[0], both[1]
-            sigmoid_gate = jax.nn.sigmoid(gate)
-            active = gate * sigmoid_gate
-            hidden.append((active * up).astype(jnp.bfloat16))
-            first = c * chunk + s * part
-            grad_in = d_hidden[first : first + part].astype(jnp.float32)
-            d_gate = grad_in * up * sigmoid_gate * (1.0 + gate * (1.0 - sigmoid_gate))
-            d_up = grad_in * active
-            streams.append(jnp.stack([d_gate, d_up]).astype(jnp.bfloat16))
-        blocks, places_of = gather_local(jnp.stack(streams))
-        pieces += blocks
-        spots += [k * rows + c * chunk + first for k, first in places_of]
-    d_all, *term = input_grad(pieces, spots, w_gu, half, ratio, places * rows)
+    (keep_a, got_a), (keep_b, got_b) = start_forward(0), start_forward(1)
+    for step in range(1, len(bits)):
+        keep_a, got_a = next_sums(keep_a, got_a, step)
+        keep_b, got_b = next_sums(keep_b, got_b, step)
+    hidden_b, streams_b = gradients(keep_b, got_b, chunk)
+    hidden_a, streams_a = gradients(keep_a, after(got_a, streams_b), 0)
+    direct_a, direct_b = send_direct(streams_a), send_direct(streams_b)
+    rest_a, rest_b = forward_rest(streams_a, direct_a), forward_rest(streams_b, direct_b)
+    filled = input_grad(*rest_b, w_gu, half, ratio, chunk, rows, chunk, hidden_b)
+    filled = input_grad(*rest_a, w_gu, half, ratio, 0, rows, chunk, hidden_a, filled)
+    hidden = hidden_a + hidden_b
+    d_all, *term = filled
     summed = term[0].astype(jnp.float32)
     for e in range(1, ratio):
         got = permute(term[e], lambda p, h, q: (p, h ^ e, q))
@@ -245,14 +272,14 @@
     arrived = [summed[0]] + [
         permute(summed[k], lambda p, h, q: (p, h, q ^ k)) for k in range(1, places)
     ]
-    arrived = shuffle(arrived, mask)
+    flat = features.reshape(places * rows, owned)
+    scale = 1.0 / math.sqrt(rows * places)
+    grads, done = weight_grad(0, flat, d_all, scale, summed[0, :16])
+    arrived = shuffle(arrived, mask, [done])
     summands = [arrived[0]] + [
         permute(arrived[j], lambda p, h, q: (p ^ j, h, q)) for j in range(1, places)
     ]
-    scale = 1.0 / math.sqrt(rows * places)
-    turned = features.reshape(places * rows, owned).T
-    grads, _ = weight_grad(0, turned, d_all, scale, summed[0, :16])
-    grads, done = weight_grad(1, turned, d_all, scale, arrived[0][:16], grads)
+    grads, done = weight_grad(1, flat, d_all, scale, arrived[0][:16], grads)
     summands[0] = after(summands[0], done)
     d_tokens = sum(x.astype(jnp.float32) for x in summands).astype(jnp.bfloat16)
     return jnp.concatenate(hidden), d_tokens, grads

time: 129 us -> 122 us (0.946)
  waiting for transfers between devices: 54.1 us -> 37.1 us
  starting transfers between devices: 39.4 us -> 52.9 us
  other arithmetic: 6.57 us -> 4.02 us
  local copies, waits for them, and re-layouts: 3.04 us -> 0.56 us
  Pallas kernels: 20.5 us -> 21.9 us
    ppermute x28, waiting for transfers between devices: 54.1 us -> 37.1 us  [permute(): return lax.ppermute(x, AXES, pairs(move, places, ratio))]
    ppermute x28, starting transfers between devices: 39.4 us -> 52.9 us  [permute(): return lax.ppermute(x, AXES, pairs(move, places, ratio))]
    unnamed x8 -> x2, local copies, waits for them, and re-layouts: 1.85 us -> 0.01 us
    convert_element_type x3 -> x0, other arithmetic: 1.52 us -> none  [the longest x1 1.27 us: body(): hidden.append((active * up).astype(jnp.bfloat16))]
    pallas_call x1 -> x2, Pallas kernels: 3.98 us -> 4.21 us  [input_grad(): pl.pallas_call(functools.partial(input_grad_kernel, spots, ratio + 1, fir...]
  transfers between devices with their start and end apart: 28 -> 28, of which waited for: 14 -> 12; matrix products, arithmetic and copies ran while one was open for 4% -> 3% of each run, Pallas kernels for 12% -> 15%
where the time goes in v5:
time: 122 us
  starting transfers between devices  52.9 us (43%)
  waiting for transfers between devices  37.1 us (30%)
  Pallas kernels  21.9 us (18%)
  matrix products  4.59 us (4%)
  other arithmetic  4.02 us (3%)
    ppermute x28, starting transfers between devices, permute(): return lax.ppermute(x, AXES, pairs(move, places, ratio))  52.9 us
    ppermute x28, waiting for transfers between devices, permute(): return lax.ppermute(x, AXES, pairs(move, places, ratio))  37.1 us
    pallas_call x2, Pallas kernels, weight_grad(): pl.pallas_call(functools.partial(weight_grad_kernel, scale), grid=(owned...  9.32 us
    pallas_call x1, Pallas kernels, dequant(): pl.pallas_call(dequant_kernel, grid=(blocks,), in_specs=[pl.BlockSpec((2,...  6.67 us
    dot_general x4, matrix products, start_forward(): jnp.dot(flat, w_gu[g], preferred_element_type=jnp.float32)  4.59 us
    pallas_call x2, Pallas kernels, input_grad(): pl.pallas_call(functools.partial(input_grad_kernel, spots, ratio + 1, fir...  4.21 us
  transfers between devices with their start and end apart: 28, of which 12 were waited for; matrix products, arithmetic and copies ran while one was open for 3% of the time, Pallas kernels for 15%

profile of v5, /device:TPU:0, one launch (start us, length us, event | category | flops | bytes accessed | tf_op | source)
XLA Modules:
  0.0 122.1 jit_solution(2166476682579058053)
XLA Ops:
  2.2 4.8 %collective-permute-start.1 = (bf16[128,512]{1,0:T(8,128)(2,1)}, bf16[128,512]{1,0:T(8,128)(2,1)S(1)}, u32[]{:S(2)}, u32[]{:S(2)}) collective-permute-start(bf16[128,512]{1,0:T(8,128)(2,1)} %param.4), channel_id=1, source_target_pairs={{0,8},{1,0},{2,24},{3,16},{4,12},{5,4},{6,28},{7,20},{8,9},{9,1},{... | collective-permute-start | bytes 393224 | tf_op jit(solution)/shard_map/ppermute | solution.py:181
  7.0 3.5 %collective-permute-start.2 = (bf16[128,512]{1,0:T(8,128)(2,1)}, bf16[128,512]{1,0:T(8,128)(2,1)S(1)}, u32[]{:S(2)}, u32[]{:S(2)}) collective-permute-start(bf16[128,512]{1,0:T(8,128)(2,1)} %param.4), channel_id=1, source_target_pairs={{0,16},{1,24},{2,0},{3,8},{4,20},{5,28},{6,4},{7,12},{8,17},{9,25}... | collective-permute-start | bytes 393224 | tf_op jit(solution)/shard_map/ppermute | solution.py:181
  10.5 1.9 %collective-permute-start.3 = (bf16[128,512]{1,0:T(8,128)(2,1)}, bf16[128,512]{1,0:T(8,128)(2,1)S(1)}, u32[]{:S(2)}, u32[]{:S(2)}) collective-permute-start(bf16[128,512]{1,0:T(8,128)(2,1)} %param.4), channel_id=1, source_target_pairs={{0,24},{1,16},{2,8},{3,0},{4,28},{5,20},{6,12},{7,4},{8,25},{9,17}... | collective-permute-start | bytes 393224 | tf_op jit(solution)/shard_map/ppermute | solution.py:181
  13.2 6.7 %shard_map.67 = (bf16[2,1024,1792]{2,1,0:T(8,128)(2,1)S(1)}, s32[1]{0:T(128)}) custom-call(bf16[2,1024,1792]{2,1,0:T(8,128)(2,1)} %codes_ref.1, f32[2,8,1792]{2,1,0:T(8,128)S(1)} %convert_element_type.135.scales_ref), custom_call_target="tpu_custom_call" | custom-call | tf_op jit(solution)/shard_map/pallas_call | solution.py:30
  20.8 1.9 %collective-permute-done.4.refs_1_ = bf16[4,128,512]{2,1,0:T(8,128)(2,1)S(1)} collective-permute-done((bf16[4,128,512]{2,1,0:T(8,128)(2,1)S(1)}, bf16[4,128,512]{2,1,0:T(8,128)(2,1)S(1)}, u32[]{:S(2)}, u32[]{:S(2)}) %collective-permute-start.4) | collective-permute-done | bytes 524320 | tf_op jit(solution)/shard_map/ppermute | solution.py:181
  27.8 2.9 %collective-permute-start.9 = (bf16[2,2,32,1792]{3,2,1,0:T(8,128)(2,1)S(1)}, bf16[2,2,32,1792]{3,2,1,0:T(8,128)(2,1)S(1)}, u32[]{:S(2)}, u32[]{:S(2)}) collective-permute-start(bf16[2,2,32,1792]{3,2,1,0:T(8,128)(2,1)S(1)} %fusion.33), channel_id=1, source_target_pairs={{0,1},{1,0},{2,3},{3,2},{4,5},{5,4},{6,7},{7,6},{8,9},{9,8},{10,11... | collective-permute-start | bytes 1376264 | tf_op jit(solution)/shard_map/ppermute | solution.py:181
  30.7 2.6 %collective-permute-start.11 = (bf16[2,2,32,1792]{3,2,1,0:T(8,128)(2,1)S(1)}, bf16[2,2,32,1792]{3,2,1,0:T(8,128)(2,1)S(1)}, u32[]{:S(2)}, u32[]{:S(2)}) collective-permute-start(bf16[2,2,32,1792]{3,2,1,0:T(8,128)(2,1)S(1)} %pad_maximum_fusion), channel_id=1, source_target_pairs={{0,2},{1,3},{2,0},{3,1},{4,6},{5,7},{6,4},{7,5},{8,10},{9,11},{10,... | collective-permute-start | bytes 1376264 | tf_op jit(solution)/shard_map/ppermute | solution.py:181
  33.6 2.1 %collective-permute-start.5 = (bf16[2,2,32,1792]{3,2,1,0:T(8,128)(2,1)S(1)}, bf16[2,2,32,1792]{3,2,1,0:T(8,128)(2,1)S(1)}, u32[]{:S(2)}, u32[]{:S(2)}) collective-permute-start(bf16[2,2,32,1792]{3,2,1,0:T(8,128)(2,1)S(1)} %fusion.31), channel_id=1, source_target_pairs={{0,1},{1,0},{2,3},{3,2},{4,5},{5,4},{6,7},{7,6},{8,9},{9,8},{10,11... | collective-permute-start | bytes 1376264 | tf_op jit(solution)/shard_map/ppermute | solution.py:181
  35.8 6.2 %collective-permute-done.9 = bf16[2,2,32,1792]{3,2,1,0:T(8,128)(2,1)S(1)} collective-permute-done((bf16[2,2,32,1792]{3,2,1,0:T(8,128)(2,1)S(1)}, bf16[2,2,32,1792]{3,2,1,0:T(8,128)(2,1)S(1)}, u32[]{:S(2)}, u32[]{:S(2)}) %collective-permute-start.9) | collective-permute-done | bytes 458784 | tf_op jit(solution)/shard_map/ppermute | solution.py:181
  42.1 4.6 %collective-permute-start.10 = (bf16[2,1,32,1792]{3,2,1,0:T(8,128)(2,1)S(1)}, bf16[2,1,32,1792]{3,2,1,0:T(8,128)(2,1)S(1)}, u32[]{:S(2)}, u32[]{:S(2)}) collective-permute-start(bf16[2,1,32,1792]{3,2,1,0:T(8,128)(2,1)S(1)} %slice.323), channel_id=1, source_target_pairs={{0,2},{1,3},{2,0},{3,1},{4,6},{5,7},{6,4},{7,5},{8,10},{9,11},{10,... | collective-permute-start | bytes 688136 | tf_op jit(solution)/shard_map/ppermute | solution.py:181
  46.9 4.9 %collective-permute-done.5 = bf16[2,2,32,1792]{3,2,1,0:T(8,128)(2,1)S(1)} collective-permute-done((bf16[2,2,32,1792]{3,2,1,0:T(8,128)(2,1)S(1)}, bf16[2,2,32,1792]{3,2,1,0:T(8,128)(2,1)S(1)}, u32[]{:S(2)}, u32[]{:S(2)}) %collective-permute-start.5) | collective-permute-done | bytes 458784 | tf_op jit(solution)/shard_map/ppermute | solution.py:181
  52.0 4.6 %collective-permute-start.6 = (bf16[2,1,32,1792]{3,2,1,0:T(8,128)(2,1)S(1)}, bf16[2,1,32,1792]{3,2,1,0:T(8,128)(2,1)S(1)}, u32[]{:S(2)}, u32[]{:S(2)}) collective-permute-start(bf16[2,1,32,1792]{3,2,1,0:T(8,128)(2,1)S(1)} %slice.325), channel_id=1, source_target_pairs={{0,2},{1,3},{2,0},{3,1},{4,6},{5,7},{6,4},{7,5},{8,10},{9,11},{10,... | collective-permute-start | bytes 688136 | tf_op jit(solution)/shard_map/ppermute | solution.py:181
  56.8 2.6 %collective-permute-done.10 = bf16[2,1,32,1792]{3,2,1,0:T(8,128)(2,1)S(1)} collective-permute-done((bf16[2,1,32,1792]{3,2,1,0:T(8,128)(2,1)S(1)}, bf16[2,1,32,1792]{3,2,1,0:T(8,128)(2,1)S(1)}, u32[]{:S(2)}, u32[]{:S(2)}) %collective-permute-start.10) | collective-permute-done | bytes 229408 | tf_op jit(solution)/shard_map/ppermute | solution.py:181
  59.8 2.1 %collective-permute-start.17 = (bf16[2,2,32,1792]{3,2,1,0:T(8,128)(2,1)S(1)}, bf16[2,2,32,1792]{3,2,1,0:T(8,128)(2,1)S(1)}, u32[]{:S(2)}, u32[]{:S(2)}) collective-permute-start(bf16[2,2,32,1792]{3,2,1,0:T(8,128)(2,1)S(1)} %maximum_maximum_fusion.refs_0_), channel_id=1, source_target_pairs={{0,1},{1,0},{2,3},{3,2},{4,5},{5,4},{6,7},{7,6},{8,9},{9,8},{10,11... | collective-permute-start | bytes 1376264 | tf_op jit(solution)/shard_map/ppermute | solution.py:181
  61.9 2.1 %collective-permute-start.18 = (bf16[2,2,32,1792]{3,2,1,0:T(8,128)(2,1)S(1)}, bf16[2,2,32,1792]{3,2,1,0:T(8,128)(2,1)S(1)}, u32[]{:S(2)}, u32[]{:S(2)}) collective-permute-start(bf16[2,2,32,1792]{3,2,1,0:T(8,128)(2,1)S(1)} %maximum_maximum_fusion.refs_0_), channel_id=1, source_target_pairs={{0,2},{1,3},{2,0},{3,1},{4,6},{5,7},{6,4},{7,5},{8,10},{9,11},{10,... | collective-permute-start | bytes 1376264 | tf_op jit(solution)/shard_map/ppermute | solution.py:181
  64.7 2.1 %collective-permute-start.13 = (bf16[2,2,32,1792]{3,2,1,0:T(8,128)(2,1)S(1)}, bf16[2,2,32,1792]{3,2,1,0:T(8,128)(2,1)S(1)}, u32[]{:S(2)}, u32[]{:S(2)}) collective-permute-start(bf16[2,2,32,1792]{3,2,1,0:T(8,128)(2,1)S(1)} %maximum_maximum_fusion.1.refs_0_), channel_id=1, source_target_pairs={{0,1},{1,0},{2,3},{3,2},{4,5},{5,4},{6,7},{7,6},{8,9},{9,8},{10,11... | collective-permute-start | bytes 1376264 | tf_op jit(solution)/shard_map/ppermute | solution.py:181
  66.8 2.1 %collective-permute-start.14 = (bf16[2,2,32,1792]{3,2,1,0:T(8,128)(2,1)S(1)}, bf16[2,2,32,1792]{3,2,1,0:T(8,128)(2,1)S(1)}, u32[]{:S(2)}, u32[]{:S(2)}) collective-permute-start(bf16[2,2,32,1792]{3,2,1,0:T(8,128)(2,1)S(1)} %maximum_maximum_fusion.1.refs_0_), channel_id=1, source_target_pairs={{0,2},{1,3},{2,0},{3,1},{4,6},{5,7},{6,4},{7,5},{8,10},{9,11},{10,... | collective-permute-start | bytes 1376264 | tf_op jit(solution)/shard_map/ppermute | solution.py:181
  68.9 4.8 %collective-permute-done.17.refs_1_ = bf16[2,2,32,1792]{3,2,1,0:T(8,128)(2,1)S(1)} collective-permute-done((bf16[2,2,32,1792]{3,2,1,0:T(8,128)(2,1)S(1)}, bf16[2,2,32,1792]{3,2,1,0:T(8,128)(2,1)S(1)}, u32[]{:S(2)}, u32[]{:S(2)}) %collective-permute-start.17) | collective-permute-done | bytes 458784 | tf_op jit(solution)/shard_map/ppermute | solution.py:181
  73.8 2.4 %collective-permute-start.19 = (bf16[1,2,32,1792]{3,2,1,0:T(8,128)(2,1)S(1)}, bf16[1,2,32,1792]{3,2,1,0:T(8,128)(2,1)S(1)}, u32[]{:S(2)}, u32[]{:S(2)}) collective-permute-start(bf16[1,2,32,1792]{3,2,1,0:T(8,128)(2,1)S(1)} %slice.230), channel_id=1, source_target_pairs={{0,2},{1,3},{2,0},{3,1},{4,6},{5,7},{6,4},{7,5},{8,10},{9,11},{10,... | collective-permute-start | bytes 688136 | tf_op jit(solution)/shard_map/ppermute | solution.py:181
  77.6 5.9 %collective-permute-done.13.refs_1_ = bf16[2,2,32,1792]{3,2,1,0:T(8,128)(2,1)S(1)} collective-permute-done((bf16[2,2,32,1792]{3,2,1,0:T(8,128)(2,1)S(1)}, bf16[2,2,32,1792]{3,2,1,0:T(8,128)(2,1)S(1)}, u32[]{:S(2)}, u32[]{:S(2)}) %collective-permute-start.13) | collective-permute-done | bytes 458784 | tf_op jit(solution)/shard_map/ppermute | solution.py:181
  83.6 2.4 %collective-permute-start.15 = (bf16[1,2,32,1792]{3,2,1,0:T(8,128)(2,1)S(1)}, bf16[1,2,32,1792]{3,2,1,0:T(8,128)(2,1)S(1)}, u32[]{:S(2)}, u32[]{:S(2)}) collective-permute-start(bf16[1,2,32,1792]{3,2,1,0:T(8,128)(2,1)S(1)} %slice.228), channel_id=1, source_target_pairs={{0,2},{1,3},{2,0},{3,1},{4,6},{5,7},{6,4},{7,5},{8,10},{9,11},{10,... | collective-permute-start | bytes 688136 | tf_op jit(solution)/shard_map/ppermute | solution.py:181
  87.5 2.7 %collective-permute-done.19.refs_3_ = bf16[1,2,32,1792]{3,2,1,0:T(8,128)(2,1)S(1)} collective-permute-done((bf16[1,2,32,1792]{3,2,1,0:T(8,128)(2,1)S(1)}, bf16[1,2,32,1792]{3,2,1,0:T(8,128)(2,1)S(1)}, u32[]{:S(2)}, u32[]{:S(2)}) %collective-permute-start.19) | collective-permute-done | bytes 229408 | tf_op jit(solution)/shard_map/ppermute | solution.py:181
  90.2 2.1 %shard_map.70 = (bf16[2,512,1792]{2,1,0:T(8,128)(2,1)S(1)}, bf16[512,512]{1,0:T(8,128)(2,1)S(1)}, bf16[512,512]{1,0:T(8,128)(2,1)S(1)}) custom-call(s32[1]{0:T(128)} %bitcast.index_ref.half_ref, bf16[2,2,32,1792]{3,2,1,0:T(8,128)(2,1)S(1)} %maximum_maximum_fusion.refs_0_, bf16[2,2,32,1792]{3,2,1,0:T(8,128)(2,1)S(1)} %collective-permute-done.17.refs_1_, ...), custom_call_target="tpu_custom_call" | custom-call | tf_op jit(solution)/shard_map/pallas_call | solution.py:118
  93.3 2.1 %shard_map.71 = (bf16[2,512,1792]{2,1,0:T(8,128)(2,1)S(1)}, bf16[512,512]{1,0:T(8,128)(2,1)S(1)}, bf16[512,512]{1,0:T(8,128)(2,1)S(1)}) custom-call(s32[1]{0:T(128)} %bitcast.index_ref.half_ref, bf16[2,2,32,1792]{3,2,1,0:T(8,128)(2,1)S(1)} %maximum_maximum_fusion.1.refs_0_, ...), custom_call_target="tpu_custom_call", output_to_operand_aliasing={{0}: (9, {}), {1}: (10, {}), {2}: (11, {})} | custom-call | tf_op jit(solution)/shard_map/pallas_call | solution.py:118
  95.5 1.9 %collective-permute-done.21 = bf16[512,512]{1,0:T(8,128)(2,1)S(1)} collective-permute-done((bf16[512,512]{1,0:T(8,128)(2,1)S(1)}, bf16[512,512]{1,0:T(8,128)(2,1)S(1)}, u32[]{:S(2)}, u32[]{:S(2)}) %collective-permute-start.21) | collective-permute-done | bytes 524320 | tf_op jit(solution)/shard_map/ppermute | solution.py:181
  97.6 1.8 %collective-permute-start.22 = (bf16[128,512]{1,0:T(8,128)(2,1)S(1)}, bf16[128,512]{1,0:T(8,128)(2,1)S(1)}, u32[]{:S(2)}, u32[]{:S(2)}) collective-permute-start(bf16[128,512]{1,0:T(8,128)(2,1)S(1)} %get-tuple-element.69), channel_id=1, source_target_pairs={{0,1},{1,0},{2,3},{3,2},{4,5},{5,4},{6,7},{7,6},{8,9},{9,8},{10,11... | collective-permute-start | bytes 393224 | tf_op jit(solution)/shard_map/ppermute | solution.py:181
  99.3 1.7 %collective-permute-start.23 = (bf16[128,512]{1,0:T(8,128)(2,1)S(1)}, bf16[128,512]{1,0:T(8,128)(2,1)S(1)}, u32[]{:S(2)}, u32[]{:S(2)}) collective-permute-start(bf16[128,512]{1,0:T(8,128)(2,1)S(1)} %get-tuple-element.68), channel_id=1, source_target_pairs={{0,2},{1,3},{2,0},{3,1},{4,6},{5,7},{6,4},{7,5},{8,10},{9,11},{10,... | collective-permute-start | bytes 393224 | tf_op jit(solution)/shard_map/ppermute | solution.py:181
  101.1 4.7 %shard_map.72 = (f32[2,1024,1792]{2,1,0:T(8,128)}, s32[1]{0:T(128)}) custom-call(bf16[512,1024]{1,0:T(8,128)(2,1)S(1)} %bitcast.146, bf16[2,512,1792]{2,1,0:T(8,128)(2,1)S(1)} %get-tuple-element.35.d_ref, bf16[16,512]{1,0:T(8,128)(2,1)S(1)} %slice_bitcast_fusion.16.refs_0_), custom_call_target="tpu_custom_call" | custom-call | tf_op jit(solution)/shard_map/pallas_call | solution.py:146
  108.2 2.2 %collective-permute-start.27 = (bf16[128,512]{1,0:T(8,128)(2,1)S(1)}, bf16[128,512]{1,0:T(8,128)(2,1)S(1)}, u32[]{:S(2)}, u32[]{:S(2)}) collective-permute-start(bf16[128,512]{1,0:T(8,128)(2,1)S(1)} %get-tuple-element.40), channel_id=1, source_target_pairs={{0,24},{1,25},{2,26},{3,27},{4,28},{5,29},{6,30},{7,31},{8,16},{9,... | collective-permute-start | bytes 393224 | tf_op jit(solution)/shard_map/ppermute | solution.py:181
  110.5 2.2 %collective-permute-start.25 = (bf16[128,512]{1,0:T(8,128)(2,1)S(1)}, bf16[128,512]{1,0:T(8,128)(2,1)S(1)}, u32[]{:S(2)}, u32[]{:S(2)}) collective-permute-start(bf16[128,512]{1,0:T(8,128)(2,1)S(1)} %get-tuple-element.38), channel_id=1, source_target_pairs={{0,8},{1,9},{2,10},{3,11},{4,12},{5,13},{6,14},{7,15},{8,0},{9,1},... | collective-permute-start | bytes 393224 | tf_op jit(solution)/shard_map/ppermute | solution.py:181
  113.5 4.7 %shard_map.74 = (f32[2,1024,1792]{2,1,0:T(8,128)}, s32[1]{0:T(128)}) custom-call(bf16[512,1024]{1,0:T(8,128)(2,1)S(1)} %bitcast.147, bf16[2,512,1792]{2,1,0:T(8,128)(2,1)S(1)} %get-tuple-element.35.d_ref, bf16[16,512]{1,0:T(8,128)(2,1)S(1)} %slice.197.refs_0_, f32[2,1024,1792]{2,1,0:T(8,128)} %get-tuple-element.41.refs_1_), custom_call_target="tpu_custom_call", output_to_operand_aliasing={{0}: (3, {})} | custom-call | tf_op jit(solution)/shard_map/pallas_call | solution.py:146
  118.1 3.2 %collective-permute-done.26 = bf16[128,512]{1,0:T(8,128)(2,1)S(1)} collective-permute-done((bf16[128,512]{1,0:T(8,128)(2,1)S(1)}, bf16[128,512]{1,0:T(8,128)(2,1)S(1)}, u32[]{:S(2)}, u32[]{:S(2)}) %collective-permute-start.26) | collective-permute-done | bytes 131104 | tf_op jit(solution)/shard_map/ppermute | solution.py:181
  (74 shorter events, 18.8 us)
Async XLA Ops:
  0.6 19.3 %collective-permute-start = (bf16[128,512]{1,0:T(8,128)(2,1)}, bf16[128,512]{1,0:T(8,128)(2,1)S(1)}, u32[]{:S(2)}, u32[]{:S(2)}) collective-permute-start(bf16[128,512]{1,0:T(8,128)(2,1)} %param.4), channel_id=1, source_target_pairs={{0,0},{1,8},{2,16},{3,24},{4,4},{5,12},{6,20},{7,28},{8,1},{9,9},{... | collective-permute-start | bytes 393224 | tf_op jit(solution)/shard_map/ppermute | solution.py:181
  2.2 17.7 %collective-permute-start.1 = (bf16[128,512]{1,0:T(8,128)(2,1)}, bf16[128,512]{1,0:T(8,128)(2,1)S(1)}, u32[]{:S(2)}, u32[]{:S(2)}) collective-permute-start(bf16[128,512]{1,0:T(8,128)(2,1)} %param.4), channel_id=1, source_target_pairs={{0,8},{1,0},{2,24},{3,16},{4,12},{5,4},{6,28},{7,20},{8,9},{9,1},{... | collective-permute-start | bytes 393224 | tf_op jit(solution)/shard_map/ppermute | solution.py:181
  7.0 12.9 %collective-permute-start.2 = (bf16[128,512]{1,0:T(8,128)(2,1)}, bf16[128,512]{1,0:T(8,128)(2,1)S(1)}, u32[]{:S(2)}, u32[]{:S(2)}) collective-permute-start(bf16[128,512]{1,0:T(8,128)(2,1)} %param.4), channel_id=1, source_target_pairs={{0,16},{1,24},{2,0},{3,8},{4,20},{5,28},{6,4},{7,12},{8,17},{9,25}... | collective-permute-start | bytes 393224 | tf_op jit(solution)/shard_map/ppermute | solution.py:181
  10.5 9.5 %collective-permute-start.3 = (bf16[128,512]{1,0:T(8,128)(2,1)}, bf16[128,512]{1,0:T(8,128)(2,1)S(1)}, u32[]{:S(2)}, u32[]{:S(2)}) collective-permute-start(bf16[128,512]{1,0:T(8,128)(2,1)} %param.4), channel_id=1, source_target_pairs={{0,24},{1,16},{2,8},{3,0},{4,28},{5,20},{6,12},{7,4},{8,25},{9,17}... | collective-permute-start | bytes 393224 | tf_op jit(solution)/shard_map/ppermute | solution.py:181
  20.8 2.0 %collective-permute-start.4 = (bf16[4,128,512]{2,1,0:T(8,128)(2,1)S(1)}, bf16[4,128,512]{2,1,0:T(8,128)(2,1)S(1)}, u32[]{:S(2)}, u32[]{:S(2)}) collective-permute-start(bf16[4,128,512]{2,1,0:T(8,128)(2,1)S(1)} %shard_map.68.refs_0_), channel_id=1, source_target_pairs={{0,4},{1,5},{2,6},{3,7},{4,0},{5,1},{6,2},{7,3},{8,12},{9,13},{10,... | collective-permute-start | bytes 1572872 | tf_op jit(solution)/shard_map/ppermute | solution.py:181
  27.8 14.2 %collective-permute-start.9 = (bf16[2,2,32,1792]{3,2,1,0:T(8,128)(2,1)S(1)}, bf16[2,2,32,1792]{3,2,1,0:T(8,128)(2,1)S(1)}, u32[]{:S(2)}, u32[]{:S(2)}) collective-permute-start(bf16[2,2,32,1792]{3,2,1,0:T(8,128)(2,1)S(1)} %fusion.33), channel_id=1, source_target_pairs={{0,1},{1,0},{2,3},{3,2},{4,5},{5,4},{6,7},{7,6},{8,9},{9,8},{10,11... | collective-permute-start | bytes 1376264 | tf_op jit(solution)/shard_map/ppermute | solution.py:181
  30.7 16.0 %collective-permute-start.11 = (bf16[2,2,32,1792]{3,2,1,0:T(8,128)(2,1)S(1)}, bf16[2,2,32,1792]{3,2,1,0:T(8,128)(2,1)S(1)}, u32[]{:S(2)}, u32[]{:S(2)}) collective-permute-start(bf16[2,2,32,1792]{3,2,1,0:T(8,128)(2,1)S(1)} %pad_maximum_fusion), channel_id=1, source_target_pairs={{0,2},{1,3},{2,0},{3,1},{4,6},{5,7},{6,4},{7,5},{8,10},{9,11},{10,... | collective-permute-start | bytes 1376264 | tf_op jit(solution)/shard_map/ppermute | solution.py:181
  33.6 18.3 %collective-permute-start.5 = (bf16[2,2,32,1792]{3,2,1,0:T(8,128)(2,1)S(1)}, bf16[2,2,32,1792]{3,2,1,0:T(8,128)(2,1)S(1)}, u32[]{:S(2)}, u32[]{:S(2)}) collective-permute-start(bf16[2,2,32,1792]{3,2,1,0:T(8,128)(2,1)S(1)} %fusion.31), channel_id=1, source_target_pairs={{0,1},{1,0},{2,3},{3,2},{4,5},{5,4},{6,7},{7,6},{8,9},{9,8},{10,11... | collective-permute-start | bytes 1376264 | tf_op jit(solution)/shard_map/ppermute | solution.py:181
  35.7 20.9 %collective-permute-start.7 = (bf16[2,2,32,1792]{3,2,1,0:T(8,128)(2,1)S(1)}, bf16[2,2,32,1792]{3,2,1,0:T(8,128)(2,1)S(1)}, u32[]{:S(2)}, u32[]{:S(2)}) collective-permute-start(bf16[2,2,32,1792]{3,2,1,0:T(8,128)(2,1)S(1)} %pad_maximum_fusion.1), channel_id=1, source_target_pairs={{0,2},{1,3},{2,0},{3,1},{4,6},{5,7},{6,4},{7,5},{8,10},{9,11},{10,... | collective-permute-start | bytes 1376264 | tf_op jit(solution)/shard_map/ppermute | solution.py:181
  42.1 17.2 %collective-permute-start.10 = (bf16[2,1,32,1792]{3,2,1,0:T(8,128)(2,1)S(1)}, bf16[2,1,32,1792]{3,2,1,0:T(8,128)(2,1)S(1)}, u32[]{:S(2)}, u32[]{:S(2)}) collective-permute-start(bf16[2,1,32,1792]{3,2,1,0:T(8,128)(2,1)S(1)} %slice.323), channel_id=1, source_target_pairs={{0,2},{1,3},{2,0},{3,1},{4,6},{5,7},{6,4},{7,5},{8,10},{9,11},{10,... | collective-permute-start | bytes 688136 | tf_op jit(solution)/shard_map/ppermute | solution.py:181
  46.9 12.5 %collective-permute-start.12 = (bf16[2,1,32,1792]{3,2,1,0:T(8,128)(2,1)S(1)}, bf16[2,1,32,1792]{3,2,1,0:T(8,128)(2,1)S(1)}, u32[]{:S(2)}, u32[]{:S(2)}) collective-permute-start(bf16[2,1,32,1792]{3,2,1,0:T(8,128)(2,1)S(1)} %slice.322), channel_id=1, source_target_pairs={{0,1},{1,0},{2,3},{3,2},{4,5},{5,4},{6,7},{7,6},{8,9},{9,8},{10,11... | collective-permute-start | bytes 688136 | tf_op jit(solution)/shard_map/ppermute | solution.py:181
  51.8 7.6 %copy-start = (bf16[128,1792]{1,0:T(8,128)(2,1)S(1)}, bf16[128,1792]{1,0:T(8,128)(2,1)}, u32[]{:S(2)}) copy-start(bf16[128,1792]{1,0:T(8,128)(2,1)} %param.7) | copy-start | bytes 1376260
  52.0 12.3 %collective-permute-start.6 = (bf16[2,1,32,1792]{3,2,1,0:T(8,128)(2,1)S(1)}, bf16[2,1,32,1792]{3,2,1,0:T(8,128)(2,1)S(1)}, u32[]{:S(2)}, u32[]{:S(2)}) collective-permute-start(bf16[2,1,32,1792]{3,2,1,0:T(8,128)(2,1)S(1)} %slice.325), channel_id=1, source_target_pairs={{0,2},{1,3},{2,0},{3,1},{4,6},{5,7},{6,4},{7,5},{8,10},{9,11},{10,... | collective-permute-start | bytes 688136 | tf_op jit(solution)/shard_map/ppermute | solution.py:181
  56.7 7.6 %collective-permute-start.8 = (bf16[2,1,32,1792]{3,2,1,0:T(8,128)(2,1)S(1)}, bf16[2,1,32,1792]{3,2,1,0:T(8,128)(2,1)S(1)}, u32[]{:S(2)}, u32[]{:S(2)}) collective-permute-start(bf16[2,1,32,1792]{3,2,1,0:T(8,128)(2,1)S(1)} %slice.324), channel_id=1, source_target_pairs={{0,1},{1,0},{2,3},{3,2},{4,5},{5,4},{6,7},{7,6},{8,9},{9,8},{10,11... | collective-permute-start | bytes 688136 | tf_op jit(solution)/shard_map/ppermute | solution.py:181
  59.8 13.9 %collective-permute-start.17 = (bf16[2,2,32,1792]{3,2,1,0:T(8,128)(2,1)S(1)}, bf16[2,2,32,1792]{3,2,1,0:T(8,128)(2,1)S(1)}, u32[]{:S(2)}, u32[]{:S(2)}) collective-permute-start(bf16[2,2,32,1792]{3,2,1,0:T(8,128)(2,1)S(1)} %maximum_maximum_fusion.refs_0_), channel_id=1, source_target_pairs={{0,1},{1,0},{2,3},{3,2},{4,5},{5,4},{6,7},{7,6},{8,9},{9,8},{10,11... | collective-permute-start | bytes 1376264 | tf_op jit(solution)/shard_map/ppermute | solution.py:181
  61.9 14.2 %collective-permute-start.18 = (bf16[2,2,32,1792]{3,2,1,0:T(8,128)(2,1)S(1)}, bf16[2,2,32,1792]{3,2,1,0:T(8,128)(2,1)S(1)}, u32[]{:S(2)}, u32[]{:S(2)}) collective-permute-start(bf16[2,2,32,1792]{3,2,1,0:T(8,128)(2,1)S(1)} %maximum_maximum_fusion.refs_0_), channel_id=1, source_target_pairs={{0,2},{1,3},{2,0},{3,1},{4,6},{5,7},{6,4},{7,5},{8,10},{9,11},{10,... | collective-permute-start | bytes 1376264 | tf_op jit(solution)/shard_map/ppermute | solution.py:181
  64.7 18.8 %collective-permute-start.13 = (bf16[2,2,32,1792]{3,2,1,0:T(8,128)(2,1)S(1)}, bf16[2,2,32,1792]{3,2,1,0:T(8,128)(2,1)S(1)}, u32[]{:S(2)}, u32[]{:S(2)}) collective-permute-start(bf16[2,2,32,1792]{3,2,1,0:T(8,128)(2,1)S(1)} %maximum_maximum_fusion.1.refs_0_), channel_id=1, source_target_pairs={{0,1},{1,0},{2,3},{3,2},{4,5},{5,4},{6,7},{7,6},{8,9},{9,8},{10,11... | collective-permute-start | bytes 1376264 | tf_op jit(solution)/shard_map/ppermute | solution.py:181
  66.8 19.1 %collective-permute-start.14 = (bf16[2,2,32,1792]{3,2,1,0:T(8,128)(2,1)S(1)}, bf16[2,2,32,1792]{3,2,1,0:T(8,128)(2,1)S(1)}, u32[]{:S(2)}, u32[]{:S(2)}) collective-permute-start(bf16[2,2,32,1792]{3,2,1,0:T(8,128)(2,1)S(1)} %maximum_maximum_fusion.1.refs_0_), channel_id=1, source_target_pairs={{0,2},{1,3},{2,0},{3,1},{4,6},{5,7},{6,4},{7,5},{8,10},{9,11},{10,... | collective-permute-start | bytes 1376264 | tf_op jit(solution)/shard_map/ppermute | solution.py:181
  73.8 16.4 %collective-permute-start.19 = (bf16[1,2,32,1792]{3,2,1,0:T(8,128)(2,1)S(1)}, bf16[1,2,32,1792]{3,2,1,0:T(8,128)(2,1)S(1)}, u32[]{:S(2)}, u32[]{:S(2)}) collective-permute-start(bf16[1,2,32,1792]{3,2,1,0:T(8,128)(2,1)S(1)} %slice.230), channel_id=1, source_target_pairs={{0,2},{1,3},{2,0},{3,1},{4,6},{5,7},{6,4},{7,5},{8,10},{9,11},{10,... | collective-permute-start | bytes 688136 | tf_op jit(solution)/shard_map/ppermute | solution.py:181
  76.1 14.1 %collective-permute-start.20 = (bf16[1,2,32,1792]{3,2,1,0:T(8,128)(2,1)S(1)}, bf16[1,2,32,1792]{3,2,1,0:T(8,128)(2,1)S(1)}, u32[]{:S(2)}, u32[]{:S(2)}) collective-permute-start(bf16[1,2,32,1792]{3,2,1,0:T(8,128)(2,1)S(1)} %slice.231), channel_id=1, source_target_pairs={{0,1},{1,0},{2,3},{3,2},{4,5},{5,4},{6,7},{7,6},{8,9},{9,8},{10,11... | collective-permute-start | bytes 688136 | tf_op jit(solution)/shard_map/ppermute | solution.py:181
  83.6 9.7 %collective-permute-start.15 = (bf16[1,2,32,1792]{3,2,1,0:T(8,128)(2,1)S(1)}, bf16[1,2,32,1792]{3,2,1,0:T(8,128)(2,1)S(1)}, u32[]{:S(2)}, u32[]{:S(2)}) collective-permute-start(bf16[1,2,32,1792]{3,2,1,0:T(8,128)(2,1)S(1)} %slice.228), channel_id=1, source_target_pairs={{0,2},{1,3},{2,0},{3,1},{4,6},{5,7},{6,4},{7,5},{8,10},{9,11},{10,... | collective-permute-start | bytes 688136 | tf_op jit(solution)/shard_map/ppermute | solution.py:181
  86.0 7.3 %collective-permute-start.16 = (bf16[1,2,32,1792]{3,2,1,0:T(8,128)(2,1)S(1)}, bf16[1,2,32,1792]{3,2,1,0:T(8,128)(2,1)S(1)}, u32[]{:S(2)}, u32[]{:S(2)}) collective-permute-start(bf16[1,2,32,1792]{3,2,1,0:T(8,128)(2,1)S(1)} %slice.229), channel_id=1, source_target_pairs={{0,1},{1,0},{2,3},{3,2},{4,5},{5,4},{6,7},{7,6},{8,9},{9,8},{10,11... | collective-permute-start | bytes 688136 | tf_op jit(solution)/shard_map/ppermute | solution.py:181
  95.4 2.0 %collective-permute-start.21 = (bf16[512,512]{1,0:T(8,128)(2,1)S(1)}, bf16[512,512]{1,0:T(8,128)(2,1)S(1)}, u32[]{:S(2)}, u32[]{:S(2)}) collective-permute-start(bf16[512,512]{1,0:T(8,128)(2,1)S(1)} %get-tuple-element.34), channel_id=1, source_target_pairs={{0,4},{1,5},{2,6},{3,7},{4,0},{5,1},{6,2},{7,3},{8,12},{9,13},{10,... | collective-permute-start | bytes 1572872 | tf_op jit(solution)/shard_map/ppermute | solution.py:181
  97.6 8.2 %collective-permute-start.22 = (bf16[128,512]{1,0:T(8,128)(2,1)S(1)}, bf16[128,512]{1,0:T(8,128)(2,1)S(1)}, u32[]{:S(2)}, u32[]{:S(2)}) collective-permute-start(bf16[128,512]{1,0:T(8,128)(2,1)S(1)} %get-tuple-element.69), channel_id=1, source_target_pairs={{0,1},{1,0},{2,3},{3,2},{4,5},{5,4},{6,7},{7,6},{8,9},{9,8},{10,11... | collective-permute-start | bytes 393224 | tf_op jit(solution)/shard_map/ppermute | solution.py:181
  99.3 8.1 %collective-permute-start.23 = (bf16[128,512]{1,0:T(8,128)(2,1)S(1)}, bf16[128,512]{1,0:T(8,128)(2,1)S(1)}, u32[]{:S(2)}, u32[]{:S(2)}) collective-permute-start(bf16[128,512]{1,0:T(8,128)(2,1)S(1)} %get-tuple-element.68), channel_id=1, source_target_pairs={{0,2},{1,3},{2,0},{3,1},{4,6},{5,7},{6,4},{7,5},{8,10},{9,11},{10,... | collective-permute-start | bytes 393224 | tf_op jit(solution)/shard_map/ppermute | solution.py:181
  101.1 6.3 %collective-permute-start.24 = (bf16[128,512]{1,0:T(8,128)(2,1)S(1)}, bf16[128,512]{1,0:T(8,128)(2,1)S(1)}, u32[]{:S(2)}, u32[]{:S(2)}) collective-permute-start(bf16[128,512]{1,0:T(8,128)(2,1)S(1)} %get-tuple-element.67), channel_id=1, source_target_pairs={{0,3},{1,2},{2,1},{3,0},{4,7},{5,6},{6,5},{7,4},{8,11},{9,10},{10,... | collective-permute-start | bytes 393224 | tf_op jit(solution)/shard_map/ppermute | solution.py:181
  108.2 9.9 %collective-permute-start.27 = (bf16[128,512]{1,0:T(8,128)(2,1)S(1)}, bf16[128,512]{1,0:T(8,128)(2,1)S(1)}, u32[]{:S(2)}, u32[]{:S(2)}) collective-permute-start(bf16[128,512]{1,0:T(8,128)(2,1)S(1)} %get-tuple-element.40), channel_id=1, source_target_pairs={{0,24},{1,25},{2,26},{3,27},{4,28},{5,29},{6,30},{7,31},{8,16},{9,... | collective-permute-start | bytes 393224 | tf_op jit(solution)/shard_map/ppermute | solution.py:181
  110.4 10.9 %collective-permute-start.26 = (bf16[128,512]{1,0:T(8,128)(2,1)S(1)}, bf16[128,512]{1,0:T(8,128)(2,1)S(1)}, u32[]{:S(2)}, u32[]{:S(2)}) collective-permute-start(bf16[128,512]{1,0:T(8,128)(2,1)S(1)} %get-tuple-element.39), channel_id=1, source_target_pairs={{0,16},{1,17},{2,18},{3,19},{4,20},{5,21},{6,22},{7,23},{8,24},{9,... | collective-permute-start | bytes 393224 | tf_op jit(solution)/shard_map/ppermute | solution.py:181
  110.5 10.8 %collective-permute-start.25 = (bf16[128,512]{1,0:T(8,128)(2,1)S(1)}, bf16[128,512]{1,0:T(8,128)(2,1)S(1)}, u32[]{:S(2)}, u32[]{:S(2)}) collective-permute-start(bf16[128,512]{1,0:T(8,128)(2,1)S(1)} %get-tuple-element.38), channel_id=1, source_target_pairs={{0,8},{1,9},{2,10},{3,11},{4,12},{5,13},{6,14},{7,15},{8,0},{9,1},... | collective-permute-start | bytes 393224 | tf_op jit(solution)/shard_map/ppermute | solution.py:181

commit v6 on v5

--- a/solution.py
+++ b/solution.py
@@ -62,32 +62,89 @@
     return lax.optimization_barrier((x, earlier))[0]
 
 
-def shuffle_kernel(count, write, index_ref, *refs):
+def shuffle_kernel(order, write, index_ref, *refs):
+    count = len(order)
     choices, outs = refs[:count], refs[-1:] if write else refs[-count:]
     for i in range(count):
-        for j in range(count):
+        for j, choice in zip(order, choices):
 
             @pl.when(index_ref[0] == i ^ j)
             def _():
                 if write:
-                    write(outs[0], i, choices[j][...])
+                    write(outs[0], i, choice[...])
                 else:
-                    outs[i][...] = choices[j][...]
+                    outs[i][...] = choice[...]
 
 
 def shuffle(choices, index, earlier=(), shape=None, write=None):
     one = choices[0]
     shapes = [shape] if write else [one.shape] * len(choices)
     out = pl.pallas_call(
-        functools.partial(shuffle_kernel, len(choices), write),
+        functools.partial(shuffle_kernel, list(choices), write),
         in_specs=[pl.BlockSpec(memory_space=pltpu.SMEM)]
         + [pl.BlockSpec(memory_space=pltpu.VMEM)] * len(choices)
         + [pl.BlockSpec(memory_space=pl.ANY)] * len(earlier),
         out_specs=[pl.BlockSpec(memory_space=pltpu.VMEM)] * len(shapes),
         out_shape=[pltpu.VMEM(s, one.dtype) for s in shapes],
         compiler_params=pltpu.CompilerParams(vmem_limit_bytes=16 * 1024 * 1024),
-    )(index, *[in_vmem(x) for x in choices], *earlier)
+    )(index, *[in_vmem(x) for x in choices.values()], *earlier)
     return out[0] if write else list(out)
+
+
+def own_half_kernel(half_ref, x_ref, w_ref, out_ref):
+    places, rows, feats = x_ref.shape
+    at = pl.ds(pl.multiple_of(half_ref[0] * feats, feats), feats)
+    flat = x_ref[...].reshape(places * rows, feats)
+    for g in range(2):
+        out_ref[g] = jnp.dot(flat, w_ref[g, at, :], preferred_element_type=jnp.float32).reshape(
+            out_ref.shape[1:]
+        )
+
+
+def own_half(x, w_gu, half):
+    places, rows, _ = x.shape
+    return pl.pallas_call(
+        own_half_kernel,
+        in_specs=[pl.BlockSpec(memory_space=pltpu.SMEM)] + [pl.BlockSpec(memory_space=pltpu.VMEM)] * 2,
+        out_specs=pl.BlockSpec(memory_space=pltpu.VMEM),
+        out_shape=pltpu.VMEM((2, places, rows, w_gu.shape[2]), jnp.float32),
+        compiler_params=pltpu.CompilerParams(vmem_limit_bytes=12 * 1024 * 1024),
+    )(half, in_vmem(x), in_vmem(w_gu))
+
+
+def other_halves_kernel(count, first, chunk, aways, half_ref, *refs):
+    others, w_ref, sum_ref, outs = refs[:count], refs[count], refs[count + 1], refs[count + 2 :]
+    places, _, feats = others[0].shape
+    part = chunk // len(aways)
+    rows = pl.ds(first, chunk)
+    for g in range(2):
+        total = sum_ref[g, :, rows, :].reshape(places * chunk, -1)
+        for e, other_ref in enumerate(others, 1):
+            at = pl.ds(pl.multiple_of((half_ref[0] ^ e) * feats, feats), feats)
+            flat = other_ref[:, rows, :].reshape(places * chunk, feats)
+            total += jnp.dot(flat, w_ref[g, at, :], preferred_element_type=jnp.float32)
+        for s, away in enumerate(aways):
+            counts = [0, 0]
+            for k in range(places):
+                block = total[k * chunk + s * part : k * chunk + (s + 1) * part]
+                kind = 0 if k & away else 1
+                out_ref = outs[2 * s + kind]
+                out_ref[g, counts[kind]] = block.astype(out_ref.dtype)
+                counts[kind] += 1
+
+
+def other_halves(others, w_gu, own, half, first, chunk, aways):
+    _, places, _, group = own.shape
+    shape = (2, places // 2, chunk // len(aways), group)
+    outs = pl.pallas_call(
+        functools.partial(other_halves_kernel, len(others), first, chunk, aways),
+        in_specs=[pl.BlockSpec(memory_space=pltpu.SMEM)]
+        + [pl.BlockSpec(memory_space=pltpu.VMEM)] * (len(others) + 2),
+        out_specs=[pl.BlockSpec(memory_space=pltpu.VMEM)] * (2 * len(aways)),
+        out_shape=[pltpu.VMEM(shape, jnp.bfloat16), pltpu.VMEM(shape, jnp.float32)] * len(aways),
+        compiler_params=pltpu.CompilerParams(vmem_limit_bytes=16 * 1024 * 1024),
+    )(half, *[in_vmem(x) for x in others], in_vmem(w_gu), in_vmem(own))
+    return outs[0::2], outs[1::2]
 
 
 def input_grad_kernel(spots, outs, first, rows, chunk, half_ref, *refs):
@@ -175,23 +232,25 @@
         (tokens, (node & (ratio - 1))[None], ((node >> (ratio.bit_length() - 1)) ^ place)[None])
     )
     chunk = rows // CHUNKS
+    part = chunk // 2
     orders = (bits, bits[::-1])
 
     def permute(x, move):
         return lax.ppermute(x, AXES, pairs(move, places, ratio))
 
-    def features_of(x, earlier):
-        got = [permute(x, lambda p, h, q, j=j: (q ^ j, h, p)) for j in range(places)]
+    def own_features(x, earlier):
+        got = {j: permute(x, lambda p, h, q: (q ^ j, h, p)) for j in [*range(1, places), 0]}
 
         def by_place(out_ref, i, value):
             out_ref[i] = value
 
+        return shuffle(got, mask, earlier, (places, rows, feats), by_place)
+
+    def joined(halves):
         def by_half(out_ref, i, value):
             out_ref[:, :, i * feats : (i + 1) * feats] = value
 
-        got = shuffle(got, mask, earlier, (places, rows, feats), by_place)
-        halves = [got] + [permute(got, lambda p, h, q, e=e: (p, h ^ e, q)) for e in range(1, ratio)]
-        return shuffle(halves, half, (), (places, rows, owned), by_half)
+        return shuffle(dict(enumerate(halves)), half, (), (places, rows, owned), by_half)
 
     def sent(x, order, step):
         ks = [k for k in range(places) if not any(k & bit for bit in order[:step])]
@@ -203,16 +262,11 @@
         return keep, permute(out, lambda p, h, q: (p, h, q ^ bit))
 
     def start_forward(c):
-        part = chunk // 2
-        flat = features[:, c * chunk : (c + 1) * chunk].reshape(places * chunk, owned)
-        partial = [
-            jnp.dot(flat, w_gu[g], preferred_element_type=jnp.float32)
-            .astype(jnp.bfloat16)
-            .reshape(places, chunk, group)
-            for g in range(2)
+        aways = [order[0] for order in orders]
+        out, keep = other_halves(others, w_gu, own, half, c * chunk, chunk, aways)
+        return keep, [
+            permute(x, lambda p, h, q, bit=bit: (p, h, q ^ bit)) for x, bit in zip(out, aways)
         ]
-        halves = [jnp.stack([p[:, s * part : (s + 1) * part] for p in partial]) for s in range(2)]
-        return list(zip(*[sent(x, orders[s], 0) for s, x in enumerate(halves)]))
 
     def next_sums(keep, got, step):
         summed = [k + g.astype(jnp.float32) for k, g in zip(keep, got)]
@@ -251,7 +305,9 @@
         return pieces, spots
 
     w_gu, done = dequant(gate_up_codes, gate_up_scales)
-    features = features_of(tokens, [done])
+    mine = own_features(tokens, [done])
+    others = [permute(mine, lambda p, h, q, e=e: (p, h ^ e, q)) for e in range(1, ratio)]
+    own = own_half(mine, w_gu, half)
     (keep_a, got_a), (keep_b, got_b) = start_forward(0), start_forward(1)
     for step in range(1, len(bits)):
         keep_a, got_a = next_sums(keep_a, got_a, step)
@@ -262,7 +318,6 @@
     rest_a, rest_b = forward_rest(streams_a, direct_a), forward_rest(streams_b, direct_b)
     filled = input_grad(*rest_b, w_gu, half, ratio, chunk, rows, chunk, hidden_b)
     filled = input_grad(*rest_a, w_gu, half, ratio, 0, rows, chunk, hidden_a, filled)
-    hidden = hidden_a + hidden_b
     d_all, *term = filled
     summed = term[0].astype(jnp.float32)
     for e in range(1, ratio):
@@ -272,17 +327,17 @@
     arrived = [summed[0]] + [
         permute(summed[k], lambda p, h, q: (p, h, q ^ k)) for k in range(1, places)
     ]
-    flat = features.reshape(places * rows, owned)
+    flat = joined([mine] + others).reshape(places * rows, owned)
     scale = 1.0 / math.sqrt(rows * places)
     grads, done = weight_grad(0, flat, d_all, scale, summed[0, :16])
-    arrived = shuffle(arrived, mask, [done])
+    arrived = shuffle(dict(enumerate(arrived)), mask, [done])
     summands = [arrived[0]] + [
         permute(arrived[j], lambda p, h, q: (p ^ j, h, q)) for j in range(1, places)
     ]
     grads, done = weight_grad(1, flat, d_all, scale, arrived[0][:16], grads)
     summands[0] = after(summands[0], done)
     d_tokens = sum(x.astype(jnp.float32) for x in summands).astype(jnp.bfloat16)
-    return jnp.concatenate(hidden), d_tokens, grads
+    return jnp.concatenate(hidden_a + hidden_b), d_tokens, grads
 
 
 def solution(mesh):

time: 122 us -> 117 us (0.959)
  starting transfers between devices: 52.9 us -> 35.9 us
  waiting for transfers between devices: 37.1 us -> 49.3 us
  matrix products: 4.59 us -> 0 us
  Pallas kernels: 21.9 us -> 26.3 us
    ppermute x28, starting transfers between devices: 52.9 us -> 35.9 us  [permute(): return lax.ppermute(x, AXES, pairs(move, places, ratio))]
    ppermute x28, waiting for transfers between devices: 37.1 us -> 49.3 us  [permute(): return lax.ppermute(x, AXES, pairs(move, places, ratio))]
    dot_general x4 -> x0, matrix products: 4.59 us -> none  [start_forward(): jnp.dot(flat, w_gu[g], preferred_element_type=jnp.float32)]
    pallas_call x3 -> x6, Pallas kernels: 1.67 us -> 6.1 us  [the longest x2 2.35 us: other_halves(): pl.pallas_call(functools.partial(other_halves_kernel, len(others), first,...]
  transfers between devices with their start and end apart: 28 -> 28, of which waited for: 12 -> 15; matrix products, arithmetic and copies ran while one was open for 3% -> 3% of each run, Pallas kernels for 15% -> 18%
where the time goes in v6:
time: 117 us; the launch traced here: 116 us
  waiting for transfers between devices  49.3 us (42%)
  starting transfers between devices  35.9 us (31%)
  Pallas kernels  26.3 us (22%)
  other arithmetic  3.72 us (3%)
    ppermute x28, waiting for transfers between devices, permute(): return lax.ppermute(x, AXES, pairs(move, places, ratio))  49.3 us
    ppermute x28, starting transfers between devices, permute(): return lax.ppermute(x, AXES, pairs(move, places, ratio))  35.9 us
    pallas_call x2, Pallas kernels, weight_grad(): pl.pallas_call(functools.partial(weight_grad_kernel, scale), grid=(owned...  9.32 us
    pallas_call x1, Pallas kernels, dequant(): pl.pallas_call(dequant_kernel, grid=(blocks,), in_specs=[pl.BlockSpec((2,...  6.67 us
    pallas_call x2, Pallas kernels, input_grad(): pl.pallas_call(functools.partial(input_grad_kernel, spots, ratio + 1, fir...  4.21 us
    pallas_call x2, Pallas kernels, other_halves(): pl.pallas_call(functools.partial(other_halves_kernel, len(others), first,...  2.35 us
  transfers between devices with their start and end apart: 28, of which 15 were waited for; matrix products, arithmetic and copies ran while one was open for 3% of the time, Pallas kernels for 18%

profile of v6, /device:TPU:0, one launch (start us, length us, event | category | flops | bytes accessed | tf_op | source)
XLA Modules:
  0.0 116.3 jit_solution(3903271480714021084)
XLA Ops:
  0.6 3.1 %collective-permute-start = (bf16[128,512]{1,0:T(8,128)(2,1)}, bf16[128,512]{1,0:T(8,128)(2,1)S(1)}, u32[]{:S(2)}, u32[]{:S(2)}) collective-permute-start(bf16[128,512]{1,0:T(8,128)(2,1)} %param.4), channel_id=1, source_target_pairs={{0,8},{1,0},{2,24},{3,16},{4,12},{5,4},{6,28},{7,20},{8,9},{9,1},{... | collective-permute-start | bytes 393224 | tf_op jit(solution)/shard_map/ppermute | solution.py:239
  3.7 2.4 %collective-permute-start.1 = (bf16[128,512]{1,0:T(8,128)(2,1)}, bf16[128,512]{1,0:T(8,128)(2,1)S(1)}, u32[]{:S(2)}, u32[]{:S(2)}) collective-permute-start(bf16[128,512]{1,0:T(8,128)(2,1)} %param.4), channel_id=1, source_target_pairs={{0,16},{1,24},{2,0},{3,8},{4,20},{5,28},{6,4},{7,12},{8,17},{9,25}... | collective-permute-start | bytes 393224 | tf_op jit(solution)/shard_map/ppermute | solution.py:239
  6.1 2.5 %collective-permute-start.2 = (bf16[128,512]{1,0:T(8,128)(2,1)}, bf16[128,512]{1,0:T(8,128)(2,1)S(1)}, u32[]{:S(2)}, u32[]{:S(2)}) collective-permute-start(bf16[128,512]{1,0:T(8,128)(2,1)} %param.4), channel_id=1, source_target_pairs={{0,24},{1,16},{2,8},{3,0},{4,28},{5,20},{6,12},{7,4},{8,25},{9,17}... | collective-permute-start | bytes 393224 | tf_op jit(solution)/shard_map/ppermute | solution.py:239
  8.6 1.6 %collective-permute-start.3 = (bf16[128,512]{1,0:T(8,128)(2,1)}, bf16[128,512]{1,0:T(8,128)(2,1)S(1)}, u32[]{:S(2)}, u32[]{:S(2)}) collective-permute-start(bf16[128,512]{1,0:T(8,128)(2,1)} %param.4), channel_id=1, source_target_pairs={{0,0},{1,8},{2,16},{3,24},{4,4},{5,12},{6,20},{7,28},{8,1},{9,9},{... | collective-permute-start | bytes 393224 | tf_op jit(solution)/shard_map/ppermute | solution.py:239
  11.0 6.7 %shard_map.67 = (bf16[2,1024,1792]{2,1,0:T(8,128)(2,1)S(1)}, s32[1]{0:T(128)}) custom-call(bf16[2,1024,1792]{2,1,0:T(8,128)(2,1)} %codes_ref.1, f32[2,8,1792]{2,1,0:T(8,128)S(1)} %convert_element_type.111.scales_ref), custom_call_target="tpu_custom_call" | custom-call | tf_op jit(solution)/shard_map/pallas_call | solution.py:30
  18.6 2.1 %shard_map.69.refs_2_ = f32[2,4,128,1792]{3,2,1,0:T(8,128)S(1)} custom-call(s32[1]{0:T(128)} %bitcast.half_ref.index_ref, bf16[4,128,512]{2,1,0:T(8,128)(2,1)S(1)} %shard_map.68.x_ref.refs_0_, bf16[2,1024,1792]{2,1,0:T(8,128)(2,1)S(1)} %get-tuple-element.35.w_ref.refs_1_.refs_5_), custom_call_target="tpu_custom_call" | custom-call | tf_op jit(solution)/shard_map/pallas_call | solution.py:106
  21.9 5.1 %collective-permute-start.9 = (bf16[2,2,32,1792]{3,2,1,0:T(8,128)(2,1)S(1)}, bf16[2,2,32,1792]{3,2,1,0:T(8,128)(2,1)S(1)}, u32[]{:S(2)}, u32[]{:S(2)}) collective-permute-start(bf16[2,2,32,1792]{3,2,1,0:T(8,128)(2,1)S(1)} %get-tuple-element.41), channel_id=1, source_target_pairs={{0,1},{1,0},{2,3},{3,2},{4,5},{5,4},{6,7},{7,6},{8,9},{9,8},{10,11... | collective-permute-start | bytes 1376264 | tf_op jit(solution)/shard_map/ppermute | solution.py:239
  28.1 2.1 %collective-permute-start.7 = (bf16[2,2,32,1792]{3,2,1,0:T(8,128)(2,1)S(1)}, bf16[2,2,32,1792]{3,2,1,0:T(8,128)(2,1)S(1)}, u32[]{:S(2)}, u32[]{:S(2)}) collective-permute-start(bf16[2,2,32,1792]{3,2,1,0:T(8,128)(2,1)S(1)} %get-tuple-element.39), channel_id=1, source_target_pairs={{0,2},{1,3},{2,0},{3,1},{4,6},{5,7},{6,4},{7,5},{8,10},{9,11},{10,... | collective-permute-start | bytes 1376264 | tf_op jit(solution)/shard_map/ppermute | solution.py:239
  30.3 8.0 %collective-permute-done.9 = bf16[2,2,32,1792]{3,2,1,0:T(8,128)(2,1)S(1)} collective-permute-done((bf16[2,2,32,1792]{3,2,1,0:T(8,128)(2,1)S(1)}, bf16[2,2,32,1792]{3,2,1,0:T(8,128)(2,1)S(1)}, u32[]{:S(2)}, u32[]{:S(2)}) %collective-permute-start.9) | collective-permute-done | bytes 458784 | tf_op jit(solution)/shard_map/ppermute | solution.py:239
  38.4 1.7 %collective-permute-start.10 = (bf16[2,1,32,1792]{3,2,1,0:T(8,128)(2,1)S(1)}, bf16[2,1,32,1792]{3,2,1,0:T(8,128)(2,1)S(1)}, u32[]{:S(2)}, u32[]{:S(2)}) collective-permute-start(bf16[2,1,32,1792]{3,2,1,0:T(8,128)(2,1)S(1)} %slice.139), channel_id=1, source_target_pairs={{0,2},{1,3},{2,0},{3,1},{4,6},{5,7},{6,4},{7,5},{8,10},{9,11},{10,... | collective-permute-start | bytes 688136 | tf_op jit(solution)/shard_map/ppermute | solution.py:239
  40.7 7.5 %collective-permute-done.5 = bf16[2,2,32,1792]{3,2,1,0:T(8,128)(2,1)S(1)} collective-permute-done((bf16[2,2,32,1792]{3,2,1,0:T(8,128)(2,1)S(1)}, bf16[2,2,32,1792]{3,2,1,0:T(8,128)(2,1)S(1)}, u32[]{:S(2)}, u32[]{:S(2)}) %collective-permute-start.5) | collective-permute-done | bytes 458784 | tf_op jit(solution)/shard_map/ppermute | solution.py:239
  48.3 1.7 %collective-permute-start.6 = (bf16[2,1,32,1792]{3,2,1,0:T(8,128)(2,1)S(1)}, bf16[2,1,32,1792]{3,2,1,0:T(8,128)(2,1)S(1)}, u32[]{:S(2)}, u32[]{:S(2)}) collective-permute-start(bf16[2,1,32,1792]{3,2,1,0:T(8,128)(2,1)S(1)} %slice.141), channel_id=1, source_target_pairs={{0,2},{1,3},{2,0},{3,1},{4,6},{5,7},{6,4},{7,5},{8,10},{9,11},{10,... | collective-permute-start | bytes 688136 | tf_op jit(solution)/shard_map/ppermute | solution.py:239
  50.5 4.5 %collective-permute-done.10 = bf16[2,1,32,1792]{3,2,1,0:T(8,128)(2,1)S(1)} collective-permute-done((bf16[2,1,32,1792]{3,2,1,0:T(8,128)(2,1)S(1)}, bf16[2,1,32,1792]{3,2,1,0:T(8,128)(2,1)S(1)}, u32[]{:S(2)}, u32[]{:S(2)}) %collective-permute-start.10) | collective-permute-done | bytes 229408 | tf_op jit(solution)/shard_map/ppermute | solution.py:239
  55.6 1.7 %collective-permute-start.18 = (bf16[2,2,32,1792]{3,2,1,0:T(8,128)(2,1)S(1)}, bf16[2,2,32,1792]{3,2,1,0:T(8,128)(2,1)S(1)}, u32[]{:S(2)}, u32[]{:S(2)}) collective-permute-start(bf16[2,2,32,1792]{3,2,1,0:T(8,128)(2,1)S(1)} %maximum_maximum_fusion.refs_0_), channel_id=1, source_target_pairs={{0,2},{1,3},{2,0},{3,1},{4,6},{5,7},{6,4},{7,5},{8,10},{9,11},{10,... | collective-permute-start | bytes 1376264 | tf_op jit(solution)/shard_map/ppermute | solution.py:239
  57.3 2.7 %collective-permute-done.6 = bf16[2,1,32,1792]{3,2,1,0:T(8,128)(2,1)S(1)} collective-permute-done((bf16[2,1,32,1792]{3,2,1,0:T(8,128)(2,1)S(1)}, bf16[2,1,32,1792]{3,2,1,0:T(8,128)(2,1)S(1)}, u32[]{:S(2)}, u32[]{:S(2)}) %collective-permute-start.6) | collective-permute-done | bytes 229408 | tf_op jit(solution)/shard_map/ppermute | solution.py:239
  60.5 1.7 %collective-permute-start.14 = (bf16[2,2,32,1792]{3,2,1,0:T(8,128)(2,1)S(1)}, bf16[2,2,32,1792]{3,2,1,0:T(8,128)(2,1)S(1)}, u32[]{:S(2)}, u32[]{:S(2)}) collective-permute-start(bf16[2,2,32,1792]{3,2,1,0:T(8,128)(2,1)S(1)} %maximum_maximum_fusion.1.refs_0_), channel_id=1, source_target_pairs={{0,2},{1,3},{2,0},{3,1},{4,6},{5,7},{6,4},{7,5},{8,10},{9,11},{10,... | collective-permute-start | bytes 1376264 | tf_op jit(solution)/shard_map/ppermute | solution.py:239
  62.2 6.9 %collective-permute-done.17.refs_1_ = bf16[2,2,32,1792]{3,2,1,0:T(8,128)(2,1)S(1)} collective-permute-done((bf16[2,2,32,1792]{3,2,1,0:T(8,128)(2,1)S(1)}, bf16[2,2,32,1792]{3,2,1,0:T(8,128)(2,1)S(1)}, u32[]{:S(2)}, u32[]{:S(2)}) %collective-permute-start.17) | collective-permute-done | bytes 458784 | tf_op jit(solution)/shard_map/ppermute | solution.py:239
  69.8 1.4 %collective-permute-start.20 = (bf16[1,2,32,1792]{3,2,1,0:T(8,128)(2,1)S(1)}, bf16[1,2,32,1792]{3,2,1,0:T(8,128)(2,1)S(1)}, u32[]{:S(2)}, u32[]{:S(2)}) collective-permute-start(bf16[1,2,32,1792]{3,2,1,0:T(8,128)(2,1)S(1)} %slice.115), channel_id=1, source_target_pairs={{0,1},{1,0},{2,3},{3,2},{4,5},{5,4},{6,7},{7,6},{8,9},{9,8},{10,11... | collective-permute-start | bytes 688136 | tf_op jit(solution)/shard_map/ppermute | solution.py:239
  71.1 7.7 %collective-permute-done.13.refs_1_ = bf16[2,2,32,1792]{3,2,1,0:T(8,128)(2,1)S(1)} collective-permute-done((bf16[2,2,32,1792]{3,2,1,0:T(8,128)(2,1)S(1)}, bf16[2,2,32,1792]{3,2,1,0:T(8,128)(2,1)S(1)}, u32[]{:S(2)}, u32[]{:S(2)}) %collective-permute-start.13) | collective-permute-done | bytes 458784 | tf_op jit(solution)/shard_map/ppermute | solution.py:239
  79.6 1.4 %collective-permute-start.16 = (bf16[1,2,32,1792]{3,2,1,0:T(8,128)(2,1)S(1)}, bf16[1,2,32,1792]{3,2,1,0:T(8,128)(2,1)S(1)}, u32[]{:S(2)}, u32[]{:S(2)}) collective-permute-start(bf16[1,2,32,1792]{3,2,1,0:T(8,128)(2,1)S(1)} %slice.113), channel_id=1, source_target_pairs={{0,1},{1,0},{2,3},{3,2},{4,5},{5,4},{6,7},{7,6},{8,9},{9,8},{10,11... | collective-permute-start | bytes 688136 | tf_op jit(solution)/shard_map/ppermute | solution.py:239
  81.0 3.5 %collective-permute-done.19.refs_3_ = bf16[1,2,32,1792]{3,2,1,0:T(8,128)(2,1)S(1)} collective-permute-done((bf16[1,2,32,1792]{3,2,1,0:T(8,128)(2,1)S(1)}, bf16[1,2,32,1792]{3,2,1,0:T(8,128)(2,1)S(1)}, u32[]{:S(2)}, u32[]{:S(2)}) %collective-permute-start.19) | collective-permute-done | bytes 229408 | tf_op jit(solution)/shard_map/ppermute | solution.py:239
  84.5 2.1 %shard_map.72 = (bf16[2,512,1792]{2,1,0:T(8,128)(2,1)S(1)}, bf16[512,512]{1,0:T(8,128)(2,1)S(1)}, bf16[512,512]{1,0:T(8,128)(2,1)S(1)}) custom-call(s32[1]{0:T(128)} %bitcast.half_ref.index_ref, bf16[2,2,32,1792]{3,2,1,0:T(8,128)(2,1)S(1)} %maximum_maximum_fusion.refs_0_, bf16[2,2,32,1792]{3,2,1,0:T(8,128)(2,1)S(1)} %collective-permute-done.17.refs_1_, ...), custom_call_target="tpu_custom_call" | custom-call | tf_op jit(solution)/shard_map/pallas_call | solution.py:175
  86.6 2.1 %collective-permute-done.15.refs_3_ = bf16[1,2,32,1792]{3,2,1,0:T(8,128)(2,1)S(1)} collective-permute-done((bf16[1,2,32,1792]{3,2,1,0:T(8,128)(2,1)S(1)}, bf16[1,2,32,1792]{3,2,1,0:T(8,128)(2,1)S(1)}, u32[]{:S(2)}, u32[]{:S(2)}) %collective-permute-start.15) | collective-permute-done | bytes 229408 | tf_op jit(solution)/shard_map/ppermute | solution.py:239
  88.7 2.1 %shard_map.73 = (bf16[2,512,1792]{2,1,0:T(8,128)(2,1)S(1)}, bf16[512,512]{1,0:T(8,128)(2,1)S(1)}, bf16[512,512]{1,0:T(8,128)(2,1)S(1)}) custom-call(s32[1]{0:T(128)} %bitcast.half_ref.index_ref, bf16[2,2,32,1792]{3,2,1,0:T(8,128)(2,1)S(1)} %maximum_maximum_fusion.1.refs_0_, ...), custom_call_target="tpu_custom_call", output_to_operand_aliasing={{0}: (9, {}), {1}: (10, {}), {2}: (11, {})} | custom-call | tf_op jit(solution)/shard_map/pallas_call | solution.py:175
  91.0 1.8 %collective-permute-done.21 = bf16[512,512]{1,0:T(8,128)(2,1)S(1)} collective-permute-done((bf16[512,512]{1,0:T(8,128)(2,1)S(1)}, bf16[512,512]{1,0:T(8,128)(2,1)S(1)}, u32[]{:S(2)}, u32[]{:S(2)}) %collective-permute-start.21) | collective-permute-done | bytes 524320 | tf_op jit(solution)/shard_map/ppermute | solution.py:239
  93.4 1.3 %collective-permute-start.23 = (bf16[128,512]{1,0:T(8,128)(2,1)S(1)}, bf16[128,512]{1,0:T(8,128)(2,1)S(1)}, u32[]{:S(2)}, u32[]{:S(2)}) collective-permute-start(bf16[128,512]{1,0:T(8,128)(2,1)S(1)} %get-tuple-element.68), channel_id=1, source_target_pairs={{0,2},{1,3},{2,0},{3,1},{4,6},{5,7},{6,4},{7,5},{8,10},{9,11},{10,... | collective-permute-start | bytes 393224 | tf_op jit(solution)/shard_map/ppermute | solution.py:239
  94.8 1.8 %collective-permute-start.24 = (bf16[128,512]{1,0:T(8,128)(2,1)S(1)}, bf16[128,512]{1,0:T(8,128)(2,1)S(1)}, u32[]{:S(2)}, u32[]{:S(2)}) collective-permute-start(bf16[128,512]{1,0:T(8,128)(2,1)S(1)} %get-tuple-element.67), channel_id=1, source_target_pairs={{0,3},{1,2},{2,1},{3,0},{4,7},{5,6},{6,5},{7,4},{8,11},{9,10},{10,... | collective-permute-start | bytes 393224 | tf_op jit(solution)/shard_map/ppermute | solution.py:239
  96.6 4.7 %shard_map.75 = (f32[2,1024,1792]{2,1,0:T(8,128)}, s32[1]{0:T(128)}) custom-call(bf16[512,1024]{1,0:T(8,128)(2,1)S(1)} %bitcast.102, bf16[2,512,1792]{2,1,0:T(8,128)(2,1)S(1)} %get-tuple-element.51.d_ref, bf16[16,512]{1,0:T(8,128)(2,1)S(1)} %slice_bitcast_fusion.8.refs_0_), custom_call_target="tpu_custom_call" | custom-call | tf_op jit(solution)/shard_map/pallas_call | solution.py:203
  102.3 1.8 %collective-permute-start.27 = (bf16[128,512]{1,0:T(8,128)(2,1)S(1)}, bf16[128,512]{1,0:T(8,128)(2,1)S(1)}, u32[]{:S(2)}, u32[]{:S(2)}) collective-permute-start(bf16[128,512]{1,0:T(8,128)(2,1)S(1)} %get-tuple-element.56), channel_id=1, source_target_pairs={{0,24},{1,25},{2,26},{3,27},{4,28},{5,29},{6,30},{7,31},{8,16},{9,... | collective-permute-start | bytes 393224 | tf_op jit(solution)/shard_map/ppermute | solution.py:239
  104.5 2.3 %collective-permute-start.25 = (bf16[128,512]{1,0:T(8,128)(2,1)S(1)}, bf16[128,512]{1,0:T(8,128)(2,1)S(1)}, u32[]{:S(2)}, u32[]{:S(2)}) collective-permute-start(bf16[128,512]{1,0:T(8,128)(2,1)S(1)} %get-tuple-element.54), channel_id=1, source_target_pairs={{0,8},{1,9},{2,10},{3,11},{4,12},{5,13},{6,14},{7,15},{8,0},{9,1},... | collective-permute-start | bytes 393224 | tf_op jit(solution)/shard_map/ppermute | solution.py:239
  107.5 4.7 %shard_map.77 = (f32[2,1024,1792]{2,1,0:T(8,128)}, s32[1]{0:T(128)}) custom-call(bf16[512,1024]{1,0:T(8,128)(2,1)S(1)} %bitcast.103, bf16[2,512,1792]{2,1,0:T(8,128)(2,1)S(1)} %get-tuple-element.51.d_ref, bf16[16,512]{1,0:T(8,128)(2,1)S(1)} %slice.103.refs_0_, f32[2,1024,1792]{2,1,0:T(8,128)} %get-tuple-element.57.refs_1_), custom_call_target="tpu_custom_call", output_to_operand_aliasing={{0}: (3, {})} | custom-call | tf_op jit(solution)/shard_map/pallas_call | solution.py:203
  112.2 3.4 %collective-permute-done.26 = bf16[128,512]{1,0:T(8,128)(2,1)S(1)} collective-permute-done((bf16[128,512]{1,0:T(8,128)(2,1)S(1)}, bf16[128,512]{1,0:T(8,128)(2,1)S(1)}, u32[]{:S(2)}, u32[]{:S(2)}) %collective-permute-start.26) | collective-permute-done | bytes 131104 | tf_op jit(solution)/shard_map/ppermute | solution.py:239
  (63 shorter events, 11.8 us)
Async XLA Ops:
  0.6 17.0 %collective-permute-start = (bf16[128,512]{1,0:T(8,128)(2,1)}, bf16[128,512]{1,0:T(8,128)(2,1)S(1)}, u32[]{:S(2)}, u32[]{:S(2)}) collective-permute-start(bf16[128,512]{1,0:T(8,128)(2,1)} %param.4), channel_id=1, source_target_pairs={{0,8},{1,0},{2,24},{3,16},{4,12},{5,4},{6,28},{7,20},{8,9},{9,1},{... | collective-permute-start | bytes 393224 | tf_op jit(solution)/shard_map/ppermute | solution.py:239
  3.7 14.0 %collective-permute-start.1 = (bf16[128,512]{1,0:T(8,128)(2,1)}, bf16[128,512]{1,0:T(8,128)(2,1)S(1)}, u32[]{:S(2)}, u32[]{:S(2)}) collective-permute-start(bf16[128,512]{1,0:T(8,128)(2,1)} %param.4), channel_id=1, source_target_pairs={{0,16},{1,24},{2,0},{3,8},{4,20},{5,28},{6,4},{7,12},{8,17},{9,25}... | collective-permute-start | bytes 393224 | tf_op jit(solution)/shard_map/ppermute | solution.py:239
  6.1 11.6 %collective-permute-start.2 = (bf16[128,512]{1,0:T(8,128)(2,1)}, bf16[128,512]{1,0:T(8,128)(2,1)S(1)}, u32[]{:S(2)}, u32[]{:S(2)}) collective-permute-start(bf16[128,512]{1,0:T(8,128)(2,1)} %param.4), channel_id=1, source_target_pairs={{0,24},{1,16},{2,8},{3,0},{4,28},{5,20},{6,12},{7,4},{8,25},{9,17}... | collective-permute-start | bytes 393224 | tf_op jit(solution)/shard_map/ppermute | solution.py:239
  8.6 9.1 %collective-permute-start.3 = (bf16[128,512]{1,0:T(8,128)(2,1)}, bf16[128,512]{1,0:T(8,128)(2,1)S(1)}, u32[]{:S(2)}, u32[]{:S(2)}) collective-permute-start(bf16[128,512]{1,0:T(8,128)(2,1)} %param.4), channel_id=1, source_target_pairs={{0,0},{1,8},{2,16},{3,24},{4,4},{5,12},{6,20},{7,28},{8,1},{9,9},{... | collective-permute-start | bytes 393224 | tf_op jit(solution)/shard_map/ppermute | solution.py:239
  18.5 2.2 %collective-permute-start.4 = (bf16[4,128,512]{2,1,0:T(8,128)(2,1)S(1)}, bf16[4,128,512]{2,1,0:T(8,128)(2,1)S(1)}, u32[]{:S(2)}, u32[]{:S(2)}) collective-permute-start(bf16[4,128,512]{2,1,0:T(8,128)(2,1)S(1)} %shard_map.68.x_ref.refs_0_), channel_id=1, source_target_pairs={{0,4},{1,5},{2,6},{3,7},{4,0},{5,1},{6,2},{7,3},{8,12},{9,13},{10,... | collective-permute-start | bytes 1572872 | tf_op jit(solution)/shard_map/ppermute | solution.py:239
  21.9 16.4 %collective-permute-start.9 = (bf16[2,2,32,1792]{3,2,1,0:T(8,128)(2,1)S(1)}, bf16[2,2,32,1792]{3,2,1,0:T(8,128)(2,1)S(1)}, u32[]{:S(2)}, u32[]{:S(2)}) collective-permute-start(bf16[2,2,32,1792]{3,2,1,0:T(8,128)(2,1)S(1)} %get-tuple-element.41), channel_id=1, source_target_pairs={{0,1},{1,0},{2,3},{3,2},{4,5},{5,4},{6,7},{7,6},{8,9},{9,8},{10,11... | collective-permute-start | bytes 1376264 | tf_op jit(solution)/shard_map/ppermute | solution.py:239
  26.9 13.4 %collective-permute-start.11 = (bf16[2,2,32,1792]{3,2,1,0:T(8,128)(2,1)S(1)}, bf16[2,2,32,1792]{3,2,1,0:T(8,128)(2,1)S(1)}, u32[]{:S(2)}, u32[]{:S(2)}) collective-permute-start(bf16[2,2,32,1792]{3,2,1,0:T(8,128)(2,1)S(1)} %get-tuple-element.43), channel_id=1, source_target_pairs={{0,2},{1,3},{2,0},{3,1},{4,6},{5,7},{6,4},{7,5},{8,10},{9,11},{10,... | collective-permute-start | bytes 1376264 | tf_op jit(solution)/shard_map/ppermute | solution.py:239
  28.1 27.0 %copy-start = (bf16[128,1792]{1,0:T(8,128)(2,1)S(1)}, bf16[128,1792]{1,0:T(8,128)(2,1)}, u32[]{:S(2)}) copy-start(bf16[128,1792]{1,0:T(8,128)(2,1)} %param.7) | copy-start | bytes 1376260
  28.1 22.0 %collective-permute-start.7 = (bf16[2,2,32,1792]{3,2,1,0:T(8,128)(2,1)S(1)}, bf16[2,2,32,1792]{3,2,1,0:T(8,128)(2,1)S(1)}, u32[]{:S(2)}, u32[]{:S(2)}) collective-permute-start(bf16[2,2,32,1792]{3,2,1,0:T(8,128)(2,1)S(1)} %get-tuple-element.39), channel_id=1, source_target_pairs={{0,2},{1,3},{2,0},{3,1},{4,6},{5,7},{6,4},{7,5},{8,10},{9,11},{10,... | collective-permute-start | bytes 1376264 | tf_op jit(solution)/shard_map/ppermute | solution.py:239
  30.2 17.9 %collective-permute-start.5 = (bf16[2,2,32,1792]{3,2,1,0:T(8,128)(2,1)S(1)}, bf16[2,2,32,1792]{3,2,1,0:T(8,128)(2,1)S(1)}, u32[]{:S(2)}, u32[]{:S(2)}) collective-permute-start(bf16[2,2,32,1792]{3,2,1,0:T(8,128)(2,1)S(1)} %get-tuple-element.37), channel_id=1, source_target_pairs={{0,1},{1,0},{2,3},{3,2},{4,5},{5,4},{6,7},{7,6},{8,9},{9,8},{10,11... | collective-permute-start | bytes 1376264 | tf_op jit(solution)/shard_map/ppermute | solution.py:239
  38.4 16.6 %collective-permute-start.10 = (bf16[2,1,32,1792]{3,2,1,0:T(8,128)(2,1)S(1)}, bf16[2,1,32,1792]{3,2,1,0:T(8,128)(2,1)S(1)}, u32[]{:S(2)}, u32[]{:S(2)}) collective-permute-start(bf16[2,1,32,1792]{3,2,1,0:T(8,128)(2,1)S(1)} %slice.139), channel_id=1, source_target_pairs={{0,2},{1,3},{2,0},{3,1},{4,6},{5,7},{6,4},{7,5},{8,10},{9,11},{10,... | collective-permute-start | bytes 688136 | tf_op jit(solution)/shard_map/ppermute | solution.py:239
  40.4 14.7 %collective-permute-start.12 = (bf16[2,1,32,1792]{3,2,1,0:T(8,128)(2,1)S(1)}, bf16[2,1,32,1792]{3,2,1,0:T(8,128)(2,1)S(1)}, u32[]{:S(2)}, u32[]{:S(2)}) collective-permute-start(bf16[2,1,32,1792]{3,2,1,0:T(8,128)(2,1)S(1)} %slice.138), channel_id=1, source_target_pairs={{0,1},{1,0},{2,3},{3,2},{4,5},{5,4},{6,7},{7,6},{8,9},{9,8},{10,11... | collective-permute-start | bytes 688136 | tf_op jit(solution)/shard_map/ppermute | solution.py:239
  48.3 11.7 %collective-permute-start.6 = (bf16[2,1,32,1792]{3,2,1,0:T(8,128)(2,1)S(1)}, bf16[2,1,32,1792]{3,2,1,0:T(8,128)(2,1)S(1)}, u32[]{:S(2)}, u32[]{:S(2)}) collective-permute-start(bf16[2,1,32,1792]{3,2,1,0:T(8,128)(2,1)S(1)} %slice.141), channel_id=1, source_target_pairs={{0,2},{1,3},{2,0},{3,1},{4,6},{5,7},{6,4},{7,5},{8,10},{9,11},{10,... | collective-permute-start | bytes 688136 | tf_op jit(solution)/shard_map/ppermute | solution.py:239
  50.3 9.7 %collective-permute-start.8 = (bf16[2,1,32,1792]{3,2,1,0:T(8,128)(2,1)S(1)}, bf16[2,1,32,1792]{3,2,1,0:T(8,128)(2,1)S(1)}, u32[]{:S(2)}, u32[]{:S(2)}) collective-permute-start(bf16[2,1,32,1792]{3,2,1,0:T(8,128)(2,1)S(1)} %slice.140), channel_id=1, source_target_pairs={{0,1},{1,0},{2,3},{3,2},{4,5},{5,4},{6,7},{7,6},{8,9},{9,8},{10,11... | collective-permute-start | bytes 688136 | tf_op jit(solution)/shard_map/ppermute | solution.py:239
  55.5 13.5 %collective-permute-start.17 = (bf16[2,2,32,1792]{3,2,1,0:T(8,128)(2,1)S(1)}, bf16[2,2,32,1792]{3,2,1,0:T(8,128)(2,1)S(1)}, u32[]{:S(2)}, u32[]{:S(2)}) collective-permute-start(bf16[2,2,32,1792]{3,2,1,0:T(8,128)(2,1)S(1)} %maximum_maximum_fusion.refs_0_), channel_id=1, source_target_pairs={{0,1},{1,0},{2,3},{3,2},{4,5},{5,4},{6,7},{7,6},{8,9},{9,8},{10,11... | collective-permute-start | bytes 1376264 | tf_op jit(solution)/shard_map/ppermute | solution.py:239
  55.6 14.2 %collective-permute-start.18 = (bf16[2,2,32,1792]{3,2,1,0:T(8,128)(2,1)S(1)}, bf16[2,2,32,1792]{3,2,1,0:T(8,128)(2,1)S(1)}, u32[]{:S(2)}, u32[]{:S(2)}) collective-permute-start(bf16[2,2,32,1792]{3,2,1,0:T(8,128)(2,1)S(1)} %maximum_maximum_fusion.refs_0_), channel_id=1, source_target_pairs={{0,2},{1,3},{2,0},{3,1},{4,6},{5,7},{6,4},{7,5},{8,10},{9,11},{10,... | collective-permute-start | bytes 1376264 | tf_op jit(solution)/shard_map/ppermute | solution.py:239
  60.4 18.5 %collective-permute-start.13 = (bf16[2,2,32,1792]{3,2,1,0:T(8,128)(2,1)S(1)}, bf16[2,2,32,1792]{3,2,1,0:T(8,128)(2,1)S(1)}, u32[]{:S(2)}, u32[]{:S(2)}) collective-permute-start(bf16[2,2,32,1792]{3,2,1,0:T(8,128)(2,1)S(1)} %maximum_maximum_fusion.1.refs_0_), channel_id=1, source_target_pairs={{0,1},{1,0},{2,3},{3,2},{4,5},{5,4},{6,7},{7,6},{8,9},{9,8},{10,11... | collective-permute-start | bytes 1376264 | tf_op jit(solution)/shard_map/ppermute | solution.py:239
  60.5 19.1 %collective-permute-start.14 = (bf16[2,2,32,1792]{3,2,1,0:T(8,128)(2,1)S(1)}, bf16[2,2,32,1792]{3,2,1,0:T(8,128)(2,1)S(1)}, u32[]{:S(2)}, u32[]{:S(2)}) collective-permute-start(bf16[2,2,32,1792]{3,2,1,0:T(8,128)(2,1)S(1)} %maximum_maximum_fusion.1.refs_0_), channel_id=1, source_target_pairs={{0,2},{1,3},{2,0},{3,1},{4,6},{5,7},{6,4},{7,5},{8,10},{9,11},{10,... | collective-permute-start | bytes 1376264 | tf_op jit(solution)/shard_map/ppermute | solution.py:239
  69.1 15.5 %collective-permute-start.19 = (bf16[1,2,32,1792]{3,2,1,0:T(8,128)(2,1)S(1)}, bf16[1,2,32,1792]{3,2,1,0:T(8,128)(2,1)S(1)}, u32[]{:S(2)}, u32[]{:S(2)}) collective-permute-start(bf16[1,2,32,1792]{3,2,1,0:T(8,128)(2,1)S(1)} %slice.114), channel_id=1, source_target_pairs={{0,2},{1,3},{2,0},{3,1},{4,6},{5,7},{6,4},{7,5},{8,10},{9,11},{10,... | collective-permute-start | bytes 688136 | tf_op jit(solution)/shard_map/ppermute | solution.py:239
  69.8 14.7 %collective-permute-start.20 = (bf16[1,2,32,1792]{3,2,1,0:T(8,128)(2,1)S(1)}, bf16[1,2,32,1792]{3,2,1,0:T(8,128)(2,1)S(1)}, u32[]{:S(2)}, u32[]{:S(2)}) collective-permute-start(bf16[1,2,32,1792]{3,2,1,0:T(8,128)(2,1)S(1)} %slice.115), channel_id=1, source_target_pairs={{0,1},{1,0},{2,3},{3,2},{4,5},{5,4},{6,7},{7,6},{8,9},{9,8},{10,11... | collective-permute-start | bytes 688136 | tf_op jit(solution)/shard_map/ppermute | solution.py:239
  78.9 9.8 %collective-permute-start.15 = (bf16[1,2,32,1792]{3,2,1,0:T(8,128)(2,1)S(1)}, bf16[1,2,32,1792]{3,2,1,0:T(8,128)(2,1)S(1)}, u32[]{:S(2)}, u32[]{:S(2)}) collective-permute-start(bf16[1,2,32,1792]{3,2,1,0:T(8,128)(2,1)S(1)} %slice.112), channel_id=1, source_target_pairs={{0,2},{1,3},{2,0},{3,1},{4,6},{5,7},{6,4},{7,5},{8,10},{9,11},{10,... | collective-permute-start | bytes 688136 | tf_op jit(solution)/shard_map/ppermute | solution.py:239
  79.6 9.1 %collective-permute-start.16 = (bf16[1,2,32,1792]{3,2,1,0:T(8,128)(2,1)S(1)}, bf16[1,2,32,1792]{3,2,1,0:T(8,128)(2,1)S(1)}, u32[]{:S(2)}, u32[]{:S(2)}) collective-permute-start(bf16[1,2,32,1792]{3,2,1,0:T(8,128)(2,1)S(1)} %slice.113), channel_id=1, source_target_pairs={{0,1},{1,0},{2,3},{3,2},{4,5},{5,4},{6,7},{7,6},{8,9},{9,8},{10,11... | collective-permute-start | bytes 688136 | tf_op jit(solution)/shard_map/ppermute | solution.py:239
  90.8 2.0 %collective-permute-start.21 = (bf16[512,512]{1,0:T(8,128)(2,1)S(1)}, bf16[512,512]{1,0:T(8,128)(2,1)S(1)}, u32[]{:S(2)}, u32[]{:S(2)}) collective-permute-start(bf16[512,512]{1,0:T(8,128)(2,1)S(1)} %get-tuple-element.50), channel_id=1, source_target_pairs={{0,4},{1,5},{2,6},{3,7},{4,0},{5,1},{6,2},{7,3},{8,12},{9,13},{10,... | collective-permute-start | bytes 1572872 | tf_op jit(solution)/shard_map/ppermute | solution.py:239
  93.0 8.2 %collective-permute-start.22 = (bf16[128,512]{1,0:T(8,128)(2,1)S(1)}, bf16[128,512]{1,0:T(8,128)(2,1)S(1)}, u32[]{:S(2)}, u32[]{:S(2)}) collective-permute-start(bf16[128,512]{1,0:T(8,128)(2,1)S(1)} %get-tuple-element.69), channel_id=1, source_target_pairs={{0,1},{1,0},{2,3},{3,2},{4,5},{5,4},{6,7},{7,6},{8,9},{9,8},{10,11... | collective-permute-start | bytes 393224 | tf_op jit(solution)/shard_map/ppermute | solution.py:239
  93.4 8.1 %collective-permute-start.23 = (bf16[128,512]{1,0:T(8,128)(2,1)S(1)}, bf16[128,512]{1,0:T(8,128)(2,1)S(1)}, u32[]{:S(2)}, u32[]{:S(2)}) collective-permute-start(bf16[128,512]{1,0:T(8,128)(2,1)S(1)} %get-tuple-element.68), channel_id=1, source_target_pairs={{0,2},{1,3},{2,0},{3,1},{4,6},{5,7},{6,4},{7,5},{8,10},{9,11},{10,... | collective-permute-start | bytes 393224 | tf_op jit(solution)/shard_map/ppermute | solution.py:239
  94.8 6.7 %collective-permute-start.24 = (bf16[128,512]{1,0:T(8,128)(2,1)S(1)}, bf16[128,512]{1,0:T(8,128)(2,1)S(1)}, u32[]{:S(2)}, u32[]{:S(2)}) collective-permute-start(bf16[128,512]{1,0:T(8,128)(2,1)S(1)} %get-tuple-element.67), channel_id=1, source_target_pairs={{0,3},{1,2},{2,1},{3,0},{4,7},{5,6},{6,5},{7,4},{8,11},{9,10},{10,... | collective-permute-start | bytes 393224 | tf_op jit(solution)/shard_map/ppermute | solution.py:239
  102.3 9.9 %collective-permute-start.27 = (bf16[128,512]{1,0:T(8,128)(2,1)S(1)}, bf16[128,512]{1,0:T(8,128)(2,1)S(1)}, u32[]{:S(2)}, u32[]{:S(2)}) collective-permute-start(bf16[128,512]{1,0:T(8,128)(2,1)S(1)} %get-tuple-element.56), channel_id=1, source_target_pairs={{0,24},{1,25},{2,26},{3,27},{4,28},{5,29},{6,30},{7,31},{8,16},{9,... | collective-permute-start | bytes 393224 | tf_op jit(solution)/shard_map/ppermute | solution.py:239
  104.1 11.5 %collective-permute-start.26 = (bf16[128,512]{1,0:T(8,128)(2,1)S(1)}, bf16[128,512]{1,0:T(8,128)(2,1)S(1)}, u32[]{:S(2)}, u32[]{:S(2)}) collective-permute-start(bf16[128,512]{1,0:T(8,128)(2,1)S(1)} %get-tuple-element.55), channel_id=1, source_target_pairs={{0,16},{1,17},{2,18},{3,19},{4,20},{5,21},{6,22},{7,23},{8,24},{9,... | collective-permute-start | bytes 393224 | tf_op jit(solution)/shard_map/ppermute | solution.py:239
  104.5 11.2 %collective-permute-start.25 = (bf16[128,512]{1,0:T(8,128)(2,1)S(1)}, bf16[128,512]{1,0:T(8,128)(2,1)S(1)}, u32[]{:S(2)}, u32[]{:S(2)}) collective-permute-start(bf16[128,512]{1,0:T(8,128)(2,1)S(1)} %get-tuple-element.54), channel_id=1, source_target_pairs={{0,8},{1,9},{2,10},{3,11},{4,12},{5,13},{6,14},{7,15},{8,0},{9,1},... | collective-permute-start | bytes 393224 | tf_op jit(solution)/shard_map/ppermute | solution.py:239

commit v7 on v6

--- a/solution.py
+++ b/solution.py
@@ -17,33 +17,47 @@
     return pltpu.with_memory_space_constraint(x, pltpu.VMEM)
 
 
-def dequant_kernel(codes_ref, scales_ref, w_ref, done_ref):
+def dequant_kernel(codes_ref, scales_ref, w_ref, done_ref, narrow_ref, wide_ref, sem, scales_sem):
     done_ref[0] = 0
-    row = pl.ds(pl.program_id(0), 1)
-    for g in range(2):
-        w_ref[g] = (codes_ref[g].astype(jnp.float32) * scales_ref[g, row, :]).astype(jnp.bfloat16)
+    _, owned, group = w_ref.shape
+    tile = 16
+
+    def copy(b):
+        at = pl.ds(b * BLOCK, BLOCK)
+        return pltpu.make_async_copy(codes_ref.at[:, at, :], w_ref.at[:, at, :], sem.at[b])
+
+    scales = pltpu.make_async_copy(scales_ref, narrow_ref, scales_sem)
+    scales.start()
+    for b in range(owned // BLOCK):
+        copy(b).start()
+    scales.wait()
+    wide_ref[...] = narrow_ref[...].astype(jnp.float32)
+    for b in range(owned // BLOCK):
+        copy(b).wait()
+        for g in range(2):
+            scale = jnp.broadcast_to(wide_ref[g, b : b + 1, :], (tile, group)).astype(jnp.bfloat16)
+            for t in range(b * BLOCK, (b + 1) * BLOCK, tile):
+                w_ref[g, t : t + tile] = w_ref[g, t : t + tile] * scale
 
 
 def dequant(codes, scales):
-    _, owned, group = codes.shape
-    blocks = owned // BLOCK
+    codes, scales = (pltpu.with_memory_space_constraint(x, pltpu.HBM) for x in (codes, scales))
     return pl.pallas_call(
         dequant_kernel,
-        grid=(blocks,),
-        in_specs=[
-            pl.BlockSpec((2, BLOCK, group), lambda i: (0, i, 0)),
-            pl.BlockSpec((2, blocks, group), lambda i: (0, 0, 0)),
-        ],
-        out_specs=[
-            pl.BlockSpec((2, BLOCK, group), lambda i: (0, i, 0)),
-            pl.BlockSpec(memory_space=pltpu.SMEM),
-        ],
+        in_specs=[pl.BlockSpec(memory_space=pl.ANY)] * 2,
+        out_specs=[pl.BlockSpec(memory_space=pltpu.VMEM), pl.BlockSpec(memory_space=pltpu.SMEM)],
         out_shape=[
             pltpu.VMEM(codes.shape, jnp.bfloat16),
             jax.ShapeDtypeStruct((1,), jnp.int32),
         ],
-        compiler_params=pltpu.CompilerParams(vmem_limit_bytes=16 * 1024 * 1024),
-    )(pltpu.with_memory_space_constraint(codes, pltpu.HBM), scales.astype(jnp.float32))
+        scratch_shapes=[
+            pltpu.VMEM(scales.shape, jnp.bfloat16),
+            pltpu.VMEM(scales.shape, jnp.float32),
+            pltpu.SemaphoreType.DMA((codes.shape[1] // BLOCK,)),
+            pltpu.SemaphoreType.DMA,
+        ],
+        compiler_params=pltpu.CompilerParams(vmem_limit_bytes=12 * 1024 * 1024),
+    )(codes, scales)
 
 
 def pairs(move, places, ratio):
@@ -324,15 +338,15 @@
         got = permute(term[e], lambda p, h, q: (p, h ^ e, q))
         summed = summed + got.astype(jnp.float32)
     summed = summed.astype(jnp.bfloat16).reshape(places, rows, feats)
-    arrived = [summed[0]] + [
-        permute(summed[k], lambda p, h, q: (p, h, q ^ k)) for k in range(1, places)
-    ]
+    far_first = [*range(places // 2, places), *range(1, places // 2)]
+    arrived = {k: permute(summed[k], lambda p, h, q: (p, h, q ^ k)) for k in range(1, places)}
+    arrived[0] = summed[0]
     flat = joined([mine] + others).reshape(places * rows, owned)
     scale = 1.0 / math.sqrt(rows * places)
     grads, done = weight_grad(0, flat, d_all, scale, summed[0, :16])
-    arrived = shuffle(dict(enumerate(arrived)), mask, [done])
+    arrived = shuffle(arrived, mask, [done])
     summands = [arrived[0]] + [
-        permute(arrived[j], lambda p, h, q: (p ^ j, h, q)) for j in range(1, places)
+        permute(arrived[j], lambda p, h, q: (p ^ j, h, q)) for j in reversed(far_first)
     ]
     grads, done = weight_grad(1, flat, d_all, scale, arrived[0][:16], grads)
     summands[0] = after(summands[0], done)

time: 117 us -> 114 us (0.974)
  Pallas kernels: 26.3 us -> 23.4 us
  starting transfers between devices: 35.9 us -> 38.7 us
  waiting for transfers between devices: 49.3 us -> 48.1 us
    pallas_call x1, Pallas kernels: 6.67 us -> 3.82 us  [dequant(): pl.pallas_call(dequant_kernel, in_specs=[pl.BlockSpec(memory_space=pl.ANY...]
    ppermute x28, starting transfers between devices: 35.9 us -> 38.7 us  [permute(): return lax.ppermute(x, AXES, pairs(move, places, ratio))]
    ppermute x28, waiting for transfers between devices: 49.3 us -> 48.1 us  [permute(): return lax.ppermute(x, AXES, pairs(move, places, ratio))]
  transfers between devices with their start and end apart: 28 -> 28, of which waited for: 15 -> 16; matrix products, arithmetic and copies ran while one was open for 3% -> 2% of each run, Pallas kernels for 18% -> 16%
where the time goes in v7:
time: 114 us
  waiting for transfers between devices  48.1 us (42%)
  starting transfers between devices  38.7 us (34%)
  Pallas kernels  23.4 us (21%)
  other arithmetic  2.9 us (3%)
    ppermute x28, waiting for transfers between devices, permute(): return lax.ppermute(x, AXES, pairs(move, places, ratio))  48.1 us
    ppermute x28, starting transfers between devices, permute(): return lax.ppermute(x, AXES, pairs(move, places, ratio))  38.7 us
    pallas_call x2, Pallas kernels, weight_grad(): pl.pallas_call(functools.partial(weight_grad_kernel, scale), grid=(owned...  9.32 us
    pallas_call x2, Pallas kernels, input_grad(): pl.pallas_call(functools.partial(input_grad_kernel, spots, ratio + 1, fir...  4.21 us
    pallas_call x1, Pallas kernels, dequant(): pl.pallas_call(dequant_kernel, in_specs=[pl.BlockSpec(memory_space=pl.ANY...  3.82 us
    pallas_call x2, Pallas kernels, other_halves(): pl.pallas_call(functools.partial(other_halves_kernel, len(others), first,...  2.35 us
  transfers between devices with their start and end apart: 28, of which 16 were waited for; matrix products, arithmetic and copies ran while one was open for 2% of the time, Pallas kernels for 16%

profile of v7, /device:TPU:0, one launch (start us, length us, event | category | flops | bytes accessed | tf_op | source)
XLA Modules:
  0.0 114.2 jit_solution(8077466300644058618)
XLA Ops:
  0.6 3.1 %collective-permute-start = (bf16[128,512]{1,0:T(8,128)(2,1)}, bf16[128,512]{1,0:T(8,128)(2,1)S(1)}, u32[]{:S(2)}, u32[]{:S(2)}) collective-permute-start(bf16[128,512]{1,0:T(8,128)(2,1)} %param.4), channel_id=1, source_target_pairs={{0,8},{1,0},{2,24},{3,16},{4,12},{5,4},{6,28},{7,20},{8,9},{9,1},{... | collective-permute-start | bytes 393224 | tf_op jit(solution)/shard_map/ppermute | solution.py:253
  3.7 2.4 %collective-permute-start.1 = (bf16[128,512]{1,0:T(8,128)(2,1)}, bf16[128,512]{1,0:T(8,128)(2,1)S(1)}, u32[]{:S(2)}, u32[]{:S(2)}) collective-permute-start(bf16[128,512]{1,0:T(8,128)(2,1)} %param.4), channel_id=1, source_target_pairs={{0,16},{1,24},{2,0},{3,8},{4,20},{5,28},{6,4},{7,12},{8,17},{9,25}... | collective-permute-start | bytes 393224 | tf_op jit(solution)/shard_map/ppermute | solution.py:253
  6.1 2.5 %collective-permute-start.2 = (bf16[128,512]{1,0:T(8,128)(2,1)}, bf16[128,512]{1,0:T(8,128)(2,1)S(1)}, u32[]{:S(2)}, u32[]{:S(2)}) collective-permute-start(bf16[128,512]{1,0:T(8,128)(2,1)} %param.4), channel_id=1, source_target_pairs={{0,24},{1,16},{2,8},{3,0},{4,28},{5,20},{6,12},{7,4},{8,25},{9,17}... | collective-permute-start | bytes 393224 | tf_op jit(solution)/shard_map/ppermute | solution.py:253
  8.6 1.6 %collective-permute-start.3 = (bf16[128,512]{1,0:T(8,128)(2,1)}, bf16[128,512]{1,0:T(8,128)(2,1)S(1)}, u32[]{:S(2)}, u32[]{:S(2)}) collective-permute-start(bf16[128,512]{1,0:T(8,128)(2,1)} %param.4), channel_id=1, source_target_pairs={{0,0},{1,8},{2,16},{3,24},{4,4},{5,12},{6,20},{7,28},{8,1},{9,9},{... | collective-permute-start | bytes 393224 | tf_op jit(solution)/shard_map/ppermute | solution.py:253
  10.2 3.8 %shard_map.67 = (bf16[2,1024,1792]{2,1,0:T(8,128)(2,1)S(1)}, s32[1]{0:T(128)}) custom-call(bf16[2,1024,1792]{2,1,0:T(8,128)(2,1)} %codes_ref.1, bf16[2,8,1792]{2,1,0:T(8,128)(2,1)} %scales_ref.1), custom_call_target="tpu_custom_call" | custom-call | tf_op jit(solution)/shard_map/pallas_call | solution.py:45
  14.9 2.1 %shard_map.69.refs_2_ = f32[2,4,128,1792]{3,2,1,0:T(8,128)S(1)} custom-call(s32[1]{0:T(128)} %bitcast.half_ref.index_ref, bf16[4,128,512]{2,1,0:T(8,128)(2,1)S(1)} %shard_map.68.x_ref.refs_0_, bf16[2,1024,1792]{2,1,0:T(8,128)(2,1)S(1)} %get-tuple-element.35.w_ref.refs_1_.refs_5_), custom_call_target="tpu_custom_call" | custom-call | tf_op jit(solution)/shard_map/pallas_call | solution.py:120
  18.2 8.7 %collective-permute-start.9 = (bf16[2,2,32,1792]{3,2,1,0:T(8,128)(2,1)S(1)}, bf16[2,2,32,1792]{3,2,1,0:T(8,128)(2,1)S(1)}, u32[]{:S(2)}, u32[]{:S(2)}) collective-permute-start(bf16[2,2,32,1792]{3,2,1,0:T(8,128)(2,1)S(1)} %get-tuple-element.41), channel_id=1, source_target_pairs={{0,1},{1,0},{2,3},{3,2},{4,5},{5,4},{6,7},{7,6},{8,9},{9,8},{10,11... | collective-permute-start | bytes 1376264 | tf_op jit(solution)/shard_map/ppermute | solution.py:253
  28.1 2.1 %collective-permute-start.7 = (bf16[2,2,32,1792]{3,2,1,0:T(8,128)(2,1)S(1)}, bf16[2,2,32,1792]{3,2,1,0:T(8,128)(2,1)S(1)}, u32[]{:S(2)}, u32[]{:S(2)}) collective-permute-start(bf16[2,2,32,1792]{3,2,1,0:T(8,128)(2,1)S(1)} %get-tuple-element.39), channel_id=1, source_target_pairs={{0,2},{1,3},{2,0},{3,1},{4,6},{5,7},{6,4},{7,5},{8,10},{9,11},{10,... | collective-permute-start | bytes 1376264 | tf_op jit(solution)/shard_map/ppermute | solution.py:253
  30.3 8.0 %collective-permute-done.9 = bf16[2,2,32,1792]{3,2,1,0:T(8,128)(2,1)S(1)} collective-permute-done((bf16[2,2,32,1792]{3,2,1,0:T(8,128)(2,1)S(1)}, bf16[2,2,32,1792]{3,2,1,0:T(8,128)(2,1)S(1)}, u32[]{:S(2)}, u32[]{:S(2)}) %collective-permute-start.9) | collective-permute-done | bytes 458784 | tf_op jit(solution)/shard_map/ppermute | solution.py:253
  38.4 1.7 %collective-permute-start.10 = (bf16[2,1,32,1792]{3,2,1,0:T(8,128)(2,1)S(1)}, bf16[2,1,32,1792]{3,2,1,0:T(8,128)(2,1)S(1)}, u32[]{:S(2)}, u32[]{:S(2)}) collective-permute-start(bf16[2,1,32,1792]{3,2,1,0:T(8,128)(2,1)S(1)} %slice.139), channel_id=1, source_target_pairs={{0,2},{1,3},{2,0},{3,1},{4,6},{5,7},{6,4},{7,5},{8,10},{9,11},{10,... | collective-permute-start | bytes 688136 | tf_op jit(solution)/shard_map/ppermute | solution.py:253
  40.7 7.5 %collective-permute-done.5 = bf16[2,2,32,1792]{3,2,1,0:T(8,128)(2,1)S(1)} collective-permute-done((bf16[2,2,32,1792]{3,2,1,0:T(8,128)(2,1)S(1)}, bf16[2,2,32,1792]{3,2,1,0:T(8,128)(2,1)S(1)}, u32[]{:S(2)}, u32[]{:S(2)}) %collective-permute-start.5) | collective-permute-done | bytes 458784 | tf_op jit(solution)/shard_map/ppermute | solution.py:253
  48.3 1.7 %collective-permute-start.6 = (bf16[2,1,32,1792]{3,2,1,0:T(8,128)(2,1)S(1)}, bf16[2,1,32,1792]{3,2,1,0:T(8,128)(2,1)S(1)}, u32[]{:S(2)}, u32[]{:S(2)}) collective-permute-start(bf16[2,1,32,1792]{3,2,1,0:T(8,128)(2,1)S(1)} %slice.141), channel_id=1, source_target_pairs={{0,2},{1,3},{2,0},{3,1},{4,6},{5,7},{6,4},{7,5},{8,10},{9,11},{10,... | collective-permute-start | bytes 688136 | tf_op jit(solution)/shard_map/ppermute | solution.py:253
  50.5 4.5 %collective-permute-done.10 = bf16[2,1,32,1792]{3,2,1,0:T(8,128)(2,1)S(1)} collective-permute-done((bf16[2,1,32,1792]{3,2,1,0:T(8,128)(2,1)S(1)}, bf16[2,1,32,1792]{3,2,1,0:T(8,128)(2,1)S(1)}, u32[]{:S(2)}, u32[]{:S(2)}) %collective-permute-start.10) | collective-permute-done | bytes 229408 | tf_op jit(solution)/shard_map/ppermute | solution.py:253
  55.6 1.7 %collective-permute-start.18 = (bf16[2,2,32,1792]{3,2,1,0:T(8,128)(2,1)S(1)}, bf16[2,2,32,1792]{3,2,1,0:T(8,128)(2,1)S(1)}, u32[]{:S(2)}, u32[]{:S(2)}) collective-permute-start(bf16[2,2,32,1792]{3,2,1,0:T(8,128)(2,1)S(1)} %maximum_maximum_fusion.refs_0_), channel_id=1, source_target_pairs={{0,2},{1,3},{2,0},{3,1},{4,6},{5,7},{6,4},{7,5},{8,10},{9,11},{10,... | collective-permute-start | bytes 1376264 | tf_op jit(solution)/shard_map/ppermute | solution.py:253
  57.3 2.7 %collective-permute-done.6 = bf16[2,1,32,1792]{3,2,1,0:T(8,128)(2,1)S(1)} collective-permute-done((bf16[2,1,32,1792]{3,2,1,0:T(8,128)(2,1)S(1)}, bf16[2,1,32,1792]{3,2,1,0:T(8,128)(2,1)S(1)}, u32[]{:S(2)}, u32[]{:S(2)}) %collective-permute-start.6) | collective-permute-done | bytes 229408 | tf_op jit(solution)/shard_map/ppermute | solution.py:253
  60.5 1.7 %collective-permute-start.14 = (bf16[2,2,32,1792]{3,2,1,0:T(8,128)(2,1)S(1)}, bf16[2,2,32,1792]{3,2,1,0:T(8,128)(2,1)S(1)}, u32[]{:S(2)}, u32[]{:S(2)}) collective-permute-start(bf16[2,2,32,1792]{3,2,1,0:T(8,128)(2,1)S(1)} %maximum_maximum_fusion.1.refs_0_), channel_id=1, source_target_pairs={{0,2},{1,3},{2,0},{3,1},{4,6},{5,7},{6,4},{7,5},{8,10},{9,11},{10,... | collective-permute-start | bytes 1376264 | tf_op jit(solution)/shard_map/ppermute | solution.py:253
  62.2 6.9 %collective-permute-done.17.refs_1_ = bf16[2,2,32,1792]{3,2,1,0:T(8,128)(2,1)S(1)} collective-permute-done((bf16[2,2,32,1792]{3,2,1,0:T(8,128)(2,1)S(1)}, bf16[2,2,32,1792]{3,2,1,0:T(8,128)(2,1)S(1)}, u32[]{:S(2)}, u32[]{:S(2)}) %collective-permute-start.17) | collective-permute-done | bytes 458784 | tf_op jit(solution)/shard_map/ppermute | solution.py:253
  69.8 1.4 %collective-permute-start.20 = (bf16[1,2,32,1792]{3,2,1,0:T(8,128)(2,1)S(1)}, bf16[1,2,32,1792]{3,2,1,0:T(8,128)(2,1)S(1)}, u32[]{:S(2)}, u32[]{:S(2)}) collective-permute-start(bf16[1,2,32,1792]{3,2,1,0:T(8,128)(2,1)S(1)} %slice.115), channel_id=1, source_target_pairs={{0,1},{1,0},{2,3},{3,2},{4,5},{5,4},{6,7},{7,6},{8,9},{9,8},{10,11... | collective-permute-start | bytes 688136 | tf_op jit(solution)/shard_map/ppermute | solution.py:253
  71.1 7.7 %collective-permute-done.13.refs_1_ = bf16[2,2,32,1792]{3,2,1,0:T(8,128)(2,1)S(1)} collective-permute-done((bf16[2,2,32,1792]{3,2,1,0:T(8,128)(2,1)S(1)}, bf16[2,2,32,1792]{3,2,1,0:T(8,128)(2,1)S(1)}, u32[]{:S(2)}, u32[]{:S(2)}) %collective-permute-start.13) | collective-permute-done | bytes 458784 | tf_op jit(solution)/shard_map/ppermute | solution.py:253
  79.6 1.4 %collective-permute-start.16 = (bf16[1,2,32,1792]{3,2,1,0:T(8,128)(2,1)S(1)}, bf16[1,2,32,1792]{3,2,1,0:T(8,128)(2,1)S(1)}, u32[]{:S(2)}, u32[]{:S(2)}) collective-permute-start(bf16[1,2,32,1792]{3,2,1,0:T(8,128)(2,1)S(1)} %slice.113), channel_id=1, source_target_pairs={{0,1},{1,0},{2,3},{3,2},{4,5},{5,4},{6,7},{7,6},{8,9},{9,8},{10,11... | collective-permute-start | bytes 688136 | tf_op jit(solution)/shard_map/ppermute | solution.py:253
  81.0 3.5 %collective-permute-done.19.refs_3_ = bf16[1,2,32,1792]{3,2,1,0:T(8,128)(2,1)S(1)} collective-permute-done((bf16[1,2,32,1792]{3,2,1,0:T(8,128)(2,1)S(1)}, bf16[1,2,32,1792]{3,2,1,0:T(8,128)(2,1)S(1)}, u32[]{:S(2)}, u32[]{:S(2)}) %collective-permute-start.19) | collective-permute-done | bytes 229408 | tf_op jit(solution)/shard_map/ppermute | solution.py:253
  84.5 2.1 %shard_map.72 = (bf16[2,512,1792]{2,1,0:T(8,128)(2,1)S(1)}, bf16[512,512]{1,0:T(8,128)(2,1)S(1)}, bf16[512,512]{1,0:T(8,128)(2,1)S(1)}) custom-call(s32[1]{0:T(128)} %bitcast.half_ref.index_ref, bf16[2,2,32,1792]{3,2,1,0:T(8,128)(2,1)S(1)} %maximum_maximum_fusion.refs_0_, bf16[2,2,32,1792]{3,2,1,0:T(8,128)(2,1)S(1)} %collective-permute-done.17.refs_1_, ...), custom_call_target="tpu_custom_call" | custom-call | tf_op jit(solution)/shard_map/pallas_call | solution.py:189
  86.6 2.1 %collective-permute-done.15.refs_3_ = bf16[1,2,32,1792]{3,2,1,0:T(8,128)(2,1)S(1)} collective-permute-done((bf16[1,2,32,1792]{3,2,1,0:T(8,128)(2,1)S(1)}, bf16[1,2,32,1792]{3,2,1,0:T(8,128)(2,1)S(1)}, u32[]{:S(2)}, u32[]{:S(2)}) %collective-permute-start.15) | collective-permute-done | bytes 229408 | tf_op jit(solution)/shard_map/ppermute | solution.py:253
  88.7 2.1 %shard_map.73 = (bf16[2,512,1792]{2,1,0:T(8,128)(2,1)S(1)}, bf16[512,512]{1,0:T(8,128)(2,1)S(1)}, bf16[512,512]{1,0:T(8,128)(2,1)S(1)}) custom-call(s32[1]{0:T(128)} %bitcast.half_ref.index_ref, bf16[2,2,32,1792]{3,2,1,0:T(8,128)(2,1)S(1)} %maximum_maximum_fusion.1.refs_0_, ...), custom_call_target="tpu_custom_call", output_to_operand_aliasing={{0}: (9, {}), {1}: (10, {}), {2}: (11, {})} | custom-call | tf_op jit(solution)/shard_map/pallas_call | solution.py:189
  91.0 1.8 %collective-permute-done.21 = bf16[512,512]{1,0:T(8,128)(2,1)S(1)} collective-permute-done((bf16[512,512]{1,0:T(8,128)(2,1)S(1)}, bf16[512,512]{1,0:T(8,128)(2,1)S(1)}, u32[]{:S(2)}, u32[]{:S(2)}) %collective-permute-start.21) | collective-permute-done | bytes 524320 | tf_op jit(solution)/shard_map/ppermute | solution.py:253
  93.4 1.3 %collective-permute-start.23 = (bf16[128,512]{1,0:T(8,128)(2,1)S(1)}, bf16[128,512]{1,0:T(8,128)(2,1)S(1)}, u32[]{:S(2)}, u32[]{:S(2)}) collective-permute-start(bf16[128,512]{1,0:T(8,128)(2,1)S(1)} %get-tuple-element.69), channel_id=1, source_target_pairs={{0,2},{1,3},{2,0},{3,1},{4,6},{5,7},{6,4},{7,5},{8,10},{9,11},{10,... | collective-permute-start | bytes 393224 | tf_op jit(solution)/shard_map/ppermute | solution.py:253
  94.8 1.8 %collective-permute-start.24 = (bf16[128,512]{1,0:T(8,128)(2,1)S(1)}, bf16[128,512]{1,0:T(8,128)(2,1)S(1)}, u32[]{:S(2)}, u32[]{:S(2)}) collective-permute-start(bf16[128,512]{1,0:T(8,128)(2,1)S(1)} %get-tuple-element.68), channel_id=1, source_target_pairs={{0,3},{1,2},{2,1},{3,0},{4,7},{5,6},{6,5},{7,4},{8,11},{9,10},{10,... | collective-permute-start | bytes 393224 | tf_op jit(solution)/shard_map/ppermute | solution.py:253
  96.6 4.7 %shard_map.75 = (f32[2,1024,1792]{2,1,0:T(8,128)}, s32[1]{0:T(128)}) custom-call(bf16[512,1024]{1,0:T(8,128)(2,1)S(1)} %bitcast.102, bf16[2,512,1792]{2,1,0:T(8,128)(2,1)S(1)} %get-tuple-element.51.d_ref, bf16[16,512]{1,0:T(8,128)(2,1)S(1)} %slice_bitcast_fusion.8.refs_0_), custom_call_target="tpu_custom_call" | custom-call | tf_op jit(solution)/shard_map/pallas_call | solution.py:217
  102.8 1.8 %collective-permute-start.26 = (bf16[128,512]{1,0:T(8,128)(2,1)S(1)}, bf16[128,512]{1,0:T(8,128)(2,1)S(1)}, u32[]{:S(2)}, u32[]{:S(2)}) collective-permute-start(bf16[128,512]{1,0:T(8,128)(2,1)S(1)} %get-tuple-element.55), channel_id=1, source_target_pairs={{0,24},{1,25},{2,26},{3,27},{4,28},{5,29},{6,30},{7,31},{8,16},{9,... | collective-permute-start | bytes 393224 | tf_op jit(solution)/shard_map/ppermute | solution.py:253
  104.6 1.3 %collective-permute-start.25 = (bf16[128,512]{1,0:T(8,128)(2,1)S(1)}, bf16[128,512]{1,0:T(8,128)(2,1)S(1)}, u32[]{:S(2)}, u32[]{:S(2)}) collective-permute-start(bf16[128,512]{1,0:T(8,128)(2,1)S(1)} %get-tuple-element.54), channel_id=1, source_target_pairs={{0,8},{1,9},{2,10},{3,11},{4,12},{5,13},{6,14},{7,15},{8,0},{9,1},... | collective-permute-start | bytes 393224 | tf_op jit(solution)/shard_map/ppermute | solution.py:253
  106.6 4.7 %shard_map.77 = (f32[2,1024,1792]{2,1,0:T(8,128)}, s32[1]{0:T(128)}) custom-call(bf16[512,1024]{1,0:T(8,128)(2,1)S(1)} %bitcast.103, bf16[2,512,1792]{2,1,0:T(8,128)(2,1)S(1)} %get-tuple-element.51.d_ref, bf16[16,512]{1,0:T(8,128)(2,1)S(1)} %slice.103.refs_0_, f32[2,1024,1792]{2,1,0:T(8,128)} %get-tuple-element.57.refs_1_), custom_call_target="tpu_custom_call", output_to_operand_aliasing={{0}: (3, {})} | custom-call | tf_op jit(solution)/shard_map/pallas_call | solution.py:217
  111.3 1.8 %collective-permute-done.27 = bf16[128,512]{1,0:T(8,128)(2,1)S(1)} collective-permute-done((bf16[128,512]{1,0:T(8,128)(2,1)S(1)}, bf16[128,512]{1,0:T(8,128)(2,1)S(1)}, u32[]{:S(2)}, u32[]{:S(2)}) %collective-permute-start.27) | collective-permute-done | bytes 131104 | tf_op jit(solution)/shard_map/ppermute | solution.py:253
  (62 shorter events, 11.5 us)
Async XLA Ops:
  0.6 13.4 %collective-permute-start = (bf16[128,512]{1,0:T(8,128)(2,1)}, bf16[128,512]{1,0:T(8,128)(2,1)S(1)}, u32[]{:S(2)}, u32[]{:S(2)}) collective-permute-start(bf16[128,512]{1,0:T(8,128)(2,1)} %param.4), channel_id=1, source_target_pairs={{0,8},{1,0},{2,24},{3,16},{4,12},{5,4},{6,28},{7,20},{8,9},{9,1},{... | collective-permute-start | bytes 393224 | tf_op jit(solution)/shard_map/ppermute | solution.py:253
  3.7 10.3 %collective-permute-start.1 = (bf16[128,512]{1,0:T(8,128)(2,1)}, bf16[128,512]{1,0:T(8,128)(2,1)S(1)}, u32[]{:S(2)}, u32[]{:S(2)}) collective-permute-start(bf16[128,512]{1,0:T(8,128)(2,1)} %param.4), channel_id=1, source_target_pairs={{0,16},{1,24},{2,0},{3,8},{4,20},{5,28},{6,4},{7,12},{8,17},{9,25}... | collective-permute-start | bytes 393224 | tf_op jit(solution)/shard_map/ppermute | solution.py:253
  6.1 7.9 %collective-permute-start.2 = (bf16[128,512]{1,0:T(8,128)(2,1)}, bf16[128,512]{1,0:T(8,128)(2,1)S(1)}, u32[]{:S(2)}, u32[]{:S(2)}) collective-permute-start(bf16[128,512]{1,0:T(8,128)(2,1)} %param.4), channel_id=1, source_target_pairs={{0,24},{1,16},{2,8},{3,0},{4,28},{5,20},{6,12},{7,4},{8,25},{9,17}... | collective-permute-start | bytes 393224 | tf_op jit(solution)/shard_map/ppermute | solution.py:253
  8.6 5.4 %collective-permute-start.3 = (bf16[128,512]{1,0:T(8,128)(2,1)}, bf16[128,512]{1,0:T(8,128)(2,1)S(1)}, u32[]{:S(2)}, u32[]{:S(2)}) collective-permute-start(bf16[128,512]{1,0:T(8,128)(2,1)} %param.4), channel_id=1, source_target_pairs={{0,0},{1,8},{2,16},{3,24},{4,4},{5,12},{6,20},{7,28},{8,1},{9,9},{... | collective-permute-start | bytes 393224 | tf_op jit(solution)/shard_map/ppermute | solution.py:253
  14.8 2.2 %collective-permute-start.4 = (bf16[4,128,512]{2,1,0:T(8,128)(2,1)S(1)}, bf16[4,128,512]{2,1,0:T(8,128)(2,1)S(1)}, u32[]{:S(2)}, u32[]{:S(2)}) collective-permute-start(bf16[4,128,512]{2,1,0:T(8,128)(2,1)S(1)} %shard_map.68.x_ref.refs_0_), channel_id=1, source_target_pairs={{0,4},{1,5},{2,6},{3,7},{4,0},{5,1},{6,2},{7,3},{8,12},{9,13},{10,... | collective-permute-start | bytes 1572872 | tf_op jit(solution)/shard_map/ppermute | solution.py:253
  18.2 20.1 %collective-permute-start.9 = (bf16[2,2,32,1792]{3,2,1,0:T(8,128)(2,1)S(1)}, bf16[2,2,32,1792]{3,2,1,0:T(8,128)(2,1)S(1)}, u32[]{:S(2)}, u32[]{:S(2)}) collective-permute-start(bf16[2,2,32,1792]{3,2,1,0:T(8,128)(2,1)S(1)} %get-tuple-element.41), channel_id=1, source_target_pairs={{0,1},{1,0},{2,3},{3,2},{4,5},{5,4},{6,7},{7,6},{8,9},{9,8},{10,11... | collective-permute-start | bytes 1376264 | tf_op jit(solution)/shard_map/ppermute | solution.py:253
  26.9 13.4 %collective-permute-start.11 = (bf16[2,2,32,1792]{3,2,1,0:T(8,128)(2,1)S(1)}, bf16[2,2,32,1792]{3,2,1,0:T(8,128)(2,1)S(1)}, u32[]{:S(2)}, u32[]{:S(2)}) collective-permute-start(bf16[2,2,32,1792]{3,2,1,0:T(8,128)(2,1)S(1)} %get-tuple-element.43), channel_id=1, source_target_pairs={{0,2},{1,3},{2,0},{3,1},{4,6},{5,7},{6,4},{7,5},{8,10},{9,11},{10,... | collective-permute-start | bytes 1376264 | tf_op jit(solution)/shard_map/ppermute | solution.py:253
  28.1 27.0 %copy-start = (bf16[128,1792]{1,0:T(8,128)(2,1)S(1)}, bf16[128,1792]{1,0:T(8,128)(2,1)}, u32[]{:S(2)}) copy-start(bf16[128,1792]{1,0:T(8,128)(2,1)} %param.7) | copy-start | bytes 1376260
  28.1 22.0 %collective-permute-start.7 = (bf16[2,2,32,1792]{3,2,1,0:T(8,128)(2,1)S(1)}, bf16[2,2,32,1792]{3,2,1,0:T(8,128)(2,1)S(1)}, u32[]{:S(2)}, u32[]{:S(2)}) collective-permute-start(bf16[2,2,32,1792]{3,2,1,0:T(8,128)(2,1)S(1)} %get-tuple-element.39), channel_id=1, source_target_pairs={{0,2},{1,3},{2,0},{3,1},{4,6},{5,7},{6,4},{7,5},{8,10},{9,11},{10,... | collective-permute-start | bytes 1376264 | tf_op jit(solution)/shard_map/ppermute | solution.py:253
  30.2 17.9 %collective-permute-start.5 = (bf16[2,2,32,1792]{3,2,1,0:T(8,128)(2,1)S(1)}, bf16[2,2,32,1792]{3,2,1,0:T(8,128)(2,1)S(1)}, u32[]{:S(2)}, u32[]{:S(2)}) collective-permute-start(bf16[2,2,32,1792]{3,2,1,0:T(8,128)(2,1)S(1)} %get-tuple-element.37), channel_id=1, source_target_pairs={{0,1},{1,0},{2,3},{3,2},{4,5},{5,4},{6,7},{7,6},{8,9},{9,8},{10,11... | collective-permute-start | bytes 1376264 | tf_op jit(solution)/shard_map/ppermute | solution.py:253
  38.4 16.6 %collective-permute-start.10 = (bf16[2,1,32,1792]{3,2,1,0:T(8,128)(2,1)S(1)}, bf16[2,1,32,1792]{3,2,1,0:T(8,128)(2,1)S(1)}, u32[]{:S(2)}, u32[]{:S(2)}) collective-permute-start(bf16[2,1,32,1792]{3,2,1,0:T(8,128)(2,1)S(1)} %slice.139), channel_id=1, source_target_pairs={{0,2},{1,3},{2,0},{3,1},{4,6},{5,7},{6,4},{7,5},{8,10},{9,11},{10,... | collective-permute-start | bytes 688136 | tf_op jit(solution)/shard_map/ppermute | solution.py:253
  40.4 14.7 %collective-permute-start.12 = (bf16[2,1,32,1792]{3,2,1,0:T(8,128)(2,1)S(1)}, bf16[2,1,32,1792]{3,2,1,0:T(8,128)(2,1)S(1)}, u32[]{:S(2)}, u32[]{:S(2)}) collective-permute-start(bf16[2,1,32,1792]{3,2,1,0:T(8,128)(2,1)S(1)} %slice.138), channel_id=1, source_target_pairs={{0,1},{1,0},{2,3},{3,2},{4,5},{5,4},{6,7},{7,6},{8,9},{9,8},{10,11... | collective-permute-start | bytes 688136 | tf_op jit(solution)/shard_map/ppermute | solution.py:253
  48.3 11.7 %collective-permute-start.6 = (bf16[2,1,32,1792]{3,2,1,0:T(8,128)(2,1)S(1)}, bf16[2,1,32,1792]{3,2,1,0:T(8,128)(2,1)S(1)}, u32[]{:S(2)}, u32[]{:S(2)}) collective-permute-start(bf16[2,1,32,1792]{3,2,1,0:T(8,128)(2,1)S(1)} %slice.141), channel_id=1, source_target_pairs={{0,2},{1,3},{2,0},{3,1},{4,6},{5,7},{6,4},{7,5},{8,10},{9,11},{10,... | collective-permute-start | bytes 688136 | tf_op jit(solution)/shard_map/ppermute | solution.py:253
  50.3 9.7 %collective-permute-start.8 = (bf16[2,1,32,1792]{3,2,1,0:T(8,128)(2,1)S(1)}, bf16[2,1,32,1792]{3,2,1,0:T(8,128)(2,1)S(1)}, u32[]{:S(2)}, u32[]{:S(2)}) collective-permute-start(bf16[2,1,32,1792]{3,2,1,0:T(8,128)(2,1)S(1)} %slice.140), channel_id=1, source_target_pairs={{0,1},{1,0},{2,3},{3,2},{4,5},{5,4},{6,7},{7,6},{8,9},{9,8},{10,11... | collective-permute-start | bytes 688136 | tf_op jit(solution)/shard_map/ppermute | solution.py:253
  55.5 13.5 %collective-permute-start.17 = (bf16[2,2,32,1792]{3,2,1,0:T(8,128)(2,1)S(1)}, bf16[2,2,32,1792]{3,2,1,0:T(8,128)(2,1)S(1)}, u32[]{:S(2)}, u32[]{:S(2)}) collective-permute-start(bf16[2,2,32,1792]{3,2,1,0:T(8,128)(2,1)S(1)} %maximum_maximum_fusion.refs_0_), channel_id=1, source_target_pairs={{0,1},{1,0},{2,3},{3,2},{4,5},{5,4},{6,7},{7,6},{8,9},{9,8},{10,11... | collective-permute-start | bytes 1376264 | tf_op jit(solution)/shard_map/ppermute | solution.py:253
  55.6 14.2 %collective-permute-start.18 = (bf16[2,2,32,1792]{3,2,1,0:T(8,128)(2,1)S(1)}, bf16[2,2,32,1792]{3,2,1,0:T(8,128)(2,1)S(1)}, u32[]{:S(2)}, u32[]{:S(2)}) collective-permute-start(bf16[2,2,32,1792]{3,2,1,0:T(8,128)(2,1)S(1)} %maximum_maximum_fusion.refs_0_), channel_id=1, source_target_pairs={{0,2},{1,3},{2,0},{3,1},{4,6},{5,7},{6,4},{7,5},{8,10},{9,11},{10,... | collective-permute-start | bytes 1376264 | tf_op jit(solution)/shard_map/ppermute | solution.py:253
  60.4 18.5 %collective-permute-start.13 = (bf16[2,2,32,1792]{3,2,1,0:T(8,128)(2,1)S(1)}, bf16[2,2,32,1792]{3,2,1,0:T(8,128)(2,1)S(1)}, u32[]{:S(2)}, u32[]{:S(2)}) collective-permute-start(bf16[2,2,32,1792]{3,2,1,0:T(8,128)(2,1)S(1)} %maximum_maximum_fusion.1.refs_0_), channel_id=1, source_target_pairs={{0,1},{1,0},{2,3},{3,2},{4,5},{5,4},{6,7},{7,6},{8,9},{9,8},{10,11... | collective-permute-start | bytes 1376264 | tf_op jit(solution)/shard_map/ppermute | solution.py:253
  60.5 19.1 %collective-permute-start.14 = (bf16[2,2,32,1792]{3,2,1,0:T(8,128)(2,1)S(1)}, bf16[2,2,32,1792]{3,2,1,0:T(8,128)(2,1)S(1)}, u32[]{:S(2)}, u32[]{:S(2)}) collective-permute-start(bf16[2,2,32,1792]{3,2,1,0:T(8,128)(2,1)S(1)} %maximum_maximum_fusion.1.refs_0_), channel_id=1, source_target_pairs={{0,2},{1,3},{2,0},{3,1},{4,6},{5,7},{6,4},{7,5},{8,10},{9,11},{10,... | collective-permute-start | bytes 1376264 | tf_op jit(solution)/shard_map/ppermute | solution.py:253
  69.1 15.5 %collective-permute-start.19 = (bf16[1,2,32,1792]{3,2,1,0:T(8,128)(2,1)S(1)}, bf16[1,2,32,1792]{3,2,1,0:T(8,128)(2,1)S(1)}, u32[]{:S(2)}, u32[]{:S(2)}) collective-permute-start(bf16[1,2,32,1792]{3,2,1,0:T(8,128)(2,1)S(1)} %slice.114), channel_id=1, source_target_pairs={{0,2},{1,3},{2,0},{3,1},{4,6},{5,7},{6,4},{7,5},{8,10},{9,11},{10,... | collective-permute-start | bytes 688136 | tf_op jit(solution)/shard_map/ppermute | solution.py:253
  69.8 14.7 %collective-permute-start.20 = (bf16[1,2,32,1792]{3,2,1,0:T(8,128)(2,1)S(1)}, bf16[1,2,32,1792]{3,2,1,0:T(8,128)(2,1)S(1)}, u32[]{:S(2)}, u32[]{:S(2)}) collective-permute-start(bf16[1,2,32,1792]{3,2,1,0:T(8,128)(2,1)S(1)} %slice.115), channel_id=1, source_target_pairs={{0,1},{1,0},{2,3},{3,2},{4,5},{5,4},{6,7},{7,6},{8,9},{9,8},{10,11... | collective-permute-start | bytes 688136 | tf_op jit(solution)/shard_map/ppermute | solution.py:253
  78.9 9.8 %collective-permute-start.15 = (bf16[1,2,32,1792]{3,2,1,0:T(8,128)(2,1)S(1)}, bf16[1,2,32,1792]{3,2,1,0:T(8,128)(2,1)S(1)}, u32[]{:S(2)}, u32[]{:S(2)}) collective-permute-start(bf16[1,2,32,1792]{3,2,1,0:T(8,128)(2,1)S(1)} %slice.112), channel_id=1, source_target_pairs={{0,2},{1,3},{2,0},{3,1},{4,6},{5,7},{6,4},{7,5},{8,10},{9,11},{10,... | collective-permute-start | bytes 688136 | tf_op jit(solution)/shard_map/ppermute | solution.py:253
  79.6 9.1 %collective-permute-start.16 = (bf16[1,2,32,1792]{3,2,1,0:T(8,128)(2,1)S(1)}, bf16[1,2,32,1792]{3,2,1,0:T(8,128)(2,1)S(1)}, u32[]{:S(2)}, u32[]{:S(2)}) collective-permute-start(bf16[1,2,32,1792]{3,2,1,0:T(8,128)(2,1)S(1)} %slice.113), channel_id=1, source_target_pairs={{0,1},{1,0},{2,3},{3,2},{4,5},{5,4},{6,7},{7,6},{8,9},{9,8},{10,11... | collective-permute-start | bytes 688136 | tf_op jit(solution)/shard_map/ppermute | solution.py:253
  90.8 2.0 %collective-permute-start.21 = (bf16[512,512]{1,0:T(8,128)(2,1)S(1)}, bf16[512,512]{1,0:T(8,128)(2,1)S(1)}, u32[]{:S(2)}, u32[]{:S(2)}) collective-permute-start(bf16[512,512]{1,0:T(8,128)(2,1)S(1)} %get-tuple-element.50), channel_id=1, source_target_pairs={{0,4},{1,5},{2,6},{3,7},{4,0},{5,1},{6,2},{7,3},{8,12},{9,13},{10,... | collective-permute-start | bytes 1572872 | tf_op jit(solution)/shard_map/ppermute | solution.py:253
  93.0 8.2 %collective-permute-start.22 = (bf16[128,512]{1,0:T(8,128)(2,1)S(1)}, bf16[128,512]{1,0:T(8,128)(2,1)S(1)}, u32[]{:S(2)}, u32[]{:S(2)}) collective-permute-start(bf16[128,512]{1,0:T(8,128)(2,1)S(1)} %get-tuple-element.70), channel_id=1, source_target_pairs={{0,1},{1,0},{2,3},{3,2},{4,5},{5,4},{6,7},{7,6},{8,9},{9,8},{10,11... | collective-permute-start | bytes 393224 | tf_op jit(solution)/shard_map/ppermute | solution.py:253
  93.4 8.1 %collective-permute-start.23 = (bf16[128,512]{1,0:T(8,128)(2,1)S(1)}, bf16[128,512]{1,0:T(8,128)(2,1)S(1)}, u32[]{:S(2)}, u32[]{:S(2)}) collective-permute-start(bf16[128,512]{1,0:T(8,128)(2,1)S(1)} %get-tuple-element.69), channel_id=1, source_target_pairs={{0,2},{1,3},{2,0},{3,1},{4,6},{5,7},{6,4},{7,5},{8,10},{9,11},{10,... | collective-permute-start | bytes 393224 | tf_op jit(solution)/shard_map/ppermute | solution.py:253
  94.8 6.7 %collective-permute-start.24 = (bf16[128,512]{1,0:T(8,128)(2,1)S(1)}, bf16[128,512]{1,0:T(8,128)(2,1)S(1)}, u32[]{:S(2)}, u32[]{:S(2)}) collective-permute-start(bf16[128,512]{1,0:T(8,128)(2,1)S(1)} %get-tuple-element.68), channel_id=1, source_target_pairs={{0,3},{1,2},{2,1},{3,0},{4,7},{5,6},{6,5},{7,4},{8,11},{9,10},{10,... | collective-permute-start | bytes 393224 | tf_op jit(solution)/shard_map/ppermute | solution.py:253
  102.3 10.8 %collective-permute-start.27 = (bf16[128,512]{1,0:T(8,128)(2,1)S(1)}, bf16[128,512]{1,0:T(8,128)(2,1)S(1)}, u32[]{:S(2)}, u32[]{:S(2)}) collective-permute-start(bf16[128,512]{1,0:T(8,128)(2,1)S(1)} %get-tuple-element.56), channel_id=1, source_target_pairs={{0,16},{1,17},{2,18},{3,19},{4,20},{5,21},{6,22},{7,23},{8,24},{9,... | collective-permute-start | bytes 393224 | tf_op jit(solution)/shard_map/ppermute | solution.py:253
  102.8 10.3 %collective-permute-start.26 = (bf16[128,512]{1,0:T(8,128)(2,1)S(1)}, bf16[128,512]{1,0:T(8,128)(2,1)S(1)}, u32[]{:S(2)}, u32[]{:S(2)}) collective-permute-start(bf16[128,512]{1,0:T(8,128)(2,1)S(1)} %get-tuple-element.55), channel_id=1, source_target_pairs={{0,24},{1,25},{2,26},{3,27},{4,28},{5,29},{6,30},{7,31},{8,16},{9,... | collective-permute-start | bytes 393224 | tf_op jit(solution)/shard_map/ppermute | solution.py:253
  104.6 8.9 %collective-permute-start.25 = (bf16[128,512]{1,0:T(8,128)(2,1)S(1)}, bf16[128,512]{1,0:T(8,128)(2,1)S(1)}, u32[]{:S(2)}, u32[]{:S(2)}) collective-permute-start(bf16[128,512]{1,0:T(8,128)(2,1)S(1)} %get-tuple-element.54), channel_id=1, source_target_pairs={{0,8},{1,9},{2,10},{3,11},{4,12},{5,13},{6,14},{7,15},{8,0},{9,1},... | collective-permute-start | bytes 393224 | tf_op jit(solution)/shard_map/ppermute | solution.py:253

commit v8 on v7

--- a/solution.py
+++ b/solution.py
@@ -17,8 +17,20 @@
     return pltpu.with_memory_space_constraint(x, pltpu.VMEM)
 
 
-def dequant_kernel(codes_ref, scales_ref, w_ref, done_ref, narrow_ref, wide_ref, sem, scales_sem):
-    done_ref[0] = 0
+def mark(marks_ref, mask_ref):
+    for i in range(marks_ref.shape[0]):
+        marks_ref[i : i + 1, :] = jnp.where(mask_ref[0] == i, 1.0, 0.0) * jnp.ones_like(marks_ref[:1, :])
+
+
+def pick(choices, i, marks):
+    out = choices[i]
+    for m in reversed(range(1, len(choices))):
+        out = jnp.where(marks[m : m + 1] > 0.5, choices[i ^ m], out)
+    return out
+
+
+def dequant_kernel(mask_ref, codes_ref, scales_ref, w_ref, marks_ref, narrow_ref, wide_ref, sem, scales_sem):
+    mark(marks_ref, mask_ref)
     _, owned, group = w_ref.shape
     tile = 16
 
@@ -40,15 +52,15 @@
                 w_ref[g, t : t + tile] = w_ref[g, t : t + tile] * scale
 
 
-def dequant(codes, scales):
+def dequant(codes, scales, mask, marks_shape):
     codes, scales = (pltpu.with_memory_space_constraint(x, pltpu.HBM) for x in (codes, scales))
     return pl.pallas_call(
         dequant_kernel,
-        in_specs=[pl.BlockSpec(memory_space=pl.ANY)] * 2,
-        out_specs=[pl.BlockSpec(memory_space=pltpu.VMEM), pl.BlockSpec(memory_space=pltpu.SMEM)],
+        in_specs=[pl.BlockSpec(memory_space=pltpu.SMEM)] + [pl.BlockSpec(memory_space=pl.ANY)] * 2,
+        out_specs=[pl.BlockSpec(memory_space=pltpu.VMEM)] * 2,
         out_shape=[
             pltpu.VMEM(codes.shape, jnp.bfloat16),
-            jax.ShapeDtypeStruct((1,), jnp.int32),
+            pltpu.VMEM(marks_shape, jnp.float32),
         ],
         scratch_shapes=[
             pltpu.VMEM(scales.shape, jnp.bfloat16),
@@ -57,7 +69,7 @@
             pltpu.SemaphoreType.DMA,
         ],
         compiler_params=pltpu.CompilerParams(vmem_limit_bytes=12 * 1024 * 1024),
-    )(codes, scales)
+    )(mask, codes, scales)
 
 
 def pairs(move, places, ratio):
@@ -161,76 +173,75 @@
     return outs[0::2], outs[1::2]
 
 
-def input_grad_kernel(spots, outs, first, rows, chunk, half_ref, *refs):
+def input_grad_kernel(spots, outs, first, count, half_ref, *refs):
     pieces, w_ref = refs[: len(spots)], refs[len(spots)]
-    d_ref, *term_refs = refs[len(refs) - outs - 1 : -1]
-    mine_ref = refs[-1]
-    for piece, (k, row) in zip(pieces, spots):
+    d_ref, *term_refs = refs[len(refs) - outs :]
+    for piece, row in zip(pieces, spots):
         streams, _, part, _ = piece.shape
         for s in range(streams):
-            d_ref[:, pl.ds(k * rows + first + row + s * part, part), :] = piece[s]
-            mine_ref[:, pl.ds(k * chunk + row + s * part, part), :] = piece[s]
+            d_ref[:, pl.ds(row + s * part, part), :] = piece[s]
+    mine = pl.ds(first, count)
     numbers = (((1,), (1,)), ((), ()))
     for e, term_ref in enumerate(term_refs):
         feats = term_ref.shape[1]
         at = pl.ds(pl.multiple_of((half_ref[0] ^ e) * feats, feats), feats)
-        term = lax.dot_general(mine_ref[0], w_ref[0, at, :], numbers, preferred_element_type=jnp.float32)
-        term += lax.dot_general(mine_ref[1], w_ref[1, at, :], numbers, preferred_element_type=jnp.float32)
-        term = term.astype(jnp.bfloat16)
-        for k in range(mine_ref.shape[1] // chunk):
-            term_ref[pl.ds(k * rows + first, chunk), :] = term[k * chunk : (k + 1) * chunk]
-
-
-def input_grad(pieces, spots, w_gu, half, ratio, first, rows, chunk, earlier, filled=()):
+        term = lax.dot_general(
+            d_ref[0, mine, :], w_ref[0, at, :], numbers, preferred_element_type=jnp.float32
+        ) + lax.dot_general(
+            d_ref[1, mine, :], w_ref[1, at, :], numbers, preferred_element_type=jnp.float32
+        )
+        term_ref[mine, :] = term.astype(jnp.bfloat16)
+
+
+def input_grad(pieces, spots, w_gu, half, ratio, total, first, count, earlier, filled=()):
     _, owned, group = w_gu.shape
     feats = owned // ratio
-    places = 1 + max(k for k, _ in spots)
     operands = [half, *[in_vmem(x) for x in pieces], in_vmem(w_gu), *earlier, *[in_vmem(x) for x in filled]]
     return pl.pallas_call(
-        functools.partial(input_grad_kernel, spots, ratio + 1, first, rows, chunk),
+        functools.partial(input_grad_kernel, spots, ratio + 1, first, count),
         in_specs=[pl.BlockSpec(memory_space=pltpu.SMEM)]
         + [pl.BlockSpec(memory_space=pltpu.VMEM)] * (len(pieces) + 1)
         + [pl.BlockSpec(memory_space=pl.ANY)] * len(earlier)
         + [pl.BlockSpec(memory_space=pltpu.VMEM)] * len(filled),
         out_specs=[pl.BlockSpec(memory_space=pltpu.VMEM)] * (ratio + 1),
-        out_shape=[pltpu.VMEM((2, places * rows, group), jnp.bfloat16)]
-        + [pltpu.VMEM((places * rows, feats), jnp.bfloat16)] * ratio,
-        scratch_shapes=[pltpu.VMEM((2, places * chunk, group), jnp.bfloat16)],
+        out_shape=[pltpu.VMEM((2, total, group), jnp.bfloat16)]
+        + [pltpu.VMEM((total, feats), jnp.bfloat16)] * ratio,
         input_output_aliases={len(operands) - len(filled) + i: i for i in range(len(filled))},
         compiler_params=pltpu.CompilerParams(vmem_limit_bytes=16 * 1024 * 1024),
     )(*operands)
 
 
-def weight_grad_kernel(scale, features_ref, d_ref, *refs):
-    out_ref, done_ref = refs[-2:]
-    done_ref[0] = 0
+def weight_grad_kernel(scale, features_ref, d_ref, mask_ref, *refs):
+    out_ref, marks_ref = refs[-2:]
+    mark(marks_ref, mask_ref)
     out_ref[0] = scale * lax.dot_general(
         features_ref[...], d_ref[0], (((0,), (0,)), ((), ())), preferred_element_type=jnp.float32
     )
 
 
-def weight_grad(which, features, d_both, scale, earlier, grads=None):
+def weight_grad(which, features, d_both, scale, mask, marks_shape, earlier, grads=None):
     total, owned = features.shape
     group = d_both.shape[2]
     step = min(owned, 256)
-    operands = [features, in_vmem(d_both), earlier] + ([] if grads is None else [grads])
+    operands = [features, in_vmem(d_both), mask, earlier] + ([] if grads is None else [grads])
     return pl.pallas_call(
         functools.partial(weight_grad_kernel, scale),
         grid=(owned // step,),
         in_specs=[
             pl.BlockSpec((total, step), lambda i: (0, i)),
             pl.BlockSpec((1, total, group), lambda i: (which, 0, 0)),
+            pl.BlockSpec(memory_space=pltpu.SMEM),
         ]
-        + [pl.BlockSpec(memory_space=pl.ANY)] * (len(operands) - 2),
+        + [pl.BlockSpec(memory_space=pl.ANY)] * (len(operands) - 3),
         out_specs=[
             pl.BlockSpec((1, step, group), lambda i: (which, i, 0)),
-            pl.BlockSpec(memory_space=pltpu.SMEM),
+            pl.BlockSpec(marks_shape, lambda i: (0, 0)),
         ],
         out_shape=[
             jax.ShapeDtypeStruct((2, owned, group), jnp.float32),
-            jax.ShapeDtypeStruct((1,), jnp.int32),
+            pltpu.VMEM(marks_shape, jnp.float32),
         ],
-        input_output_aliases={} if grads is None else {3: 0},
+        input_output_aliases={} if grads is None else {4: 0},
         compiler_params=pltpu.CompilerParams(vmem_limit_bytes=16 * 1024 * 1024),
     )(*operands)
 
@@ -252,19 +263,16 @@
     def permute(x, move):
         return lax.ppermute(x, AXES, pairs(move, places, ratio))
 
-    def own_features(x, earlier):
+    def own_features(x, marks):
         got = {j: permute(x, lambda p, h, q: (q ^ j, h, p)) for j in [*range(1, places), 0]}
-
-        def by_place(out_ref, i, value):
-            out_ref[i] = value
-
-        return shuffle(got, mask, earlier, (places, rows, feats), by_place)
+        return jnp.stack([pick(got, k, marks) for k in range(places)])
 
     def joined(halves):
         def by_half(out_ref, i, value):
-            out_ref[:, :, i * feats : (i + 1) * feats] = value
-
-        return shuffle(dict(enumerate(halves)), half, (), (places, rows, owned), by_half)
+            for c in range(CHUNKS):
+                out_ref[c, :, :, i * feats : (i + 1) * feats] = value[:, c * chunk : (c + 1) * chunk]
+
+        return shuffle(dict(enumerate(halves)), half, (), (CHUNKS, places, chunk, owned), by_half)
 
     def sent(x, order, step):
         ks = [k for k in range(places) if not any(k & bit for bit in order[:step])]
@@ -303,9 +311,8 @@
     def send_direct(x):
         return {bit: permute(x, lambda p, h, q: (p, h, q ^ bit)) for bit in bits}
 
-    def forward_rest(x, direct):
-        part = x.shape[2]
-        pieces, spots = [x] + [direct[bit] for bit in bits], [(0, 0)] + [(bit, 0) for bit in bits]
+    def forward_rest(c, x, direct):
+        pieces, spots = [x] + [direct[bit] for bit in bits], [(c * places + k) * chunk for k in [0] + bits]
         for s, order in enumerate(orders):
             held = {0: None}
             for bit in order:
@@ -315,11 +322,11 @@
                     else:
                         held[k ^ bit] = permute(held[k], lambda p, h, q: (p, h, q ^ bit))
                         pieces.append(held[k ^ bit])
-                        spots.append((k ^ bit, s * part))
+                        spots.append((c * places + (k ^ bit)) * chunk + s * part)
         return pieces, spots
 
-    w_gu, done = dequant(gate_up_codes, gate_up_scales)
-    mine = own_features(tokens, [done])
+    w_gu, marks = dequant(gate_up_codes, gate_up_scales, mask, (places, feats))
+    mine = own_features(tokens, marks)
     others = [permute(mine, lambda p, h, q, e=e: (p, h ^ e, q)) for e in range(1, ratio)]
     own = own_half(mine, w_gu, half)
     (keep_a, got_a), (keep_b, got_b) = start_forward(0), start_forward(1)
@@ -329,27 +336,35 @@
     hidden_b, streams_b = gradients(keep_b, got_b, chunk)
     hidden_a, streams_a = gradients(keep_a, after(got_a, streams_b), 0)
     direct_a, direct_b = send_direct(streams_a), send_direct(streams_b)
-    rest_a, rest_b = forward_rest(streams_a, direct_a), forward_rest(streams_b, direct_b)
-    filled = input_grad(*rest_b, w_gu, half, ratio, chunk, rows, chunk, hidden_b)
-    filled = input_grad(*rest_a, w_gu, half, ratio, 0, rows, chunk, hidden_a, filled)
-    d_all, *term = filled
+    pieces_a, spots_a = forward_rest(0, streams_a, direct_a)
+    pieces_b, spots_b = forward_rest(1, streams_b, direct_b)
+    near, total, count = 1 + len(bits), places * rows, places * chunk
+    filled = input_grad(
+        pieces_b + pieces_a[:near],
+        spots_b + spots_a[:near],
+        w_gu, half, ratio, total, count, count, hidden_a + hidden_b,
+    )
+    d_all, *term = input_grad(
+        pieces_a[near:], spots_a[near:], w_gu, half, ratio, total, 0, count, [], filled
+    )
     summed = term[0].astype(jnp.float32)
     for e in range(1, ratio):
         got = permute(term[e], lambda p, h, q: (p, h ^ e, q))
         summed = summed + got.astype(jnp.float32)
-    summed = summed.astype(jnp.bfloat16).reshape(places, rows, feats)
+    summed = summed.reshape(CHUNKS, places, chunk, feats).astype(jnp.bfloat16)
+    summed = [summed[:, k].reshape(rows, feats) for k in range(places)]
     far_first = [*range(places // 2, places), *range(1, places // 2)]
     arrived = {k: permute(summed[k], lambda p, h, q: (p, h, q ^ k)) for k in range(1, places)}
     arrived[0] = summed[0]
-    flat = joined([mine] + others).reshape(places * rows, owned)
+    flat = joined([mine] + others).reshape(total, owned)
     scale = 1.0 / math.sqrt(rows * places)
-    grads, done = weight_grad(0, flat, d_all, scale, summed[0, :16])
-    arrived = shuffle(arrived, mask, [done])
+    grads, marks = weight_grad(0, flat, d_all, scale, mask, marks.shape, summed[0][:16])
+    arrived = [pick(arrived, j, marks) for j in range(places)]
     summands = [arrived[0]] + [
         permute(arrived[j], lambda p, h, q: (p ^ j, h, q)) for j in reversed(far_first)
     ]
-    grads, done = weight_grad(1, flat, d_all, scale, arrived[0][:16], grads)
-    summands[0] = after(summands[0], done)
+    grads, marks = weight_grad(1, flat, d_all, scale, mask, marks.shape, arrived[0][:16], grads)
+    summands[0] = after(summands[0], marks)
     d_tokens = sum(x.astype(jnp.float32) for x in summands).astype(jnp.bfloat16)
     return jnp.concatenate(hidden_a + hidden_b), d_tokens, grads
 

time: 114 us -> 113 us (level)
  Pallas kernels: 23.4 us -> 21.4 us
    pallas_call x3 -> x1, Pallas kernels: 1.67 us -> 0.09 us  [shuffle(): pl.pallas_call(functools.partial(shuffle_kernel, list(choices), write), i...]
where the time goes in v8:
time: 113 us
  waiting for transfers between devices  48 us (42%)
  starting transfers between devices  39 us (35%)
  Pallas kernels  21.4 us (19%)
  other arithmetic  3.14 us (3%)
    ppermute x28, waiting for transfers between devices, permute(): return lax.ppermute(x, AXES, pairs(move, places, ratio))  48 us
    ppermute x28, starting transfers between devices, permute(): return lax.ppermute(x, AXES, pairs(move, places, ratio))  39 us
    pallas_call x2, Pallas kernels, weight_grad(): pl.pallas_call(functools.partial(weight_grad_kernel, scale), grid=(owned...  9.32 us
    pallas_call x2, Pallas kernels, input_grad(): pl.pallas_call(functools.partial(input_grad_kernel, spots, ratio + 1, fir...  4.33 us
    pallas_call x1, Pallas kernels, dequant(): pl.pallas_call(dequant_kernel, in_specs=[pl.BlockSpec(memory_space=pltpu....  3.38 us
  transfers between devices with their start and end apart: 28, of which 16 were waited for; matrix products, arithmetic and copies ran while one was open for 2% of the time, Pallas kernels for 16%

profile of v8, /device:TPU:0, one launch (start us, length us, event | category | flops | bytes accessed | tf_op | source)
XLA Modules:
  0.0 112.8 jit_solution(1593775310332319313)
XLA Ops:
  0.6 3.1 %collective-permute-start = (bf16[128,512]{1,0:T(8,128)(2,1)}, bf16[128,512]{1,0:T(8,128)(2,1)S(1)}, u32[]{:S(2)}, u32[]{:S(2)}) collective-permute-start(bf16[128,512]{1,0:T(8,128)(2,1)} %param.4), channel_id=1, source_target_pairs={{0,8},{1,0},{2,24},{3,16},{4,12},{5,4},{6,28},{7,20},{8,9},{9,1},{... | collective-permute-start | bytes 393224 | tf_op jit(solution)/shard_map/ppermute | solution.py:264
  3.7 2.4 %collective-permute-start.1 = (bf16[128,512]{1,0:T(8,128)(2,1)}, bf16[128,512]{1,0:T(8,128)(2,1)S(1)}, u32[]{:S(2)}, u32[]{:S(2)}) collective-permute-start(bf16[128,512]{1,0:T(8,128)(2,1)} %param.4), channel_id=1, source_target_pairs={{0,16},{1,24},{2,0},{3,8},{4,20},{5,28},{6,4},{7,12},{8,17},{9,25}... | collective-permute-start | bytes 393224 | tf_op jit(solution)/shard_map/ppermute | solution.py:264
  6.1 2.5 %collective-permute-start.2 = (bf16[128,512]{1,0:T(8,128)(2,1)}, bf16[128,512]{1,0:T(8,128)(2,1)S(1)}, u32[]{:S(2)}, u32[]{:S(2)}) collective-permute-start(bf16[128,512]{1,0:T(8,128)(2,1)} %param.4), channel_id=1, source_target_pairs={{0,24},{1,16},{2,8},{3,0},{4,28},{5,20},{6,12},{7,4},{8,25},{9,17}... | collective-permute-start | bytes 393224 | tf_op jit(solution)/shard_map/ppermute | solution.py:264
  8.6 1.6 %collective-permute-start.3 = (bf16[128,512]{1,0:T(8,128)(2,1)}, bf16[128,512]{1,0:T(8,128)(2,1)S(1)}, u32[]{:S(2)}, u32[]{:S(2)}) collective-permute-start(bf16[128,512]{1,0:T(8,128)(2,1)} %param.4), channel_id=1, source_target_pairs={{0,0},{1,8},{2,16},{3,24},{4,4},{5,12},{6,20},{7,28},{8,1},{9,9},{... | collective-permute-start | bytes 393224 | tf_op jit(solution)/shard_map/ppermute | solution.py:264
  10.2 3.4 %shard_map.67 = (bf16[2,1024,1792]{2,1,0:T(8,128)(2,1)S(1)}, f32[4,512]{1,0:T(4,128)S(1)}) custom-call(s32[1]{0:T(128)} %bitcast.1.mask_ref, bf16[2,1024,1792]{2,1,0:T(8,128)(2,1)} %codes_ref.1, bf16[2,8,1792]{2,1,0:T(8,128)(2,1)} %scales_ref.1), custom_call_target="tpu_custom_call" | custom-call | tf_op jit(solution)/shard_map/pallas_call | solution.py:57
  13.9 2.1 %shard_map.68.refs_2_ = f32[2,4,128,1792]{3,2,1,0:T(8,128)S(1)} custom-call(s32[1]{0:T(128)} %bitcast.half_ref.index_ref, bf16[4,128,512]{2,1,0:T(8,128)(2,1)S(1)} %pad_maximum_fusion.x_ref.refs_0_, bf16[2,1024,1792]{2,1,0:T(8,128)(2,1)S(1)} %get-tuple-element.31.w_ref.refs_1_.refs_8_.refs_2_), custom_call_target="tpu_custom_call" | custom-call | tf_op jit(solution)/shard_map/pallas_call | solution.py:132
  17.1 9.1 %collective-permute-start.9 = (bf16[2,2,32,1792]{3,2,1,0:T(8,128)(2,1)S(1)}, bf16[2,2,32,1792]{3,2,1,0:T(8,128)(2,1)S(1)}, u32[]{:S(2)}, u32[]{:S(2)}) collective-permute-start(bf16[2,2,32,1792]{3,2,1,0:T(8,128)(2,1)S(1)} %get-tuple-element.37), channel_id=1, source_target_pairs={{0,1},{1,0},{2,3},{3,2},{4,5},{5,4},{6,7},{7,6},{8,9},{9,8},{10,11... | collective-permute-start | bytes 1376264 | tf_op jit(solution)/shard_map/ppermute | solution.py:264
  27.4 2.1 %collective-permute-start.7 = (bf16[2,2,32,1792]{3,2,1,0:T(8,128)(2,1)S(1)}, bf16[2,2,32,1792]{3,2,1,0:T(8,128)(2,1)S(1)}, u32[]{:S(2)}, u32[]{:S(2)}) collective-permute-start(bf16[2,2,32,1792]{3,2,1,0:T(8,128)(2,1)S(1)} %get-tuple-element.35), channel_id=1, source_target_pairs={{0,2},{1,3},{2,0},{3,1},{4,6},{5,7},{6,4},{7,5},{8,10},{9,11},{10,... | collective-permute-start | bytes 1376264 | tf_op jit(solution)/shard_map/ppermute | solution.py:264
  29.5 8.1 %collective-permute-done.9 = bf16[2,2,32,1792]{3,2,1,0:T(8,128)(2,1)S(1)} collective-permute-done((bf16[2,2,32,1792]{3,2,1,0:T(8,128)(2,1)S(1)}, bf16[2,2,32,1792]{3,2,1,0:T(8,128)(2,1)S(1)}, u32[]{:S(2)}, u32[]{:S(2)}) %collective-permute-start.9) | collective-permute-done | bytes 458784 | tf_op jit(solution)/shard_map/ppermute | solution.py:264
  37.7 1.7 %collective-permute-start.10 = (bf16[2,1,32,1792]{3,2,1,0:T(8,128)(2,1)S(1)}, bf16[2,1,32,1792]{3,2,1,0:T(8,128)(2,1)S(1)}, u32[]{:S(2)}, u32[]{:S(2)}) collective-permute-start(bf16[2,1,32,1792]{3,2,1,0:T(8,128)(2,1)S(1)} %slice.183), channel_id=1, source_target_pairs={{0,2},{1,3},{2,0},{3,1},{4,6},{5,7},{6,4},{7,5},{8,10},{9,11},{10,... | collective-permute-start | bytes 688136 | tf_op jit(solution)/shard_map/ppermute | solution.py:264
  39.9 7.5 %collective-permute-done.5 = bf16[2,2,32,1792]{3,2,1,0:T(8,128)(2,1)S(1)} collective-permute-done((bf16[2,2,32,1792]{3,2,1,0:T(8,128)(2,1)S(1)}, bf16[2,2,32,1792]{3,2,1,0:T(8,128)(2,1)S(1)}, u32[]{:S(2)}, u32[]{:S(2)}) %collective-permute-start.5) | collective-permute-done | bytes 458784 | tf_op jit(solution)/shard_map/ppermute | solution.py:264
  47.6 1.7 %collective-permute-start.6 = (bf16[2,1,32,1792]{3,2,1,0:T(8,128)(2,1)S(1)}, bf16[2,1,32,1792]{3,2,1,0:T(8,128)(2,1)S(1)}, u32[]{:S(2)}, u32[]{:S(2)}) collective-permute-start(bf16[2,1,32,1792]{3,2,1,0:T(8,128)(2,1)S(1)} %slice.185), channel_id=1, source_target_pairs={{0,2},{1,3},{2,0},{3,1},{4,6},{5,7},{6,4},{7,5},{8,10},{9,11},{10,... | collective-permute-start | bytes 688136 | tf_op jit(solution)/shard_map/ppermute | solution.py:264
  49.8 4.5 %collective-permute-done.10 = bf16[2,1,32,1792]{3,2,1,0:T(8,128)(2,1)S(1)} collective-permute-done((bf16[2,1,32,1792]{3,2,1,0:T(8,128)(2,1)S(1)}, bf16[2,1,32,1792]{3,2,1,0:T(8,128)(2,1)S(1)}, u32[]{:S(2)}, u32[]{:S(2)}) %collective-permute-start.10) | collective-permute-done | bytes 229408 | tf_op jit(solution)/shard_map/ppermute | solution.py:264
  54.9 1.7 %collective-permute-start.18 = (bf16[2,2,32,1792]{3,2,1,0:T(8,128)(2,1)S(1)}, bf16[2,2,32,1792]{3,2,1,0:T(8,128)(2,1)S(1)}, u32[]{:S(2)}, u32[]{:S(2)}) collective-permute-start(bf16[2,2,32,1792]{3,2,1,0:T(8,128)(2,1)S(1)} %maximum_maximum_fusion.refs_0_), channel_id=1, source_target_pairs={{0,2},{1,3},{2,0},{3,1},{4,6},{5,7},{6,4},{7,5},{8,10},{9,11},{10,... | collective-permute-start | bytes 1376264 | tf_op jit(solution)/shard_map/ppermute | solution.py:264
  56.6 2.7 %collective-permute-done.6 = bf16[2,1,32,1792]{3,2,1,0:T(8,128)(2,1)S(1)} collective-permute-done((bf16[2,1,32,1792]{3,2,1,0:T(8,128)(2,1)S(1)}, bf16[2,1,32,1792]{3,2,1,0:T(8,128)(2,1)S(1)}, u32[]{:S(2)}, u32[]{:S(2)}) %collective-permute-start.6) | collective-permute-done | bytes 229408 | tf_op jit(solution)/shard_map/ppermute | solution.py:264
  59.8 1.7 %collective-permute-start.15 = (bf16[2,2,32,1792]{3,2,1,0:T(8,128)(2,1)S(1)}, bf16[2,2,32,1792]{3,2,1,0:T(8,128)(2,1)S(1)}, u32[]{:S(2)}, u32[]{:S(2)}) collective-permute-start(bf16[2,2,32,1792]{3,2,1,0:T(8,128)(2,1)S(1)} %maximum_maximum_fusion.1.refs_5_), channel_id=1, source_target_pairs={{0,2},{1,3},{2,0},{3,1},{4,6},{5,7},{6,4},{7,5},{8,10},{9,11},{10,... | collective-permute-start | bytes 1376264 | tf_op jit(solution)/shard_map/ppermute | solution.py:264
  61.5 6.9 %collective-permute-done.17.refs_1_ = bf16[2,2,32,1792]{3,2,1,0:T(8,128)(2,1)S(1)} collective-permute-done((bf16[2,2,32,1792]{3,2,1,0:T(8,128)(2,1)S(1)}, bf16[2,2,32,1792]{3,2,1,0:T(8,128)(2,1)S(1)}, u32[]{:S(2)}, u32[]{:S(2)}) %collective-permute-start.17) | collective-permute-done | bytes 458784 | tf_op jit(solution)/shard_map/ppermute | solution.py:264
  69.1 1.3 %collective-permute-start.20 = (bf16[1,2,32,1792]{3,2,1,0:T(8,128)(2,1)S(1)}, bf16[1,2,32,1792]{3,2,1,0:T(8,128)(2,1)S(1)}, u32[]{:S(2)}, u32[]{:S(2)}) collective-permute-start(bf16[1,2,32,1792]{3,2,1,0:T(8,128)(2,1)S(1)} %slice.153), channel_id=1, source_target_pairs={{0,1},{1,0},{2,3},{3,2},{4,5},{5,4},{6,7},{7,6},{8,9},{9,8},{10,11... | collective-permute-start | bytes 688136 | tf_op jit(solution)/shard_map/ppermute | solution.py:264
  70.4 7.7 %collective-permute-done.13.refs_6_ = bf16[2,2,32,1792]{3,2,1,0:T(8,128)(2,1)S(1)} collective-permute-done((bf16[2,2,32,1792]{3,2,1,0:T(8,128)(2,1)S(1)}, bf16[2,2,32,1792]{3,2,1,0:T(8,128)(2,1)S(1)}, u32[]{:S(2)}, u32[]{:S(2)}) %collective-permute-start.13) | collective-permute-done | bytes 458784 | tf_op jit(solution)/shard_map/ppermute | solution.py:264
  78.9 1.3 %collective-permute-start.16 = (bf16[1,2,32,1792]{3,2,1,0:T(8,128)(2,1)S(1)}, bf16[1,2,32,1792]{3,2,1,0:T(8,128)(2,1)S(1)}, u32[]{:S(2)}, u32[]{:S(2)}) collective-permute-start(bf16[1,2,32,1792]{3,2,1,0:T(8,128)(2,1)S(1)} %slice.151), channel_id=1, source_target_pairs={{0,1},{1,0},{2,3},{3,2},{4,5},{5,4},{6,7},{7,6},{8,9},{9,8},{10,11... | collective-permute-start | bytes 688136 | tf_op jit(solution)/shard_map/ppermute | solution.py:264
  80.3 3.5 %collective-permute-done.19.refs_3_ = bf16[1,2,32,1792]{3,2,1,0:T(8,128)(2,1)S(1)} collective-permute-done((bf16[1,2,32,1792]{3,2,1,0:T(8,128)(2,1)S(1)}, bf16[1,2,32,1792]{3,2,1,0:T(8,128)(2,1)S(1)}, u32[]{:S(2)}, u32[]{:S(2)}) %collective-permute-start.19) | collective-permute-done | bytes 229408 | tf_op jit(solution)/shard_map/ppermute | solution.py:264
  83.8 2.2 %shard_map.72 = (bf16[2,512,1792]{2,1,0:T(8,128)(2,1)S(1)}, bf16[512,512]{1,0:T(8,128)(2,1)S(1)}, bf16[512,512]{1,0:T(8,128)(2,1)S(1)}) custom-call(s32[1]{0:T(128)} %bitcast.half_ref.index_ref, bf16[2,2,32,1792]{3,2,1,0:T(8,128)(2,1)S(1)} %maximum_maximum_fusion.refs_0_, bf16[2,2,32,1792]{3,2,1,0:T(8,128)(2,1)S(1)} %collective-permute-done.17.refs_1_, ...), custom_call_target="tpu_custom_call" | custom-call | tf_op jit(solution)/shard_map/pallas_call | solution.py:200
  86.1 1.9 %collective-permute-done.14.refs_0_ = bf16[1,2,32,1792]{3,2,1,0:T(8,128)(2,1)S(1)} collective-permute-done((bf16[1,2,32,1792]{3,2,1,0:T(8,128)(2,1)S(1)}, bf16[1,2,32,1792]{3,2,1,0:T(8,128)(2,1)S(1)}, u32[]{:S(2)}, u32[]{:S(2)}) %collective-permute-start.14) | collective-permute-done | bytes 229408 | tf_op jit(solution)/shard_map/ppermute | solution.py:264
  88.0 2.1 %shard_map.73 = (bf16[2,512,1792]{2,1,0:T(8,128)(2,1)S(1)}, bf16[512,512]{1,0:T(8,128)(2,1)S(1)}, bf16[512,512]{1,0:T(8,128)(2,1)S(1)}) custom-call(s32[1]{0:T(128)} %bitcast.half_ref.index_ref, bf16[1,2,32,1792]{3,2,1,0:T(8,128)(2,1)S(1)} %collective-permute-done.14.refs_0_, ...), custom_call_target="tpu_custom_call", output_to_operand_aliasing={{0}: (4, {}), {1}: (5, {}), {2}: (6, {})} | custom-call | tf_op jit(solution)/shard_map/pallas_call | solution.py:200
  90.2 1.9 %collective-permute-done.21 = bf16[512,512]{1,0:T(8,128)(2,1)S(1)} collective-permute-done((bf16[512,512]{1,0:T(8,128)(2,1)S(1)}, bf16[512,512]{1,0:T(8,128)(2,1)S(1)}, u32[]{:S(2)}, u32[]{:S(2)}) %collective-permute-start.21) | collective-permute-done | bytes 524320 | tf_op jit(solution)/shard_map/ppermute | solution.py:264
  92.7 1.3 %collective-permute-start.23 = (bf16[128,512]{1,0:T(8,128)(2,1)S(1)}, bf16[128,512]{1,0:T(8,128)(2,1)S(1)}, u32[]{:S(2)}, u32[]{:S(2)}) collective-permute-start(bf16[128,512]{1,0:T(8,128)(2,1)S(1)} %bitcast.129), channel_id=1, source_target_pairs={{0,2},{1,3},{2,0},{3,1},{4,6},{5,7},{6,4},{7,5},{8,10},{9,11},{10,... | collective-permute-start | bytes 393224 | tf_op jit(solution)/shard_map/ppermute | solution.py:264
  94.0 1.8 %collective-permute-start.24 = (bf16[128,512]{1,0:T(8,128)(2,1)S(1)}, bf16[128,512]{1,0:T(8,128)(2,1)S(1)}, u32[]{:S(2)}, u32[]{:S(2)}) collective-permute-start(bf16[128,512]{1,0:T(8,128)(2,1)S(1)} %bitcast.128), channel_id=1, source_target_pairs={{0,3},{1,2},{2,1},{3,0},{4,7},{5,6},{6,5},{7,4},{8,11},{9,10},{10,... | collective-permute-start | bytes 393224 | tf_op jit(solution)/shard_map/ppermute | solution.py:264
  95.9 4.7 %shard_map.74 = (f32[2,1024,1792]{2,1,0:T(8,128)}, f32[4,512]{1,0:T(4,128)S(1)}) custom-call(bf16[512,1024]{1,0:T(8,128)(2,1)S(1)} %bitcast.124, bf16[2,512,1792]{2,1,0:T(8,128)(2,1)S(1)} %get-tuple-element.45.d_ref, s32[1]{0:T(128)} %bitcast.1.mask_ref, bf16[16,512]{1,0:T(8,128)(2,1)S(1)} %slice.155.refs_0_), custom_call_target="tpu_custom_call" | custom-call | tf_op jit(solution)/shard_map/pallas_call | solution.py:227
  101.4 1.8 %collective-permute-start.26 = (bf16[128,512]{1,0:T(8,128)(2,1)S(1)}, bf16[128,512]{1,0:T(8,128)(2,1)S(1)}, u32[]{:S(2)}, u32[]{:S(2)}) collective-permute-start(bf16[128,512]{1,0:T(8,128)(2,1)S(1)} %get-tuple-element.67), channel_id=1, source_target_pairs={{0,24},{1,25},{2,26},{3,27},{4,28},{5,29},{6,30},{7,31},{8,16},{9,... | collective-permute-start | bytes 393224 | tf_op jit(solution)/shard_map/ppermute | solution.py:264
  103.1 1.3 %collective-permute-start.25 = (bf16[128,512]{1,0:T(8,128)(2,1)S(1)}, bf16[128,512]{1,0:T(8,128)(2,1)S(1)}, u32[]{:S(2)}, u32[]{:S(2)}) collective-permute-start(bf16[128,512]{1,0:T(8,128)(2,1)S(1)} %get-tuple-element.68), channel_id=1, source_target_pairs={{0,8},{1,9},{2,10},{3,11},{4,12},{5,13},{6,14},{7,15},{8,0},{9,1},... | collective-permute-start | bytes 393224 | tf_op jit(solution)/shard_map/ppermute | solution.py:264
  105.2 4.6 %shard_map.75 = (f32[2,1024,1792]{2,1,0:T(8,128)}, f32[4,512]{1,0:T(4,128)}) custom-call(bf16[512,1024]{1,0:T(8,128)(2,1)S(1)} %bitcast.125, bf16[2,512,1792]{2,1,0:T(8,128)(2,1)S(1)} %get-tuple-element.45.d_ref, s32[1]{0:T(128)} %bitcast.1.mask_ref, bf16[16,512]{1,0:T(8,128)(2,1)S(1)} %slice.159.refs_0_, ...), custom_call_target="tpu_custom_call", output_to_operand_aliasing={{0}: (4, {})} | custom-call | tf_op jit(solution)/shard_map/pallas_call | solution.py:227
  109.9 2.0 %collective-permute-done.27 = bf16[128,512]{1,0:T(8,128)(2,1)S(1)} collective-permute-done((bf16[128,512]{1,0:T(8,128)(2,1)S(1)}, bf16[128,512]{1,0:T(8,128)(2,1)S(1)}, u32[]{:S(2)}, u32[]{:S(2)}) %collective-permute-start.27) | collective-permute-done | bytes 131104 | tf_op jit(solution)/shard_map/ppermute | solution.py:264
  (65 shorter events, 9.7 us)
Async XLA Ops:
  0.6 12.9 %collective-permute-start = (bf16[128,512]{1,0:T(8,128)(2,1)}, bf16[128,512]{1,0:T(8,128)(2,1)S(1)}, u32[]{:S(2)}, u32[]{:S(2)}) collective-permute-start(bf16[128,512]{1,0:T(8,128)(2,1)} %param.4), channel_id=1, source_target_pairs={{0,8},{1,0},{2,24},{3,16},{4,12},{5,4},{6,28},{7,20},{8,9},{9,1},{... | collective-permute-start | bytes 393224 | tf_op jit(solution)/shard_map/ppermute | solution.py:264
  3.7 9.9 %collective-permute-start.1 = (bf16[128,512]{1,0:T(8,128)(2,1)}, bf16[128,512]{1,0:T(8,128)(2,1)S(1)}, u32[]{:S(2)}, u32[]{:S(2)}) collective-permute-start(bf16[128,512]{1,0:T(8,128)(2,1)} %param.4), channel_id=1, source_target_pairs={{0,16},{1,24},{2,0},{3,8},{4,20},{5,28},{6,4},{7,12},{8,17},{9,25}... | collective-permute-start | bytes 393224 | tf_op jit(solution)/shard_map/ppermute | solution.py:264
  6.1 7.5 %collective-permute-start.2 = (bf16[128,512]{1,0:T(8,128)(2,1)}, bf16[128,512]{1,0:T(8,128)(2,1)S(1)}, u32[]{:S(2)}, u32[]{:S(2)}) collective-permute-start(bf16[128,512]{1,0:T(8,128)(2,1)} %param.4), channel_id=1, source_target_pairs={{0,24},{1,16},{2,8},{3,0},{4,28},{5,20},{6,12},{7,4},{8,25},{9,17}... | collective-permute-start | bytes 393224 | tf_op jit(solution)/shard_map/ppermute | solution.py:264
  8.6 5.0 %collective-permute-start.3 = (bf16[128,512]{1,0:T(8,128)(2,1)}, bf16[128,512]{1,0:T(8,128)(2,1)S(1)}, u32[]{:S(2)}, u32[]{:S(2)}) collective-permute-start(bf16[128,512]{1,0:T(8,128)(2,1)} %param.4), channel_id=1, source_target_pairs={{0,0},{1,8},{2,16},{3,24},{4,4},{5,12},{6,20},{7,28},{8,1},{9,9},{... | collective-permute-start | bytes 393224 | tf_op jit(solution)/shard_map/ppermute | solution.py:264
  13.8 2.2 %collective-permute-start.4 = (bf16[4,128,512]{2,1,0:T(8,128)(2,1)S(1)}, bf16[4,128,512]{2,1,0:T(8,128)(2,1)S(1)}, u32[]{:S(2)}, u32[]{:S(2)}) collective-permute-start(bf16[4,128,512]{2,1,0:T(8,128)(2,1)S(1)} %pad_maximum_fusion.x_ref.refs_0_), channel_id=1, source_target_pairs={{0,4},{1,5},{2,6},{3,7},{4,0},{5,1},{6,2},{7,3},{8,12},{9,13},{10,... | collective-permute-start | bytes 1572872 | tf_op jit(solution)/shard_map/ppermute | solution.py:264
  17.1 20.5 %collective-permute-start.9 = (bf16[2,2,32,1792]{3,2,1,0:T(8,128)(2,1)S(1)}, bf16[2,2,32,1792]{3,2,1,0:T(8,128)(2,1)S(1)}, u32[]{:S(2)}, u32[]{:S(2)}) collective-permute-start(bf16[2,2,32,1792]{3,2,1,0:T(8,128)(2,1)S(1)} %get-tuple-element.37), channel_id=1, source_target_pairs={{0,1},{1,0},{2,3},{3,2},{4,5},{5,4},{6,7},{7,6},{8,9},{9,8},{10,11... | collective-permute-start | bytes 1376264 | tf_op jit(solution)/shard_map/ppermute | solution.py:264
  26.2 13.4 %collective-permute-start.11 = (bf16[2,2,32,1792]{3,2,1,0:T(8,128)(2,1)S(1)}, bf16[2,2,32,1792]{3,2,1,0:T(8,128)(2,1)S(1)}, u32[]{:S(2)}, u32[]{:S(2)}) collective-permute-start(bf16[2,2,32,1792]{3,2,1,0:T(8,128)(2,1)S(1)} %get-tuple-element.39), channel_id=1, source_target_pairs={{0,2},{1,3},{2,0},{3,1},{4,6},{5,7},{6,4},{7,5},{8,10},{9,11},{10,... | collective-permute-start | bytes 1376264 | tf_op jit(solution)/shard_map/ppermute | solution.py:264
  27.4 27.1 %copy-start = (bf16[128,1792]{1,0:T(8,128)(2,1)S(1)}, bf16[128,1792]{1,0:T(8,128)(2,1)}, u32[]{:S(2)}) copy-start(bf16[128,1792]{1,0:T(8,128)(2,1)} %param.7) | copy-start | bytes 1376260
  27.4 22.0 %collective-permute-start.7 = (bf16[2,2,32,1792]{3,2,1,0:T(8,128)(2,1)S(1)}, bf16[2,2,32,1792]{3,2,1,0:T(8,128)(2,1)S(1)}, u32[]{:S(2)}, u32[]{:S(2)}) collective-permute-start(bf16[2,2,32,1792]{3,2,1,0:T(8,128)(2,1)S(1)} %get-tuple-element.35), channel_id=1, source_target_pairs={{0,2},{1,3},{2,0},{3,1},{4,6},{5,7},{6,4},{7,5},{8,10},{9,11},{10,... | collective-permute-start | bytes 1376264 | tf_op jit(solution)/shard_map/ppermute | solution.py:264
  29.5 18.0 %collective-permute-start.5 = (bf16[2,2,32,1792]{3,2,1,0:T(8,128)(2,1)S(1)}, bf16[2,2,32,1792]{3,2,1,0:T(8,128)(2,1)S(1)}, u32[]{:S(2)}, u32[]{:S(2)}) collective-permute-start(bf16[2,2,32,1792]{3,2,1,0:T(8,128)(2,1)S(1)} %get-tuple-element.33), channel_id=1, source_target_pairs={{0,1},{1,0},{2,3},{3,2},{4,5},{5,4},{6,7},{7,6},{8,9},{9,8},{10,11... | collective-permute-start | bytes 1376264 | tf_op jit(solution)/shard_map/ppermute | solution.py:264
  37.7 16.6 %collective-permute-start.10 = (bf16[2,1,32,1792]{3,2,1,0:T(8,128)(2,1)S(1)}, bf16[2,1,32,1792]{3,2,1,0:T(8,128)(2,1)S(1)}, u32[]{:S(2)}, u32[]{:S(2)}) collective-permute-start(bf16[2,1,32,1792]{3,2,1,0:T(8,128)(2,1)S(1)} %slice.183), channel_id=1, source_target_pairs={{0,2},{1,3},{2,0},{3,1},{4,6},{5,7},{6,4},{7,5},{8,10},{9,11},{10,... | collective-permute-start | bytes 688136 | tf_op jit(solution)/shard_map/ppermute | solution.py:264
  39.7 14.7 %collective-permute-start.12 = (bf16[2,1,32,1792]{3,2,1,0:T(8,128)(2,1)S(1)}, bf16[2,1,32,1792]{3,2,1,0:T(8,128)(2,1)S(1)}, u32[]{:S(2)}, u32[]{:S(2)}) collective-permute-start(bf16[2,1,32,1792]{3,2,1,0:T(8,128)(2,1)S(1)} %slice.182), channel_id=1, source_target_pairs={{0,1},{1,0},{2,3},{3,2},{4,5},{5,4},{6,7},{7,6},{8,9},{9,8},{10,11... | collective-permute-start | bytes 688136 | tf_op jit(solution)/shard_map/ppermute | solution.py:264
  47.6 11.7 %collective-permute-start.6 = (bf16[2,1,32,1792]{3,2,1,0:T(8,128)(2,1)S(1)}, bf16[2,1,32,1792]{3,2,1,0:T(8,128)(2,1)S(1)}, u32[]{:S(2)}, u32[]{:S(2)}) collective-permute-start(bf16[2,1,32,1792]{3,2,1,0:T(8,128)(2,1)S(1)} %slice.185), channel_id=1, source_target_pairs={{0,2},{1,3},{2,0},{3,1},{4,6},{5,7},{6,4},{7,5},{8,10},{9,11},{10,... | collective-permute-start | bytes 688136 | tf_op jit(solution)/shard_map/ppermute | solution.py:264
  49.6 9.7 %collective-permute-start.8 = (bf16[2,1,32,1792]{3,2,1,0:T(8,128)(2,1)S(1)}, bf16[2,1,32,1792]{3,2,1,0:T(8,128)(2,1)S(1)}, u32[]{:S(2)}, u32[]{:S(2)}) collective-permute-start(bf16[2,1,32,1792]{3,2,1,0:T(8,128)(2,1)S(1)} %slice.184), channel_id=1, source_target_pairs={{0,1},{1,0},{2,3},{3,2},{4,5},{5,4},{6,7},{7,6},{8,9},{9,8},{10,11... | collective-permute-start | bytes 688136 | tf_op jit(solution)/shard_map/ppermute | solution.py:264
  54.8 13.5 %collective-permute-start.17 = (bf16[2,2,32,1792]{3,2,1,0:T(8,128)(2,1)S(1)}, bf16[2,2,32,1792]{3,2,1,0:T(8,128)(2,1)S(1)}, u32[]{:S(2)}, u32[]{:S(2)}) collective-permute-start(bf16[2,2,32,1792]{3,2,1,0:T(8,128)(2,1)S(1)} %maximum_maximum_fusion.refs_0_), channel_id=1, source_target_pairs={{0,1},{1,0},{2,3},{3,2},{4,5},{5,4},{6,7},{7,6},{8,9},{9,8},{10,11... | collective-permute-start | bytes 1376264 | tf_op jit(solution)/shard_map/ppermute | solution.py:264
  54.9 14.2 %collective-permute-start.18 = (bf16[2,2,32,1792]{3,2,1,0:T(8,128)(2,1)S(1)}, bf16[2,2,32,1792]{3,2,1,0:T(8,128)(2,1)S(1)}, u32[]{:S(2)}, u32[]{:S(2)}) collective-permute-start(bf16[2,2,32,1792]{3,2,1,0:T(8,128)(2,1)S(1)} %maximum_maximum_fusion.refs_0_), channel_id=1, source_target_pairs={{0,2},{1,3},{2,0},{3,1},{4,6},{5,7},{6,4},{7,5},{8,10},{9,11},{10,... | collective-permute-start | bytes 1376264 | tf_op jit(solution)/shard_map/ppermute | solution.py:264
  59.7 18.5 %collective-permute-start.13 = (bf16[2,2,32,1792]{3,2,1,0:T(8,128)(2,1)S(1)}, bf16[2,2,32,1792]{3,2,1,0:T(8,128)(2,1)S(1)}, u32[]{:S(2)}, u32[]{:S(2)}) collective-permute-start(bf16[2,2,32,1792]{3,2,1,0:T(8,128)(2,1)S(1)} %maximum_maximum_fusion.1.refs_5_), channel_id=1, source_target_pairs={{0,1},{1,0},{2,3},{3,2},{4,5},{5,4},{6,7},{7,6},{8,9},{9,8},{10,11... | collective-permute-start | bytes 1376264 | tf_op jit(solution)/shard_map/ppermute | solution.py:264
  59.8 19.1 %collective-permute-start.15 = (bf16[2,2,32,1792]{3,2,1,0:T(8,128)(2,1)S(1)}, bf16[2,2,32,1792]{3,2,1,0:T(8,128)(2,1)S(1)}, u32[]{:S(2)}, u32[]{:S(2)}) collective-permute-start(bf16[2,2,32,1792]{3,2,1,0:T(8,128)(2,1)S(1)} %maximum_maximum_fusion.1.refs_5_), channel_id=1, source_target_pairs={{0,2},{1,3},{2,0},{3,1},{4,6},{5,7},{6,4},{7,5},{8,10},{9,11},{10,... | collective-permute-start | bytes 1376264 | tf_op jit(solution)/shard_map/ppermute | solution.py:264
  68.4 15.5 %collective-permute-start.19 = (bf16[1,2,32,1792]{3,2,1,0:T(8,128)(2,1)S(1)}, bf16[1,2,32,1792]{3,2,1,0:T(8,128)(2,1)S(1)}, u32[]{:S(2)}, u32[]{:S(2)}) collective-permute-start(bf16[1,2,32,1792]{3,2,1,0:T(8,128)(2,1)S(1)} %slice.152), channel_id=1, source_target_pairs={{0,2},{1,3},{2,0},{3,1},{4,6},{5,7},{6,4},{7,5},{8,10},{9,11},{10,... | collective-permute-start | bytes 688136 | tf_op jit(solution)/shard_map/ppermute | solution.py:264
  69.1 14.7 %collective-permute-start.20 = (bf16[1,2,32,1792]{3,2,1,0:T(8,128)(2,1)S(1)}, bf16[1,2,32,1792]{3,2,1,0:T(8,128)(2,1)S(1)}, u32[]{:S(2)}, u32[]{:S(2)}) collective-permute-start(bf16[1,2,32,1792]{3,2,1,0:T(8,128)(2,1)S(1)} %slice.153), channel_id=1, source_target_pairs={{0,1},{1,0},{2,3},{3,2},{4,5},{5,4},{6,7},{7,6},{8,9},{9,8},{10,11... | collective-permute-start | bytes 688136 | tf_op jit(solution)/shard_map/ppermute | solution.py:264
  78.2 9.8 %collective-permute-start.14 = (bf16[1,2,32,1792]{3,2,1,0:T(8,128)(2,1)S(1)}, bf16[1,2,32,1792]{3,2,1,0:T(8,128)(2,1)S(1)}, u32[]{:S(2)}, u32[]{:S(2)}) collective-permute-start(bf16[1,2,32,1792]{3,2,1,0:T(8,128)(2,1)S(1)} %slice.150), channel_id=1, source_target_pairs={{0,2},{1,3},{2,0},{3,1},{4,6},{5,7},{6,4},{7,5},{8,10},{9,11},{10,... | collective-permute-start | bytes 688136 | tf_op jit(solution)/shard_map/ppermute | solution.py:264
  78.9 9.1 %collective-permute-start.16 = (bf16[1,2,32,1792]{3,2,1,0:T(8,128)(2,1)S(1)}, bf16[1,2,32,1792]{3,2,1,0:T(8,128)(2,1)S(1)}, u32[]{:S(2)}, u32[]{:S(2)}) collective-permute-start(bf16[1,2,32,1792]{3,2,1,0:T(8,128)(2,1)S(1)} %slice.151), channel_id=1, source_target_pairs={{0,1},{1,0},{2,3},{3,2},{4,5},{5,4},{6,7},{7,6},{8,9},{9,8},{10,11... | collective-permute-start | bytes 688136 | tf_op jit(solution)/shard_map/ppermute | solution.py:264
  90.1 2.0 %collective-permute-start.21 = (bf16[512,512]{1,0:T(8,128)(2,1)S(1)}, bf16[512,512]{1,0:T(8,128)(2,1)S(1)}, u32[]{:S(2)}, u32[]{:S(2)}) collective-permute-start(bf16[512,512]{1,0:T(8,128)(2,1)S(1)} %get-tuple-element.47), channel_id=1, source_target_pairs={{0,4},{1,5},{2,6},{3,7},{4,0},{5,1},{6,2},{7,3},{8,12},{9,13},{10,... | collective-permute-start | bytes 1572872 | tf_op jit(solution)/shard_map/ppermute | solution.py:264
  92.3 8.4 %collective-permute-start.22 = (bf16[128,512]{1,0:T(8,128)(2,1)S(1)}, bf16[128,512]{1,0:T(8,128)(2,1)S(1)}, u32[]{:S(2)}, u32[]{:S(2)}) collective-permute-start(bf16[128,512]{1,0:T(8,128)(2,1)S(1)} %bitcast.130), channel_id=1, source_target_pairs={{0,1},{1,0},{2,3},{3,2},{4,5},{5,4},{6,7},{7,6},{8,9},{9,8},{10,11... | collective-permute-start | bytes 393224 | tf_op jit(solution)/shard_map/ppermute | solution.py:264
  92.7 8.1 %collective-permute-start.23 = (bf16[128,512]{1,0:T(8,128)(2,1)S(1)}, bf16[128,512]{1,0:T(8,128)(2,1)S(1)}, u32[]{:S(2)}, u32[]{:S(2)}) collective-permute-start(bf16[128,512]{1,0:T(8,128)(2,1)S(1)} %bitcast.129), channel_id=1, source_target_pairs={{0,2},{1,3},{2,0},{3,1},{4,6},{5,7},{6,4},{7,5},{8,10},{9,11},{10,... | collective-permute-start | bytes 393224 | tf_op jit(solution)/shard_map/ppermute | solution.py:264
  94.0 6.7 %collective-permute-start.24 = (bf16[128,512]{1,0:T(8,128)(2,1)S(1)}, bf16[128,512]{1,0:T(8,128)(2,1)S(1)}, u32[]{:S(2)}, u32[]{:S(2)}) collective-permute-start(bf16[128,512]{1,0:T(8,128)(2,1)S(1)} %bitcast.128), channel_id=1, source_target_pairs={{0,3},{1,2},{2,1},{3,0},{4,7},{5,6},{6,5},{7,4},{8,11},{9,10},{10,... | collective-permute-start | bytes 393224 | tf_op jit(solution)/shard_map/ppermute | solution.py:264
  100.9 11.0 %collective-permute-start.27 = (bf16[128,512]{1,0:T(8,128)(2,1)S(1)}, bf16[128,512]{1,0:T(8,128)(2,1)S(1)}, u32[]{:S(2)}, u32[]{:S(2)}) collective-permute-start(bf16[128,512]{1,0:T(8,128)(2,1)S(1)} %get-tuple-element.66), channel_id=1, source_target_pairs={{0,16},{1,17},{2,18},{3,19},{4,20},{5,21},{6,22},{7,23},{8,24},{9,... | collective-permute-start | bytes 393224 | tf_op jit(solution)/shard_map/ppermute | solution.py:264
  101.4 10.5 %collective-permute-start.26 = (bf16[128,512]{1,0:T(8,128)(2,1)S(1)}, bf16[128,512]{1,0:T(8,128)(2,1)S(1)}, u32[]{:S(2)}, u32[]{:S(2)}) collective-permute-start(bf16[128,512]{1,0:T(8,128)(2,1)S(1)} %get-tuple-element.67), channel_id=1, source_target_pairs={{0,24},{1,25},{2,26},{3,27},{4,28},{5,29},{6,30},{7,31},{8,16},{9,... | collective-permute-start | bytes 393224 | tf_op jit(solution)/shard_map/ppermute | solution.py:264
  103.1 8.9 %collective-permute-start.25 = (bf16[128,512]{1,0:T(8,128)(2,1)S(1)}, bf16[128,512]{1,0:T(8,128)(2,1)S(1)}, u32[]{:S(2)}, u32[]{:S(2)}) collective-permute-start(bf16[128,512]{1,0:T(8,128)(2,1)S(1)} %get-tuple-element.68), channel_id=1, source_target_pairs={{0,8},{1,9},{2,10},{3,11},{4,12},{5,13},{6,14},{7,15},{8,0},{9,1},... | collective-permute-start | bytes 393224 | tf_op jit(solution)/shard_map/ppermute | solution.py:264

commit v9 on v8

--- a/solution.py
+++ b/solution.py
@@ -117,37 +117,38 @@
     return out[0] if write else list(out)
 
 
-def own_half_kernel(half_ref, x_ref, w_ref, out_ref):
-    places, rows, feats = x_ref.shape
+def own_half_kernel(first, half_ref, x_ref, w_ref, out_ref):
+    _, places, chunk, _ = out_ref.shape
+    feats = x_ref.shape[2]
     at = pl.ds(pl.multiple_of(half_ref[0] * feats, feats), feats)
-    flat = x_ref[...].reshape(places * rows, feats)
+    flat = x_ref[:, pl.ds(first, chunk), :].reshape(places * chunk, feats)
     for g in range(2):
         out_ref[g] = jnp.dot(flat, w_ref[g, at, :], preferred_element_type=jnp.float32).reshape(
             out_ref.shape[1:]
         )
 
 
-def own_half(x, w_gu, half):
-    places, rows, _ = x.shape
+def own_half(x, w_gu, half, first, chunk):
+    places = x.shape[0]
     return pl.pallas_call(
-        own_half_kernel,
+        functools.partial(own_half_kernel, first),
         in_specs=[pl.BlockSpec(memory_space=pltpu.SMEM)] + [pl.BlockSpec(memory_space=pltpu.VMEM)] * 2,
         out_specs=pl.BlockSpec(memory_space=pltpu.VMEM),
-        out_shape=pltpu.VMEM((2, places, rows, w_gu.shape[2]), jnp.float32),
+        out_shape=pltpu.VMEM((2, places, chunk, w_gu.shape[2]), jnp.float32),
         compiler_params=pltpu.CompilerParams(vmem_limit_bytes=12 * 1024 * 1024),
     )(half, in_vmem(x), in_vmem(w_gu))
 
 
-def other_halves_kernel(count, first, chunk, aways, half_ref, *refs):
-    others, w_ref, sum_ref, outs = refs[:count], refs[count], refs[count + 1], refs[count + 2 :]
-    places, _, feats = others[0].shape
+def partial_sums_kernel(es, summed, first, chunk, aways, half_ref, *refs):
+    xs, w_ref, outs = refs[: len(es)], refs[len(es)], refs[-2 * len(aways) :]
+    places, _, feats = xs[0].shape
     part = chunk // len(aways)
     rows = pl.ds(first, chunk)
     for g in range(2):
-        total = sum_ref[g, :, rows, :].reshape(places * chunk, -1)
-        for e, other_ref in enumerate(others, 1):
+        total = refs[len(es) + 1][g].reshape(places * chunk, -1) if summed else 0.0
+        for e, x_ref in zip(es, xs):
             at = pl.ds(pl.multiple_of((half_ref[0] ^ e) * feats, feats), feats)
-            flat = other_ref[:, rows, :].reshape(places * chunk, feats)
+            flat = x_ref[:, rows, :].reshape(places * chunk, feats)
             total += jnp.dot(flat, w_ref[g, at, :], preferred_element_type=jnp.float32)
         for s, away in enumerate(aways):
             counts = [0, 0]
@@ -159,30 +160,31 @@
                 counts[kind] += 1
 
 
-def other_halves(others, w_gu, own, half, first, chunk, aways):
-    _, places, _, group = own.shape
+def partial_sums(xs, w_gu, summed, half, first, chunk, aways):
+    places, group = xs[max(xs)].shape[0], w_gu.shape[2]
     shape = (2, places // 2, chunk // len(aways), group)
+    operands = [*xs.values(), w_gu, *summed]
     outs = pl.pallas_call(
-        functools.partial(other_halves_kernel, len(others), first, chunk, aways),
+        functools.partial(partial_sums_kernel, list(xs), bool(summed), first, chunk, aways),
         in_specs=[pl.BlockSpec(memory_space=pltpu.SMEM)]
-        + [pl.BlockSpec(memory_space=pltpu.VMEM)] * (len(others) + 2),
+        + [pl.BlockSpec(memory_space=pltpu.VMEM)] * len(operands),
         out_specs=[pl.BlockSpec(memory_space=pltpu.VMEM)] * (2 * len(aways)),
         out_shape=[pltpu.VMEM(shape, jnp.bfloat16), pltpu.VMEM(shape, jnp.float32)] * len(aways),
         compiler_params=pltpu.CompilerParams(vmem_limit_bytes=16 * 1024 * 1024),
-    )(half, *[in_vmem(x) for x in others], in_vmem(w_gu), in_vmem(own))
+    )(half, *[in_vmem(x) for x in operands])
     return outs[0::2], outs[1::2]
 
 
-def input_grad_kernel(spots, outs, first, count, half_ref, *refs):
+def input_grad_kernel(spots, es, first, count, half_ref, *refs):
     pieces, w_ref = refs[: len(spots)], refs[len(spots)]
-    d_ref, *term_refs = refs[len(refs) - outs :]
+    d_ref, *term_refs = refs[len(refs) - 1 - len(es) :]
     for piece, row in zip(pieces, spots):
         streams, _, part, _ = piece.shape
         for s in range(streams):
             d_ref[:, pl.ds(row + s * part, part), :] = piece[s]
     mine = pl.ds(first, count)
     numbers = (((1,), (1,)), ((), ()))
-    for e, term_ref in enumerate(term_refs):
+    for e, term_ref in zip(es, term_refs):
         feats = term_ref.shape[1]
         at = pl.ds(pl.multiple_of((half_ref[0] ^ e) * feats, feats), feats)
         term = lax.dot_general(
@@ -193,19 +195,19 @@
         term_ref[mine, :] = term.astype(jnp.bfloat16)
 
 
-def input_grad(pieces, spots, w_gu, half, ratio, total, first, count, earlier, filled=()):
+def input_grad(pieces, spots, w_gu, half, es, ratio, total, first, count, earlier, filled=()):
     _, owned, group = w_gu.shape
     feats = owned // ratio
     operands = [half, *[in_vmem(x) for x in pieces], in_vmem(w_gu), *earlier, *[in_vmem(x) for x in filled]]
     return pl.pallas_call(
-        functools.partial(input_grad_kernel, spots, ratio + 1, first, count),
+        functools.partial(input_grad_kernel, spots, es, first, count),
         in_specs=[pl.BlockSpec(memory_space=pltpu.SMEM)]
         + [pl.BlockSpec(memory_space=pltpu.VMEM)] * (len(pieces) + 1)
         + [pl.BlockSpec(memory_space=pl.ANY)] * len(earlier)
         + [pl.BlockSpec(memory_space=pltpu.VMEM)] * len(filled),
-        out_specs=[pl.BlockSpec(memory_space=pltpu.VMEM)] * (ratio + 1),
+        out_specs=[pl.BlockSpec(memory_space=pltpu.VMEM)] * (len(es) + 1),
         out_shape=[pltpu.VMEM((2, total, group), jnp.bfloat16)]
-        + [pltpu.VMEM((total, feats), jnp.bfloat16)] * ratio,
+        + [pltpu.VMEM((total, feats), jnp.bfloat16)] * len(es),
         input_output_aliases={len(operands) - len(filled) + i: i for i in range(len(filled))},
         compiler_params=pltpu.CompilerParams(vmem_limit_bytes=16 * 1024 * 1024),
     )(*operands)
@@ -283,9 +285,11 @@
         keep = jnp.stack([x[:, i] for i in stay], axis=1).astype(jnp.float32)
         return keep, permute(out, lambda p, h, q: (p, h, q ^ bit))
 
-    def start_forward(c):
+    def start_forward(c, early):
         aways = [order[0] for order in orders]
-        out, keep = other_halves(others, w_gu, own, half, c * chunk, chunk, aways)
+        xs = dict(enumerate([mine] + others))
+        summed = [own_half(xs.pop(0), w_gu, half, c * chunk, chunk)] if early else []
+        out, keep = partial_sums(xs, w_gu, summed, half, c * chunk, chunk, aways)
         return keep, [
             permute(x, lambda p, h, q, bit=bit: (p, h, q ^ bit)) for x, bit in zip(out, aways)
         ]
@@ -328,8 +332,7 @@
     w_gu, marks = dequant(gate_up_codes, gate_up_scales, mask, (places, feats))
     mine = own_features(tokens, marks)
     others = [permute(mine, lambda p, h, q, e=e: (p, h ^ e, q)) for e in range(1, ratio)]
-    own = own_half(mine, w_gu, half)
-    (keep_a, got_a), (keep_b, got_b) = start_forward(0), start_forward(1)
+    (keep_a, got_a), (keep_b, got_b) = start_forward(0, False), start_forward(1, True)
     for step in range(1, len(bits)):
         keep_a, got_a = next_sums(keep_a, got_a, step)
         keep_b, got_b = next_sums(keep_b, got_b, step)
@@ -339,17 +342,20 @@
     pieces_a, spots_a = forward_rest(0, streams_a, direct_a)
     pieces_b, spots_b = forward_rest(1, streams_b, direct_b)
     near, total, count = 1 + len(bits), places * rows, places * chunk
-    filled = input_grad(
+    d_all, own_term, *other_terms = input_grad(
         pieces_b + pieces_a[:near],
         spots_b + spots_a[:near],
-        w_gu, half, ratio, total, count, count, hidden_a + hidden_b,
-    )
-    d_all, *term = input_grad(
-        pieces_a[near:], spots_a[near:], w_gu, half, ratio, total, 0, count, [], filled
-    )
-    summed = term[0].astype(jnp.float32)
-    for e in range(1, ratio):
-        got = permute(term[e], lambda p, h, q: (p, h ^ e, q))
+        w_gu, half, list(range(ratio)), ratio, total, count, count, hidden_a + hidden_b,
+    )
+    d_all, *other_terms = input_grad(
+        pieces_a[near:],
+        spots_a[near:],
+        w_gu, half, list(range(1, ratio)), ratio, total, 0, count, [], [d_all, *other_terms],
+    )
+    d_all, own_term = input_grad([], [], w_gu, half, [0], ratio, total, 0, count, [], [d_all, own_term])
+    summed = own_term.astype(jnp.float32)
+    for e, term in enumerate(other_terms, 1):
+        got = permute(term, lambda p, h, q: (p, h ^ e, q))
         summed = summed + got.astype(jnp.float32)
     summed = summed.reshape(CHUNKS, places, chunk, feats).astype(jnp.bfloat16)
     summed = [summed[:, k].reshape(rows, feats) for k in range(places)]

time: 113 us -> 111 us (0.982)
  waiting for transfers between devices: 48 us -> 46.1 us
    ppermute x28, waiting for transfers between devices: 48 us -> 46.1 us  [permute(): return lax.ppermute(x, AXES, pairs(move, places, ratio))]
    pallas_call x5 -> x6, Pallas kernels: 8.66 us -> 8.84 us  [the longest x3 4.53 us: input_grad(): pl.pallas_call(functools.partial(input_grad_kernel, spots, es, first, cou...]
  transfers between devices with their start and end apart: 28 -> 28, of which waited for: 16 -> 17; matrix products, arithmetic and copies ran while one was open for 2% -> 2% of each run, Pallas kernels for 16% -> 17%
where the time goes in v9:
time: 111 us
  waiting for transfers between devices  46.1 us (42%)
  starting transfers between devices  39.3 us (35%)
  Pallas kernels  21.6 us (19%)
  other arithmetic  3.15 us (3%)
    ppermute x28, waiting for transfers between devices, permute(): return lax.ppermute(x, AXES, pairs(move, places, ratio))  46.1 us
    ppermute x28, starting transfers between devices, permute(): return lax.ppermute(x, AXES, pairs(move, places, ratio))  39.3 us
    pallas_call x2, Pallas kernels, weight_grad(): pl.pallas_call(functools.partial(weight_grad_kernel, scale), grid=(owned...  9.32 us
    pallas_call x3, Pallas kernels, input_grad(): pl.pallas_call(functools.partial(input_grad_kernel, spots, es, first, cou...  4.53 us
    pallas_call x1, Pallas kernels, dequant(): pl.pallas_call(dequant_kernel, in_specs=[pl.BlockSpec(memory_space=pltpu....  3.38 us
    pallas_call x2, Pallas kernels, partial_sums(): pl.pallas_call(functools.partial(partial_sums_kernel, list(xs), bool(summ...  3.19 us
  transfers between devices with their start and end apart: 28, of which 17 were waited for; matrix products, arithmetic and copies ran while one was open for 2% of the time, Pallas kernels for 17%

profile of v9, /device:TPU:0, one launch (start us, length us, event | category | flops | bytes accessed | tf_op | source)
XLA Modules:
  0.0 111.3 jit_solution(16133315512606090052)
XLA Ops:
  0.6 3.1 %collective-permute-start = (bf16[128,512]{1,0:T(8,128)(2,1)}, bf16[128,512]{1,0:T(8,128)(2,1)S(1)}, u32[]{:S(2)}, u32[]{:S(2)}) collective-permute-start(bf16[128,512]{1,0:T(8,128)(2,1)} %param.4), channel_id=1, source_target_pairs={{0,8},{1,0},{2,24},{3,16},{4,12},{5,4},{6,28},{7,20},{8,9},{9,1},{... | collective-permute-start | bytes 393224 | tf_op jit(solution)/shard_map/ppermute | solution.py:266
  3.7 2.4 %collective-permute-start.1 = (bf16[128,512]{1,0:T(8,128)(2,1)}, bf16[128,512]{1,0:T(8,128)(2,1)S(1)}, u32[]{:S(2)}, u32[]{:S(2)}) collective-permute-start(bf16[128,512]{1,0:T(8,128)(2,1)} %param.4), channel_id=1, source_target_pairs={{0,16},{1,24},{2,0},{3,8},{4,20},{5,28},{6,4},{7,12},{8,17},{9,25}... | collective-permute-start | bytes 393224 | tf_op jit(solution)/shard_map/ppermute | solution.py:266
  6.1 2.5 %collective-permute-start.2 = (bf16[128,512]{1,0:T(8,128)(2,1)}, bf16[128,512]{1,0:T(8,128)(2,1)S(1)}, u32[]{:S(2)}, u32[]{:S(2)}) collective-permute-start(bf16[128,512]{1,0:T(8,128)(2,1)} %param.4), channel_id=1, source_target_pairs={{0,24},{1,16},{2,8},{3,0},{4,28},{5,20},{6,12},{7,4},{8,25},{9,17}... | collective-permute-start | bytes 393224 | tf_op jit(solution)/shard_map/ppermute | solution.py:266
  8.6 1.6 %collective-permute-start.3 = (bf16[128,512]{1,0:T(8,128)(2,1)}, bf16[128,512]{1,0:T(8,128)(2,1)S(1)}, u32[]{:S(2)}, u32[]{:S(2)}) collective-permute-start(bf16[128,512]{1,0:T(8,128)(2,1)} %param.4), channel_id=1, source_target_pairs={{0,0},{1,8},{2,16},{3,24},{4,4},{5,12},{6,20},{7,28},{8,1},{9,9},{... | collective-permute-start | bytes 393224 | tf_op jit(solution)/shard_map/ppermute | solution.py:266
  10.2 3.4 %shard_map.67 = (bf16[2,1024,1792]{2,1,0:T(8,128)(2,1)S(1)}, f32[4,512]{1,0:T(4,128)S(1)}) custom-call(s32[1]{0:T(128)} %bitcast.1.mask_ref, bf16[2,1024,1792]{2,1,0:T(8,128)(2,1)} %codes_ref.1, bf16[2,8,1792]{2,1,0:T(8,128)(2,1)} %scales_ref.1), custom_call_target="tpu_custom_call" | custom-call | tf_op jit(solution)/shard_map/pallas_call | solution.py:57
  16.9 9.1 %collective-permute-start.9 = (bf16[2,2,32,1792]{3,2,1,0:T(8,128)(2,1)S(1)}, bf16[2,2,32,1792]{3,2,1,0:T(8,128)(2,1)S(1)}, u32[]{:S(2)}, u32[]{:S(2)}) collective-permute-start(bf16[2,2,32,1792]{3,2,1,0:T(8,128)(2,1)S(1)} %get-tuple-element.38), channel_id=1, source_target_pairs={{0,1},{1,0},{2,3},{3,2},{4,5},{5,4},{6,7},{7,6},{8,9},{9,8},{10,11... | collective-permute-start | bytes 1376264 | tf_op jit(solution)/shard_map/ppermute | solution.py:266
  26.0 2.1 %shard_map.68 = (bf16[2,2,32,1792]{3,2,1,0:T(8,128)(2,1)S(1)}, f32[2,2,32,1792]{3,2,1,0:T(8,128)S(1)}, bf16[2,2,32,1792]{3,2,1,0:T(8,128)(2,1)S(1)}, f32[2,2,32,1792]{3,2,1,0:T(8,128)S(1)}) custom-call(s32[1]{0:T(128)} %bitcast.half_ref.index_ref, bf16[4,128,512]{2,1,0:T(8,128)(2,1)S(1)} %pad_maximum_fusion.refs_0_.x_ref, ...), custom_call_target="tpu_custom_call" | custom-call | tf_op jit(solution)/shard_map/pallas_call | solution.py:167
  28.1 2.1 %collective-permute-start.7 = (bf16[2,2,32,1792]{3,2,1,0:T(8,128)(2,1)S(1)}, bf16[2,2,32,1792]{3,2,1,0:T(8,128)(2,1)S(1)}, u32[]{:S(2)}, u32[]{:S(2)}) collective-permute-start(bf16[2,2,32,1792]{3,2,1,0:T(8,128)(2,1)S(1)} %get-tuple-element.36), channel_id=1, source_target_pairs={{0,2},{1,3},{2,0},{3,1},{4,6},{5,7},{6,4},{7,5},{8,10},{9,11},{10,... | collective-permute-start | bytes 1376264 | tf_op jit(solution)/shard_map/ppermute | solution.py:266
  30.3 7.0 %collective-permute-done.9 = bf16[2,2,32,1792]{3,2,1,0:T(8,128)(2,1)S(1)} collective-permute-done((bf16[2,2,32,1792]{3,2,1,0:T(8,128)(2,1)S(1)}, bf16[2,2,32,1792]{3,2,1,0:T(8,128)(2,1)S(1)}, u32[]{:S(2)}, u32[]{:S(2)}) %collective-permute-start.9) | collective-permute-done | bytes 458784 | tf_op jit(solution)/shard_map/ppermute | solution.py:266
  37.5 1.8 %collective-permute-start.10 = (bf16[2,1,32,1792]{3,2,1,0:T(8,128)(2,1)S(1)}, bf16[2,1,32,1792]{3,2,1,0:T(8,128)(2,1)S(1)}, u32[]{:S(2)}, u32[]{:S(2)}) collective-permute-start(bf16[2,1,32,1792]{3,2,1,0:T(8,128)(2,1)S(1)} %slice.183), channel_id=1, source_target_pairs={{0,2},{1,3},{2,0},{3,1},{4,6},{5,7},{6,4},{7,5},{8,10},{9,11},{10,... | collective-permute-start | bytes 688136 | tf_op jit(solution)/shard_map/ppermute | solution.py:266
  39.8 7.4 %collective-permute-done.5 = bf16[2,2,32,1792]{3,2,1,0:T(8,128)(2,1)S(1)} collective-permute-done((bf16[2,2,32,1792]{3,2,1,0:T(8,128)(2,1)S(1)}, bf16[2,2,32,1792]{3,2,1,0:T(8,128)(2,1)S(1)}, u32[]{:S(2)}, u32[]{:S(2)}) %collective-permute-start.5) | collective-permute-done | bytes 458784 | tf_op jit(solution)/shard_map/ppermute | solution.py:266
  47.3 1.8 %collective-permute-start.6 = (bf16[2,1,32,1792]{3,2,1,0:T(8,128)(2,1)S(1)}, bf16[2,1,32,1792]{3,2,1,0:T(8,128)(2,1)S(1)}, u32[]{:S(2)}, u32[]{:S(2)}) collective-permute-start(bf16[2,1,32,1792]{3,2,1,0:T(8,128)(2,1)S(1)} %slice.185), channel_id=1, source_target_pairs={{0,2},{1,3},{2,0},{3,1},{4,6},{5,7},{6,4},{7,5},{8,10},{9,11},{10,... | collective-permute-start | bytes 688136 | tf_op jit(solution)/shard_map/ppermute | solution.py:266
  49.6 4.5 %collective-permute-done.10 = bf16[2,1,32,1792]{3,2,1,0:T(8,128)(2,1)S(1)} collective-permute-done((bf16[2,1,32,1792]{3,2,1,0:T(8,128)(2,1)S(1)}, bf16[2,1,32,1792]{3,2,1,0:T(8,128)(2,1)S(1)}, u32[]{:S(2)}, u32[]{:S(2)}) %collective-permute-start.10) | collective-permute-done | bytes 229408 | tf_op jit(solution)/shard_map/ppermute | solution.py:266
  54.8 1.7 %collective-permute-start.18 = (bf16[2,2,32,1792]{3,2,1,0:T(8,128)(2,1)S(1)}, bf16[2,2,32,1792]{3,2,1,0:T(8,128)(2,1)S(1)}, u32[]{:S(2)}, u32[]{:S(2)}) collective-permute-start(bf16[2,2,32,1792]{3,2,1,0:T(8,128)(2,1)S(1)} %maximum_maximum_fusion.refs_0_), channel_id=1, source_target_pairs={{0,2},{1,3},{2,0},{3,1},{4,6},{5,7},{6,4},{7,5},{8,10},{9,11},{10,... | collective-permute-start | bytes 1376264 | tf_op jit(solution)/shard_map/ppermute | solution.py:266
  56.4 2.7 %collective-permute-done.6 = bf16[2,1,32,1792]{3,2,1,0:T(8,128)(2,1)S(1)} collective-permute-done((bf16[2,1,32,1792]{3,2,1,0:T(8,128)(2,1)S(1)}, bf16[2,1,32,1792]{3,2,1,0:T(8,128)(2,1)S(1)}, u32[]{:S(2)}, u32[]{:S(2)}) %collective-permute-start.6) | collective-permute-done | bytes 229408 | tf_op jit(solution)/shard_map/ppermute | solution.py:266
  59.7 1.7 %collective-permute-start.15 = (bf16[2,2,32,1792]{3,2,1,0:T(8,128)(2,1)S(1)}, bf16[2,2,32,1792]{3,2,1,0:T(8,128)(2,1)S(1)}, u32[]{:S(2)}, u32[]{:S(2)}) collective-permute-start(bf16[2,2,32,1792]{3,2,1,0:T(8,128)(2,1)S(1)} %maximum_maximum_fusion.1.refs_5_), channel_id=1, source_target_pairs={{0,2},{1,3},{2,0},{3,1},{4,6},{5,7},{6,4},{7,5},{8,10},{9,11},{10,... | collective-permute-start | bytes 1376264 | tf_op jit(solution)/shard_map/ppermute | solution.py:266
  61.3 6.9 %collective-permute-done.17.refs_1_ = bf16[2,2,32,1792]{3,2,1,0:T(8,128)(2,1)S(1)} collective-permute-done((bf16[2,2,32,1792]{3,2,1,0:T(8,128)(2,1)S(1)}, bf16[2,2,32,1792]{3,2,1,0:T(8,128)(2,1)S(1)}, u32[]{:S(2)}, u32[]{:S(2)}) %collective-permute-start.17) | collective-permute-done | bytes 458784 | tf_op jit(solution)/shard_map/ppermute | solution.py:266
  68.9 1.3 %collective-permute-start.20 = (bf16[1,2,32,1792]{3,2,1,0:T(8,128)(2,1)S(1)}, bf16[1,2,32,1792]{3,2,1,0:T(8,128)(2,1)S(1)}, u32[]{:S(2)}, u32[]{:S(2)}) collective-permute-start(bf16[1,2,32,1792]{3,2,1,0:T(8,128)(2,1)S(1)} %slice.153), channel_id=1, source_target_pairs={{0,1},{1,0},{2,3},{3,2},{4,5},{5,4},{6,7},{7,6},{8,9},{9,8},{10,11... | collective-permute-start | bytes 688136 | tf_op jit(solution)/shard_map/ppermute | solution.py:266
  70.3 7.7 %collective-permute-done.13.refs_6_ = bf16[2,2,32,1792]{3,2,1,0:T(8,128)(2,1)S(1)} collective-permute-done((bf16[2,2,32,1792]{3,2,1,0:T(8,128)(2,1)S(1)}, bf16[2,2,32,1792]{3,2,1,0:T(8,128)(2,1)S(1)}, u32[]{:S(2)}, u32[]{:S(2)}) %collective-permute-start.13) | collective-permute-done | bytes 458784 | tf_op jit(solution)/shard_map/ppermute | solution.py:266
  78.8 1.3 %collective-permute-start.16 = (bf16[1,2,32,1792]{3,2,1,0:T(8,128)(2,1)S(1)}, bf16[1,2,32,1792]{3,2,1,0:T(8,128)(2,1)S(1)}, u32[]{:S(2)}, u32[]{:S(2)}) collective-permute-start(bf16[1,2,32,1792]{3,2,1,0:T(8,128)(2,1)S(1)} %slice.151), channel_id=1, source_target_pairs={{0,1},{1,0},{2,3},{3,2},{4,5},{5,4},{6,7},{7,6},{8,9},{9,8},{10,11... | collective-permute-start | bytes 688136 | tf_op jit(solution)/shard_map/ppermute | solution.py:266
  80.1 3.5 %collective-permute-done.19.refs_3_ = bf16[1,2,32,1792]{3,2,1,0:T(8,128)(2,1)S(1)} collective-permute-done((bf16[1,2,32,1792]{3,2,1,0:T(8,128)(2,1)S(1)}, bf16[1,2,32,1792]{3,2,1,0:T(8,128)(2,1)S(1)}, u32[]{:S(2)}, u32[]{:S(2)}) %collective-permute-start.19) | collective-permute-done | bytes 229408 | tf_op jit(solution)/shard_map/ppermute | solution.py:266
  83.7 2.2 %shard_map.72 = (bf16[2,512,1792]{2,1,0:T(8,128)(2,1)S(1)}, bf16[512,512]{1,0:T(8,128)(2,1)S(1)}, bf16[512,512]{1,0:T(8,128)(2,1)S(1)}) custom-call(s32[1]{0:T(128)} %bitcast.half_ref.index_ref, bf16[2,2,32,1792]{3,2,1,0:T(8,128)(2,1)S(1)} %maximum_maximum_fusion.refs_0_, bf16[2,2,32,1792]{3,2,1,0:T(8,128)(2,1)S(1)} %collective-permute-done.17.refs_1_, ...), custom_call_target="tpu_custom_call" | custom-call | tf_op jit(solution)/shard_map/pallas_call | solution.py:202
  85.9 1.5 %collective-permute-done.14.refs_0_ = bf16[1,2,32,1792]{3,2,1,0:T(8,128)(2,1)S(1)} collective-permute-done((bf16[1,2,32,1792]{3,2,1,0:T(8,128)(2,1)S(1)}, bf16[1,2,32,1792]{3,2,1,0:T(8,128)(2,1)S(1)}, u32[]{:S(2)}, u32[]{:S(2)}) %collective-permute-start.14) | collective-permute-done | bytes 229408 | tf_op jit(solution)/shard_map/ppermute | solution.py:266
  87.5 1.1 %shard_map.73 = (bf16[2,512,1792]{2,1,0:T(8,128)(2,1)S(1)}, bf16[512,512]{1,0:T(8,128)(2,1)S(1)}) custom-call(s32[1]{0:T(128)} %bitcast.half_ref.index_ref, bf16[1,2,32,1792]{3,2,1,0:T(8,128)(2,1)S(1)} %collective-permute-done.14.refs_0_, bf16[1,2,32,1792]{3,2,1,0:T(8,128)(2,1)S(1)} %collective-permute-done.16.refs_1_, ...), custom_call_target="tpu_custom_call", output_to_operand_aliasing={{0}: (4, {}), {1}: (5, {})} | custom-call | tf_op jit(solution)/shard_map/pallas_call | solution.py:202
  88.7 1.1 %shard_map.74 = (bf16[2,512,1792]{2,1,0:T(8,128)(2,1)S(1)}, bf16[512,512]{1,0:T(8,128)(2,1)S(1)}) custom-call(s32[1]{0:T(128)} %bitcast.half_ref.index_ref, bf16[2,1024,1792]{2,1,0:T(8,128)(2,1)S(1)} %get-tuple-element.32.refs_2_.w_ref.refs_1_.refs_8_.refs_0_, ...), custom_call_target="tpu_custom_call", output_to_operand_aliasing={{0}: (2, {}), {1}: (3, {})} | custom-call | tf_op jit(solution)/shard_map/pallas_call | solution.py:202
  91.2 1.3 %collective-permute-start.23 = (bf16[128,512]{1,0:T(8,128)(2,1)S(1)}, bf16[128,512]{1,0:T(8,128)(2,1)S(1)}, u32[]{:S(2)}, u32[]{:S(2)}) collective-permute-start(bf16[128,512]{1,0:T(8,128)(2,1)S(1)} %bitcast.129), channel_id=1, source_target_pairs={{0,2},{1,3},{2,0},{3,1},{4,6},{5,7},{6,4},{7,5},{8,10},{9,11},{10,... | collective-permute-start | bytes 393224 | tf_op jit(solution)/shard_map/ppermute | solution.py:266
  92.5 1.8 %collective-permute-start.24 = (bf16[128,512]{1,0:T(8,128)(2,1)S(1)}, bf16[128,512]{1,0:T(8,128)(2,1)S(1)}, u32[]{:S(2)}, u32[]{:S(2)}) collective-permute-start(bf16[128,512]{1,0:T(8,128)(2,1)S(1)} %bitcast.128), channel_id=1, source_target_pairs={{0,3},{1,2},{2,1},{3,0},{4,7},{5,6},{6,5},{7,4},{8,11},{9,10},{10,... | collective-permute-start | bytes 393224 | tf_op jit(solution)/shard_map/ppermute | solution.py:266
  94.4 4.7 %shard_map.75 = (f32[2,1024,1792]{2,1,0:T(8,128)}, f32[4,512]{1,0:T(4,128)S(1)}) custom-call(bf16[512,1024]{1,0:T(8,128)(2,1)S(1)} %bitcast.124, bf16[2,512,1792]{2,1,0:T(8,128)(2,1)S(1)} %get-tuple-element.47.d_ref, s32[1]{0:T(128)} %bitcast.1.mask_ref, bf16[16,512]{1,0:T(8,128)(2,1)S(1)} %slice.155.refs_0_), custom_call_target="tpu_custom_call" | custom-call | tf_op jit(solution)/shard_map/pallas_call | solution.py:229
  99.8 1.8 %collective-permute-start.26 = (bf16[128,512]{1,0:T(8,128)(2,1)S(1)}, bf16[128,512]{1,0:T(8,128)(2,1)S(1)}, u32[]{:S(2)}, u32[]{:S(2)}) collective-permute-start(bf16[128,512]{1,0:T(8,128)(2,1)S(1)} %get-tuple-element.69), channel_id=1, source_target_pairs={{0,24},{1,25},{2,26},{3,27},{4,28},{5,29},{6,30},{7,31},{8,16},{9,... | collective-permute-start | bytes 393224 | tf_op jit(solution)/shard_map/ppermute | solution.py:266
  101.6 1.3 %collective-permute-start.25 = (bf16[128,512]{1,0:T(8,128)(2,1)S(1)}, bf16[128,512]{1,0:T(8,128)(2,1)S(1)}, u32[]{:S(2)}, u32[]{:S(2)}) collective-permute-start(bf16[128,512]{1,0:T(8,128)(2,1)S(1)} %get-tuple-element.70), channel_id=1, source_target_pairs={{0,8},{1,9},{2,10},{3,11},{4,12},{5,13},{6,14},{7,15},{8,0},{9,1},... | collective-permute-start | bytes 393224 | tf_op jit(solution)/shard_map/ppermute | solution.py:266
  103.7 4.6 %shard_map.76 = (f32[2,1024,1792]{2,1,0:T(8,128)}, f32[4,512]{1,0:T(4,128)}) custom-call(bf16[512,1024]{1,0:T(8,128)(2,1)S(1)} %bitcast.125, bf16[2,512,1792]{2,1,0:T(8,128)(2,1)S(1)} %get-tuple-element.47.d_ref, s32[1]{0:T(128)} %bitcast.1.mask_ref, bf16[16,512]{1,0:T(8,128)(2,1)S(1)} %slice.159.refs_0_, ...), custom_call_target="tpu_custom_call", output_to_operand_aliasing={{0}: (4, {})} | custom-call | tf_op jit(solution)/shard_map/pallas_call | solution.py:229
  108.4 2.0 %collective-permute-done.27 = bf16[128,512]{1,0:T(8,128)(2,1)S(1)} collective-permute-done((bf16[128,512]{1,0:T(8,128)(2,1)S(1)}, bf16[128,512]{1,0:T(8,128)(2,1)S(1)}, u32[]{:S(2)}, u32[]{:S(2)}) %collective-permute-start.27) | collective-permute-done | bytes 131104 | tf_op jit(solution)/shard_map/ppermute | solution.py:266
  (66 shorter events, 11.2 us)
Async XLA Ops:
  0.6 12.9 %collective-permute-start = (bf16[128,512]{1,0:T(8,128)(2,1)}, bf16[128,512]{1,0:T(8,128)(2,1)S(1)}, u32[]{:S(2)}, u32[]{:S(2)}) collective-permute-start(bf16[128,512]{1,0:T(8,128)(2,1)} %param.4), channel_id=1, source_target_pairs={{0,8},{1,0},{2,24},{3,16},{4,12},{5,4},{6,28},{7,20},{8,9},{9,1},{... | collective-permute-start | bytes 393224 | tf_op jit(solution)/shard_map/ppermute | solution.py:266
  3.7 9.9 %collective-permute-start.1 = (bf16[128,512]{1,0:T(8,128)(2,1)}, bf16[128,512]{1,0:T(8,128)(2,1)S(1)}, u32[]{:S(2)}, u32[]{:S(2)}) collective-permute-start(bf16[128,512]{1,0:T(8,128)(2,1)} %param.4), channel_id=1, source_target_pairs={{0,16},{1,24},{2,0},{3,8},{4,20},{5,28},{6,4},{7,12},{8,17},{9,25}... | collective-permute-start | bytes 393224 | tf_op jit(solution)/shard_map/ppermute | solution.py:266
  6.1 7.5 %collective-permute-start.2 = (bf16[128,512]{1,0:T(8,128)(2,1)}, bf16[128,512]{1,0:T(8,128)(2,1)S(1)}, u32[]{:S(2)}, u32[]{:S(2)}) collective-permute-start(bf16[128,512]{1,0:T(8,128)(2,1)} %param.4), channel_id=1, source_target_pairs={{0,24},{1,16},{2,8},{3,0},{4,28},{5,20},{6,12},{7,4},{8,25},{9,17}... | collective-permute-start | bytes 393224 | tf_op jit(solution)/shard_map/ppermute | solution.py:266
  8.6 5.0 %collective-permute-start.3 = (bf16[128,512]{1,0:T(8,128)(2,1)}, bf16[128,512]{1,0:T(8,128)(2,1)S(1)}, u32[]{:S(2)}, u32[]{:S(2)}) collective-permute-start(bf16[128,512]{1,0:T(8,128)(2,1)} %param.4), channel_id=1, source_target_pairs={{0,0},{1,8},{2,16},{3,24},{4,4},{5,12},{6,20},{7,28},{8,1},{9,9},{... | collective-permute-start | bytes 393224 | tf_op jit(solution)/shard_map/ppermute | solution.py:266
  13.8 2.0 %collective-permute-start.4 = (bf16[4,128,512]{2,1,0:T(8,128)(2,1)S(1)}, bf16[4,128,512]{2,1,0:T(8,128)(2,1)S(1)}, u32[]{:S(2)}, u32[]{:S(2)}) collective-permute-start(bf16[4,128,512]{2,1,0:T(8,128)(2,1)S(1)} %pad_maximum_fusion.refs_0_.x_ref), channel_id=1, source_target_pairs={{0,4},{1,5},{2,6},{3,7},{4,0},{5,1},{6,2},{7,3},{8,12},{9,13},{10,... | collective-permute-start | bytes 1572872 | tf_op jit(solution)/shard_map/ppermute | solution.py:266
  16.9 20.5 %collective-permute-start.9 = (bf16[2,2,32,1792]{3,2,1,0:T(8,128)(2,1)S(1)}, bf16[2,2,32,1792]{3,2,1,0:T(8,128)(2,1)S(1)}, u32[]{:S(2)}, u32[]{:S(2)}) collective-permute-start(bf16[2,2,32,1792]{3,2,1,0:T(8,128)(2,1)S(1)} %get-tuple-element.38), channel_id=1, source_target_pairs={{0,1},{1,0},{2,3},{3,2},{4,5},{5,4},{6,7},{7,6},{8,9},{9,8},{10,11... | collective-permute-start | bytes 1376264 | tf_op jit(solution)/shard_map/ppermute | solution.py:266
  26.0 13.4 %collective-permute-start.11 = (bf16[2,2,32,1792]{3,2,1,0:T(8,128)(2,1)S(1)}, bf16[2,2,32,1792]{3,2,1,0:T(8,128)(2,1)S(1)}, u32[]{:S(2)}, u32[]{:S(2)}) collective-permute-start(bf16[2,2,32,1792]{3,2,1,0:T(8,128)(2,1)S(1)} %get-tuple-element.40), channel_id=1, source_target_pairs={{0,2},{1,3},{2,0},{3,1},{4,6},{5,7},{6,4},{7,5},{8,10},{9,11},{10,... | collective-permute-start | bytes 1376264 | tf_op jit(solution)/shard_map/ppermute | solution.py:266
  28.1 26.2 %copy-start = (bf16[128,1792]{1,0:T(8,128)(2,1)S(1)}, bf16[128,1792]{1,0:T(8,128)(2,1)}, u32[]{:S(2)}) copy-start(bf16[128,1792]{1,0:T(8,128)(2,1)} %param.7) | copy-start | bytes 1376260
  28.1 21.1 %collective-permute-start.7 = (bf16[2,2,32,1792]{3,2,1,0:T(8,128)(2,1)S(1)}, bf16[2,2,32,1792]{3,2,1,0:T(8,128)(2,1)S(1)}, u32[]{:S(2)}, u32[]{:S(2)}) collective-permute-start(bf16[2,2,32,1792]{3,2,1,0:T(8,128)(2,1)S(1)} %get-tuple-element.36), channel_id=1, source_target_pairs={{0,2},{1,3},{2,0},{3,1},{4,6},{5,7},{6,4},{7,5},{8,10},{9,11},{10,... | collective-permute-start | bytes 1376264 | tf_op jit(solution)/shard_map/ppermute | solution.py:266
  30.2 17.0 %collective-permute-start.5 = (bf16[2,2,32,1792]{3,2,1,0:T(8,128)(2,1)S(1)}, bf16[2,2,32,1792]{3,2,1,0:T(8,128)(2,1)S(1)}, u32[]{:S(2)}, u32[]{:S(2)}) collective-permute-start(bf16[2,2,32,1792]{3,2,1,0:T(8,128)(2,1)S(1)} %get-tuple-element.34), channel_id=1, source_target_pairs={{0,1},{1,0},{2,3},{3,2},{4,5},{5,4},{6,7},{7,6},{8,9},{9,8},{10,11... | collective-permute-start | bytes 1376264 | tf_op jit(solution)/shard_map/ppermute | solution.py:266
  37.5 16.7 %collective-permute-start.10 = (bf16[2,1,32,1792]{3,2,1,0:T(8,128)(2,1)S(1)}, bf16[2,1,32,1792]{3,2,1,0:T(8,128)(2,1)S(1)}, u32[]{:S(2)}, u32[]{:S(2)}) collective-permute-start(bf16[2,1,32,1792]{3,2,1,0:T(8,128)(2,1)S(1)} %slice.183), channel_id=1, source_target_pairs={{0,2},{1,3},{2,0},{3,1},{4,6},{5,7},{6,4},{7,5},{8,10},{9,11},{10,... | collective-permute-start | bytes 688136 | tf_op jit(solution)/shard_map/ppermute | solution.py:266
  39.5 14.7 %collective-permute-start.12 = (bf16[2,1,32,1792]{3,2,1,0:T(8,128)(2,1)S(1)}, bf16[2,1,32,1792]{3,2,1,0:T(8,128)(2,1)S(1)}, u32[]{:S(2)}, u32[]{:S(2)}) collective-permute-start(bf16[2,1,32,1792]{3,2,1,0:T(8,128)(2,1)S(1)} %slice.182), channel_id=1, source_target_pairs={{0,1},{1,0},{2,3},{3,2},{4,5},{5,4},{6,7},{7,6},{8,9},{9,8},{10,11... | collective-permute-start | bytes 688136 | tf_op jit(solution)/shard_map/ppermute | solution.py:266
  47.3 11.8 %collective-permute-start.6 = (bf16[2,1,32,1792]{3,2,1,0:T(8,128)(2,1)S(1)}, bf16[2,1,32,1792]{3,2,1,0:T(8,128)(2,1)S(1)}, u32[]{:S(2)}, u32[]{:S(2)}) collective-permute-start(bf16[2,1,32,1792]{3,2,1,0:T(8,128)(2,1)S(1)} %slice.185), channel_id=1, source_target_pairs={{0,2},{1,3},{2,0},{3,1},{4,6},{5,7},{6,4},{7,5},{8,10},{9,11},{10,... | collective-permute-start | bytes 688136 | tf_op jit(solution)/shard_map/ppermute | solution.py:266
  49.4 9.7 %collective-permute-start.8 = (bf16[2,1,32,1792]{3,2,1,0:T(8,128)(2,1)S(1)}, bf16[2,1,32,1792]{3,2,1,0:T(8,128)(2,1)S(1)}, u32[]{:S(2)}, u32[]{:S(2)}) collective-permute-start(bf16[2,1,32,1792]{3,2,1,0:T(8,128)(2,1)S(1)} %slice.184), channel_id=1, source_target_pairs={{0,1},{1,0},{2,3},{3,2},{4,5},{5,4},{6,7},{7,6},{8,9},{9,8},{10,11... | collective-permute-start | bytes 688136 | tf_op jit(solution)/shard_map/ppermute | solution.py:266
  54.7 13.5 %collective-permute-start.17 = (bf16[2,2,32,1792]{3,2,1,0:T(8,128)(2,1)S(1)}, bf16[2,2,32,1792]{3,2,1,0:T(8,128)(2,1)S(1)}, u32[]{:S(2)}, u32[]{:S(2)}) collective-permute-start(bf16[2,2,32,1792]{3,2,1,0:T(8,128)(2,1)S(1)} %maximum_maximum_fusion.refs_0_), channel_id=1, source_target_pairs={{0,1},{1,0},{2,3},{3,2},{4,5},{5,4},{6,7},{7,6},{8,9},{9,8},{10,11... | collective-permute-start | bytes 1376264 | tf_op jit(solution)/shard_map/ppermute | solution.py:266
  54.8 14.2 %collective-permute-start.18 = (bf16[2,2,32,1792]{3,2,1,0:T(8,128)(2,1)S(1)}, bf16[2,2,32,1792]{3,2,1,0:T(8,128)(2,1)S(1)}, u32[]{:S(2)}, u32[]{:S(2)}) collective-permute-start(bf16[2,2,32,1792]{3,2,1,0:T(8,128)(2,1)S(1)} %maximum_maximum_fusion.refs_0_), channel_id=1, source_target_pairs={{0,2},{1,3},{2,0},{3,1},{4,6},{5,7},{6,4},{7,5},{8,10},{9,11},{10,... | collective-permute-start | bytes 1376264 | tf_op jit(solution)/shard_map/ppermute | solution.py:266
  59.5 18.5 %collective-permute-start.13 = (bf16[2,2,32,1792]{3,2,1,0:T(8,128)(2,1)S(1)}, bf16[2,2,32,1792]{3,2,1,0:T(8,128)(2,1)S(1)}, u32[]{:S(2)}, u32[]{:S(2)}) collective-permute-start(bf16[2,2,32,1792]{3,2,1,0:T(8,128)(2,1)S(1)} %maximum_maximum_fusion.1.refs_5_), channel_id=1, source_target_pairs={{0,1},{1,0},{2,3},{3,2},{4,5},{5,4},{6,7},{7,6},{8,9},{9,8},{10,11... | collective-permute-start | bytes 1376264 | tf_op jit(solution)/shard_map/ppermute | solution.py:266
  59.7 19.1 %collective-permute-start.15 = (bf16[2,2,32,1792]{3,2,1,0:T(8,128)(2,1)S(1)}, bf16[2,2,32,1792]{3,2,1,0:T(8,128)(2,1)S(1)}, u32[]{:S(2)}, u32[]{:S(2)}) collective-permute-start(bf16[2,2,32,1792]{3,2,1,0:T(8,128)(2,1)S(1)} %maximum_maximum_fusion.1.refs_5_), channel_id=1, source_target_pairs={{0,2},{1,3},{2,0},{3,1},{4,6},{5,7},{6,4},{7,5},{8,10},{9,11},{10,... | collective-permute-start | bytes 1376264 | tf_op jit(solution)/shard_map/ppermute | solution.py:266
  68.2 15.5 %collective-permute-start.19 = (bf16[1,2,32,1792]{3,2,1,0:T(8,128)(2,1)S(1)}, bf16[1,2,32,1792]{3,2,1,0:T(8,128)(2,1)S(1)}, u32[]{:S(2)}, u32[]{:S(2)}) collective-permute-start(bf16[1,2,32,1792]{3,2,1,0:T(8,128)(2,1)S(1)} %slice.152), channel_id=1, source_target_pairs={{0,2},{1,3},{2,0},{3,1},{4,6},{5,7},{6,4},{7,5},{8,10},{9,11},{10,... | collective-permute-start | bytes 688136 | tf_op jit(solution)/shard_map/ppermute | solution.py:266
  68.9 14.7 %collective-permute-start.20 = (bf16[1,2,32,1792]{3,2,1,0:T(8,128)(2,1)S(1)}, bf16[1,2,32,1792]{3,2,1,0:T(8,128)(2,1)S(1)}, u32[]{:S(2)}, u32[]{:S(2)}) collective-permute-start(bf16[1,2,32,1792]{3,2,1,0:T(8,128)(2,1)S(1)} %slice.153), channel_id=1, source_target_pairs={{0,1},{1,0},{2,3},{3,2},{4,5},{5,4},{6,7},{7,6},{8,9},{9,8},{10,11... | collective-permute-start | bytes 688136 | tf_op jit(solution)/shard_map/ppermute | solution.py:266
  78.0 9.4 %collective-permute-start.14 = (bf16[1,2,32,1792]{3,2,1,0:T(8,128)(2,1)S(1)}, bf16[1,2,32,1792]{3,2,1,0:T(8,128)(2,1)S(1)}, u32[]{:S(2)}, u32[]{:S(2)}) collective-permute-start(bf16[1,2,32,1792]{3,2,1,0:T(8,128)(2,1)S(1)} %slice.150), channel_id=1, source_target_pairs={{0,2},{1,3},{2,0},{3,1},{4,6},{5,7},{6,4},{7,5},{8,10},{9,11},{10,... | collective-permute-start | bytes 688136 | tf_op jit(solution)/shard_map/ppermute | solution.py:266
  78.8 8.7 %collective-permute-start.16 = (bf16[1,2,32,1792]{3,2,1,0:T(8,128)(2,1)S(1)}, bf16[1,2,32,1792]{3,2,1,0:T(8,128)(2,1)S(1)}, u32[]{:S(2)}, u32[]{:S(2)}) collective-permute-start(bf16[1,2,32,1792]{3,2,1,0:T(8,128)(2,1)S(1)} %slice.151), channel_id=1, source_target_pairs={{0,1},{1,0},{2,3},{3,2},{4,5},{5,4},{6,7},{7,6},{8,9},{9,8},{10,11... | collective-permute-start | bytes 688136 | tf_op jit(solution)/shard_map/ppermute | solution.py:266
  88.6 2.0 %collective-permute-start.21 = (bf16[512,512]{1,0:T(8,128)(2,1)S(1)}, bf16[512,512]{1,0:T(8,128)(2,1)S(1)}, u32[]{:S(2)}, u32[]{:S(2)}) collective-permute-start(bf16[512,512]{1,0:T(8,128)(2,1)S(1)} %get-tuple-element.49), channel_id=1, source_target_pairs={{0,4},{1,5},{2,6},{3,7},{4,0},{5,1},{6,2},{7,3},{8,12},{9,13},{10,... | collective-permute-start | bytes 1572872 | tf_op jit(solution)/shard_map/ppermute | solution.py:266
  90.8 8.4 %collective-permute-start.22 = (bf16[128,512]{1,0:T(8,128)(2,1)S(1)}, bf16[128,512]{1,0:T(8,128)(2,1)S(1)}, u32[]{:S(2)}, u32[]{:S(2)}) collective-permute-start(bf16[128,512]{1,0:T(8,128)(2,1)S(1)} %bitcast.130), channel_id=1, source_target_pairs={{0,1},{1,0},{2,3},{3,2},{4,5},{5,4},{6,7},{7,6},{8,9},{9,8},{10,11... | collective-permute-start | bytes 393224 | tf_op jit(solution)/shard_map/ppermute | solution.py:266
  91.2 8.1 %collective-permute-start.23 = (bf16[128,512]{1,0:T(8,128)(2,1)S(1)}, bf16[128,512]{1,0:T(8,128)(2,1)S(1)}, u32[]{:S(2)}, u32[]{:S(2)}) collective-permute-start(bf16[128,512]{1,0:T(8,128)(2,1)S(1)} %bitcast.129), channel_id=1, source_target_pairs={{0,2},{1,3},{2,0},{3,1},{4,6},{5,7},{6,4},{7,5},{8,10},{9,11},{10,... | collective-permute-start | bytes 393224 | tf_op jit(solution)/shard_map/ppermute | solution.py:266
  92.5 6.7 %collective-permute-start.24 = (bf16[128,512]{1,0:T(8,128)(2,1)S(1)}, bf16[128,512]{1,0:T(8,128)(2,1)S(1)}, u32[]{:S(2)}, u32[]{:S(2)}) collective-permute-start(bf16[128,512]{1,0:T(8,128)(2,1)S(1)} %bitcast.128), channel_id=1, source_target_pairs={{0,3},{1,2},{2,1},{3,0},{4,7},{5,6},{6,5},{7,4},{8,11},{9,10},{10,... | collective-permute-start | bytes 393224 | tf_op jit(solution)/shard_map/ppermute | solution.py:266
  99.4 11.0 %collective-permute-start.27 = (bf16[128,512]{1,0:T(8,128)(2,1)S(1)}, bf16[128,512]{1,0:T(8,128)(2,1)S(1)}, u32[]{:S(2)}, u32[]{:S(2)}) collective-permute-start(bf16[128,512]{1,0:T(8,128)(2,1)S(1)} %get-tuple-element.68), channel_id=1, source_target_pairs={{0,16},{1,17},{2,18},{3,19},{4,20},{5,21},{6,22},{7,23},{8,24},{9,... | collective-permute-start | bytes 393224 | tf_op jit(solution)/shard_map/ppermute | solution.py:266
  99.8 10.5 %collective-permute-start.26 = (bf16[128,512]{1,0:T(8,128)(2,1)S(1)}, bf16[128,512]{1,0:T(8,128)(2,1)S(1)}, u32[]{:S(2)}, u32[]{:S(2)}) collective-permute-start(bf16[128,512]{1,0:T(8,128)(2,1)S(1)} %get-tuple-element.69), channel_id=1, source_target_pairs={{0,24},{1,25},{2,26},{3,27},{4,28},{5,29},{6,30},{7,31},{8,16},{9,... | collective-permute-start | bytes 393224 | tf_op jit(solution)/shard_map/ppermute | solution.py:266
  101.6 8.9 %collective-permute-start.25 = (bf16[128,512]{1,0:T(8,128)(2,1)S(1)}, bf16[128,512]{1,0:T(8,128)(2,1)S(1)}, u32[]{:S(2)}, u32[]{:S(2)}) collective-permute-start(bf16[128,512]{1,0:T(8,128)(2,1)S(1)} %get-tuple-element.70), channel_id=1, source_target_pairs={{0,8},{1,9},{2,10},{3,11},{4,12},{5,13},{6,14},{7,15},{8,0},{9,1},... | collective-permute-start | bytes 393224 | tf_op jit(solution)/shard_map/ppermute | solution.py:266

commit v10 on v9

--- a/solution.py
+++ b/solution.py
@@ -29,7 +29,7 @@
     return out
 
 
-def dequant_kernel(mask_ref, codes_ref, scales_ref, w_ref, marks_ref, narrow_ref, wide_ref, sem, scales_sem):
+def dequant_kernel(mask_ref, codes_ref, scales_ref, w_ref, marks_ref, wide_ref, sem):
     mark(marks_ref, mask_ref)
     _, owned, group = w_ref.shape
     tile = 16
@@ -38,12 +38,9 @@
         at = pl.ds(b * BLOCK, BLOCK)
         return pltpu.make_async_copy(codes_ref.at[:, at, :], w_ref.at[:, at, :], sem.at[b])
 
-    scales = pltpu.make_async_copy(scales_ref, narrow_ref, scales_sem)
-    scales.start()
     for b in range(owned // BLOCK):
         copy(b).start()
-    scales.wait()
-    wide_ref[...] = narrow_ref[...].astype(jnp.float32)
+    wide_ref[...] = scales_ref[...].astype(jnp.float32)
     for b in range(owned // BLOCK):
         copy(b).wait()
         for g in range(2):
@@ -53,23 +50,25 @@
 
 
 def dequant(codes, scales, mask, marks_shape):
-    codes, scales = (pltpu.with_memory_space_constraint(x, pltpu.HBM) for x in (codes, scales))
+    codes = pltpu.with_memory_space_constraint(codes, pltpu.HBM)
     return pl.pallas_call(
         dequant_kernel,
-        in_specs=[pl.BlockSpec(memory_space=pltpu.SMEM)] + [pl.BlockSpec(memory_space=pl.ANY)] * 2,
+        in_specs=[
+            pl.BlockSpec(memory_space=pltpu.SMEM),
+            pl.BlockSpec(memory_space=pl.ANY),
+            pl.BlockSpec(memory_space=pltpu.VMEM),
+        ],
         out_specs=[pl.BlockSpec(memory_space=pltpu.VMEM)] * 2,
         out_shape=[
             pltpu.VMEM(codes.shape, jnp.bfloat16),
             pltpu.VMEM(marks_shape, jnp.float32),
         ],
         scratch_shapes=[
-            pltpu.VMEM(scales.shape, jnp.bfloat16),
             pltpu.VMEM(scales.shape, jnp.float32),
             pltpu.SemaphoreType.DMA((codes.shape[1] // BLOCK,)),
-            pltpu.SemaphoreType.DMA,
         ],
         compiler_params=pltpu.CompilerParams(vmem_limit_bytes=12 * 1024 * 1024),
-    )(mask, codes, scales)
+    )(mask, codes, in_vmem(scales))
 
 
 def pairs(move, places, ratio):

time: 111 us -> 111 us (level)
  no operation moved by 1% of the time
where the time goes in v10:
time: 111 us
  waiting for transfers between devices  46.1 us (42%)
  starting transfers between devices  38.6 us (35%)
  Pallas kernels  21.5 us (19%)
  other arithmetic  3.15 us (3%)
    ppermute x28, waiting for transfers between devices, permute(): return lax.ppermute(x, AXES, pairs(move, places, ratio))  46.1 us
    ppermute x28, starting transfers between devices, permute(): return lax.ppermute(x, AXES, pairs(move, places, ratio))  38.6 us
    pallas_call x2, Pallas kernels, weight_grad(): pl.pallas_call(functools.partial(weight_grad_kernel, scale), grid=(owned...  9.32 us
    pallas_call x3, Pallas kernels, input_grad(): pl.pallas_call(functools.partial(input_grad_kernel, spots, es, first, cou...  4.53 us
    pallas_call x1, Pallas kernels, dequant(): pl.pallas_call(dequant_kernel, in_specs=[pl.BlockSpec(memory_space=pltpu....  3.24 us
    pallas_call x2, Pallas kernels, partial_sums(): pl.pallas_call(functools.partial(partial_sums_kernel, list(xs), bool(summ...  3.19 us
  transfers between devices with their start and end apart: 28, of which 17 were waited for; matrix products, arithmetic and copies ran while one was open for 2% of the time, Pallas kernels for 17%

profile of v10, /device:TPU:0, one launch (start us, length us, event | category | flops | bytes accessed | tf_op | source)
XLA Modules:
  0.0 111.3 jit_solution(2628626876389683599)
XLA Ops:
  0.6 3.1 %collective-permute-start = (bf16[128,512]{1,0:T(8,128)(2,1)}, bf16[128,512]{1,0:T(8,128)(2,1)S(1)}, u32[]{:S(2)}, u32[]{:S(2)}) collective-permute-start(bf16[128,512]{1,0:T(8,128)(2,1)} %param.4), channel_id=1, source_target_pairs={{0,8},{1,0},{2,24},{3,16},{4,12},{5,4},{6,28},{7,20},{8,9},{9,1},{... | collective-permute-start | bytes 393224 | tf_op jit(solution)/shard_map/ppermute | solution.py:265
  3.7 2.4 %collective-permute-start.1 = (bf16[128,512]{1,0:T(8,128)(2,1)}, bf16[128,512]{1,0:T(8,128)(2,1)S(1)}, u32[]{:S(2)}, u32[]{:S(2)}) collective-permute-start(bf16[128,512]{1,0:T(8,128)(2,1)} %param.4), channel_id=1, source_target_pairs={{0,16},{1,24},{2,0},{3,8},{4,20},{5,28},{6,4},{7,12},{8,17},{9,25}... | collective-permute-start | bytes 393224 | tf_op jit(solution)/shard_map/ppermute | solution.py:265
  6.1 2.5 %collective-permute-start.2 = (bf16[128,512]{1,0:T(8,128)(2,1)}, bf16[128,512]{1,0:T(8,128)(2,1)S(1)}, u32[]{:S(2)}, u32[]{:S(2)}) collective-permute-start(bf16[128,512]{1,0:T(8,128)(2,1)} %param.4), channel_id=1, source_target_pairs={{0,24},{1,16},{2,8},{3,0},{4,28},{5,20},{6,12},{7,4},{8,25},{9,17}... | collective-permute-start | bytes 393224 | tf_op jit(solution)/shard_map/ppermute | solution.py:265
  8.6 1.6 %collective-permute-start.3 = (bf16[128,512]{1,0:T(8,128)(2,1)}, bf16[128,512]{1,0:T(8,128)(2,1)S(1)}, u32[]{:S(2)}, u32[]{:S(2)}) collective-permute-start(bf16[128,512]{1,0:T(8,128)(2,1)} %param.4), channel_id=1, source_target_pairs={{0,0},{1,8},{2,16},{3,24},{4,4},{5,12},{6,20},{7,28},{8,1},{9,9},{... | collective-permute-start | bytes 393224 | tf_op jit(solution)/shard_map/ppermute | solution.py:265
  11.0 3.2 %shard_map.67 = (bf16[2,1024,1792]{2,1,0:T(8,128)(2,1)S(1)}, f32[4,512]{1,0:T(4,128)S(1)}) custom-call(s32[1]{0:T(128)} %bitcast.1.mask_ref, bf16[2,1024,1792]{2,1,0:T(8,128)(2,1)} %codes_ref.1, bf16[2,8,1792]{2,1,0:T(8,128)(2,1)S(1)} %copy-done), custom_call_target="tpu_custom_call" | custom-call | tf_op jit(solution)/shard_map/pallas_call | solution.py:54
  17.6 8.5 %collective-permute-start.9 = (bf16[2,2,32,1792]{3,2,1,0:T(8,128)(2,1)S(1)}, bf16[2,2,32,1792]{3,2,1,0:T(8,128)(2,1)S(1)}, u32[]{:S(2)}, u32[]{:S(2)}) collective-permute-start(bf16[2,2,32,1792]{3,2,1,0:T(8,128)(2,1)S(1)} %get-tuple-element.38), channel_id=1, source_target_pairs={{0,1},{1,0},{2,3},{3,2},{4,5},{5,4},{6,7},{7,6},{8,9},{9,8},{10,11... | collective-permute-start | bytes 1376264 | tf_op jit(solution)/shard_map/ppermute | solution.py:265
  26.0 2.1 %shard_map.68 = (bf16[2,2,32,1792]{3,2,1,0:T(8,128)(2,1)S(1)}, f32[2,2,32,1792]{3,2,1,0:T(8,128)S(1)}, bf16[2,2,32,1792]{3,2,1,0:T(8,128)(2,1)S(1)}, f32[2,2,32,1792]{3,2,1,0:T(8,128)S(1)}) custom-call(s32[1]{0:T(128)} %bitcast.half_ref.index_ref, bf16[4,128,512]{2,1,0:T(8,128)(2,1)S(1)} %pad_maximum_fusion.refs_0_.x_ref, ...), custom_call_target="tpu_custom_call" | custom-call | tf_op jit(solution)/shard_map/pallas_call | solution.py:166
  28.1 2.1 %collective-permute-start.7 = (bf16[2,2,32,1792]{3,2,1,0:T(8,128)(2,1)S(1)}, bf16[2,2,32,1792]{3,2,1,0:T(8,128)(2,1)S(1)}, u32[]{:S(2)}, u32[]{:S(2)}) collective-permute-start(bf16[2,2,32,1792]{3,2,1,0:T(8,128)(2,1)S(1)} %get-tuple-element.36), channel_id=1, source_target_pairs={{0,2},{1,3},{2,0},{3,1},{4,6},{5,7},{6,4},{7,5},{8,10},{9,11},{10,... | collective-permute-start | bytes 1376264 | tf_op jit(solution)/shard_map/ppermute | solution.py:265
  30.3 7.0 %collective-permute-done.9 = bf16[2,2,32,1792]{3,2,1,0:T(8,128)(2,1)S(1)} collective-permute-done((bf16[2,2,32,1792]{3,2,1,0:T(8,128)(2,1)S(1)}, bf16[2,2,32,1792]{3,2,1,0:T(8,128)(2,1)S(1)}, u32[]{:S(2)}, u32[]{:S(2)}) %collective-permute-start.9) | collective-permute-done | bytes 458784 | tf_op jit(solution)/shard_map/ppermute | solution.py:265
  37.5 1.8 %collective-permute-start.10 = (bf16[2,1,32,1792]{3,2,1,0:T(8,128)(2,1)S(1)}, bf16[2,1,32,1792]{3,2,1,0:T(8,128)(2,1)S(1)}, u32[]{:S(2)}, u32[]{:S(2)}) collective-permute-start(bf16[2,1,32,1792]{3,2,1,0:T(8,128)(2,1)S(1)} %slice.183), channel_id=1, source_target_pairs={{0,2},{1,3},{2,0},{3,1},{4,6},{5,7},{6,4},{7,5},{8,10},{9,11},{10,... | collective-permute-start | bytes 688136 | tf_op jit(solution)/shard_map/ppermute | solution.py:265
  39.8 7.4 %collective-permute-done.5 = bf16[2,2,32,1792]{3,2,1,0:T(8,128)(2,1)S(1)} collective-permute-done((bf16[2,2,32,1792]{3,2,1,0:T(8,128)(2,1)S(1)}, bf16[2,2,32,1792]{3,2,1,0:T(8,128)(2,1)S(1)}, u32[]{:S(2)}, u32[]{:S(2)}) %collective-permute-start.5) | collective-permute-done | bytes 458784 | tf_op jit(solution)/shard_map/ppermute | solution.py:265
  47.3 1.8 %collective-permute-start.6 = (bf16[2,1,32,1792]{3,2,1,0:T(8,128)(2,1)S(1)}, bf16[2,1,32,1792]{3,2,1,0:T(8,128)(2,1)S(1)}, u32[]{:S(2)}, u32[]{:S(2)}) collective-permute-start(bf16[2,1,32,1792]{3,2,1,0:T(8,128)(2,1)S(1)} %slice.185), channel_id=1, source_target_pairs={{0,2},{1,3},{2,0},{3,1},{4,6},{5,7},{6,4},{7,5},{8,10},{9,11},{10,... | collective-permute-start | bytes 688136 | tf_op jit(solution)/shard_map/ppermute | solution.py:265
  49.6 4.5 %collective-permute-done.10 = bf16[2,1,32,1792]{3,2,1,0:T(8,128)(2,1)S(1)} collective-permute-done((bf16[2,1,32,1792]{3,2,1,0:T(8,128)(2,1)S(1)}, bf16[2,1,32,1792]{3,2,1,0:T(8,128)(2,1)S(1)}, u32[]{:S(2)}, u32[]{:S(2)}) %collective-permute-start.10) | collective-permute-done | bytes 229408 | tf_op jit(solution)/shard_map/ppermute | solution.py:265
  54.8 1.7 %collective-permute-start.18 = (bf16[2,2,32,1792]{3,2,1,0:T(8,128)(2,1)S(1)}, bf16[2,2,32,1792]{3,2,1,0:T(8,128)(2,1)S(1)}, u32[]{:S(2)}, u32[]{:S(2)}) collective-permute-start(bf16[2,2,32,1792]{3,2,1,0:T(8,128)(2,1)S(1)} %maximum_maximum_fusion.refs_0_), channel_id=1, source_target_pairs={{0,2},{1,3},{2,0},{3,1},{4,6},{5,7},{6,4},{7,5},{8,10},{9,11},{10,... | collective-permute-start | bytes 1376264 | tf_op jit(solution)/shard_map/ppermute | solution.py:265
  56.4 2.7 %collective-permute-done.6 = bf16[2,1,32,1792]{3,2,1,0:T(8,128)(2,1)S(1)} collective-permute-done((bf16[2,1,32,1792]{3,2,1,0:T(8,128)(2,1)S(1)}, bf16[2,1,32,1792]{3,2,1,0:T(8,128)(2,1)S(1)}, u32[]{:S(2)}, u32[]{:S(2)}) %collective-permute-start.6) | collective-permute-done | bytes 229408 | tf_op jit(solution)/shard_map/ppermute | solution.py:265
  59.7 1.7 %collective-permute-start.15 = (bf16[2,2,32,1792]{3,2,1,0:T(8,128)(2,1)S(1)}, bf16[2,2,32,1792]{3,2,1,0:T(8,128)(2,1)S(1)}, u32[]{:S(2)}, u32[]{:S(2)}) collective-permute-start(bf16[2,2,32,1792]{3,2,1,0:T(8,128)(2,1)S(1)} %maximum_maximum_fusion.1.refs_5_), channel_id=1, source_target_pairs={{0,2},{1,3},{2,0},{3,1},{4,6},{5,7},{6,4},{7,5},{8,10},{9,11},{10,... | collective-permute-start | bytes 1376264 | tf_op jit(solution)/shard_map/ppermute | solution.py:265
  61.3 6.9 %collective-permute-done.17.refs_1_ = bf16[2,2,32,1792]{3,2,1,0:T(8,128)(2,1)S(1)} collective-permute-done((bf16[2,2,32,1792]{3,2,1,0:T(8,128)(2,1)S(1)}, bf16[2,2,32,1792]{3,2,1,0:T(8,128)(2,1)S(1)}, u32[]{:S(2)}, u32[]{:S(2)}) %collective-permute-start.17) | collective-permute-done | bytes 458784 | tf_op jit(solution)/shard_map/ppermute | solution.py:265
  68.9 1.3 %collective-permute-start.20 = (bf16[1,2,32,1792]{3,2,1,0:T(8,128)(2,1)S(1)}, bf16[1,2,32,1792]{3,2,1,0:T(8,128)(2,1)S(1)}, u32[]{:S(2)}, u32[]{:S(2)}) collective-permute-start(bf16[1,2,32,1792]{3,2,1,0:T(8,128)(2,1)S(1)} %slice.153), channel_id=1, source_target_pairs={{0,1},{1,0},{2,3},{3,2},{4,5},{5,4},{6,7},{7,6},{8,9},{9,8},{10,11... | collective-permute-start | bytes 688136 | tf_op jit(solution)/shard_map/ppermute | solution.py:265
  70.3 7.7 %collective-permute-done.13.refs_6_ = bf16[2,2,32,1792]{3,2,1,0:T(8,128)(2,1)S(1)} collective-permute-done((bf16[2,2,32,1792]{3,2,1,0:T(8,128)(2,1)S(1)}, bf16[2,2,32,1792]{3,2,1,0:T(8,128)(2,1)S(1)}, u32[]{:S(2)}, u32[]{:S(2)}) %collective-permute-start.13) | collective-permute-done | bytes 458784 | tf_op jit(solution)/shard_map/ppermute | solution.py:265
  78.8 1.3 %collective-permute-start.16 = (bf16[1,2,32,1792]{3,2,1,0:T(8,128)(2,1)S(1)}, bf16[1,2,32,1792]{3,2,1,0:T(8,128)(2,1)S(1)}, u32[]{:S(2)}, u32[]{:S(2)}) collective-permute-start(bf16[1,2,32,1792]{3,2,1,0:T(8,128)(2,1)S(1)} %slice.151), channel_id=1, source_target_pairs={{0,1},{1,0},{2,3},{3,2},{4,5},{5,4},{6,7},{7,6},{8,9},{9,8},{10,11... | collective-permute-start | bytes 688136 | tf_op jit(solution)/shard_map/ppermute | solution.py:265
  80.1 3.5 %collective-permute-done.19.refs_3_ = bf16[1,2,32,1792]{3,2,1,0:T(8,128)(2,1)S(1)} collective-permute-done((bf16[1,2,32,1792]{3,2,1,0:T(8,128)(2,1)S(1)}, bf16[1,2,32,1792]{3,2,1,0:T(8,128)(2,1)S(1)}, u32[]{:S(2)}, u32[]{:S(2)}) %collective-permute-start.19) | collective-permute-done | bytes 229408 | tf_op jit(solution)/shard_map/ppermute | solution.py:265
  83.7 2.2 %shard_map.72 = (bf16[2,512,1792]{2,1,0:T(8,128)(2,1)S(1)}, bf16[512,512]{1,0:T(8,128)(2,1)S(1)}, bf16[512,512]{1,0:T(8,128)(2,1)S(1)}) custom-call(s32[1]{0:T(128)} %bitcast.half_ref.index_ref, bf16[2,2,32,1792]{3,2,1,0:T(8,128)(2,1)S(1)} %maximum_maximum_fusion.refs_0_, bf16[2,2,32,1792]{3,2,1,0:T(8,128)(2,1)S(1)} %collective-permute-done.17.refs_1_, ...), custom_call_target="tpu_custom_call" | custom-call | tf_op jit(solution)/shard_map/pallas_call | solution.py:201
  85.9 1.5 %collective-permute-done.14.refs_0_ = bf16[1,2,32,1792]{3,2,1,0:T(8,128)(2,1)S(1)} collective-permute-done((bf16[1,2,32,1792]{3,2,1,0:T(8,128)(2,1)S(1)}, bf16[1,2,32,1792]{3,2,1,0:T(8,128)(2,1)S(1)}, u32[]{:S(2)}, u32[]{:S(2)}) %collective-permute-start.14) | collective-permute-done | bytes 229408 | tf_op jit(solution)/shard_map/ppermute | solution.py:265
  87.5 1.1 %shard_map.73 = (bf16[2,512,1792]{2,1,0:T(8,128)(2,1)S(1)}, bf16[512,512]{1,0:T(8,128)(2,1)S(1)}) custom-call(s32[1]{0:T(128)} %bitcast.half_ref.index_ref, bf16[1,2,32,1792]{3,2,1,0:T(8,128)(2,1)S(1)} %collective-permute-done.14.refs_0_, bf16[1,2,32,1792]{3,2,1,0:T(8,128)(2,1)S(1)} %collective-permute-done.16.refs_1_, ...), custom_call_target="tpu_custom_call", output_to_operand_aliasing={{0}: (4, {}), {1}: (5, {})} | custom-call | tf_op jit(solution)/shard_map/pallas_call | solution.py:201
  88.7 1.1 %shard_map.74 = (bf16[2,512,1792]{2,1,0:T(8,128)(2,1)S(1)}, bf16[512,512]{1,0:T(8,128)(2,1)S(1)}) custom-call(s32[1]{0:T(128)} %bitcast.half_ref.index_ref, bf16[2,1024,1792]{2,1,0:T(8,128)(2,1)S(1)} %get-tuple-element.32.refs_2_.w_ref.refs_1_.refs_8_.refs_0_, ...), custom_call_target="tpu_custom_call", output_to_operand_aliasing={{0}: (2, {}), {1}: (3, {})} | custom-call | tf_op jit(solution)/shard_map/pallas_call | solution.py:201
  91.2 1.3 %collective-permute-start.23 = (bf16[128,512]{1,0:T(8,128)(2,1)S(1)}, bf16[128,512]{1,0:T(8,128)(2,1)S(1)}, u32[]{:S(2)}, u32[]{:S(2)}) collective-permute-start(bf16[128,512]{1,0:T(8,128)(2,1)S(1)} %bitcast.129), channel_id=1, source_target_pairs={{0,2},{1,3},{2,0},{3,1},{4,6},{5,7},{6,4},{7,5},{8,10},{9,11},{10,... | collective-permute-start | bytes 393224 | tf_op jit(solution)/shard_map/ppermute | solution.py:265
  92.5 1.8 %collective-permute-start.24 = (bf16[128,512]{1,0:T(8,128)(2,1)S(1)}, bf16[128,512]{1,0:T(8,128)(2,1)S(1)}, u32[]{:S(2)}, u32[]{:S(2)}) collective-permute-start(bf16[128,512]{1,0:T(8,128)(2,1)S(1)} %bitcast.128), channel_id=1, source_target_pairs={{0,3},{1,2},{2,1},{3,0},{4,7},{5,6},{6,5},{7,4},{8,11},{9,10},{10,... | collective-permute-start | bytes 393224 | tf_op jit(solution)/shard_map/ppermute | solution.py:265
  94.4 4.7 %shard_map.75 = (f32[2,1024,1792]{2,1,0:T(8,128)}, f32[4,512]{1,0:T(4,128)S(1)}) custom-call(bf16[512,1024]{1,0:T(8,128)(2,1)S(1)} %bitcast.124, bf16[2,512,1792]{2,1,0:T(8,128)(2,1)S(1)} %get-tuple-element.47.d_ref, s32[1]{0:T(128)} %bitcast.1.mask_ref, bf16[16,512]{1,0:T(8,128)(2,1)S(1)} %slice.155.refs_0_), custom_call_target="tpu_custom_call" | custom-call | tf_op jit(solution)/shard_map/pallas_call | solution.py:228
  99.8 1.8 %collective-permute-start.26 = (bf16[128,512]{1,0:T(8,128)(2,1)S(1)}, bf16[128,512]{1,0:T(8,128)(2,1)S(1)}, u32[]{:S(2)}, u32[]{:S(2)}) collective-permute-start(bf16[128,512]{1,0:T(8,128)(2,1)S(1)} %get-tuple-element.69), channel_id=1, source_target_pairs={{0,24},{1,25},{2,26},{3,27},{4,28},{5,29},{6,30},{7,31},{8,16},{9,... | collective-permute-start | bytes 393224 | tf_op jit(solution)/shard_map/ppermute | solution.py:265
  101.6 1.3 %collective-permute-start.25 = (bf16[128,512]{1,0:T(8,128)(2,1)S(1)}, bf16[128,512]{1,0:T(8,128)(2,1)S(1)}, u32[]{:S(2)}, u32[]{:S(2)}) collective-permute-start(bf16[128,512]{1,0:T(8,128)(2,1)S(1)} %get-tuple-element.70), channel_id=1, source_target_pairs={{0,8},{1,9},{2,10},{3,11},{4,12},{5,13},{6,14},{7,15},{8,0},{9,1},... | collective-permute-start | bytes 393224 | tf_op jit(solution)/shard_map/ppermute | solution.py:265
  103.7 4.6 %shard_map.76 = (f32[2,1024,1792]{2,1,0:T(8,128)}, f32[4,512]{1,0:T(4,128)}) custom-call(bf16[512,1024]{1,0:T(8,128)(2,1)S(1)} %bitcast.125, bf16[2,512,1792]{2,1,0:T(8,128)(2,1)S(1)} %get-tuple-element.47.d_ref, s32[1]{0:T(128)} %bitcast.1.mask_ref, bf16[16,512]{1,0:T(8,128)(2,1)S(1)} %slice.159.refs_0_, ...), custom_call_target="tpu_custom_call", output_to_operand_aliasing={{0}: (4, {})} | custom-call | tf_op jit(solution)/shard_map/pallas_call | solution.py:228
  108.4 2.0 %collective-permute-done.27 = bf16[128,512]{1,0:T(8,128)(2,1)S(1)} collective-permute-done((bf16[128,512]{1,0:T(8,128)(2,1)S(1)}, bf16[128,512]{1,0:T(8,128)(2,1)S(1)}, u32[]{:S(2)}, u32[]{:S(2)}) %collective-permute-start.27) | collective-permute-done | bytes 131104 | tf_op jit(solution)/shard_map/ppermute | solution.py:265
  (68 shorter events, 12.0 us)
Async XLA Ops:
  0.6 13.6 %collective-permute-start = (bf16[128,512]{1,0:T(8,128)(2,1)}, bf16[128,512]{1,0:T(8,128)(2,1)S(1)}, u32[]{:S(2)}, u32[]{:S(2)}) collective-permute-start(bf16[128,512]{1,0:T(8,128)(2,1)} %param.4), channel_id=1, source_target_pairs={{0,8},{1,0},{2,24},{3,16},{4,12},{5,4},{6,28},{7,20},{8,9},{9,1},{... | collective-permute-start | bytes 393224 | tf_op jit(solution)/shard_map/ppermute | solution.py:265
  3.7 10.6 %collective-permute-start.1 = (bf16[128,512]{1,0:T(8,128)(2,1)}, bf16[128,512]{1,0:T(8,128)(2,1)S(1)}, u32[]{:S(2)}, u32[]{:S(2)}) collective-permute-start(bf16[128,512]{1,0:T(8,128)(2,1)} %param.4), channel_id=1, source_target_pairs={{0,16},{1,24},{2,0},{3,8},{4,20},{5,28},{6,4},{7,12},{8,17},{9,25}... | collective-permute-start | bytes 393224 | tf_op jit(solution)/shard_map/ppermute | solution.py:265
  6.1 8.2 %collective-permute-start.2 = (bf16[128,512]{1,0:T(8,128)(2,1)}, bf16[128,512]{1,0:T(8,128)(2,1)S(1)}, u32[]{:S(2)}, u32[]{:S(2)}) collective-permute-start(bf16[128,512]{1,0:T(8,128)(2,1)} %param.4), channel_id=1, source_target_pairs={{0,24},{1,16},{2,8},{3,0},{4,28},{5,20},{6,12},{7,4},{8,25},{9,17}... | collective-permute-start | bytes 393224 | tf_op jit(solution)/shard_map/ppermute | solution.py:265
  8.6 5.7 %collective-permute-start.3 = (bf16[128,512]{1,0:T(8,128)(2,1)}, bf16[128,512]{1,0:T(8,128)(2,1)S(1)}, u32[]{:S(2)}, u32[]{:S(2)}) collective-permute-start(bf16[128,512]{1,0:T(8,128)(2,1)} %param.4), channel_id=1, source_target_pairs={{0,0},{1,8},{2,16},{3,24},{4,4},{5,12},{6,20},{7,28},{8,1},{9,9},{... | collective-permute-start | bytes 393224 | tf_op jit(solution)/shard_map/ppermute | solution.py:265
  10.2 0.8 copy-start
  14.5 2.0 %collective-permute-start.4 = (bf16[4,128,512]{2,1,0:T(8,128)(2,1)S(1)}, bf16[4,128,512]{2,1,0:T(8,128)(2,1)S(1)}, u32[]{:S(2)}, u32[]{:S(2)}) collective-permute-start(bf16[4,128,512]{2,1,0:T(8,128)(2,1)S(1)} %pad_maximum_fusion.refs_0_.x_ref), channel_id=1, source_target_pairs={{0,4},{1,5},{2,6},{3,7},{4,0},{5,1},{6,2},{7,3},{8,12},{9,13},{10,... | collective-permute-start | bytes 1572872 | tf_op jit(solution)/shard_map/ppermute | solution.py:265
  17.6 19.8 %collective-permute-start.9 = (bf16[2,2,32,1792]{3,2,1,0:T(8,128)(2,1)S(1)}, bf16[2,2,32,1792]{3,2,1,0:T(8,128)(2,1)S(1)}, u32[]{:S(2)}, u32[]{:S(2)}) collective-permute-start(bf16[2,2,32,1792]{3,2,1,0:T(8,128)(2,1)S(1)} %get-tuple-element.38), channel_id=1, source_target_pairs={{0,1},{1,0},{2,3},{3,2},{4,5},{5,4},{6,7},{7,6},{8,9},{9,8},{10,11... | collective-permute-start | bytes 1376264 | tf_op jit(solution)/shard_map/ppermute | solution.py:265
  26.0 13.4 %collective-permute-start.11 = (bf16[2,2,32,1792]{3,2,1,0:T(8,128)(2,1)S(1)}, bf16[2,2,32,1792]{3,2,1,0:T(8,128)(2,1)S(1)}, u32[]{:S(2)}, u32[]{:S(2)}) collective-permute-start(bf16[2,2,32,1792]{3,2,1,0:T(8,128)(2,1)S(1)} %get-tuple-element.40), channel_id=1, source_target_pairs={{0,2},{1,3},{2,0},{3,1},{4,6},{5,7},{6,4},{7,5},{8,10},{9,11},{10,... | collective-permute-start | bytes 1376264 | tf_op jit(solution)/shard_map/ppermute | solution.py:265
  28.1 26.2 %copy-start.1 = (bf16[128,1792]{1,0:T(8,128)(2,1)S(1)}, bf16[128,1792]{1,0:T(8,128)(2,1)}, u32[]{:S(2)}) copy-start(bf16[128,1792]{1,0:T(8,128)(2,1)} %param.7) | copy-start | bytes 1376260
  28.1 21.1 %collective-permute-start.7 = (bf16[2,2,32,1792]{3,2,1,0:T(8,128)(2,1)S(1)}, bf16[2,2,32,1792]{3,2,1,0:T(8,128)(2,1)S(1)}, u32[]{:S(2)}, u32[]{:S(2)}) collective-permute-start(bf16[2,2,32,1792]{3,2,1,0:T(8,128)(2,1)S(1)} %get-tuple-element.36), channel_id=1, source_target_pairs={{0,2},{1,3},{2,0},{3,1},{4,6},{5,7},{6,4},{7,5},{8,10},{9,11},{10,... | collective-permute-start | bytes 1376264 | tf_op jit(solution)/shard_map/ppermute | solution.py:265
  30.2 17.0 %collective-permute-start.5 = (bf16[2,2,32,1792]{3,2,1,0:T(8,128)(2,1)S(1)}, bf16[2,2,32,1792]{3,2,1,0:T(8,128)(2,1)S(1)}, u32[]{:S(2)}, u32[]{:S(2)}) collective-permute-start(bf16[2,2,32,1792]{3,2,1,0:T(8,128)(2,1)S(1)} %get-tuple-element.34), channel_id=1, source_target_pairs={{0,1},{1,0},{2,3},{3,2},{4,5},{5,4},{6,7},{7,6},{8,9},{9,8},{10,11... | collective-permute-start | bytes 1376264 | tf_op jit(solution)/shard_map/ppermute | solution.py:265
  37.5 16.7 %collective-permute-start.10 = (bf16[2,1,32,1792]{3,2,1,0:T(8,128)(2,1)S(1)}, bf16[2,1,32,1792]{3,2,1,0:T(8,128)(2,1)S(1)}, u32[]{:S(2)}, u32[]{:S(2)}) collective-permute-start(bf16[2,1,32,1792]{3,2,1,0:T(8,128)(2,1)S(1)} %slice.183), channel_id=1, source_target_pairs={{0,2},{1,3},{2,0},{3,1},{4,6},{5,7},{6,4},{7,5},{8,10},{9,11},{10,... | collective-permute-start | bytes 688136 | tf_op jit(solution)/shard_map/ppermute | solution.py:265
  39.5 14.7 %collective-permute-start.12 = (bf16[2,1,32,1792]{3,2,1,0:T(8,128)(2,1)S(1)}, bf16[2,1,32,1792]{3,2,1,0:T(8,128)(2,1)S(1)}, u32[]{:S(2)}, u32[]{:S(2)}) collective-permute-start(bf16[2,1,32,1792]{3,2,1,0:T(8,128)(2,1)S(1)} %slice.182), channel_id=1, source_target_pairs={{0,1},{1,0},{2,3},{3,2},{4,5},{5,4},{6,7},{7,6},{8,9},{9,8},{10,11... | collective-permute-start | bytes 688136 | tf_op jit(solution)/shard_map/ppermute | solution.py:265
  47.3 11.8 %collective-permute-start.6 = (bf16[2,1,32,1792]{3,2,1,0:T(8,128)(2,1)S(1)}, bf16[2,1,32,1792]{3,2,1,0:T(8,128)(2,1)S(1)}, u32[]{:S(2)}, u32[]{:S(2)}) collective-permute-start(bf16[2,1,32,1792]{3,2,1,0:T(8,128)(2,1)S(1)} %slice.185), channel_id=1, source_target_pairs={{0,2},{1,3},{2,0},{3,1},{4,6},{5,7},{6,4},{7,5},{8,10},{9,11},{10,... | collective-permute-start | bytes 688136 | tf_op jit(solution)/shard_map/ppermute | solution.py:265
  49.4 9.7 %collective-permute-start.8 = (bf16[2,1,32,1792]{3,2,1,0:T(8,128)(2,1)S(1)}, bf16[2,1,32,1792]{3,2,1,0:T(8,128)(2,1)S(1)}, u32[]{:S(2)}, u32[]{:S(2)}) collective-permute-start(bf16[2,1,32,1792]{3,2,1,0:T(8,128)(2,1)S(1)} %slice.184), channel_id=1, source_target_pairs={{0,1},{1,0},{2,3},{3,2},{4,5},{5,4},{6,7},{7,6},{8,9},{9,8},{10,11... | collective-permute-start | bytes 688136 | tf_op jit(solution)/shard_map/ppermute | solution.py:265
  54.7 13.5 %collective-permute-start.17 = (bf16[2,2,32,1792]{3,2,1,0:T(8,128)(2,1)S(1)}, bf16[2,2,32,1792]{3,2,1,0:T(8,128)(2,1)S(1)}, u32[]{:S(2)}, u32[]{:S(2)}) collective-permute-start(bf16[2,2,32,1792]{3,2,1,0:T(8,128)(2,1)S(1)} %maximum_maximum_fusion.refs_0_), channel_id=1, source_target_pairs={{0,1},{1,0},{2,3},{3,2},{4,5},{5,4},{6,7},{7,6},{8,9},{9,8},{10,11... | collective-permute-start | bytes 1376264 | tf_op jit(solution)/shard_map/ppermute | solution.py:265
  54.8 14.2 %collective-permute-start.18 = (bf16[2,2,32,1792]{3,2,1,0:T(8,128)(2,1)S(1)}, bf16[2,2,32,1792]{3,2,1,0:T(8,128)(2,1)S(1)}, u32[]{:S(2)}, u32[]{:S(2)}) collective-permute-start(bf16[2,2,32,1792]{3,2,1,0:T(8,128)(2,1)S(1)} %maximum_maximum_fusion.refs_0_), channel_id=1, source_target_pairs={{0,2},{1,3},{2,0},{3,1},{4,6},{5,7},{6,4},{7,5},{8,10},{9,11},{10,... | collective-permute-start | bytes 1376264 | tf_op jit(solution)/shard_map/ppermute | solution.py:265
  59.5 18.5 %collective-permute-start.13 = (bf16[2,2,32,1792]{3,2,1,0:T(8,128)(2,1)S(1)}, bf16[2,2,32,1792]{3,2,1,0:T(8,128)(2,1)S(1)}, u32[]{:S(2)}, u32[]{:S(2)}) collective-permute-start(bf16[2,2,32,1792]{3,2,1,0:T(8,128)(2,1)S(1)} %maximum_maximum_fusion.1.refs_5_), channel_id=1, source_target_pairs={{0,1},{1,0},{2,3},{3,2},{4,5},{5,4},{6,7},{7,6},{8,9},{9,8},{10,11... | collective-permute-start | bytes 1376264 | tf_op jit(solution)/shard_map/ppermute | solution.py:265
  59.7 19.1 %collective-permute-start.15 = (bf16[2,2,32,1792]{3,2,1,0:T(8,128)(2,1)S(1)}, bf16[2,2,32,1792]{3,2,1,0:T(8,128)(2,1)S(1)}, u32[]{:S(2)}, u32[]{:S(2)}) collective-permute-start(bf16[2,2,32,1792]{3,2,1,0:T(8,128)(2,1)S(1)} %maximum_maximum_fusion.1.refs_5_), channel_id=1, source_target_pairs={{0,2},{1,3},{2,0},{3,1},{4,6},{5,7},{6,4},{7,5},{8,10},{9,11},{10,... | collective-permute-start | bytes 1376264 | tf_op jit(solution)/shard_map/ppermute | solution.py:265
  68.2 15.5 %collective-permute-start.19 = (bf16[1,2,32,1792]{3,2,1,0:T(8,128)(2,1)S(1)}, bf16[1,2,32,1792]{3,2,1,0:T(8,128)(2,1)S(1)}, u32[]{:S(2)}, u32[]{:S(2)}) collective-permute-start(bf16[1,2,32,1792]{3,2,1,0:T(8,128)(2,1)S(1)} %slice.152), channel_id=1, source_target_pairs={{0,2},{1,3},{2,0},{3,1},{4,6},{5,7},{6,4},{7,5},{8,10},{9,11},{10,... | collective-permute-start | bytes 688136 | tf_op jit(solution)/shard_map/ppermute | solution.py:265
  68.9 14.7 %collective-permute-start.20 = (bf16[1,2,32,1792]{3,2,1,0:T(8,128)(2,1)S(1)}, bf16[1,2,32,1792]{3,2,1,0:T(8,128)(2,1)S(1)}, u32[]{:S(2)}, u32[]{:S(2)}) collective-permute-start(bf16[1,2,32,1792]{3,2,1,0:T(8,128)(2,1)S(1)} %slice.153), channel_id=1, source_target_pairs={{0,1},{1,0},{2,3},{3,2},{4,5},{5,4},{6,7},{7,6},{8,9},{9,8},{10,11... | collective-permute-start | bytes 688136 | tf_op jit(solution)/shard_map/ppermute | solution.py:265
  78.0 9.4 %collective-permute-start.14 = (bf16[1,2,32,1792]{3,2,1,0:T(8,128)(2,1)S(1)}, bf16[1,2,32,1792]{3,2,1,0:T(8,128)(2,1)S(1)}, u32[]{:S(2)}, u32[]{:S(2)}) collective-permute-start(bf16[1,2,32,1792]{3,2,1,0:T(8,128)(2,1)S(1)} %slice.150), channel_id=1, source_target_pairs={{0,2},{1,3},{2,0},{3,1},{4,6},{5,7},{6,4},{7,5},{8,10},{9,11},{10,... | collective-permute-start | bytes 688136 | tf_op jit(solution)/shard_map/ppermute | solution.py:265
  78.8 8.7 %collective-permute-start.16 = (bf16[1,2,32,1792]{3,2,1,0:T(8,128)(2,1)S(1)}, bf16[1,2,32,1792]{3,2,1,0:T(8,128)(2,1)S(1)}, u32[]{:S(2)}, u32[]{:S(2)}) collective-permute-start(bf16[1,2,32,1792]{3,2,1,0:T(8,128)(2,1)S(1)} %slice.151), channel_id=1, source_target_pairs={{0,1},{1,0},{2,3},{3,2},{4,5},{5,4},{6,7},{7,6},{8,9},{9,8},{10,11... | collective-permute-start | bytes 688136 | tf_op jit(solution)/shard_map/ppermute | solution.py:265
  88.6 2.0 %collective-permute-start.21 = (bf16[512,512]{1,0:T(8,128)(2,1)S(1)}, bf16[512,512]{1,0:T(8,128)(2,1)S(1)}, u32[]{:S(2)}, u32[]{:S(2)}) collective-permute-start(bf16[512,512]{1,0:T(8,128)(2,1)S(1)} %get-tuple-element.49), channel_id=1, source_target_pairs={{0,4},{1,5},{2,6},{3,7},{4,0},{5,1},{6,2},{7,3},{8,12},{9,13},{10,... | collective-permute-start | bytes 1572872 | tf_op jit(solution)/shard_map/ppermute | solution.py:265
  90.8 8.4 %collective-permute-start.22 = (bf16[128,512]{1,0:T(8,128)(2,1)S(1)}, bf16[128,512]{1,0:T(8,128)(2,1)S(1)}, u32[]{:S(2)}, u32[]{:S(2)}) collective-permute-start(bf16[128,512]{1,0:T(8,128)(2,1)S(1)} %bitcast.130), channel_id=1, source_target_pairs={{0,1},{1,0},{2,3},{3,2},{4,5},{5,4},{6,7},{7,6},{8,9},{9,8},{10,11... | collective-permute-start | bytes 393224 | tf_op jit(solution)/shard_map/ppermute | solution.py:265
  91.2 8.1 %collective-permute-start.23 = (bf16[128,512]{1,0:T(8,128)(2,1)S(1)}, bf16[128,512]{1,0:T(8,128)(2,1)S(1)}, u32[]{:S(2)}, u32[]{:S(2)}) collective-permute-start(bf16[128,512]{1,0:T(8,128)(2,1)S(1)} %bitcast.129), channel_id=1, source_target_pairs={{0,2},{1,3},{2,0},{3,1},{4,6},{5,7},{6,4},{7,5},{8,10},{9,11},{10,... | collective-permute-start | bytes 393224 | tf_op jit(solution)/shard_map/ppermute | solution.py:265
  92.5 6.7 %collective-permute-start.24 = (bf16[128,512]{1,0:T(8,128)(2,1)S(1)}, bf16[128,512]{1,0:T(8,128)(2,1)S(1)}, u32[]{:S(2)}, u32[]{:S(2)}) collective-permute-start(bf16[128,512]{1,0:T(8,128)(2,1)S(1)} %bitcast.128), channel_id=1, source_target_pairs={{0,3},{1,2},{2,1},{3,0},{4,7},{5,6},{6,5},{7,4},{8,11},{9,10},{10,... | collective-permute-start | bytes 393224 | tf_op jit(solution)/shard_map/ppermute | solution.py:265
  99.4 11.0 %collective-permute-start.27 = (bf16[128,512]{1,0:T(8,128)(2,1)S(1)}, bf16[128,512]{1,0:T(8,128)(2,1)S(1)}, u32[]{:S(2)}, u32[]{:S(2)}) collective-permute-start(bf16[128,512]{1,0:T(8,128)(2,1)S(1)} %get-tuple-element.68), channel_id=1, source_target_pairs={{0,16},{1,17},{2,18},{3,19},{4,20},{5,21},{6,22},{7,23},{8,24},{9,... | collective-permute-start | bytes 393224 | tf_op jit(solution)/shard_map/ppermute | solution.py:265
  99.8 10.5 %collective-permute-start.26 = (bf16[128,512]{1,0:T(8,128)(2,1)S(1)}, bf16[128,512]{1,0:T(8,128)(2,1)S(1)}, u32[]{:S(2)}, u32[]{:S(2)}) collective-permute-start(bf16[128,512]{1,0:T(8,128)(2,1)S(1)} %get-tuple-element.69), channel_id=1, source_target_pairs={{0,24},{1,25},{2,26},{3,27},{4,28},{5,29},{6,30},{7,31},{8,16},{9,... | collective-permute-start | bytes 393224 | tf_op jit(solution)/shard_map/ppermute | solution.py:265
  101.6 8.9 %collective-permute-start.25 = (bf16[128,512]{1,0:T(8,128)(2,1)S(1)}, bf16[128,512]{1,0:T(8,128)(2,1)S(1)}, u32[]{:S(2)}, u32[]{:S(2)}) collective-permute-start(bf16[128,512]{1,0:T(8,128)(2,1)S(1)} %get-tuple-element.70), channel_id=1, source_target_pairs={{0,8},{1,9},{2,10},{3,11},{4,12},{5,13},{6,14},{7,15},{8,0},{9,1},... | collective-permute-start | bytes 393224 | tf_op jit(solution)/shard_map/ppermute | solution.py:265

commit v11 on v10

--- a/solution.py
+++ b/solution.py
@@ -10,6 +10,7 @@
 
 BLOCK = 128
 CHUNKS = 2
+GRAD_ROWS = 256
 AXES = ("node", "local")
 
 
@@ -220,22 +221,23 @@
     )
 
 
-def weight_grad(which, features, d_both, scale, mask, marks_shape, earlier, grads=None):
+def weight_grad(first, count, features, d_both, scale, mask, marks_shape, earlier, grads=None):
     total, owned = features.shape
     group = d_both.shape[2]
-    step = min(owned, 256)
+    step = min(owned, GRAD_ROWS)
+    parts = owned // step
     operands = [features, in_vmem(d_both), mask, earlier] + ([] if grads is None else [grads])
     return pl.pallas_call(
         functools.partial(weight_grad_kernel, scale),
-        grid=(owned // step,),
+        grid=(count,),
         in_specs=[
-            pl.BlockSpec((total, step), lambda i: (0, i)),
-            pl.BlockSpec((1, total, group), lambda i: (which, 0, 0)),
+            pl.BlockSpec((total, step), lambda i: (0, (first + i) % parts)),
+            pl.BlockSpec((1, total, group), lambda i: ((first + i) // parts, 0, 0)),
             pl.BlockSpec(memory_space=pltpu.SMEM),
         ]
         + [pl.BlockSpec(memory_space=pl.ANY)] * (len(operands) - 3),
         out_specs=[
-            pl.BlockSpec((1, step, group), lambda i: (which, i, 0)),
+            pl.BlockSpec((1, step, group), lambda i: ((first + i) // parts, (first + i) % parts, 0)),
             pl.BlockSpec(marks_shape, lambda i: (0, 0)),
         ],
         out_shape=[
@@ -363,12 +365,16 @@
     arrived[0] = summed[0]
     flat = joined([mine] + others).reshape(total, owned)
     scale = 1.0 / math.sqrt(rows * places)
-    grads, marks = weight_grad(0, flat, d_all, scale, mask, marks.shape, summed[0][:16])
+    blocks = 2 * (owned // min(owned, GRAD_ROWS))
+    early = max(1, 2 * blocks // 8)
+    grads, marks = weight_grad(0, early, flat, d_all, scale, mask, marks.shape, summed[0][:16])
     arrived = [pick(arrived, j, marks) for j in range(places)]
     summands = [arrived[0]] + [
         permute(arrived[j], lambda p, h, q: (p ^ j, h, q)) for j in reversed(far_first)
     ]
-    grads, marks = weight_grad(1, flat, d_all, scale, mask, marks.shape, arrived[0][:16], grads)
+    grads, marks = weight_grad(
+        early, blocks - early, flat, d_all, scale, mask, marks.shape, arrived[0][:16], grads
+    )
     summands[0] = after(summands[0], marks)
     d_tokens = sum(x.astype(jnp.float32) for x in summands).astype(jnp.bfloat16)
     return jnp.concatenate(hidden_a + hidden_b), d_tokens, grads

time: 111 us -> 111 us (level)
  transfers between devices with their start and end apart: 28 -> 28, of which waited for: 17 -> 16; matrix products, arithmetic and copies ran while one was open for 2% -> 2% of each run, Pallas kernels for 17% -> 17%
where the time goes in v11:
time: 111 us
  waiting for transfers between devices  46 us (41%)
  starting transfers between devices  38.6 us (35%)
  Pallas kernels  21.5 us (19%)
  other arithmetic  3.15 us (3%)
    ppermute x28, waiting for transfers between devices, permute(): return lax.ppermute(x, AXES, pairs(move, places, ratio))  46 us
    ppermute x28, starting transfers between devices, permute(): return lax.ppermute(x, AXES, pairs(move, places, ratio))  38.6 us
    pallas_call x2, Pallas kernels, weight_grad(): pl.pallas_call(functools.partial(weight_grad_kernel, scale), grid=(count,...  9.38 us
    pallas_call x3, Pallas kernels, input_grad(): pl.pallas_call(functools.partial(input_grad_kernel, spots, es, first, cou...  4.53 us
    pallas_call x1, Pallas kernels, dequant(): pl.pallas_call(dequant_kernel, in_specs=[pl.BlockSpec(memory_space=pltpu....  3.24 us
    pallas_call x2, Pallas kernels, partial_sums(): pl.pallas_call(functools.partial(partial_sums_kernel, list(xs), bool(summ...  3.19 us
  transfers between devices with their start and end apart: 28, of which 16 were waited for; matrix products, arithmetic and copies ran while one was open for 2% of the time, Pallas kernels for 17%

profile of v11, /device:TPU:0, one launch (start us, length us, event | category | flops | bytes accessed | tf_op | source)
XLA Modules:
  0.0 111.3 jit_solution(4243517153377362686)
XLA Ops:
  0.6 3.1 %collective-permute-start = (bf16[128,512]{1,0:T(8,128)(2,1)}, bf16[128,512]{1,0:T(8,128)(2,1)S(1)}, u32[]{:S(2)}, u32[]{:S(2)}) collective-permute-start(bf16[128,512]{1,0:T(8,128)(2,1)} %param.4), channel_id=1, source_target_pairs={{0,8},{1,0},{2,24},{3,16},{4,12},{5,4},{6,28},{7,20},{8,9},{9,1},{... | collective-permute-start | bytes 393224 | tf_op jit(solution)/shard_map/ppermute | solution.py:267
  3.7 2.4 %collective-permute-start.1 = (bf16[128,512]{1,0:T(8,128)(2,1)}, bf16[128,512]{1,0:T(8,128)(2,1)S(1)}, u32[]{:S(2)}, u32[]{:S(2)}) collective-permute-start(bf16[128,512]{1,0:T(8,128)(2,1)} %param.4), channel_id=1, source_target_pairs={{0,16},{1,24},{2,0},{3,8},{4,20},{5,28},{6,4},{7,12},{8,17},{9,25}... | collective-permute-start | bytes 393224 | tf_op jit(solution)/shard_map/ppermute | solution.py:267
  6.1 2.5 %collective-permute-start.2 = (bf16[128,512]{1,0:T(8,128)(2,1)}, bf16[128,512]{1,0:T(8,128)(2,1)S(1)}, u32[]{:S(2)}, u32[]{:S(2)}) collective-permute-start(bf16[128,512]{1,0:T(8,128)(2,1)} %param.4), channel_id=1, source_target_pairs={{0,24},{1,16},{2,8},{3,0},{4,28},{5,20},{6,12},{7,4},{8,25},{9,17}... | collective-permute-start | bytes 393224 | tf_op jit(solution)/shard_map/ppermute | solution.py:267
  8.6 1.6 %collective-permute-start.3 = (bf16[128,512]{1,0:T(8,128)(2,1)}, bf16[128,512]{1,0:T(8,128)(2,1)S(1)}, u32[]{:S(2)}, u32[]{:S(2)}) collective-permute-start(bf16[128,512]{1,0:T(8,128)(2,1)} %param.4), channel_id=1, source_target_pairs={{0,0},{1,8},{2,16},{3,24},{4,4},{5,12},{6,20},{7,28},{8,1},{9,9},{... | collective-permute-start | bytes 393224 | tf_op jit(solution)/shard_map/ppermute | solution.py:267
  11.0 3.2 %shard_map.67 = (bf16[2,1024,1792]{2,1,0:T(8,128)(2,1)S(1)}, f32[4,512]{1,0:T(4,128)S(1)}) custom-call(s32[1]{0:T(128)} %bitcast.1.mask_ref, bf16[2,1024,1792]{2,1,0:T(8,128)(2,1)} %codes_ref.1, bf16[2,8,1792]{2,1,0:T(8,128)(2,1)S(1)} %copy-done), custom_call_target="tpu_custom_call" | custom-call | tf_op jit(solution)/shard_map/pallas_call | solution.py:55
  17.6 8.5 %collective-permute-start.9 = (bf16[2,2,32,1792]{3,2,1,0:T(8,128)(2,1)S(1)}, bf16[2,2,32,1792]{3,2,1,0:T(8,128)(2,1)S(1)}, u32[]{:S(2)}, u32[]{:S(2)}) collective-permute-start(bf16[2,2,32,1792]{3,2,1,0:T(8,128)(2,1)S(1)} %get-tuple-element.38), channel_id=1, source_target_pairs={{0,1},{1,0},{2,3},{3,2},{4,5},{5,4},{6,7},{7,6},{8,9},{9,8},{10,11... | collective-permute-start | bytes 1376264 | tf_op jit(solution)/shard_map/ppermute | solution.py:267
  26.0 2.1 %shard_map.68 = (bf16[2,2,32,1792]{3,2,1,0:T(8,128)(2,1)S(1)}, f32[2,2,32,1792]{3,2,1,0:T(8,128)S(1)}, bf16[2,2,32,1792]{3,2,1,0:T(8,128)(2,1)S(1)}, f32[2,2,32,1792]{3,2,1,0:T(8,128)S(1)}) custom-call(s32[1]{0:T(128)} %bitcast.half_ref.index_ref, bf16[4,128,512]{2,1,0:T(8,128)(2,1)S(1)} %pad_maximum_fusion.refs_0_.x_ref, ...), custom_call_target="tpu_custom_call" | custom-call | tf_op jit(solution)/shard_map/pallas_call | solution.py:167
  28.1 2.1 %collective-permute-start.7 = (bf16[2,2,32,1792]{3,2,1,0:T(8,128)(2,1)S(1)}, bf16[2,2,32,1792]{3,2,1,0:T(8,128)(2,1)S(1)}, u32[]{:S(2)}, u32[]{:S(2)}) collective-permute-start(bf16[2,2,32,1792]{3,2,1,0:T(8,128)(2,1)S(1)} %get-tuple-element.36), channel_id=1, source_target_pairs={{0,2},{1,3},{2,0},{3,1},{4,6},{5,7},{6,4},{7,5},{8,10},{9,11},{10,... | collective-permute-start | bytes 1376264 | tf_op jit(solution)/shard_map/ppermute | solution.py:267
  30.3 7.0 %collective-permute-done.9 = bf16[2,2,32,1792]{3,2,1,0:T(8,128)(2,1)S(1)} collective-permute-done((bf16[2,2,32,1792]{3,2,1,0:T(8,128)(2,1)S(1)}, bf16[2,2,32,1792]{3,2,1,0:T(8,128)(2,1)S(1)}, u32[]{:S(2)}, u32[]{:S(2)}) %collective-permute-start.9) | collective-permute-done | bytes 458784 | tf_op jit(solution)/shard_map/ppermute | solution.py:267
  37.5 1.8 %collective-permute-start.10 = (bf16[2,1,32,1792]{3,2,1,0:T(8,128)(2,1)S(1)}, bf16[2,1,32,1792]{3,2,1,0:T(8,128)(2,1)S(1)}, u32[]{:S(2)}, u32[]{:S(2)}) collective-permute-start(bf16[2,1,32,1792]{3,2,1,0:T(8,128)(2,1)S(1)} %slice.183), channel_id=1, source_target_pairs={{0,2},{1,3},{2,0},{3,1},{4,6},{5,7},{6,4},{7,5},{8,10},{9,11},{10,... | collective-permute-start | bytes 688136 | tf_op jit(solution)/shard_map/ppermute | solution.py:267
  39.8 7.4 %collective-permute-done.5 = bf16[2,2,32,1792]{3,2,1,0:T(8,128)(2,1)S(1)} collective-permute-done((bf16[2,2,32,1792]{3,2,1,0:T(8,128)(2,1)S(1)}, bf16[2,2,32,1792]{3,2,1,0:T(8,128)(2,1)S(1)}, u32[]{:S(2)}, u32[]{:S(2)}) %collective-permute-start.5) | collective-permute-done | bytes 458784 | tf_op jit(solution)/shard_map/ppermute | solution.py:267
  47.3 1.8 %collective-permute-start.6 = (bf16[2,1,32,1792]{3,2,1,0:T(8,128)(2,1)S(1)}, bf16[2,1,32,1792]{3,2,1,0:T(8,128)(2,1)S(1)}, u32[]{:S(2)}, u32[]{:S(2)}) collective-permute-start(bf16[2,1,32,1792]{3,2,1,0:T(8,128)(2,1)S(1)} %slice.185), channel_id=1, source_target_pairs={{0,2},{1,3},{2,0},{3,1},{4,6},{5,7},{6,4},{7,5},{8,10},{9,11},{10,... | collective-permute-start | bytes 688136 | tf_op jit(solution)/shard_map/ppermute | solution.py:267
  49.6 4.5 %collective-permute-done.10 = bf16[2,1,32,1792]{3,2,1,0:T(8,128)(2,1)S(1)} collective-permute-done((bf16[2,1,32,1792]{3,2,1,0:T(8,128)(2,1)S(1)}, bf16[2,1,32,1792]{3,2,1,0:T(8,128)(2,1)S(1)}, u32[]{:S(2)}, u32[]{:S(2)}) %collective-permute-start.10) | collective-permute-done | bytes 229408 | tf_op jit(solution)/shard_map/ppermute | solution.py:267
  54.8 1.7 %collective-permute-start.18 = (bf16[2,2,32,1792]{3,2,1,0:T(8,128)(2,1)S(1)}, bf16[2,2,32,1792]{3,2,1,0:T(8,128)(2,1)S(1)}, u32[]{:S(2)}, u32[]{:S(2)}) collective-permute-start(bf16[2,2,32,1792]{3,2,1,0:T(8,128)(2,1)S(1)} %maximum_maximum_fusion.refs_0_), channel_id=1, source_target_pairs={{0,2},{1,3},{2,0},{3,1},{4,6},{5,7},{6,4},{7,5},{8,10},{9,11},{10,... | collective-permute-start | bytes 1376264 | tf_op jit(solution)/shard_map/ppermute | solution.py:267
  56.4 2.7 %collective-permute-done.6 = bf16[2,1,32,1792]{3,2,1,0:T(8,128)(2,1)S(1)} collective-permute-done((bf16[2,1,32,1792]{3,2,1,0:T(8,128)(2,1)S(1)}, bf16[2,1,32,1792]{3,2,1,0:T(8,128)(2,1)S(1)}, u32[]{:S(2)}, u32[]{:S(2)}) %collective-permute-start.6) | collective-permute-done | bytes 229408 | tf_op jit(solution)/shard_map/ppermute | solution.py:267
  59.7 1.7 %collective-permute-start.15 = (bf16[2,2,32,1792]{3,2,1,0:T(8,128)(2,1)S(1)}, bf16[2,2,32,1792]{3,2,1,0:T(8,128)(2,1)S(1)}, u32[]{:S(2)}, u32[]{:S(2)}) collective-permute-start(bf16[2,2,32,1792]{3,2,1,0:T(8,128)(2,1)S(1)} %maximum_maximum_fusion.1.refs_5_), channel_id=1, source_target_pairs={{0,2},{1,3},{2,0},{3,1},{4,6},{5,7},{6,4},{7,5},{8,10},{9,11},{10,... | collective-permute-start | bytes 1376264 | tf_op jit(solution)/shard_map/ppermute | solution.py:267
  61.3 6.9 %collective-permute-done.17.refs_1_ = bf16[2,2,32,1792]{3,2,1,0:T(8,128)(2,1)S(1)} collective-permute-done((bf16[2,2,32,1792]{3,2,1,0:T(8,128)(2,1)S(1)}, bf16[2,2,32,1792]{3,2,1,0:T(8,128)(2,1)S(1)}, u32[]{:S(2)}, u32[]{:S(2)}) %collective-permute-start.17) | collective-permute-done | bytes 458784 | tf_op jit(solution)/shard_map/ppermute | solution.py:267
  68.9 1.3 %collective-permute-start.20 = (bf16[1,2,32,1792]{3,2,1,0:T(8,128)(2,1)S(1)}, bf16[1,2,32,1792]{3,2,1,0:T(8,128)(2,1)S(1)}, u32[]{:S(2)}, u32[]{:S(2)}) collective-permute-start(bf16[1,2,32,1792]{3,2,1,0:T(8,128)(2,1)S(1)} %slice.153), channel_id=1, source_target_pairs={{0,1},{1,0},{2,3},{3,2},{4,5},{5,4},{6,7},{7,6},{8,9},{9,8},{10,11... | collective-permute-start | bytes 688136 | tf_op jit(solution)/shard_map/ppermute | solution.py:267
  70.3 7.7 %collective-permute-done.13.refs_6_ = bf16[2,2,32,1792]{3,2,1,0:T(8,128)(2,1)S(1)} collective-permute-done((bf16[2,2,32,1792]{3,2,1,0:T(8,128)(2,1)S(1)}, bf16[2,2,32,1792]{3,2,1,0:T(8,128)(2,1)S(1)}, u32[]{:S(2)}, u32[]{:S(2)}) %collective-permute-start.13) | collective-permute-done | bytes 458784 | tf_op jit(solution)/shard_map/ppermute | solution.py:267
  78.8 1.3 %collective-permute-start.16 = (bf16[1,2,32,1792]{3,2,1,0:T(8,128)(2,1)S(1)}, bf16[1,2,32,1792]{3,2,1,0:T(8,128)(2,1)S(1)}, u32[]{:S(2)}, u32[]{:S(2)}) collective-permute-start(bf16[1,2,32,1792]{3,2,1,0:T(8,128)(2,1)S(1)} %slice.151), channel_id=1, source_target_pairs={{0,1},{1,0},{2,3},{3,2},{4,5},{5,4},{6,7},{7,6},{8,9},{9,8},{10,11... | collective-permute-start | bytes 688136 | tf_op jit(solution)/shard_map/ppermute | solution.py:267
  80.1 3.5 %collective-permute-done.19.refs_3_ = bf16[1,2,32,1792]{3,2,1,0:T(8,128)(2,1)S(1)} collective-permute-done((bf16[1,2,32,1792]{3,2,1,0:T(8,128)(2,1)S(1)}, bf16[1,2,32,1792]{3,2,1,0:T(8,128)(2,1)S(1)}, u32[]{:S(2)}, u32[]{:S(2)}) %collective-permute-start.19) | collective-permute-done | bytes 229408 | tf_op jit(solution)/shard_map/ppermute | solution.py:267
  83.7 2.2 %shard_map.72 = (bf16[2,512,1792]{2,1,0:T(8,128)(2,1)S(1)}, bf16[512,512]{1,0:T(8,128)(2,1)S(1)}, bf16[512,512]{1,0:T(8,128)(2,1)S(1)}) custom-call(s32[1]{0:T(128)} %bitcast.half_ref.index_ref, bf16[2,2,32,1792]{3,2,1,0:T(8,128)(2,1)S(1)} %maximum_maximum_fusion.refs_0_, bf16[2,2,32,1792]{3,2,1,0:T(8,128)(2,1)S(1)} %collective-permute-done.17.refs_1_, ...), custom_call_target="tpu_custom_call" | custom-call | tf_op jit(solution)/shard_map/pallas_call | solution.py:202
  85.9 1.5 %collective-permute-done.14.refs_0_ = bf16[1,2,32,1792]{3,2,1,0:T(8,128)(2,1)S(1)} collective-permute-done((bf16[1,2,32,1792]{3,2,1,0:T(8,128)(2,1)S(1)}, bf16[1,2,32,1792]{3,2,1,0:T(8,128)(2,1)S(1)}, u32[]{:S(2)}, u32[]{:S(2)}) %collective-permute-start.14) | collective-permute-done | bytes 229408 | tf_op jit(solution)/shard_map/ppermute | solution.py:267
  87.5 1.1 %shard_map.73 = (bf16[2,512,1792]{2,1,0:T(8,128)(2,1)S(1)}, bf16[512,512]{1,0:T(8,128)(2,1)S(1)}) custom-call(s32[1]{0:T(128)} %bitcast.half_ref.index_ref, bf16[1,2,32,1792]{3,2,1,0:T(8,128)(2,1)S(1)} %collective-permute-done.14.refs_0_, bf16[1,2,32,1792]{3,2,1,0:T(8,128)(2,1)S(1)} %collective-permute-done.16.refs_1_, ...), custom_call_target="tpu_custom_call", output_to_operand_aliasing={{0}: (4, {}), {1}: (5, {})} | custom-call | tf_op jit(solution)/shard_map/pallas_call | solution.py:202
  88.7 1.1 %shard_map.74 = (bf16[2,512,1792]{2,1,0:T(8,128)(2,1)S(1)}, bf16[512,512]{1,0:T(8,128)(2,1)S(1)}) custom-call(s32[1]{0:T(128)} %bitcast.half_ref.index_ref, bf16[2,1024,1792]{2,1,0:T(8,128)(2,1)S(1)} %get-tuple-element.32.refs_2_.w_ref.refs_1_.refs_8_.refs_0_, ...), custom_call_target="tpu_custom_call", output_to_operand_aliasing={{0}: (2, {}), {1}: (3, {})} | custom-call | tf_op jit(solution)/shard_map/pallas_call | solution.py:202
  91.2 1.3 %collective-permute-start.23 = (bf16[128,512]{1,0:T(8,128)(2,1)S(1)}, bf16[128,512]{1,0:T(8,128)(2,1)S(1)}, u32[]{:S(2)}, u32[]{:S(2)}) collective-permute-start(bf16[128,512]{1,0:T(8,128)(2,1)S(1)} %bitcast.129), channel_id=1, source_target_pairs={{0,2},{1,3},{2,0},{3,1},{4,6},{5,7},{6,4},{7,5},{8,10},{9,11},{10,... | collective-permute-start | bytes 393224 | tf_op jit(solution)/shard_map/ppermute | solution.py:267
  92.5 1.8 %collective-permute-start.24 = (bf16[128,512]{1,0:T(8,128)(2,1)S(1)}, bf16[128,512]{1,0:T(8,128)(2,1)S(1)}, u32[]{:S(2)}, u32[]{:S(2)}) collective-permute-start(bf16[128,512]{1,0:T(8,128)(2,1)S(1)} %bitcast.128), channel_id=1, source_target_pairs={{0,3},{1,2},{2,1},{3,0},{4,7},{5,6},{6,5},{7,4},{8,11},{9,10},{10,... | collective-permute-start | bytes 393224 | tf_op jit(solution)/shard_map/ppermute | solution.py:267
  94.4 2.8 %shard_map.75 = (f32[2,1024,1792]{2,1,0:T(8,128)}, f32[4,512]{1,0:T(4,128)S(1)}) custom-call(bf16[512,1024]{1,0:T(8,128)(2,1)S(1)} %bitcast.124, bf16[2,512,1792]{2,1,0:T(8,128)(2,1)S(1)} %get-tuple-element.47.d_ref, s32[1]{0:T(128)} %bitcast.1.mask_ref, bf16[16,512]{1,0:T(8,128)(2,1)S(1)} %slice.155.refs_0_), custom_call_target="tpu_custom_call" | custom-call | tf_op jit(solution)/shard_map/pallas_call | solution.py:230
  97.2 2.0 %collective-permute-done.23 = bf16[128,512]{1,0:T(8,128)(2,1)S(1)} collective-permute-done((bf16[128,512]{1,0:T(8,128)(2,1)S(1)}, bf16[128,512]{1,0:T(8,128)(2,1)S(1)}, u32[]{:S(2)}, u32[]{:S(2)}) %collective-permute-start.23) | collective-permute-done | bytes 131104 | tf_op jit(solution)/shard_map/ppermute | solution.py:267
  99.8 1.8 %collective-permute-start.26 = (bf16[128,512]{1,0:T(8,128)(2,1)S(1)}, bf16[128,512]{1,0:T(8,128)(2,1)S(1)}, u32[]{:S(2)}, u32[]{:S(2)}) collective-permute-start(bf16[128,512]{1,0:T(8,128)(2,1)S(1)} %get-tuple-element.69), channel_id=1, source_target_pairs={{0,24},{1,25},{2,26},{3,27},{4,28},{5,29},{6,30},{7,31},{8,16},{9,... | collective-permute-start | bytes 393224 | tf_op jit(solution)/shard_map/ppermute | solution.py:267
  101.6 1.3 %collective-permute-start.25 = (bf16[128,512]{1,0:T(8,128)(2,1)S(1)}, bf16[128,512]{1,0:T(8,128)(2,1)S(1)}, u32[]{:S(2)}, u32[]{:S(2)}) collective-permute-start(bf16[128,512]{1,0:T(8,128)(2,1)S(1)} %get-tuple-element.70), channel_id=1, source_target_pairs={{0,8},{1,9},{2,10},{3,11},{4,12},{5,13},{6,14},{7,15},{8,0},{9,1},... | collective-permute-start | bytes 393224 | tf_op jit(solution)/shard_map/ppermute | solution.py:267
  103.7 6.6 %shard_map.76 = (f32[2,1024,1792]{2,1,0:T(8,128)}, f32[4,512]{1,0:T(4,128)}) custom-call(bf16[512,1024]{1,0:T(8,128)(2,1)S(1)} %bitcast.125, bf16[2,512,1792]{2,1,0:T(8,128)(2,1)S(1)} %get-tuple-element.47.d_ref, s32[1]{0:T(128)} %bitcast.1.mask_ref, bf16[16,512]{1,0:T(8,128)(2,1)S(1)} %slice.159.refs_0_, ...), custom_call_target="tpu_custom_call", output_to_operand_aliasing={{0}: (4, {})} | custom-call | tf_op jit(solution)/shard_map/pallas_call | solution.py:230
  (68 shorter events, 11.9 us)
Async XLA Ops:
  0.6 13.6 %collective-permute-start = (bf16[128,512]{1,0:T(8,128)(2,1)}, bf16[128,512]{1,0:T(8,128)(2,1)S(1)}, u32[]{:S(2)}, u32[]{:S(2)}) collective-permute-start(bf16[128,512]{1,0:T(8,128)(2,1)} %param.4), channel_id=1, source_target_pairs={{0,8},{1,0},{2,24},{3,16},{4,12},{5,4},{6,28},{7,20},{8,9},{9,1},{... | collective-permute-start | bytes 393224 | tf_op jit(solution)/shard_map/ppermute | solution.py:267
  3.7 10.6 %collective-permute-start.1 = (bf16[128,512]{1,0:T(8,128)(2,1)}, bf16[128,512]{1,0:T(8,128)(2,1)S(1)}, u32[]{:S(2)}, u32[]{:S(2)}) collective-permute-start(bf16[128,512]{1,0:T(8,128)(2,1)} %param.4), channel_id=1, source_target_pairs={{0,16},{1,24},{2,0},{3,8},{4,20},{5,28},{6,4},{7,12},{8,17},{9,25}... | collective-permute-start | bytes 393224 | tf_op jit(solution)/shard_map/ppermute | solution.py:267
  6.1 8.2 %collective-permute-start.2 = (bf16[128,512]{1,0:T(8,128)(2,1)}, bf16[128,512]{1,0:T(8,128)(2,1)S(1)}, u32[]{:S(2)}, u32[]{:S(2)}) collective-permute-start(bf16[128,512]{1,0:T(8,128)(2,1)} %param.4), channel_id=1, source_target_pairs={{0,24},{1,16},{2,8},{3,0},{4,28},{5,20},{6,12},{7,4},{8,25},{9,17}... | collective-permute-start | bytes 393224 | tf_op jit(solution)/shard_map/ppermute | solution.py:267
  8.6 5.7 %collective-permute-start.3 = (bf16[128,512]{1,0:T(8,128)(2,1)}, bf16[128,512]{1,0:T(8,128)(2,1)S(1)}, u32[]{:S(2)}, u32[]{:S(2)}) collective-permute-start(bf16[128,512]{1,0:T(8,128)(2,1)} %param.4), channel_id=1, source_target_pairs={{0,0},{1,8},{2,16},{3,24},{4,4},{5,12},{6,20},{7,28},{8,1},{9,9},{... | collective-permute-start | bytes 393224 | tf_op jit(solution)/shard_map/ppermute | solution.py:267
  10.2 0.8 copy-start
  14.5 2.0 %collective-permute-start.4 = (bf16[4,128,512]{2,1,0:T(8,128)(2,1)S(1)}, bf16[4,128,512]{2,1,0:T(8,128)(2,1)S(1)}, u32[]{:S(2)}, u32[]{:S(2)}) collective-permute-start(bf16[4,128,512]{2,1,0:T(8,128)(2,1)S(1)} %pad_maximum_fusion.refs_0_.x_ref), channel_id=1, source_target_pairs={{0,4},{1,5},{2,6},{3,7},{4,0},{5,1},{6,2},{7,3},{8,12},{9,13},{10,... | collective-permute-start | bytes 1572872 | tf_op jit(solution)/shard_map/ppermute | solution.py:267
  17.6 19.8 %collective-permute-start.9 = (bf16[2,2,32,1792]{3,2,1,0:T(8,128)(2,1)S(1)}, bf16[2,2,32,1792]{3,2,1,0:T(8,128)(2,1)S(1)}, u32[]{:S(2)}, u32[]{:S(2)}) collective-permute-start(bf16[2,2,32,1792]{3,2,1,0:T(8,128)(2,1)S(1)} %get-tuple-element.38), channel_id=1, source_target_pairs={{0,1},{1,0},{2,3},{3,2},{4,5},{5,4},{6,7},{7,6},{8,9},{9,8},{10,11... | collective-permute-start | bytes 1376264 | tf_op jit(solution)/shard_map/ppermute | solution.py:267
  26.0 13.4 %collective-permute-start.11 = (bf16[2,2,32,1792]{3,2,1,0:T(8,128)(2,1)S(1)}, bf16[2,2,32,1792]{3,2,1,0:T(8,128)(2,1)S(1)}, u32[]{:S(2)}, u32[]{:S(2)}) collective-permute-start(bf16[2,2,32,1792]{3,2,1,0:T(8,128)(2,1)S(1)} %get-tuple-element.40), channel_id=1, source_target_pairs={{0,2},{1,3},{2,0},{3,1},{4,6},{5,7},{6,4},{7,5},{8,10},{9,11},{10,... | collective-permute-start | bytes 1376264 | tf_op jit(solution)/shard_map/ppermute | solution.py:267
  28.1 26.2 %copy-start.1 = (bf16[128,1792]{1,0:T(8,128)(2,1)S(1)}, bf16[128,1792]{1,0:T(8,128)(2,1)}, u32[]{:S(2)}) copy-start(bf16[128,1792]{1,0:T(8,128)(2,1)} %param.7) | copy-start | bytes 1376260
  28.1 21.1 %collective-permute-start.7 = (bf16[2,2,32,1792]{3,2,1,0:T(8,128)(2,1)S(1)}, bf16[2,2,32,1792]{3,2,1,0:T(8,128)(2,1)S(1)}, u32[]{:S(2)}, u32[]{:S(2)}) collective-permute-start(bf16[2,2,32,1792]{3,2,1,0:T(8,128)(2,1)S(1)} %get-tuple-element.36), channel_id=1, source_target_pairs={{0,2},{1,3},{2,0},{3,1},{4,6},{5,7},{6,4},{7,5},{8,10},{9,11},{10,... | collective-permute-start | bytes 1376264 | tf_op jit(solution)/shard_map/ppermute | solution.py:267
  30.2 17.0 %collective-permute-start.5 = (bf16[2,2,32,1792]{3,2,1,0:T(8,128)(2,1)S(1)}, bf16[2,2,32,1792]{3,2,1,0:T(8,128)(2,1)S(1)}, u32[]{:S(2)}, u32[]{:S(2)}) collective-permute-start(bf16[2,2,32,1792]{3,2,1,0:T(8,128)(2,1)S(1)} %get-tuple-element.34), channel_id=1, source_target_pairs={{0,1},{1,0},{2,3},{3,2},{4,5},{5,4},{6,7},{7,6},{8,9},{9,8},{10,11... | collective-permute-start | bytes 1376264 | tf_op jit(solution)/shard_map/ppermute | solution.py:267
  37.5 16.7 %collective-permute-start.10 = (bf16[2,1,32,1792]{3,2,1,0:T(8,128)(2,1)S(1)}, bf16[2,1,32,1792]{3,2,1,0:T(8,128)(2,1)S(1)}, u32[]{:S(2)}, u32[]{:S(2)}) collective-permute-start(bf16[2,1,32,1792]{3,2,1,0:T(8,128)(2,1)S(1)} %slice.183), channel_id=1, source_target_pairs={{0,2},{1,3},{2,0},{3,1},{4,6},{5,7},{6,4},{7,5},{8,10},{9,11},{10,... | collective-permute-start | bytes 688136 | tf_op jit(solution)/shard_map/ppermute | solution.py:267
  39.5 14.7 %collective-permute-start.12 = (bf16[2,1,32,1792]{3,2,1,0:T(8,128)(2,1)S(1)}, bf16[2,1,32,1792]{3,2,1,0:T(8,128)(2,1)S(1)}, u32[]{:S(2)}, u32[]{:S(2)}) collective-permute-start(bf16[2,1,32,1792]{3,2,1,0:T(8,128)(2,1)S(1)} %slice.182), channel_id=1, source_target_pairs={{0,1},{1,0},{2,3},{3,2},{4,5},{5,4},{6,7},{7,6},{8,9},{9,8},{10,11... | collective-permute-start | bytes 688136 | tf_op jit(solution)/shard_map/ppermute | solution.py:267
  47.3 11.8 %collective-permute-start.6 = (bf16[2,1,32,1792]{3,2,1,0:T(8,128)(2,1)S(1)}, bf16[2,1,32,1792]{3,2,1,0:T(8,128)(2,1)S(1)}, u32[]{:S(2)}, u32[]{:S(2)}) collective-permute-start(bf16[2,1,32,1792]{3,2,1,0:T(8,128)(2,1)S(1)} %slice.185), channel_id=1, source_target_pairs={{0,2},{1,3},{2,0},{3,1},{4,6},{5,7},{6,4},{7,5},{8,10},{9,11},{10,... | collective-permute-start | bytes 688136 | tf_op jit(solution)/shard_map/ppermute | solution.py:267
  49.4 9.7 %collective-permute-start.8 = (bf16[2,1,32,1792]{3,2,1,0:T(8,128)(2,1)S(1)}, bf16[2,1,32,1792]{3,2,1,0:T(8,128)(2,1)S(1)}, u32[]{:S(2)}, u32[]{:S(2)}) collective-permute-start(bf16[2,1,32,1792]{3,2,1,0:T(8,128)(2,1)S(1)} %slice.184), channel_id=1, source_target_pairs={{0,1},{1,0},{2,3},{3,2},{4,5},{5,4},{6,7},{7,6},{8,9},{9,8},{10,11... | collective-permute-start | bytes 688136 | tf_op jit(solution)/shard_map/ppermute | solution.py:267
  54.7 13.5 %collective-permute-start.17 = (bf16[2,2,32,1792]{3,2,1,0:T(8,128)(2,1)S(1)}, bf16[2,2,32,1792]{3,2,1,0:T(8,128)(2,1)S(1)}, u32[]{:S(2)}, u32[]{:S(2)}) collective-permute-start(bf16[2,2,32,1792]{3,2,1,0:T(8,128)(2,1)S(1)} %maximum_maximum_fusion.refs_0_), channel_id=1, source_target_pairs={{0,1},{1,0},{2,3},{3,2},{4,5},{5,4},{6,7},{7,6},{8,9},{9,8},{10,11... | collective-permute-start | bytes 1376264 | tf_op jit(solution)/shard_map/ppermute | solution.py:267
  54.8 14.2 %collective-permute-start.18 = (bf16[2,2,32,1792]{3,2,1,0:T(8,128)(2,1)S(1)}, bf16[2,2,32,1792]{3,2,1,0:T(8,128)(2,1)S(1)}, u32[]{:S(2)}, u32[]{:S(2)}) collective-permute-start(bf16[2,2,32,1792]{3,2,1,0:T(8,128)(2,1)S(1)} %maximum_maximum_fusion.refs_0_), channel_id=1, source_target_pairs={{0,2},{1,3},{2,0},{3,1},{4,6},{5,7},{6,4},{7,5},{8,10},{9,11},{10,... | collective-permute-start | bytes 1376264 | tf_op jit(solution)/shard_map/ppermute | solution.py:267
  59.5 18.5 %collective-permute-start.13 = (bf16[2,2,32,1792]{3,2,1,0:T(8,128)(2,1)S(1)}, bf16[2,2,32,1792]{3,2,1,0:T(8,128)(2,1)S(1)}, u32[]{:S(2)}, u32[]{:S(2)}) collective-permute-start(bf16[2,2,32,1792]{3,2,1,0:T(8,128)(2,1)S(1)} %maximum_maximum_fusion.1.refs_5_), channel_id=1, source_target_pairs={{0,1},{1,0},{2,3},{3,2},{4,5},{5,4},{6,7},{7,6},{8,9},{9,8},{10,11... | collective-permute-start | bytes 1376264 | tf_op jit(solution)/shard_map/ppermute | solution.py:267
  59.7 19.1 %collective-permute-start.15 = (bf16[2,2,32,1792]{3,2,1,0:T(8,128)(2,1)S(1)}, bf16[2,2,32,1792]{3,2,1,0:T(8,128)(2,1)S(1)}, u32[]{:S(2)}, u32[]{:S(2)}) collective-permute-start(bf16[2,2,32,1792]{3,2,1,0:T(8,128)(2,1)S(1)} %maximum_maximum_fusion.1.refs_5_), channel_id=1, source_target_pairs={{0,2},{1,3},{2,0},{3,1},{4,6},{5,7},{6,4},{7,5},{8,10},{9,11},{10,... | collective-permute-start | bytes 1376264 | tf_op jit(solution)/shard_map/ppermute | solution.py:267
  68.2 15.5 %collective-permute-start.19 = (bf16[1,2,32,1792]{3,2,1,0:T(8,128)(2,1)S(1)}, bf16[1,2,32,1792]{3,2,1,0:T(8,128)(2,1)S(1)}, u32[]{:S(2)}, u32[]{:S(2)}) collective-permute-start(bf16[1,2,32,1792]{3,2,1,0:T(8,128)(2,1)S(1)} %slice.152), channel_id=1, source_target_pairs={{0,2},{1,3},{2,0},{3,1},{4,6},{5,7},{6,4},{7,5},{8,10},{9,11},{10,... | collective-permute-start | bytes 688136 | tf_op jit(solution)/shard_map/ppermute | solution.py:267
  68.9 14.7 %collective-permute-start.20 = (bf16[1,2,32,1792]{3,2,1,0:T(8,128)(2,1)S(1)}, bf16[1,2,32,1792]{3,2,1,0:T(8,128)(2,1)S(1)}, u32[]{:S(2)}, u32[]{:S(2)}) collective-permute-start(bf16[1,2,32,1792]{3,2,1,0:T(8,128)(2,1)S(1)} %slice.153), channel_id=1, source_target_pairs={{0,1},{1,0},{2,3},{3,2},{4,5},{5,4},{6,7},{7,6},{8,9},{9,8},{10,11... | collective-permute-start | bytes 688136 | tf_op jit(solution)/shard_map/ppermute | solution.py:267
  78.0 9.4 %collective-permute-start.14 = (bf16[1,2,32,1792]{3,2,1,0:T(8,128)(2,1)S(1)}, bf16[1,2,32,1792]{3,2,1,0:T(8,128)(2,1)S(1)}, u32[]{:S(2)}, u32[]{:S(2)}) collective-permute-start(bf16[1,2,32,1792]{3,2,1,0:T(8,128)(2,1)S(1)} %slice.150), channel_id=1, source_target_pairs={{0,2},{1,3},{2,0},{3,1},{4,6},{5,7},{6,4},{7,5},{8,10},{9,11},{10,... | collective-permute-start | bytes 688136 | tf_op jit(solution)/shard_map/ppermute | solution.py:267
  78.8 8.7 %collective-permute-start.16 = (bf16[1,2,32,1792]{3,2,1,0:T(8,128)(2,1)S(1)}, bf16[1,2,32,1792]{3,2,1,0:T(8,128)(2,1)S(1)}, u32[]{:S(2)}, u32[]{:S(2)}) collective-permute-start(bf16[1,2,32,1792]{3,2,1,0:T(8,128)(2,1)S(1)} %slice.151), channel_id=1, source_target_pairs={{0,1},{1,0},{2,3},{3,2},{4,5},{5,4},{6,7},{7,6},{8,9},{9,8},{10,11... | collective-permute-start | bytes 688136 | tf_op jit(solution)/shard_map/ppermute | solution.py:267
  88.6 2.0 %collective-permute-start.21 = (bf16[512,512]{1,0:T(8,128)(2,1)S(1)}, bf16[512,512]{1,0:T(8,128)(2,1)S(1)}, u32[]{:S(2)}, u32[]{:S(2)}) collective-permute-start(bf16[512,512]{1,0:T(8,128)(2,1)S(1)} %get-tuple-element.49), channel_id=1, source_target_pairs={{0,4},{1,5},{2,6},{3,7},{4,0},{5,1},{6,2},{7,3},{8,12},{9,13},{10,... | collective-permute-start | bytes 1572872 | tf_op jit(solution)/shard_map/ppermute | solution.py:267
  90.8 6.5 %collective-permute-start.22 = (bf16[128,512]{1,0:T(8,128)(2,1)S(1)}, bf16[128,512]{1,0:T(8,128)(2,1)S(1)}, u32[]{:S(2)}, u32[]{:S(2)}) collective-permute-start(bf16[128,512]{1,0:T(8,128)(2,1)S(1)} %bitcast.130), channel_id=1, source_target_pairs={{0,1},{1,0},{2,3},{3,2},{4,5},{5,4},{6,7},{7,6},{8,9},{9,8},{10,11... | collective-permute-start | bytes 393224 | tf_op jit(solution)/shard_map/ppermute | solution.py:267
  91.2 8.1 %collective-permute-start.23 = (bf16[128,512]{1,0:T(8,128)(2,1)S(1)}, bf16[128,512]{1,0:T(8,128)(2,1)S(1)}, u32[]{:S(2)}, u32[]{:S(2)}) collective-permute-start(bf16[128,512]{1,0:T(8,128)(2,1)S(1)} %bitcast.129), channel_id=1, source_target_pairs={{0,2},{1,3},{2,0},{3,1},{4,6},{5,7},{6,4},{7,5},{8,10},{9,11},{10,... | collective-permute-start | bytes 393224 | tf_op jit(solution)/shard_map/ppermute | solution.py:267
  92.5 6.7 %collective-permute-start.24 = (bf16[128,512]{1,0:T(8,128)(2,1)S(1)}, bf16[128,512]{1,0:T(8,128)(2,1)S(1)}, u32[]{:S(2)}, u32[]{:S(2)}) collective-permute-start(bf16[128,512]{1,0:T(8,128)(2,1)S(1)} %bitcast.128), channel_id=1, source_target_pairs={{0,3},{1,2},{2,1},{3,0},{4,7},{5,6},{6,5},{7,4},{8,11},{9,10},{10,... | collective-permute-start | bytes 393224 | tf_op jit(solution)/shard_map/ppermute | solution.py:267
  99.4 11.0 %collective-permute-start.27 = (bf16[128,512]{1,0:T(8,128)(2,1)S(1)}, bf16[128,512]{1,0:T(8,128)(2,1)S(1)}, u32[]{:S(2)}, u32[]{:S(2)}) collective-permute-start(bf16[128,512]{1,0:T(8,128)(2,1)S(1)} %get-tuple-element.68), channel_id=1, source_target_pairs={{0,16},{1,17},{2,18},{3,19},{4,20},{5,21},{6,22},{7,23},{8,24},{9,... | collective-permute-start | bytes 393224 | tf_op jit(solution)/shard_map/ppermute | solution.py:267
  99.8 10.5 %collective-permute-start.26 = (bf16[128,512]{1,0:T(8,128)(2,1)S(1)}, bf16[128,512]{1,0:T(8,128)(2,1)S(1)}, u32[]{:S(2)}, u32[]{:S(2)}) collective-permute-start(bf16[128,512]{1,0:T(8,128)(2,1)S(1)} %get-tuple-element.69), channel_id=1, source_target_pairs={{0,24},{1,25},{2,26},{3,27},{4,28},{5,29},{6,30},{7,31},{8,16},{9,... | collective-permute-start | bytes 393224 | tf_op jit(solution)/shard_map/ppermute | solution.py:267
  101.6 8.9 %collective-permute-start.25 = (bf16[128,512]{1,0:T(8,128)(2,1)S(1)}, bf16[128,512]{1,0:T(8,128)(2,1)S(1)}, u32[]{:S(2)}, u32[]{:S(2)}) collective-permute-start(bf16[128,512]{1,0:T(8,128)(2,1)S(1)} %get-tuple-element.70), channel_id=1, source_target_pairs={{0,8},{1,9},{2,10},{3,11},{4,12},{5,13},{6,14},{7,15},{8,0},{9,1},... | collective-permute-start | bytes 393224 | tf_op jit(solution)/shard_map/ppermute | solution.py:267

commit v12 on v10

--- a/solution.py
+++ b/solution.py
@@ -344,7 +344,7 @@
     d_all, own_term, *other_terms = input_grad(
         pieces_b + pieces_a[:near],
         spots_b + spots_a[:near],
-        w_gu, half, list(range(ratio)), ratio, total, count, count, hidden_a + hidden_b,
+        w_gu, half, list(range(ratio)), ratio, total, count, count, hidden_b + hidden_a,
     )
     d_all, *other_terms = input_grad(
         pieces_a[near:],

time: 111 us -> 111 us (level)
  no operation moved by 1% of the time
where the time goes in v12:
time: 111 us
  waiting for transfers between devices  46.1 us (42%)
  starting transfers between devices  38.6 us (35%)
  Pallas kernels  21.5 us (19%)
  other arithmetic  3.15 us (3%)
    ppermute x28, waiting for transfers between devices, permute(): return lax.ppermute(x, AXES, pairs(move, places, ratio))  46.1 us
    ppermute x28, starting transfers between devices, permute(): return lax.ppermute(x, AXES, pairs(move, places, ratio))  38.6 us
    pallas_call x2, Pallas kernels, weight_grad(): pl.pallas_call(functools.partial(weight_grad_kernel, scale), grid=(owned...  9.32 us
    pallas_call x3, Pallas kernels, input_grad(): pl.pallas_call(functools.partial(input_grad_kernel, spots, es, first, cou...  4.53 us
    pallas_call x1, Pallas kernels, dequant(): pl.pallas_call(dequant_kernel, in_specs=[pl.BlockSpec(memory_space=pltpu....  3.24 us
    pallas_call x2, Pallas kernels, partial_sums(): pl.pallas_call(functools.partial(partial_sums_kernel, list(xs), bool(summ...  3.19 us
  transfers between devices with their start and end apart: 28, of which 17 were waited for; matrix products, arithmetic and copies ran while one was open for 2% of the time, Pallas kernels for 17%

profile of v12, /device:TPU:0, one launch (start us, length us, event | category | flops | bytes accessed | tf_op | source)
XLA Modules:
  0.0 111.3 jit_solution(14445444517190385798)
XLA Ops:
  0.6 3.1 %collective-permute-start = (bf16[128,512]{1,0:T(8,128)(2,1)}, bf16[128,512]{1,0:T(8,128)(2,1)S(1)}, u32[]{:S(2)}, u32[]{:S(2)}) collective-permute-start(bf16[128,512]{1,0:T(8,128)(2,1)} %param.4), channel_id=1, source_target_pairs={{0,8},{1,0},{2,24},{3,16},{4,12},{5,4},{6,28},{7,20},{8,9},{9,1},{... | collective-permute-start | bytes 393224 | tf_op jit(solution)/shard_map/ppermute | solution.py:265
  3.7 2.4 %collective-permute-start.1 = (bf16[128,512]{1,0:T(8,128)(2,1)}, bf16[128,512]{1,0:T(8,128)(2,1)S(1)}, u32[]{:S(2)}, u32[]{:S(2)}) collective-permute-start(bf16[128,512]{1,0:T(8,128)(2,1)} %param.4), channel_id=1, source_target_pairs={{0,16},{1,24},{2,0},{3,8},{4,20},{5,28},{6,4},{7,12},{8,17},{9,25}... | collective-permute-start | bytes 393224 | tf_op jit(solution)/shard_map/ppermute | solution.py:265
  6.1 2.5 %collective-permute-start.2 = (bf16[128,512]{1,0:T(8,128)(2,1)}, bf16[128,512]{1,0:T(8,128)(2,1)S(1)}, u32[]{:S(2)}, u32[]{:S(2)}) collective-permute-start(bf16[128,512]{1,0:T(8,128)(2,1)} %param.4), channel_id=1, source_target_pairs={{0,24},{1,16},{2,8},{3,0},{4,28},{5,20},{6,12},{7,4},{8,25},{9,17}... | collective-permute-start | bytes 393224 | tf_op jit(solution)/shard_map/ppermute | solution.py:265
  8.6 1.6 %collective-permute-start.3 = (bf16[128,512]{1,0:T(8,128)(2,1)}, bf16[128,512]{1,0:T(8,128)(2,1)S(1)}, u32[]{:S(2)}, u32[]{:S(2)}) collective-permute-start(bf16[128,512]{1,0:T(8,128)(2,1)} %param.4), channel_id=1, source_target_pairs={{0,0},{1,8},{2,16},{3,24},{4,4},{5,12},{6,20},{7,28},{8,1},{9,9},{... | collective-permute-start | bytes 393224 | tf_op jit(solution)/shard_map/ppermute | solution.py:265
  11.0 3.2 %shard_map.67 = (bf16[2,1024,1792]{2,1,0:T(8,128)(2,1)S(1)}, f32[4,512]{1,0:T(4,128)S(1)}) custom-call(s32[1]{0:T(128)} %bitcast.1.mask_ref, bf16[2,1024,1792]{2,1,0:T(8,128)(2,1)} %codes_ref.1, bf16[2,8,1792]{2,1,0:T(8,128)(2,1)S(1)} %copy-done), custom_call_target="tpu_custom_call" | custom-call | tf_op jit(solution)/shard_map/pallas_call | solution.py:54
  17.6 8.5 %collective-permute-start.9 = (bf16[2,2,32,1792]{3,2,1,0:T(8,128)(2,1)S(1)}, bf16[2,2,32,1792]{3,2,1,0:T(8,128)(2,1)S(1)}, u32[]{:S(2)}, u32[]{:S(2)}) collective-permute-start(bf16[2,2,32,1792]{3,2,1,0:T(8,128)(2,1)S(1)} %get-tuple-element.38), channel_id=1, source_target_pairs={{0,1},{1,0},{2,3},{3,2},{4,5},{5,4},{6,7},{7,6},{8,9},{9,8},{10,11... | collective-permute-start | bytes 1376264 | tf_op jit(solution)/shard_map/ppermute | solution.py:265
  26.0 2.1 %shard_map.68 = (bf16[2,2,32,1792]{3,2,1,0:T(8,128)(2,1)S(1)}, f32[2,2,32,1792]{3,2,1,0:T(8,128)S(1)}, bf16[2,2,32,1792]{3,2,1,0:T(8,128)(2,1)S(1)}, f32[2,2,32,1792]{3,2,1,0:T(8,128)S(1)}) custom-call(s32[1]{0:T(128)} %bitcast.half_ref.index_ref, bf16[4,128,512]{2,1,0:T(8,128)(2,1)S(1)} %pad_maximum_fusion.refs_0_.x_ref, ...), custom_call_target="tpu_custom_call" | custom-call | tf_op jit(solution)/shard_map/pallas_call | solution.py:166
  28.1 2.1 %collective-permute-start.7 = (bf16[2,2,32,1792]{3,2,1,0:T(8,128)(2,1)S(1)}, bf16[2,2,32,1792]{3,2,1,0:T(8,128)(2,1)S(1)}, u32[]{:S(2)}, u32[]{:S(2)}) collective-permute-start(bf16[2,2,32,1792]{3,2,1,0:T(8,128)(2,1)S(1)} %get-tuple-element.36), channel_id=1, source_target_pairs={{0,2},{1,3},{2,0},{3,1},{4,6},{5,7},{6,4},{7,5},{8,10},{9,11},{10,... | collective-permute-start | bytes 1376264 | tf_op jit(solution)/shard_map/ppermute | solution.py:265
  30.3 7.0 %collective-permute-done.9 = bf16[2,2,32,1792]{3,2,1,0:T(8,128)(2,1)S(1)} collective-permute-done((bf16[2,2,32,1792]{3,2,1,0:T(8,128)(2,1)S(1)}, bf16[2,2,32,1792]{3,2,1,0:T(8,128)(2,1)S(1)}, u32[]{:S(2)}, u32[]{:S(2)}) %collective-permute-start.9) | collective-permute-done | bytes 458784 | tf_op jit(solution)/shard_map/ppermute | solution.py:265
  37.5 1.8 %collective-permute-start.10 = (bf16[2,1,32,1792]{3,2,1,0:T(8,128)(2,1)S(1)}, bf16[2,1,32,1792]{3,2,1,0:T(8,128)(2,1)S(1)}, u32[]{:S(2)}, u32[]{:S(2)}) collective-permute-start(bf16[2,1,32,1792]{3,2,1,0:T(8,128)(2,1)S(1)} %slice.183), channel_id=1, source_target_pairs={{0,2},{1,3},{2,0},{3,1},{4,6},{5,7},{6,4},{7,5},{8,10},{9,11},{10,... | collective-permute-start | bytes 688136 | tf_op jit(solution)/shard_map/ppermute | solution.py:265
  39.8 7.4 %collective-permute-done.5 = bf16[2,2,32,1792]{3,2,1,0:T(8,128)(2,1)S(1)} collective-permute-done((bf16[2,2,32,1792]{3,2,1,0:T(8,128)(2,1)S(1)}, bf16[2,2,32,1792]{3,2,1,0:T(8,128)(2,1)S(1)}, u32[]{:S(2)}, u32[]{:S(2)}) %collective-permute-start.5) | collective-permute-done | bytes 458784 | tf_op jit(solution)/shard_map/ppermute | solution.py:265
  47.3 1.8 %collective-permute-start.6 = (bf16[2,1,32,1792]{3,2,1,0:T(8,128)(2,1)S(1)}, bf16[2,1,32,1792]{3,2,1,0:T(8,128)(2,1)S(1)}, u32[]{:S(2)}, u32[]{:S(2)}) collective-permute-start(bf16[2,1,32,1792]{3,2,1,0:T(8,128)(2,1)S(1)} %slice.185), channel_id=1, source_target_pairs={{0,2},{1,3},{2,0},{3,1},{4,6},{5,7},{6,4},{7,5},{8,10},{9,11},{10,... | collective-permute-start | bytes 688136 | tf_op jit(solution)/shard_map/ppermute | solution.py:265
  49.6 4.5 %collective-permute-done.10 = bf16[2,1,32,1792]{3,2,1,0:T(8,128)(2,1)S(1)} collective-permute-done((bf16[2,1,32,1792]{3,2,1,0:T(8,128)(2,1)S(1)}, bf16[2,1,32,1792]{3,2,1,0:T(8,128)(2,1)S(1)}, u32[]{:S(2)}, u32[]{:S(2)}) %collective-permute-start.10) | collective-permute-done | bytes 229408 | tf_op jit(solution)/shard_map/ppermute | solution.py:265
  54.8 1.7 %collective-permute-start.18 = (bf16[2,2,32,1792]{3,2,1,0:T(8,128)(2,1)S(1)}, bf16[2,2,32,1792]{3,2,1,0:T(8,128)(2,1)S(1)}, u32[]{:S(2)}, u32[]{:S(2)}) collective-permute-start(bf16[2,2,32,1792]{3,2,1,0:T(8,128)(2,1)S(1)} %maximum_maximum_fusion.refs_0_), channel_id=1, source_target_pairs={{0,2},{1,3},{2,0},{3,1},{4,6},{5,7},{6,4},{7,5},{8,10},{9,11},{10,... | collective-permute-start | bytes 1376264 | tf_op jit(solution)/shard_map/ppermute | solution.py:265
  56.4 2.7 %collective-permute-done.6 = bf16[2,1,32,1792]{3,2,1,0:T(8,128)(2,1)S(1)} collective-permute-done((bf16[2,1,32,1792]{3,2,1,0:T(8,128)(2,1)S(1)}, bf16[2,1,32,1792]{3,2,1,0:T(8,128)(2,1)S(1)}, u32[]{:S(2)}, u32[]{:S(2)}) %collective-permute-start.6) | collective-permute-done | bytes 229408 | tf_op jit(solution)/shard_map/ppermute | solution.py:265
  59.7 1.7 %collective-permute-start.15 = (bf16[2,2,32,1792]{3,2,1,0:T(8,128)(2,1)S(1)}, bf16[2,2,32,1792]{3,2,1,0:T(8,128)(2,1)S(1)}, u32[]{:S(2)}, u32[]{:S(2)}) collective-permute-start(bf16[2,2,32,1792]{3,2,1,0:T(8,128)(2,1)S(1)} %maximum_maximum_fusion.1.refs_5_), channel_id=1, source_target_pairs={{0,2},{1,3},{2,0},{3,1},{4,6},{5,7},{6,4},{7,5},{8,10},{9,11},{10,... | collective-permute-start | bytes 1376264 | tf_op jit(solution)/shard_map/ppermute | solution.py:265
  61.3 6.9 %collective-permute-done.17.refs_1_ = bf16[2,2,32,1792]{3,2,1,0:T(8,128)(2,1)S(1)} collective-permute-done((bf16[2,2,32,1792]{3,2,1,0:T(8,128)(2,1)S(1)}, bf16[2,2,32,1792]{3,2,1,0:T(8,128)(2,1)S(1)}, u32[]{:S(2)}, u32[]{:S(2)}) %collective-permute-start.17) | collective-permute-done | bytes 458784 | tf_op jit(solution)/shard_map/ppermute | solution.py:265
  68.9 1.3 %collective-permute-start.20 = (bf16[1,2,32,1792]{3,2,1,0:T(8,128)(2,1)S(1)}, bf16[1,2,32,1792]{3,2,1,0:T(8,128)(2,1)S(1)}, u32[]{:S(2)}, u32[]{:S(2)}) collective-permute-start(bf16[1,2,32,1792]{3,2,1,0:T(8,128)(2,1)S(1)} %slice.153), channel_id=1, source_target_pairs={{0,1},{1,0},{2,3},{3,2},{4,5},{5,4},{6,7},{7,6},{8,9},{9,8},{10,11... | collective-permute-start | bytes 688136 | tf_op jit(solution)/shard_map/ppermute | solution.py:265
  70.3 7.7 %collective-permute-done.13.refs_6_ = bf16[2,2,32,1792]{3,2,1,0:T(8,128)(2,1)S(1)} collective-permute-done((bf16[2,2,32,1792]{3,2,1,0:T(8,128)(2,1)S(1)}, bf16[2,2,32,1792]{3,2,1,0:T(8,128)(2,1)S(1)}, u32[]{:S(2)}, u32[]{:S(2)}) %collective-permute-start.13) | collective-permute-done | bytes 458784 | tf_op jit(solution)/shard_map/ppermute | solution.py:265
  78.8 1.3 %collective-permute-start.16 = (bf16[1,2,32,1792]{3,2,1,0:T(8,128)(2,1)S(1)}, bf16[1,2,32,1792]{3,2,1,0:T(8,128)(2,1)S(1)}, u32[]{:S(2)}, u32[]{:S(2)}) collective-permute-start(bf16[1,2,32,1792]{3,2,1,0:T(8,128)(2,1)S(1)} %slice.151), channel_id=1, source_target_pairs={{0,1},{1,0},{2,3},{3,2},{4,5},{5,4},{6,7},{7,6},{8,9},{9,8},{10,11... | collective-permute-start | bytes 688136 | tf_op jit(solution)/shard_map/ppermute | solution.py:265
  80.1 3.5 %collective-permute-done.19.refs_3_ = bf16[1,2,32,1792]{3,2,1,0:T(8,128)(2,1)S(1)} collective-permute-done((bf16[1,2,32,1792]{3,2,1,0:T(8,128)(2,1)S(1)}, bf16[1,2,32,1792]{3,2,1,0:T(8,128)(2,1)S(1)}, u32[]{:S(2)}, u32[]{:S(2)}) %collective-permute-start.19) | collective-permute-done | bytes 229408 | tf_op jit(solution)/shard_map/ppermute | solution.py:265
  83.7 2.2 %shard_map.72 = (bf16[2,512,1792]{2,1,0:T(8,128)(2,1)S(1)}, bf16[512,512]{1,0:T(8,128)(2,1)S(1)}, bf16[512,512]{1,0:T(8,128)(2,1)S(1)}) custom-call(s32[1]{0:T(128)} %bitcast.half_ref.index_ref, bf16[2,2,32,1792]{3,2,1,0:T(8,128)(2,1)S(1)} %maximum_maximum_fusion.refs_0_, bf16[2,2,32,1792]{3,2,1,0:T(8,128)(2,1)S(1)} %collective-permute-done.17.refs_1_, ...), custom_call_target="tpu_custom_call" | custom-call | tf_op jit(solution)/shard_map/pallas_call | solution.py:201
  85.9 1.5 %collective-permute-done.14.refs_0_ = bf16[1,2,32,1792]{3,2,1,0:T(8,128)(2,1)S(1)} collective-permute-done((bf16[1,2,32,1792]{3,2,1,0:T(8,128)(2,1)S(1)}, bf16[1,2,32,1792]{3,2,1,0:T(8,128)(2,1)S(1)}, u32[]{:S(2)}, u32[]{:S(2)}) %collective-permute-start.14) | collective-permute-done | bytes 229408 | tf_op jit(solution)/shard_map/ppermute | solution.py:265
  87.5 1.1 %shard_map.73 = (bf16[2,512,1792]{2,1,0:T(8,128)(2,1)S(1)}, bf16[512,512]{1,0:T(8,128)(2,1)S(1)}) custom-call(s32[1]{0:T(128)} %bitcast.half_ref.index_ref, bf16[1,2,32,1792]{3,2,1,0:T(8,128)(2,1)S(1)} %collective-permute-done.14.refs_0_, bf16[1,2,32,1792]{3,2,1,0:T(8,128)(2,1)S(1)} %collective-permute-done.16.refs_1_, ...), custom_call_target="tpu_custom_call", output_to_operand_aliasing={{0}: (4, {}), {1}: (5, {})} | custom-call | tf_op jit(solution)/shard_map/pallas_call | solution.py:201
  88.7 1.1 %shard_map.74 = (bf16[2,512,1792]{2,1,0:T(8,128)(2,1)S(1)}, bf16[512,512]{1,0:T(8,128)(2,1)S(1)}) custom-call(s32[1]{0:T(128)} %bitcast.half_ref.index_ref, bf16[2,1024,1792]{2,1,0:T(8,128)(2,1)S(1)} %get-tuple-element.32.refs_2_.w_ref.refs_1_.refs_8_.refs_0_, ...), custom_call_target="tpu_custom_call", output_to_operand_aliasing={{0}: (2, {}), {1}: (3, {})} | custom-call | tf_op jit(solution)/shard_map/pallas_call | solution.py:201
  91.2 1.3 %collective-permute-start.23 = (bf16[128,512]{1,0:T(8,128)(2,1)S(1)}, bf16[128,512]{1,0:T(8,128)(2,1)S(1)}, u32[]{:S(2)}, u32[]{:S(2)}) collective-permute-start(bf16[128,512]{1,0:T(8,128)(2,1)S(1)} %bitcast.129), channel_id=1, source_target_pairs={{0,2},{1,3},{2,0},{3,1},{4,6},{5,7},{6,4},{7,5},{8,10},{9,11},{10,... | collective-permute-start | bytes 393224 | tf_op jit(solution)/shard_map/ppermute | solution.py:265
  92.5 1.8 %collective-permute-start.24 = (bf16[128,512]{1,0:T(8,128)(2,1)S(1)}, bf16[128,512]{1,0:T(8,128)(2,1)S(1)}, u32[]{:S(2)}, u32[]{:S(2)}) collective-permute-start(bf16[128,512]{1,0:T(8,128)(2,1)S(1)} %bitcast.128), channel_id=1, source_target_pairs={{0,3},{1,2},{2,1},{3,0},{4,7},{5,6},{6,5},{7,4},{8,11},{9,10},{10,... | collective-permute-start | bytes 393224 | tf_op jit(solution)/shard_map/ppermute | solution.py:265
  94.4 4.7 %shard_map.75 = (f32[2,1024,1792]{2,1,0:T(8,128)}, f32[4,512]{1,0:T(4,128)S(1)}) custom-call(bf16[512,1024]{1,0:T(8,128)(2,1)S(1)} %bitcast.124, bf16[2,512,1792]{2,1,0:T(8,128)(2,1)S(1)} %get-tuple-element.47.d_ref, s32[1]{0:T(128)} %bitcast.1.mask_ref, bf16[16,512]{1,0:T(8,128)(2,1)S(1)} %slice.155.refs_0_), custom_call_target="tpu_custom_call" | custom-call | tf_op jit(solution)/shard_map/pallas_call | solution.py:228
  99.8 1.8 %collective-permute-start.26 = (bf16[128,512]{1,0:T(8,128)(2,1)S(1)}, bf16[128,512]{1,0:T(8,128)(2,1)S(1)}, u32[]{:S(2)}, u32[]{:S(2)}) collective-permute-start(bf16[128,512]{1,0:T(8,128)(2,1)S(1)} %get-tuple-element.69), channel_id=1, source_target_pairs={{0,24},{1,25},{2,26},{3,27},{4,28},{5,29},{6,30},{7,31},{8,16},{9,... | collective-permute-start | bytes 393224 | tf_op jit(solution)/shard_map/ppermute | solution.py:265
  101.6 1.3 %collective-permute-start.25 = (bf16[128,512]{1,0:T(8,128)(2,1)S(1)}, bf16[128,512]{1,0:T(8,128)(2,1)S(1)}, u32[]{:S(2)}, u32[]{:S(2)}) collective-permute-start(bf16[128,512]{1,0:T(8,128)(2,1)S(1)} %get-tuple-element.70), channel_id=1, source_target_pairs={{0,8},{1,9},{2,10},{3,11},{4,12},{5,13},{6,14},{7,15},{8,0},{9,1},... | collective-permute-start | bytes 393224 | tf_op jit(solution)/shard_map/ppermute | solution.py:265
  103.7 4.6 %shard_map.76 = (f32[2,1024,1792]{2,1,0:T(8,128)}, f32[4,512]{1,0:T(4,128)}) custom-call(bf16[512,1024]{1,0:T(8,128)(2,1)S(1)} %bitcast.125, bf16[2,512,1792]{2,1,0:T(8,128)(2,1)S(1)} %get-tuple-element.47.d_ref, s32[1]{0:T(128)} %bitcast.1.mask_ref, bf16[16,512]{1,0:T(8,128)(2,1)S(1)} %slice.159.refs_0_, ...), custom_call_target="tpu_custom_call", output_to_operand_aliasing={{0}: (4, {})} | custom-call | tf_op jit(solution)/shard_map/pallas_call | solution.py:228
  108.4 2.0 %collective-permute-done.27 = bf16[128,512]{1,0:T(8,128)(2,1)S(1)} collective-permute-done((bf16[128,512]{1,0:T(8,128)(2,1)S(1)}, bf16[128,512]{1,0:T(8,128)(2,1)S(1)}, u32[]{:S(2)}, u32[]{:S(2)}) %collective-permute-start.27) | collective-permute-done | bytes 131104 | tf_op jit(solution)/shard_map/ppermute | solution.py:265
  (68 shorter events, 12.0 us)
Async XLA Ops:
  0.6 13.6 %collective-permute-start = (bf16[128,512]{1,0:T(8,128)(2,1)}, bf16[128,512]{1,0:T(8,128)(2,1)S(1)}, u32[]{:S(2)}, u32[]{:S(2)}) collective-permute-start(bf16[128,512]{1,0:T(8,128)(2,1)} %param.4), channel_id=1, source_target_pairs={{0,8},{1,0},{2,24},{3,16},{4,12},{5,4},{6,28},{7,20},{8,9},{9,1},{... | collective-permute-start | bytes 393224 | tf_op jit(solution)/shard_map/ppermute | solution.py:265
  3.7 10.6 %collective-permute-start.1 = (bf16[128,512]{1,0:T(8,128)(2,1)}, bf16[128,512]{1,0:T(8,128)(2,1)S(1)}, u32[]{:S(2)}, u32[]{:S(2)}) collective-permute-start(bf16[128,512]{1,0:T(8,128)(2,1)} %param.4), channel_id=1, source_target_pairs={{0,16},{1,24},{2,0},{3,8},{4,20},{5,28},{6,4},{7,12},{8,17},{9,25}... | collective-permute-start | bytes 393224 | tf_op jit(solution)/shard_map/ppermute | solution.py:265
  6.1 8.2 %collective-permute-start.2 = (bf16[128,512]{1,0:T(8,128)(2,1)}, bf16[128,512]{1,0:T(8,128)(2,1)S(1)}, u32[]{:S(2)}, u32[]{:S(2)}) collective-permute-start(bf16[128,512]{1,0:T(8,128)(2,1)} %param.4), channel_id=1, source_target_pairs={{0,24},{1,16},{2,8},{3,0},{4,28},{5,20},{6,12},{7,4},{8,25},{9,17}... | collective-permute-start | bytes 393224 | tf_op jit(solution)/shard_map/ppermute | solution.py:265
  8.6 5.7 %collective-permute-start.3 = (bf16[128,512]{1,0:T(8,128)(2,1)}, bf16[128,512]{1,0:T(8,128)(2,1)S(1)}, u32[]{:S(2)}, u32[]{:S(2)}) collective-permute-start(bf16[128,512]{1,0:T(8,128)(2,1)} %param.4), channel_id=1, source_target_pairs={{0,0},{1,8},{2,16},{3,24},{4,4},{5,12},{6,20},{7,28},{8,1},{9,9},{... | collective-permute-start | bytes 393224 | tf_op jit(solution)/shard_map/ppermute | solution.py:265
  10.2 0.8 copy-start
  14.5 2.0 %collective-permute-start.4 = (bf16[4,128,512]{2,1,0:T(8,128)(2,1)S(1)}, bf16[4,128,512]{2,1,0:T(8,128)(2,1)S(1)}, u32[]{:S(2)}, u32[]{:S(2)}) collective-permute-start(bf16[4,128,512]{2,1,0:T(8,128)(2,1)S(1)} %pad_maximum_fusion.refs_0_.x_ref), channel_id=1, source_target_pairs={{0,4},{1,5},{2,6},{3,7},{4,0},{5,1},{6,2},{7,3},{8,12},{9,13},{10,... | collective-permute-start | bytes 1572872 | tf_op jit(solution)/shard_map/ppermute | solution.py:265
  17.6 19.8 %collective-permute-start.9 = (bf16[2,2,32,1792]{3,2,1,0:T(8,128)(2,1)S(1)}, bf16[2,2,32,1792]{3,2,1,0:T(8,128)(2,1)S(1)}, u32[]{:S(2)}, u32[]{:S(2)}) collective-permute-start(bf16[2,2,32,1792]{3,2,1,0:T(8,128)(2,1)S(1)} %get-tuple-element.38), channel_id=1, source_target_pairs={{0,1},{1,0},{2,3},{3,2},{4,5},{5,4},{6,7},{7,6},{8,9},{9,8},{10,11... | collective-permute-start | bytes 1376264 | tf_op jit(solution)/shard_map/ppermute | solution.py:265
  26.0 13.4 %collective-permute-start.11 = (bf16[2,2,32,1792]{3,2,1,0:T(8,128)(2,1)S(1)}, bf16[2,2,32,1792]{3,2,1,0:T(8,128)(2,1)S(1)}, u32[]{:S(2)}, u32[]{:S(2)}) collective-permute-start(bf16[2,2,32,1792]{3,2,1,0:T(8,128)(2,1)S(1)} %get-tuple-element.40), channel_id=1, source_target_pairs={{0,2},{1,3},{2,0},{3,1},{4,6},{5,7},{6,4},{7,5},{8,10},{9,11},{10,... | collective-permute-start | bytes 1376264 | tf_op jit(solution)/shard_map/ppermute | solution.py:265
  28.1 26.2 %copy-start.1 = (bf16[128,1792]{1,0:T(8,128)(2,1)S(1)}, bf16[128,1792]{1,0:T(8,128)(2,1)}, u32[]{:S(2)}) copy-start(bf16[128,1792]{1,0:T(8,128)(2,1)} %param.7) | copy-start | bytes 1376260
  28.1 21.1 %collective-permute-start.7 = (bf16[2,2,32,1792]{3,2,1,0:T(8,128)(2,1)S(1)}, bf16[2,2,32,1792]{3,2,1,0:T(8,128)(2,1)S(1)}, u32[]{:S(2)}, u32[]{:S(2)}) collective-permute-start(bf16[2,2,32,1792]{3,2,1,0:T(8,128)(2,1)S(1)} %get-tuple-element.36), channel_id=1, source_target_pairs={{0,2},{1,3},{2,0},{3,1},{4,6},{5,7},{6,4},{7,5},{8,10},{9,11},{10,... | collective-permute-start | bytes 1376264 | tf_op jit(solution)/shard_map/ppermute | solution.py:265
  30.2 17.0 %collective-permute-start.5 = (bf16[2,2,32,1792]{3,2,1,0:T(8,128)(2,1)S(1)}, bf16[2,2,32,1792]{3,2,1,0:T(8,128)(2,1)S(1)}, u32[]{:S(2)}, u32[]{:S(2)}) collective-permute-start(bf16[2,2,32,1792]{3,2,1,0:T(8,128)(2,1)S(1)} %get-tuple-element.34), channel_id=1, source_target_pairs={{0,1},{1,0},{2,3},{3,2},{4,5},{5,4},{6,7},{7,6},{8,9},{9,8},{10,11... | collective-permute-start | bytes 1376264 | tf_op jit(solution)/shard_map/ppermute | solution.py:265
  37.5 16.7 %collective-permute-start.10 = (bf16[2,1,32,1792]{3,2,1,0:T(8,128)(2,1)S(1)}, bf16[2,1,32,1792]{3,2,1,0:T(8,128)(2,1)S(1)}, u32[]{:S(2)}, u32[]{:S(2)}) collective-permute-start(bf16[2,1,32,1792]{3,2,1,0:T(8,128)(2,1)S(1)} %slice.183), channel_id=1, source_target_pairs={{0,2},{1,3},{2,0},{3,1},{4,6},{5,7},{6,4},{7,5},{8,10},{9,11},{10,... | collective-permute-start | bytes 688136 | tf_op jit(solution)/shard_map/ppermute | solution.py:265
  39.5 14.7 %collective-permute-start.12 = (bf16[2,1,32,1792]{3,2,1,0:T(8,128)(2,1)S(1)}, bf16[2,1,32,1792]{3,2,1,0:T(8,128)(2,1)S(1)}, u32[]{:S(2)}, u32[]{:S(2)}) collective-permute-start(bf16[2,1,32,1792]{3,2,1,0:T(8,128)(2,1)S(1)} %slice.182), channel_id=1, source_target_pairs={{0,1},{1,0},{2,3},{3,2},{4,5},{5,4},{6,7},{7,6},{8,9},{9,8},{10,11... | collective-permute-start | bytes 688136 | tf_op jit(solution)/shard_map/ppermute | solution.py:265
  47.3 11.8 %collective-permute-start.6 = (bf16[2,1,32,1792]{3,2,1,0:T(8,128)(2,1)S(1)}, bf16[2,1,32,1792]{3,2,1,0:T(8,128)(2,1)S(1)}, u32[]{:S(2)}, u32[]{:S(2)}) collective-permute-start(bf16[2,1,32,1792]{3,2,1,0:T(8,128)(2,1)S(1)} %slice.185), channel_id=1, source_target_pairs={{0,2},{1,3},{2,0},{3,1},{4,6},{5,7},{6,4},{7,5},{8,10},{9,11},{10,... | collective-permute-start | bytes 688136 | tf_op jit(solution)/shard_map/ppermute | solution.py:265
  49.4 9.7 %collective-permute-start.8 = (bf16[2,1,32,1792]{3,2,1,0:T(8,128)(2,1)S(1)}, bf16[2,1,32,1792]{3,2,1,0:T(8,128)(2,1)S(1)}, u32[]{:S(2)}, u32[]{:S(2)}) collective-permute-start(bf16[2,1,32,1792]{3,2,1,0:T(8,128)(2,1)S(1)} %slice.184), channel_id=1, source_target_pairs={{0,1},{1,0},{2,3},{3,2},{4,5},{5,4},{6,7},{7,6},{8,9},{9,8},{10,11... | collective-permute-start | bytes 688136 | tf_op jit(solution)/shard_map/ppermute | solution.py:265
  54.7 13.5 %collective-permute-start.17 = (bf16[2,2,32,1792]{3,2,1,0:T(8,128)(2,1)S(1)}, bf16[2,2,32,1792]{3,2,1,0:T(8,128)(2,1)S(1)}, u32[]{:S(2)}, u32[]{:S(2)}) collective-permute-start(bf16[2,2,32,1792]{3,2,1,0:T(8,128)(2,1)S(1)} %maximum_maximum_fusion.refs_0_), channel_id=1, source_target_pairs={{0,1},{1,0},{2,3},{3,2},{4,5},{5,4},{6,7},{7,6},{8,9},{9,8},{10,11... | collective-permute-start | bytes 1376264 | tf_op jit(solution)/shard_map/ppermute | solution.py:265
  54.8 14.2 %collective-permute-start.18 = (bf16[2,2,32,1792]{3,2,1,0:T(8,128)(2,1)S(1)}, bf16[2,2,32,1792]{3,2,1,0:T(8,128)(2,1)S(1)}, u32[]{:S(2)}, u32[]{:S(2)}) collective-permute-start(bf16[2,2,32,1792]{3,2,1,0:T(8,128)(2,1)S(1)} %maximum_maximum_fusion.refs_0_), channel_id=1, source_target_pairs={{0,2},{1,3},{2,0},{3,1},{4,6},{5,7},{6,4},{7,5},{8,10},{9,11},{10,... | collective-permute-start | bytes 1376264 | tf_op jit(solution)/shard_map/ppermute | solution.py:265
  59.5 18.5 %collective-permute-start.13 = (bf16[2,2,32,1792]{3,2,1,0:T(8,128)(2,1)S(1)}, bf16[2,2,32,1792]{3,2,1,0:T(8,128)(2,1)S(1)}, u32[]{:S(2)}, u32[]{:S(2)}) collective-permute-start(bf16[2,2,32,1792]{3,2,1,0:T(8,128)(2,1)S(1)} %maximum_maximum_fusion.1.refs_5_), channel_id=1, source_target_pairs={{0,1},{1,0},{2,3},{3,2},{4,5},{5,4},{6,7},{7,6},{8,9},{9,8},{10,11... | collective-permute-start | bytes 1376264 | tf_op jit(solution)/shard_map/ppermute | solution.py:265
  59.7 19.1 %collective-permute-start.15 = (bf16[2,2,32,1792]{3,2,1,0:T(8,128)(2,1)S(1)}, bf16[2,2,32,1792]{3,2,1,0:T(8,128)(2,1)S(1)}, u32[]{:S(2)}, u32[]{:S(2)}) collective-permute-start(bf16[2,2,32,1792]{3,2,1,0:T(8,128)(2,1)S(1)} %maximum_maximum_fusion.1.refs_5_), channel_id=1, source_target_pairs={{0,2},{1,3},{2,0},{3,1},{4,6},{5,7},{6,4},{7,5},{8,10},{9,11},{10,... | collective-permute-start | bytes 1376264 | tf_op jit(solution)/shard_map/ppermute | solution.py:265
  68.2 15.5 %collective-permute-start.19 = (bf16[1,2,32,1792]{3,2,1,0:T(8,128)(2,1)S(1)}, bf16[1,2,32,1792]{3,2,1,0:T(8,128)(2,1)S(1)}, u32[]{:S(2)}, u32[]{:S(2)}) collective-permute-start(bf16[1,2,32,1792]{3,2,1,0:T(8,128)(2,1)S(1)} %slice.152), channel_id=1, source_target_pairs={{0,2},{1,3},{2,0},{3,1},{4,6},{5,7},{6,4},{7,5},{8,10},{9,11},{10,... | collective-permute-start | bytes 688136 | tf_op jit(solution)/shard_map/ppermute | solution.py:265
  68.9 14.7 %collective-permute-start.20 = (bf16[1,2,32,1792]{3,2,1,0:T(8,128)(2,1)S(1)}, bf16[1,2,32,1792]{3,2,1,0:T(8,128)(2,1)S(1)}, u32[]{:S(2)}, u32[]{:S(2)}) collective-permute-start(bf16[1,2,32,1792]{3,2,1,0:T(8,128)(2,1)S(1)} %slice.153), channel_id=1, source_target_pairs={{0,1},{1,0},{2,3},{3,2},{4,5},{5,4},{6,7},{7,6},{8,9},{9,8},{10,11... | collective-permute-start | bytes 688136 | tf_op jit(solution)/shard_map/ppermute | solution.py:265
  78.0 9.4 %collective-permute-start.14 = (bf16[1,2,32,1792]{3,2,1,0:T(8,128)(2,1)S(1)}, bf16[1,2,32,1792]{3,2,1,0:T(8,128)(2,1)S(1)}, u32[]{:S(2)}, u32[]{:S(2)}) collective-permute-start(bf16[1,2,32,1792]{3,2,1,0:T(8,128)(2,1)S(1)} %slice.150), channel_id=1, source_target_pairs={{0,2},{1,3},{2,0},{3,1},{4,6},{5,7},{6,4},{7,5},{8,10},{9,11},{10,... | collective-permute-start | bytes 688136 | tf_op jit(solution)/shard_map/ppermute | solution.py:265
  78.8 8.7 %collective-permute-start.16 = (bf16[1,2,32,1792]{3,2,1,0:T(8,128)(2,1)S(1)}, bf16[1,2,32,1792]{3,2,1,0:T(8,128)(2,1)S(1)}, u32[]{:S(2)}, u32[]{:S(2)}) collective-permute-start(bf16[1,2,32,1792]{3,2,1,0:T(8,128)(2,1)S(1)} %slice.151), channel_id=1, source_target_pairs={{0,1},{1,0},{2,3},{3,2},{4,5},{5,4},{6,7},{7,6},{8,9},{9,8},{10,11... | collective-permute-start | bytes 688136 | tf_op jit(solution)/shard_map/ppermute | solution.py:265
  88.6 2.0 %collective-permute-start.21 = (bf16[512,512]{1,0:T(8,128)(2,1)S(1)}, bf16[512,512]{1,0:T(8,128)(2,1)S(1)}, u32[]{:S(2)}, u32[]{:S(2)}) collective-permute-start(bf16[512,512]{1,0:T(8,128)(2,1)S(1)} %get-tuple-element.49), channel_id=1, source_target_pairs={{0,4},{1,5},{2,6},{3,7},{4,0},{5,1},{6,2},{7,3},{8,12},{9,13},{10,... | collective-permute-start | bytes 1572872 | tf_op jit(solution)/shard_map/ppermute | solution.py:265
  90.8 8.4 %collective-permute-start.22 = (bf16[128,512]{1,0:T(8,128)(2,1)S(1)}, bf16[128,512]{1,0:T(8,128)(2,1)S(1)}, u32[]{:S(2)}, u32[]{:S(2)}) collective-permute-start(bf16[128,512]{1,0:T(8,128)(2,1)S(1)} %bitcast.130), channel_id=1, source_target_pairs={{0,1},{1,0},{2,3},{3,2},{4,5},{5,4},{6,7},{7,6},{8,9},{9,8},{10,11... | collective-permute-start | bytes 393224 | tf_op jit(solution)/shard_map/ppermute | solution.py:265
  91.2 8.1 %collective-permute-start.23 = (bf16[128,512]{1,0:T(8,128)(2,1)S(1)}, bf16[128,512]{1,0:T(8,128)(2,1)S(1)}, u32[]{:S(2)}, u32[]{:S(2)}) collective-permute-start(bf16[128,512]{1,0:T(8,128)(2,1)S(1)} %bitcast.129), channel_id=1, source_target_pairs={{0,2},{1,3},{2,0},{3,1},{4,6},{5,7},{6,4},{7,5},{8,10},{9,11},{10,... | collective-permute-start | bytes 393224 | tf_op jit(solution)/shard_map/ppermute | solution.py:265
  92.5 6.7 %collective-permute-start.24 = (bf16[128,512]{1,0:T(8,128)(2,1)S(1)}, bf16[128,512]{1,0:T(8,128)(2,1)S(1)}, u32[]{:S(2)}, u32[]{:S(2)}) collective-permute-start(bf16[128,512]{1,0:T(8,128)(2,1)S(1)} %bitcast.128), channel_id=1, source_target_pairs={{0,3},{1,2},{2,1},{3,0},{4,7},{5,6},{6,5},{7,4},{8,11},{9,10},{10,... | collective-permute-start | bytes 393224 | tf_op jit(solution)/shard_map/ppermute | solution.py:265
  99.4 11.0 %collective-permute-start.27 = (bf16[128,512]{1,0:T(8,128)(2,1)S(1)}, bf16[128,512]{1,0:T(8,128)(2,1)S(1)}, u32[]{:S(2)}, u32[]{:S(2)}) collective-permute-start(bf16[128,512]{1,0:T(8,128)(2,1)S(1)} %get-tuple-element.68), channel_id=1, source_target_pairs={{0,16},{1,17},{2,18},{3,19},{4,20},{5,21},{6,22},{7,23},{8,24},{9,... | collective-permute-start | bytes 393224 | tf_op jit(solution)/shard_map/ppermute | solution.py:265
  99.8 10.5 %collective-permute-start.26 = (bf16[128,512]{1,0:T(8,128)(2,1)S(1)}, bf16[128,512]{1,0:T(8,128)(2,1)S(1)}, u32[]{:S(2)}, u32[]{:S(2)}) collective-permute-start(bf16[128,512]{1,0:T(8,128)(2,1)S(1)} %get-tuple-element.69), channel_id=1, source_target_pairs={{0,24},{1,25},{2,26},{3,27},{4,28},{5,29},{6,30},{7,31},{8,16},{9,... | collective-permute-start | bytes 393224 | tf_op jit(solution)/shard_map/ppermute | solution.py:265
  101.6 8.9 %collective-permute-start.25 = (bf16[128,512]{1,0:T(8,128)(2,1)S(1)}, bf16[128,512]{1,0:T(8,128)(2,1)S(1)}, u32[]{:S(2)}, u32[]{:S(2)}) collective-permute-start(bf16[128,512]{1,0:T(8,128)(2,1)S(1)} %get-tuple-element.70), channel_id=1, source_target_pairs={{0,8},{1,9},{2,10},{3,11},{4,12},{5,13},{6,14},{7,15},{8,0},{9,1},... | collective-permute-start | bytes 393224 | tf_op jit(solution)/shard_map/ppermute | solution.py:265
